TPU v7x, 32 devices: a whole 2x2x4 slice. The times are simulated.
32 devices in a mesh: groups: 2 (over y), pb: 4 (over x, core), ka: 4 (over z).
Axes of the slice: x: 2, y: 2, z: 4, core: 2. Of those that a mesh axis runs over, the one named last changes fastest.
Arguments:
- queries: bfloat16 [4096, 2048], P(('groups', 'pb')), parts along dimension 0, may hold values from -6 to 6
- keys: bfloat16 [4096, 2048], P(('groups', 'ka'), 'pb'), parts along dimension 0, may hold values from -6 to 6
- values: bfloat16 [4096, 2048], P(('groups', 'ka'), 'pb'), parts along dimension 0, may hold values from -6 to 6
- step_of: int32 [4096], P('groups'), parts along dimension 0, may hold values from 0 to 255, never falling along the last dimension, each value on 1 to 16 neighbouring positions
Outputs:
- attended: bfloat16 [4096, 2048], P(('groups', 'pb', 'ka')), parts along dimension 0
There are 2 independent parts, one for each index of `groups`. A program takes and returns all parts, laid end to end along the dimension named above; each array names one. Nothing has to cross between parts.
Inputs may be any that keep to these rules, and one draw needn't show every extreme that they name: `step_of`: never falling along the episode; a step holds 1 to 16 tokens, one step exactly 16.
All inputs are finite; a program needn't handle non-finite values.
Results may differ from a plain program's by a relative error of at most 0.015.
Values may be sent and summed in bfloat16 or wider, within the bound.
No kernel may reach another device: no remote copies, remote signals or barrier semaphores. Data moves between devices by JAX's collectives and lax.ppermute only.
A program may use at most 64 MiB of HBM per device.

v0:
```python
import math

import jax
import jax.numpy as jnp
from jax import lax
from jax.sharding import PartitionSpec as P

HEAD_DIM = 128


LOW_SCORE = -1e30


def attend_half(q_rows, q_steps, keys_all, values_all, key_steps, block_keys):
    row_count, width = q_rows.shape
    head_size = HEAD_DIM
    head_count = width // head_size
    key_count = keys_all.shape[0]
    block_count = key_count // block_keys
    factor_scale = 1.0 / math.sqrt(head_size)
    q_heads = q_rows.reshape(row_count, head_count, head_size)
    blocks = (
        keys_all.reshape(block_count, block_keys, head_count, head_size),
        values_all.reshape(block_count, block_keys, head_count, head_size),
        key_steps.reshape(block_count, block_keys),
    )
    last_step = q_steps[row_count - 1]

    def compute(carry, key_block, value_block, step_block):
        run_max, run_sum, run_out = carry
        scores = (
            jnp.einsum("rhd,khd->hkr", q_heads, key_block, preferred_element_type=jnp.float32)
            * factor_scale
        )
        visible = step_block[None, :, None] <= q_steps[None, None, :]
        masked = jnp.where(visible, scores, LOW_SCORE)
        new_max = jnp.maximum(run_max, jnp.max(masked, axis=1))
        weights = jnp.where(visible, jnp.exp(masked - new_max[:, None, :]), 0.0)
        rescale = jnp.exp(run_max - new_max)
        new_sum = run_sum * rescale + jnp.sum(weights, axis=1)
        update = jnp.einsum(
            "hkr,khd->rhd",
            weights.astype(jnp.bfloat16),
            value_block,
            preferred_element_type=jnp.float32,
        )
        new_out = run_out * jnp.transpose(rescale)[:, :, None] + update
        return (new_max, new_sum, new_out)

    def visit(carry, block):
        key_block, value_block, step_block = block
        result = lax.cond(
            step_block[0] <= last_step,
            lambda state: compute(state, key_block, value_block, step_block),
            lambda state: state,
            carry,
        )
        return (result, None)

    initial = (
        jnp.full((head_count, row_count), LOW_SCORE, jnp.float32),
        jnp.zeros((head_count, row_count), jnp.float32),
        jnp.zeros((row_count, head_count, head_size), jnp.float32),
    )
    final_state, unused = lax.scan(visit, initial, blocks)
    return final_state


def on_device(queries, keys, values, step_of):
    block_rows, width = queries.shape
    head_size = HEAD_DIM
    head_count = width // head_size
    key_parts = lax.axis_size("ka")
    query_index = lax.axis_index("pb")
    key_index = lax.axis_index("ka")
    shard_rows = block_rows // key_parts
    half_rows = block_rows // 2
    key_count = keys.shape[0]
    first_steps = lax.dynamic_slice_in_dim(step_of, query_index * block_rows, half_rows)
    second_steps = lax.dynamic_slice_in_dim(
        step_of, query_index * block_rows + half_rows, half_rows
    )
    keys_mine, values_mine = (keys, values)
    key_steps = lax.dynamic_slice_in_dim(step_of, key_index * key_count, key_count)
    keys_all, values_all = (
        lax.all_gather(keys_mine, "pb", axis=1, tiled=True),
        lax.all_gather(values_mine, "pb", axis=1, tiled=True),
    )
    block_keys = math.gcd(64, key_count)
    first_state = attend_half(
        queries[:half_rows], first_steps, keys_all, values_all, key_steps, block_keys
    )
    second_state = attend_half(
        queries[half_rows:], second_steps, keys_all, values_all, key_steps, block_keys
    )
    row_max = jnp.concatenate([first_state[0], second_state[0]], axis=1)
    row_sum = jnp.concatenate([first_state[1], second_state[1]], axis=1)
    row_out = jnp.concatenate([first_state[2], second_state[2]], axis=0)
    sent = (
        jnp.transpose(row_max)[:, None, :],
        jnp.transpose(row_sum)[:, None, :],
        row_out.reshape(block_rows, 1, width),
    )
    got_max, got_sum, got_out = (
        lax.all_to_all(sent[0], "ka", split_axis=0, concat_axis=1, tiled=True),
        lax.all_to_all(sent[1], "ka", split_axis=0, concat_axis=1, tiled=True),
        lax.all_to_all(sent[2], "ka", split_axis=0, concat_axis=1, tiled=True),
    )
    best = jnp.max(got_max, axis=1, keepdims=True)
    weight = jnp.exp(got_max - best)
    total = jnp.sum(got_sum * weight, axis=1)
    shares = weight / total[:, None, :]
    pieces = got_out.reshape(shard_rows, key_parts, head_count, head_size) * shares[:, :, :, None]
    result = jnp.sum(pieces, axis=1).reshape(shard_rows, width)
    result = result.astype(jnp.bfloat16)
    return result


def solution(mesh):
    placed = (
        P(("groups", "pb"), None),
        P(("groups", "ka"), "pb"),
        P(("groups", "ka"), "pb"),
        P("groups"),
    )
    return jax.shard_map(
        on_device,
        mesh=mesh,
        in_specs=placed,
        out_specs=P(("groups", "pb", "ka"), None),
        check_vma=False,
    )
```

profile of v0, /device:TPU:2, one launch (start us, length us, event | category | flops | bytes accessed | tf_op | source)
XLA Modules:
  0.0 303.2 jit_solution(6580827301672569453)
XLA Ops:
  15.6 16.0 %all-gather.3.cloned.1.call-done = bf16[512,2048]{1,0:T(8,128)(2,1)} async-done(((bf16[512,512]{1,0:T(8,128)(2,1)}), bf16[512,2048]{1,0:T(8,128)(2,1)}) %all-gather.3.cloned.1.call-update) | async-done | bytes 2097168 | tf_op jit(solution)/shard_map/all_gather | solution.py:86
  31.6 2.2 copy.52
  33.8 1.9 copy.35
  35.7 20.1 %all-gather.5.cloned.1.call-done = bf16[512,2048]{1,0:T(8,128)(2,1)} async-done(((bf16[512,512]{1,0:T(8,128)(2,1)}), bf16[512,2048]{1,0:T(8,128)(2,1)}) %all-gather.5.cloned.1.call-update) | async-done | bytes 2097168 | tf_op jit(solution)/shard_map/all_gather | solution.py:87
  55.8 2.2 copy.53
  60.1 40.4 %while.28 = (s32[]{:T(128)}, f32[16,256]{1,0:T(8,128)S(1)}, f32[16,256]{1,0:T(8,128)S(1)}, f32[256,16,128]{2,0,1:T(8,128)S(1)}, s32[8,64]{1,0:T(8,128)S(1)}, /*i...) while((s32[]{:T(128)}, f32[16,256]{1,0:T(8,128)S(1)}, ...), condition=%wide.region_5.6_spmd, body=%wide.region_0.5_spmd.sunk | while | flops 137654272 | bytes 9243647 | solution.py:65
  60.8 4.3 %conditional.4 = ((f32[16,256]{1,0:T(8,128)S(1)}, f32[16,256]{1,0:T(8,128)S(1)}, f32[256,16,128]{2,0,1:T(8,128)S(1)})) conditional(s32[]{:T(128)} %convert_element_type.26, (f32[16,256]{1,0:T(8,128)S(1)}, f32[16,256]{1,0:T(8,128)S(1)}, f32[256,16,128]{2,0,1:T(8,128)S(1)}) %tuple.69, (s32[1,64]{1,0:T(1,128)S(1)}, s32[256]{0:T(256)S(1)}, ...), branch_computations={%region_1.1_spmd, %region_2.4_spmd} | conditional | flops 137654272 | bytes 9242912 | solution.py:52
  62.7 2.1 bitcast_add_fusion
  65.8 4.3 %conditional.4 = ((f32[16,256]{1,0:T(8,128)S(1)}, f32[16,256]{1,0:T(8,128)S(1)}, f32[256,16,128]{2,0,1:T(8,128)S(1)})) conditional(s32[]{:T(128)} %convert_element_type.26, (f32[16,256]{1,0:T(8,128)S(1)}, f32[16,256]{1,0:T(8,128)S(1)}, f32[256,16,128]{2,0,1:T(8,128)S(1)}) %tuple.69, (s32[1,64]{1,0:T(1,128)S(1)}, s32[256]{0:T(256)S(1)}, ...), branch_computations={%region_1.1_spmd, %region_2.4_spmd} | conditional | flops 137654272 | bytes 9242912 | solution.py:52
  67.8 2.1 bitcast_add_fusion
  70.9 4.3 %conditional.4 = ((f32[16,256]{1,0:T(8,128)S(1)}, f32[16,256]{1,0:T(8,128)S(1)}, f32[256,16,128]{2,0,1:T(8,128)S(1)})) conditional(s32[]{:T(128)} %convert_element_type.26, (f32[16,256]{1,0:T(8,128)S(1)}, f32[16,256]{1,0:T(8,128)S(1)}, f32[256,16,128]{2,0,1:T(8,128)S(1)}) %tuple.69, (s32[1,64]{1,0:T(1,128)S(1)}, s32[256]{0:T(256)S(1)}, ...), branch_computations={%region_1.1_spmd, %region_2.4_spmd} | conditional | flops 137654272 | bytes 9242912 | solution.py:52
  72.8 2.1 bitcast_add_fusion
  75.9 4.3 %conditional.4 = ((f32[16,256]{1,0:T(8,128)S(1)}, f32[16,256]{1,0:T(8,128)S(1)}, f32[256,16,128]{2,0,1:T(8,128)S(1)})) conditional(s32[]{:T(128)} %convert_element_type.26, (f32[16,256]{1,0:T(8,128)S(1)}, f32[16,256]{1,0:T(8,128)S(1)}, f32[256,16,128]{2,0,1:T(8,128)S(1)}) %tuple.69, (s32[1,64]{1,0:T(1,128)S(1)}, s32[256]{0:T(256)S(1)}, ...), branch_computations={%region_1.1_spmd, %region_2.4_spmd} | conditional | flops 137654272 | bytes 9242912 | solution.py:52
  77.9 2.1 bitcast_add_fusion
  81.0 4.3 %conditional.4 = ((f32[16,256]{1,0:T(8,128)S(1)}, f32[16,256]{1,0:T(8,128)S(1)}, f32[256,16,128]{2,0,1:T(8,128)S(1)})) conditional(s32[]{:T(128)} %convert_element_type.26, (f32[16,256]{1,0:T(8,128)S(1)}, f32[16,256]{1,0:T(8,128)S(1)}, f32[256,16,128]{2,0,1:T(8,128)S(1)}) %tuple.69, (s32[1,64]{1,0:T(1,128)S(1)}, s32[256]{0:T(256)S(1)}, ...), branch_computations={%region_1.1_spmd, %region_2.4_spmd} | conditional | flops 137654272 | bytes 9242912 | solution.py:52
  82.9 2.1 bitcast_add_fusion
  86.0 4.3 %conditional.4 = ((f32[16,256]{1,0:T(8,128)S(1)}, f32[16,256]{1,0:T(8,128)S(1)}, f32[256,16,128]{2,0,1:T(8,128)S(1)})) conditional(s32[]{:T(128)} %convert_element_type.26, (f32[16,256]{1,0:T(8,128)S(1)}, f32[16,256]{1,0:T(8,128)S(1)}, f32[256,16,128]{2,0,1:T(8,128)S(1)}) %tuple.69, (s32[1,64]{1,0:T(1,128)S(1)}, s32[256]{0:T(256)S(1)}, ...), branch_computations={%region_1.1_spmd, %region_2.4_spmd} | conditional | flops 137654272 | bytes 9242912 | solution.py:52
  87.9 2.1 bitcast_add_fusion
  91.0 4.3 %conditional.4 = ((f32[16,256]{1,0:T(8,128)S(1)}, f32[16,256]{1,0:T(8,128)S(1)}, f32[256,16,128]{2,0,1:T(8,128)S(1)})) conditional(s32[]{:T(128)} %convert_element_type.26, (f32[16,256]{1,0:T(8,128)S(1)}, f32[16,256]{1,0:T(8,128)S(1)}, f32[256,16,128]{2,0,1:T(8,128)S(1)}) %tuple.69, (s32[1,64]{1,0:T(1,128)S(1)}, s32[256]{0:T(256)S(1)}, ...), branch_computations={%region_1.1_spmd, %region_2.4_spmd} | conditional | flops 137654272 | bytes 9242912 | solution.py:52
  93.0 2.1 bitcast_add_fusion
  96.1 4.3 %conditional.4 = ((f32[16,256]{1,0:T(8,128)S(1)}, f32[16,256]{1,0:T(8,128)S(1)}, f32[256,16,128]{2,0,1:T(8,128)S(1)})) conditional(s32[]{:T(128)} %convert_element_type.26, (f32[16,256]{1,0:T(8,128)S(1)}, f32[16,256]{1,0:T(8,128)S(1)}, f32[256,16,128]{2,0,1:T(8,128)S(1)}) %tuple.69, (s32[1,64]{1,0:T(1,128)S(1)}, s32[256]{0:T(256)S(1)}, ...), branch_computations={%region_1.1_spmd, %region_2.4_spmd} | conditional | flops 137654272 | bytes 9242912 | solution.py:52
  98.0 2.1 bitcast_add_fusion
  102.0 36.9 %while.29 = (s32[]{:T(128)}, f32[16,256]{1,0:T(8,128)S(1)}, f32[16,256]{1,0:T(8,128)S(1)}, f32[256,16,128]{2,0,1:T(8,128)S(1)}, s32[8,64]{1,0:T(8,128)S(1)}, /*i...) while((s32[]{:T(128)}, f32[16,256]{1,0:T(8,128)S(1)}, ...), condition=%wide.region_11.12_spmd, body=%wide.region_6.11_spmd.sunk | while | flops 137654272 | bytes 9243647 | solution.py:65
  102.6 4.0 %conditional.5 = ((f32[16,256]{1,0:T(8,128)S(1)}, f32[16,256]{1,0:T(8,128)S(1)}, f32[256,16,128]{2,0,1:T(8,128)S(1)})) conditional(s32[]{:T(128)} %convert_element_type.27, (f32[16,256]{1,0:T(8,128)S(1)}, f32[16,256]{1,0:T(8,128)S(1)}, f32[256,16,128]{2,0,1:T(8,128)S(1)}) %tuple.72, (s32[1,64]{1,0:T(1,128)S(1)}, s32[256]{0:T(256)S(1)}, ...), branch_computations={%region_7.7_spmd, %region_8.10_spmd} | conditional | flops 137654272 | bytes 9242912 | solution.py:52
  104.2 2.1 bitcast_add_fusion.1
  107.3 4.0 %conditional.5 = ((f32[16,256]{1,0:T(8,128)S(1)}, f32[16,256]{1,0:T(8,128)S(1)}, f32[256,16,128]{2,0,1:T(8,128)S(1)})) conditional(s32[]{:T(128)} %convert_element_type.27, (f32[16,256]{1,0:T(8,128)S(1)}, f32[16,256]{1,0:T(8,128)S(1)}, f32[256,16,128]{2,0,1:T(8,128)S(1)}) %tuple.72, (s32[1,64]{1,0:T(1,128)S(1)}, s32[256]{0:T(256)S(1)}, ...), branch_computations={%region_7.7_spmd, %region_8.10_spmd} | conditional | flops 137654272 | bytes 9242912 | solution.py:52
  108.8 2.1 bitcast_add_fusion.1
  111.9 4.0 %conditional.5 = ((f32[16,256]{1,0:T(8,128)S(1)}, f32[16,256]{1,0:T(8,128)S(1)}, f32[256,16,128]{2,0,1:T(8,128)S(1)})) conditional(s32[]{:T(128)} %convert_element_type.27, (f32[16,256]{1,0:T(8,128)S(1)}, f32[16,256]{1,0:T(8,128)S(1)}, f32[256,16,128]{2,0,1:T(8,128)S(1)}) %tuple.72, (s32[1,64]{1,0:T(1,128)S(1)}, s32[256]{0:T(256)S(1)}, ...), branch_computations={%region_7.7_spmd, %region_8.10_spmd} | conditional | flops 137654272 | bytes 9242912 | solution.py:52
  113.4 2.1 bitcast_add_fusion.1
  116.5 4.0 %conditional.5 = ((f32[16,256]{1,0:T(8,128)S(1)}, f32[16,256]{1,0:T(8,128)S(1)}, f32[256,16,128]{2,0,1:T(8,128)S(1)})) conditional(s32[]{:T(128)} %convert_element_type.27, (f32[16,256]{1,0:T(8,128)S(1)}, f32[16,256]{1,0:T(8,128)S(1)}, f32[256,16,128]{2,0,1:T(8,128)S(1)}) %tuple.72, (s32[1,64]{1,0:T(1,128)S(1)}, s32[256]{0:T(256)S(1)}, ...), branch_computations={%region_7.7_spmd, %region_8.10_spmd} | conditional | flops 137654272 | bytes 9242912 | solution.py:52
  118.1 2.1 bitcast_add_fusion.1
  121.1 4.0 %conditional.5 = ((f32[16,256]{1,0:T(8,128)S(1)}, f32[16,256]{1,0:T(8,128)S(1)}, f32[256,16,128]{2,0,1:T(8,128)S(1)})) conditional(s32[]{:T(128)} %convert_element_type.27, (f32[16,256]{1,0:T(8,128)S(1)}, f32[16,256]{1,0:T(8,128)S(1)}, f32[256,16,128]{2,0,1:T(8,128)S(1)}) %tuple.72, (s32[1,64]{1,0:T(1,128)S(1)}, s32[256]{0:T(256)S(1)}, ...), branch_computations={%region_7.7_spmd, %region_8.10_spmd} | conditional | flops 137654272 | bytes 9242912 | solution.py:52
  122.7 2.1 bitcast_add_fusion.1
  125.7 4.0 %conditional.5 = ((f32[16,256]{1,0:T(8,128)S(1)}, f32[16,256]{1,0:T(8,128)S(1)}, f32[256,16,128]{2,0,1:T(8,128)S(1)})) conditional(s32[]{:T(128)} %convert_element_type.27, (f32[16,256]{1,0:T(8,128)S(1)}, f32[16,256]{1,0:T(8,128)S(1)}, f32[256,16,128]{2,0,1:T(8,128)S(1)}) %tuple.72, (s32[1,64]{1,0:T(1,128)S(1)}, s32[256]{0:T(256)S(1)}, ...), branch_computations={%region_7.7_spmd, %region_8.10_spmd} | conditional | flops 137654272 | bytes 9242912 | solution.py:52
  127.3 2.1 bitcast_add_fusion.1
  130.3 4.0 %conditional.5 = ((f32[16,256]{1,0:T(8,128)S(1)}, f32[16,256]{1,0:T(8,128)S(1)}, f32[256,16,128]{2,0,1:T(8,128)S(1)})) conditional(s32[]{:T(128)} %convert_element_type.27, (f32[16,256]{1,0:T(8,128)S(1)}, f32[16,256]{1,0:T(8,128)S(1)}, f32[256,16,128]{2,0,1:T(8,128)S(1)}) %tuple.72, (s32[1,64]{1,0:T(1,128)S(1)}, s32[256]{0:T(256)S(1)}, ...), branch_computations={%region_7.7_spmd, %region_8.10_spmd} | conditional | flops 137654272 | bytes 9242912 | solution.py:52
  131.9 2.1 bitcast_add_fusion.1
  134.9 4.0 %conditional.5 = ((f32[16,256]{1,0:T(8,128)S(1)}, f32[16,256]{1,0:T(8,128)S(1)}, f32[256,16,128]{2,0,1:T(8,128)S(1)})) conditional(s32[]{:T(128)} %convert_element_type.27, (f32[16,256]{1,0:T(8,128)S(1)}, f32[16,256]{1,0:T(8,128)S(1)}, f32[256,16,128]{2,0,1:T(8,128)S(1)}) %tuple.72, (s32[1,64]{1,0:T(1,128)S(1)}, s32[256]{0:T(256)S(1)}, ...), branch_computations={%region_7.7_spmd, %region_8.10_spmd} | conditional | flops 137654272 | bytes 9242912 | solution.py:52
  136.5 2.1 bitcast_add_fusion.1
  141.6 3.3 %all-to-all-start.1 = ((f32[4,1,2048]{2,1,0:T(1,128)}), f32[4,1,2048]{2,1,0:T(1,128)S(1)}, u32[]{:S(2)}, u32[]{:S(2)}) async-start(f32[4,1,2048]{2,1,0:T(1,128)} %reshape.120), calls=%async_computation.1 | async-start | bytes 65536 | tf_op jit(solution)/shard_map/all_to_all | solution.py:105
  147.0 2.9 copy.42
  151.7 5.1 %all-to-all-start.2 = ((f32[4,1,2048]{2,1,0:T(1,128)}), f32[4,1,2048]{2,1,0:T(1,128)S(1)}, u32[]{:S(2)}, u32[]{:S(2)}) async-start(f32[4,1,2048]{2,1,0:T(1,128)} %reshape.122), calls=%async_computation.2 | async-start | bytes 65536 | tf_op jit(solution)/shard_map/all_to_all | solution.py:106
  156.8 4.8 %pad_maximum_fusion = f32[512,16,128]{0,2,1:T(8,128)} fusion(f32[256,16,128]{0,2,1:T(8,128)} %copy.43, f32[256,16,128]{0,2,1:T(8,128)} %copy.42), kind=kLoop, calls=%fused_computation.42 | loop fusion | flops 1048576 | bytes 8388608 | tf_op jit(solution)/shard_map/concatenate | solution.py:98
  161.6 11.0 %copy.44 = f32[512,1,2048]{2,1,0:T(1,128)} copy(f32[512,1,2048]{0,2,1:T(8,128)} %bitcast.75) | data formatting | bytes 8388608 | tf_op jit(solution)/shard_map/reshape | solution.py:102
  172.6 5.1 %all-to-all-start = ((f32[512,1,2048]{2,1,0:T(1,128)}), f32[512,1,2048]{2,1,0:T(1,128)}, u32[]{:S(2)}, u32[]{:S(2)}) async-start(f32[512,1,2048]{2,1,0:T(1,128)} %copy.44), calls=%async_computation | async-start | bytes 8388608 | tf_op jit(solution)/shard_map/all_to_all | solution.py:107
  180.2 91.2 %all-to-all-done = f32[512,1,2048]{2,1,0:T(1,128)} async-done(((f32[512,1,2048]{2,1,0:T(1,128)}), f32[512,1,2048]{2,1,0:T(1,128)}, u32[]{:S(2)}, u32[]{:S(2)}) %all-to-all-start) | async-done | bytes 4194336 | tf_op jit(solution)/shard_map/all_to_all | solution.py:107
  271.4 10.9 %copy.45 = f32[4,128,1,2048]{1,0,3,2:T(4,128)} copy(f32[4,128,1,2048]{3,2,1,0:T(1,128)} %bitcast.17) | data formatting | bytes 8388608 | tf_op jit(solution)/shard_map/all_to_all | solution.py:107
  284.5 10.9 %fusion.30 = bf16[128,2048]{0,1:T(8,128)(2,1)S(1)} fusion(f32[4,128,1,2048]{1,0,3,2:T(4,128)S(1)} %copy-done.1, f32[128,4,1,2048]{0,1,3,2:T(4,128)S(1)} %bitcast.76), kind=kLoop, calls=%fused_computation.44 | loop fusion | flops 1835008 | bytes 8912896 | tf_op jit(solution)/shard_map/reduce_sum | solution.py:114
  (158 shorter events, 56.0 us)
Async XLA Ops:
  6.5 25.1 %all-gather.3.cloned.1.call-start = ((), (), s32[]{:S(2)}) async-start(), calls=%async_computation.3 | async-start | bytes 2621440 | tf_op jit(solution)/shard_map/all_gather | solution.py:86
  7.3 48.5 %all-gather.5.cloned.1.call-start = ((), (), s32[]{:S(2)}) async-start(), calls=%async_computation.4 | async-start | bytes 2621440 | tf_op jit(solution)/shard_map/all_gather | solution.py:87
  100.4 1.3 copy-start
  141.6 10.1 %all-to-all-start.1 = ((f32[4,1,2048]{2,1,0:T(1,128)}), f32[4,1,2048]{2,1,0:T(1,128)S(1)}, u32[]{:S(2)}, u32[]{:S(2)}) async-start(f32[4,1,2048]{2,1,0:T(1,128)} %reshape.120), calls=%async_computation.1 | async-start | bytes 65536 | tf_op jit(solution)/shard_map/all_to_all | solution.py:105
  151.7 20.9 %all-to-all-start.2 = ((f32[4,1,2048]{2,1,0:T(1,128)}), f32[4,1,2048]{2,1,0:T(1,128)S(1)}, u32[]{:S(2)}, u32[]{:S(2)}) async-start(f32[4,1,2048]{2,1,0:T(1,128)} %reshape.122), calls=%async_computation.2 | async-start | bytes 65536 | tf_op jit(solution)/shard_map/all_to_all | solution.py:106
  172.6 98.8 %all-to-all-start = ((f32[512,1,2048]{2,1,0:T(1,128)}), f32[512,1,2048]{2,1,0:T(1,128)}, u32[]{:S(2)}, u32[]{:S(2)}) async-start(f32[512,1,2048]{2,1,0:T(1,128)} %copy.44), calls=%async_computation | async-start | bytes 8388608 | tf_op jit(solution)/shard_map/all_to_all | solution.py:107
  282.3 2.2 copy-start.1
Sparse Core Ops, SparseCore 0:
  8.9 22.6 all-gather.2
  33.2 22.5 all-gather.4
where the time goes:
time: 305 us; the launch traced here: 303 us
  waiting for transfers between devices  129 us (42%)
  matrix products  60.2 us (20%)
  local copies, waits for them, and re-layouts  50.8 us (17%)
  other arithmetic  24.5 us (8%)
  between operations  13.6 us (4%)
  starting transfers between devices  13.5 us (4%)
  loops' own time  11.9 us (4%)
    all_to_all x1, waiting for transfers between devices, on_device(): lax.all_to_all(sent[2], 'ka', split_axis=0, concat_axis=1, tiled=True)  91.2 us
    dot_general x16, matrix products, compute(): jnp.einsum('hkr,khd->rhd', weights.astype(jnp.bfloat16), value_block, pre...  34.2 us
    dot_general x16, matrix products, compute(): jnp.einsum('rhd,khd->hkr', q_heads, key_block, preferred_element_type=jnp...  26.1 us
    all_gather x1, waiting for transfers between devices, on_device(): lax.all_gather(values_mine, 'pb', axis=1, tiled=True)  20.1 us
    all_gather x1, waiting for transfers between devices, on_device(): lax.all_gather(keys_mine, 'pb', axis=1, tiled=True)  16 us
    reshape x1, local copies, waits for them, and re-layouts, on_device(): row_out.reshape(block_rows, 1, width)  11 us
    all_to_all x1, local copies, waits for them, and re-layouts, on_device(): lax.all_to_all(sent[2], 'ka', split_axis=0, concat_axis=1, tiled=True)  10.9 us
    reduce_sum x1, other arithmetic, on_device(): result = jnp.sum(pieces, axis=1).reshape(shard_rows, width)  10.9 us
  transfers between devices with their start and end apart: 5, of which 3 were waited for; matrix products, arithmetic and copies ran while one was open for 12% of the time, Pallas kernels for 0%

commit v1 on v0

--- a/solution.py
+++ b/solution.py
@@ -1,14 +1,20 @@
+import functools
 import math
 
 import jax
 import jax.numpy as jnp
 from jax import lax
+from jax.experimental import pallas as pl
+from jax.experimental.pallas import tpu as pltpu
 from jax.sharding import PartitionSpec as P
 
 HEAD_DIM = 128
-
-
+LANES = 128
 LOW_SCORE = -1e30
+UNSEEN = -float(1 << 20)
+CHUNKS = (2, 2)
+GROUPS = (1, 1)
+ANY = pl.BlockSpec(memory_space=pl.ANY)
 
 
 def attend_half(q_rows, q_steps, keys_all, values_all, key_steps, block_keys):
@@ -66,7 +72,7 @@
     return final_state
 
 
-def on_device(queries, keys, values, step_of):
+def on_any(queries, keys, values, step_of):
     block_rows, width = queries.shape
     head_size = HEAD_DIM
     head_count = width // head_size
@@ -115,6 +121,306 @@
     result = result.astype(jnp.bfloat16)
     return result
 
+def attend_kernel(heads, first, q_first, scale, steps_ref, queries, q_1, q_2, q_3, keys, values, got,
+                  own, up, down, far, q_buf, k_buf, v_buf, stats_buf, parts, sem, out_sem):
+    column = lax.axis_index("pb")
+    z = lax.axis_index("ka")
+    rows = queries.shape[0]
+    half_rows = rows // 2
+    sub = rows // 4
+    width = heads * HEAD_DIM
+    held = keys.shape[0]
+    pair = 2 * held
+    upper, half = z // 2, z % 2
+
+    def place(block):
+        return (block + 4 - 2 * upper) % 4
+
+    mine = pl.multiple_of(half * held, held)
+    other = pl.multiple_of((1 - half) * held, held)
+    base = pl.multiple_of(column * keys.shape[1] + first * HEAD_DIM, HEAD_DIM)
+    at = pl.ds(first * HEAD_DIM, width)
+    q_at = pl.ds(q_first * HEAD_DIM, width)
+    copies = [
+        (keys.at[:, at], k_buf.at[pl.ds(mine, held), :]),
+        (got.at[0], k_buf.at[pl.ds(other, held), :]),
+        (queries.at[pl.ds(pl.multiple_of(half * half_rows, half_rows), half_rows), pl.ds(base, width)], q_buf.at[place(column)]),
+    ]
+    copies += [(q.at[:, q_at], q_buf.at[place(column ^ d)]) for d, q in ((1, q_1), (2, q_2), (3, q_3))]
+    for h in range(heads):
+        to = pl.ds(2 * h * HEAD_DIM, HEAD_DIM)
+        copies += [
+            (values.at[:, pl.ds((first + h) * HEAD_DIM, HEAD_DIM)], v_buf.at[pl.ds(mine, held), to]),
+            (got.at[1, :, pl.ds(h * HEAD_DIM, HEAD_DIM)], v_buf.at[pl.ds(other, held), to]),
+        ]
+    copies = [pltpu.make_async_copy(a, b, sem.at[i]) for i, (a, b) in enumerate(copies)]
+    for copy in copies:
+        copy.start()
+    for h in range(heads):
+        v_buf[:, (2 * h + 1) * HEAD_DIM:(2 * h + 2) * HEAD_DIM] = jnp.ones((pair, HEAD_DIM), jnp.bfloat16)
+    stats_buf[...] = jnp.zeros(stats_buf.shape, jnp.float32)
+    columns = jnp.transpose(steps_ref[...].astype(jnp.float32))
+    group = lax.broadcasted_iota(jnp.int32, columns.shape, 1)
+    tiles = pair // LANES
+    key_steps = steps_ref[pl.ds(pl.multiple_of(upper * tiles, tiles), tiles), :].astype(jnp.float32)
+    for copy in copies:
+        copy.wait()
+
+    def tile(slot, limit, masked_from, start=0, count=half_rows):
+        q = q_buf[slot, start:start + count, :]
+        block = (slot + 2 * upper) % 4
+        if masked_from < limit:
+            q_steps = jnp.concatenate([
+                jnp.sum(jnp.where(group == block * 4 + half * 2 + j, columns, 0.0), axis=1, keepdims=True)
+                for j in range(start // sub, (start + count) // sub)
+            ], axis=0)
+            k_steps = jnp.concatenate([key_steps[j:j + 1] for j in range(masked_from // LANES, limit // LANES)], axis=1)
+            visible = k_steps <= q_steps
+        lane = lax.broadcasted_iota(jnp.int32, (count, LANES), 1)
+        stats = stats_buf[start:start + count, :]
+        for h in range(heads):
+            cut = slice(h * HEAD_DIM, (h + 1) * HEAD_DIM)
+            scores = lax.dot_general(q[:, cut], k_buf[:limit, cut], (((1,), (1,)), ((), ())),
+                                     preferred_element_type=jnp.float32)
+            if masked_from < limit:
+                seen = jnp.where(visible, scores[:, masked_from:], UNSEEN / scale)
+                scores = seen if masked_from == 0 else jnp.concatenate([scores[:, :masked_from], seen], axis=1)
+            top = jnp.max(scores, axis=1, keepdims=True) * scale
+            top = top.astype(jnp.bfloat16).astype(jnp.float32)
+            weights = jnp.exp2(scores * scale - top).astype(jnp.bfloat16)
+            mixed = lax.dot_general(weights, v_buf[:limit, 2 * h * HEAD_DIM:(2 * h + 2) * HEAD_DIM],
+                                    (((1,), (0,)), ((), ())), preferred_element_type=jnp.float32)
+            total = mixed[:, HEAD_DIM:]
+            index = slot * heads + h
+            result = (mixed[:, :HEAD_DIM] / total).astype(jnp.bfloat16)
+            for j in range(count // sub):
+                parts[start // sub + j, 1 + index] = result[j * sub:(j + 1) * sub]
+            high = total.astype(jnp.bfloat16).astype(jnp.float32)
+            stats = jnp.where(lane == 3 * index, top, stats)
+            stats = jnp.where(lane == 3 * index + 1, high, stats)
+            stats = jnp.where(lane == 3 * index + 2, total - high, stats)
+        stats_buf[start:start + count, :] = stats
+
+    for which in (0, 1):
+        @pl.when(half == which)
+        def _():
+            reach = held // 2 + LANES if which == 0 else held + LANES
+            tile(0, reach, 0)
+            tile(1, min(held + reach, pair), held)
+
+    @pl.when(upper == 0)
+    def _():
+        tile(2, pair, pair)
+        tile(3, pair, pair)
+
+    @pl.when(z == 3)
+    def _():
+        tile(3, LANES, 0, start=sub, count=sub)
+
+    for j in range(2):
+        parts[j, 0] = stats_buf[j * sub:(j + 1) * sub, :].astype(jnp.bfloat16)
+    for which, pair_of in enumerate(((own, up), (up, far), (far, down), (down, own))):
+        @pl.when(z == which)
+        def _():
+            out = [pltpu.make_async_copy(parts.at[j, pl.ds(0, to.shape[0])], to, out_sem.at[j]) for j, to in enumerate(pair_of)]
+            for copy in out:
+                copy.start()
+            for copy in out:
+                copy.wait()
+
+
+def attend(heads, first, q_first, steps, queries, moved, keys, values, got):
+    rows = queries.shape[0]
+    held = keys.shape[0]
+    sub = rows // 4
+    part = jax.ShapeDtypeStruct((4 * heads + 1, sub, LANES), jnp.bfloat16)
+    short = jax.ShapeDtypeStruct((2 * heads + 1, sub, LANES), jnp.bfloat16)
+    exps = heads * 4 * (rows // 2) * held * 2
+    return pl.pallas_call(
+        functools.partial(attend_kernel, heads, first, q_first, math.log2(math.e) / math.sqrt(HEAD_DIM)),
+        out_shape=[part, part, short, part],
+        in_specs=[pl.BlockSpec(memory_space=pltpu.VMEM)] + [ANY] * 7,
+        out_specs=[ANY] * 4,
+        scratch_shapes=[
+            pltpu.VMEM((4, rows // 2, heads * HEAD_DIM), jnp.bfloat16),
+            pltpu.VMEM((2 * held, heads * HEAD_DIM), jnp.bfloat16),
+            pltpu.VMEM((2 * held, 2 * heads * HEAD_DIM), jnp.bfloat16),
+            pltpu.VMEM((rows // 2, LANES), jnp.float32),
+            pltpu.VMEM((2,) + part.shape, jnp.bfloat16),
+            pltpu.SemaphoreType.DMA((6 + 2 * heads,)),
+            pltpu.SemaphoreType.DMA((2,)),
+        ],
+        compiler_params=pltpu.CompilerParams(vmem_limit_bytes=40 << 20),
+        cost_estimate=pl.CostEstimate(flops=exps * 4 * HEAD_DIM, bytes_accessed=4 << 20, transcendentals=exps),
+        name="attend",
+    )(steps, queries, *moved, keys, values, got)
+
+
+def merge_kernel(chunks, *refs):
+    count = len(chunks)
+    ins, outs, (low, high, result, sem) = refs[:4 * count], refs[4 * count:4 * count + 4], refs[4 * count + 4:]
+    column = lax.axis_index("pb")
+    z = lax.axis_index("ka")
+    starts = [sum(4 * heads + 1 for heads in chunks[:c]) for c in range(count)]
+    for which in range(4):
+        @pl.when(z == which)
+        def _():
+            copies = []
+            for c, heads in enumerate(chunks):
+                own, up, down, far = ins[4 * c:4 * c + 4]
+                for held, sent in zip((low, high), ((own, far), (up, down), (up, down), (far, own))[which]):
+                    at = pl.ds(starts[c], sent.shape[0])
+                    copies.append(pltpu.make_async_copy(sent, held.at[at], sem.at[len(copies)]))
+            for copy in copies:
+                copy.start()
+            for copy in copies:
+                copy.wait()
+
+    def merge_block(block):
+        first = 0
+        for c, heads in enumerate(chunks):
+            stats = [held[starts[c]].astype(jnp.float32) for held in (low, high)]
+            for h in range(heads):
+                places = [slot * heads + h for slot in (block, (block + 2) % 4)]
+                cut = slice((first + h) * HEAD_DIM, (first + h + 1) * HEAD_DIM)
+                tops = [s[:, 3 * i:3 * i + 1] for s, i in zip(stats, places)]
+                totals = [s[:, 3 * i + 1:3 * i + 2] + s[:, 3 * i + 2:3 * i + 3] for s, i in zip(stats, places)]
+                best = jnp.maximum(*tops)
+                shares = [total * jnp.exp2(top - best) for top, total in zip(tops, totals)]
+                share = shares[0] / (shares[0] + shares[1])
+                a = low[starts[c] + 1 + places[0]].astype(jnp.float32)
+                b = high[starts[c] + 1 + places[1]].astype(jnp.float32)
+                result[block, :, cut] = (a * share + b * (1.0 - share)).astype(jnp.bfloat16)
+            first += heads
+
+    def take_block(block):
+        first = 0
+        for c, heads in enumerate(chunks):
+            for h in range(heads):
+                cut = slice((first + h) * HEAD_DIM, (first + h + 1) * HEAD_DIM)
+                result[block, :, cut] = low[starts[c] + 1 + block * heads + h]
+            first += heads
+
+    take_block(0)
+
+    @pl.when(z < 3)
+    def _():
+        take_block(1)
+
+    @pl.when(z == 3)
+    def _():
+        merge_block(1)
+
+    merge_block(2)
+    merge_block(3)
+    copies = [pltpu.make_async_copy(result.at[column ^ d], out, sem.at[d]) for d, out in enumerate(outs)]
+    for copy in copies:
+        copy.start()
+    for copy in copies:
+        copy.wait()
+
+
+def merge(chunks, parts):
+    sub = parts[0].shape[1]
+    tiles = sum(4 * heads + 1 for heads in chunks)
+    block = jax.ShapeDtypeStruct((sub, sum(chunks) * HEAD_DIM), jnp.bfloat16)
+    return pl.pallas_call(
+        functools.partial(merge_kernel, chunks),
+        out_shape=[block] * 4,
+        in_specs=[ANY] * len(parts),
+        out_specs=[ANY] * 4,
+        scratch_shapes=[
+            pltpu.VMEM((tiles, sub, LANES), jnp.bfloat16),
+            pltpu.VMEM((tiles, sub, LANES), jnp.bfloat16),
+            pltpu.VMEM((4,) + block.shape, jnp.bfloat16),
+            pltpu.SemaphoreType.DMA((max(4, 2 * len(chunks)),)),
+        ],
+        compiler_params=pltpu.CompilerParams(vmem_limit_bytes=16 << 20),
+        cost_estimate=pl.CostEstimate(flops=1 << 20, bytes_accessed=4 << 20, transcendentals=0),
+        name="merge",
+    )(*parts)
+
+
+def assemble_kernel(widths, *refs):
+    column = lax.axis_index("pb")
+    pieces, out = refs[:-1], refs[-1]
+    first = 0
+    for g, width in enumerate(widths):
+        for d in range(4):
+            at = pl.multiple_of((column ^ d) * sum(widths) + first, HEAD_DIM)
+            out[:, pl.ds(at, width)] = pieces[4 * g + d][...]
+        first += width
+
+
+def assemble(pieces):
+    sub = pieces[0].shape[0]
+    widths = [piece.shape[1] for piece in pieces[::4]]
+    return pl.pallas_call(
+        functools.partial(assemble_kernel, widths),
+        out_shape=jax.ShapeDtypeStruct((sub, 4 * sum(widths)), jnp.bfloat16),
+        in_specs=[pl.BlockSpec(memory_space=pltpu.VMEM)] * len(pieces),
+        out_specs=pl.BlockSpec(memory_space=pltpu.VMEM),
+        name="assemble",
+    )(*pieces)
+
+
+def on_line(queries, keys, values, step_of):
+    column = lax.axis_index("pb")
+    half = lax.axis_index("ka") % 2
+    half_rows = queries.shape[0] // 2
+    block = keys.shape[1]
+    steps = step_of.reshape(-1, LANES)
+    swaps = [[(i, i ^ d) for i in range(4)] for d in (1, 2, 3)]
+    ready = []
+    first = 0
+    chunk = 0
+    for size in GROUPS:
+        group = CHUNKS[chunk:chunk + size]
+        start = first
+        width = sum(group) * HEAD_DIM
+        moved = []
+        for heads in group:
+            at = slice(first * HEAD_DIM, (first + heads) * HEAD_DIM)
+            got = lax.ppermute(jnp.stack([keys[:, at], values[:, at]]), "ka", [(0, 1), (1, 0), (2, 3), (3, 2)])
+            if not moved:
+                for d in (1, 2, 3):
+                    corner = (half * half_rows, (column ^ d) * block + start * HEAD_DIM)
+                    sent = lax.dynamic_slice(queries, corner, (half_rows, width))
+                    moved.append(lax.ppermute(sent, "pb", swaps[d - 1]))
+            ready.append((heads, first, first - start, got, moved))
+            first += heads
+        chunk += size
+    pieces = []
+    chunk = 0
+    for size in GROUPS:
+        parts = []
+        for heads, first, q_first, got, moved in ready[chunk:chunk + size]:
+            own, up, down, far = attend(heads, first, q_first, steps, queries, moved, keys, values, got)
+            parts += [
+                own,
+                lax.ppermute(up, "ka", [(0, 1), (1, 2)]),
+                lax.ppermute(down, "ka", [(3, 2), (2, 1)]),
+                lax.ppermute(far, "ka", [(1, 3), (2, 0)]),
+            ]
+        sent = merge(CHUNKS[chunk:chunk + size], parts)
+        pieces += [sent[0]] + [lax.ppermute(sent[d], "pb", swaps[d - 1]) for d in (1, 2, 3)]
+        chunk += size
+    return assemble(pieces)
+
+
+def on_device(queries, keys, values, step_of):
+    rows, width = queries.shape
+    held, block = keys.shape
+    line = (
+        lax.axis_size("pb") == 4
+        and lax.axis_size("ka") == 4
+        and held == rows == 4 * LANES
+        and block == sum(CHUNKS) * HEAD_DIM
+    )
+    if line:
+        return on_line(queries, keys, values, step_of)
+    return on_any(queries, keys, values, step_of)
+
 
 def solution(mesh):
     placed = (

time: 305 us -> 63.5 us (0.21)
  the two profiles are of different devices: /device:TPU:2 before, /device:TPU:25 now
where the time goes in v1:
time: 63.5 us; the launch traced here: 63.2 us
  starting transfers between devices  31.2 us (49%)
  Pallas kernels  14.4 us (23%)
  waiting for transfers between devices  12.8 us (20%)
  local copies, waits for them, and re-layouts  2.76 us (4%)
  other arithmetic  1.69 us (3%)
    ppermute x6, starting transfers between devices, on_line(): lax.ppermute(sent[d], 'pb', swaps[d - 1])  12.3 us
    pallas_call x2, Pallas kernels, attend(): pl.pallas_call(functools.partial(attend_kernel, heads, first, q_first, ma...  9.48 us
    ppermute x2, starting transfers between devices, on_line(): lax.ppermute(down, 'ka', [(3, 2), (2, 1)])  8.61 us
    ppermute x6, waiting for transfers between devices, on_line(): moved.append(lax.ppermute(sent, 'pb', swaps[d - 1]))  5.43 us
    ppermute x6, starting transfers between devices, on_line(): moved.append(lax.ppermute(sent, 'pb', swaps[d - 1]))  4.95 us
    ppermute x6, waiting for transfers between devices, on_line(): lax.ppermute(sent[d], 'pb', swaps[d - 1])  3.55 us
    ppermute x2, waiting for transfers between devices, on_line(): lax.ppermute(jnp.stack([keys[:, at], values[:, at]]), 'ka', [(0, 1), (1,...  3.52 us
    pallas_call x2, Pallas kernels, merge(): pl.pallas_call(functools.partial(merge_kernel, chunks), out_shape=[block]...  3.02 us
  transfers between devices with their start and end apart: 20, of which 7 were waited for; matrix products, arithmetic and copies ran while one was open for 2% of the time, Pallas kernels for 20%

profile of v1, /device:TPU:25, one launch (start us, length us, event | category | flops | bytes accessed | tf_op | source)
XLA Modules:
  0.0 63.2 jit_solution(11239699755439789870)
XLA Ops:
  0.0 1.4 %slice_bitcast_fusion = (bf16[1,512,256]{2,1,0:T(8,128)(2,1)S(1)}, bf16[1,512,256]{2,1,0:T(8,128)(2,1)S(1)}, bf16[1,512,256]{2,1,0:T(8,128)(2,1)S(1)}, bf16[1,512,256]{2,1,0:T(8,128)(2,1)S(1)}) fusion(bf16[512,512]{1,0:T(8,128)(2,1)} %values.3, bf16[512,512]{1,0:T(8,128)(2,1)} %keys.3), kind=kLoop, calls=%fused_computation.2 | loop fusion | bytes 2097152 | tf_op jit(solution)/shard_map/stack | solution.py:384
  1.4 0.0 copy-start.1
  1.4 0.0 copy-start.2
  1.4 0.0 copy-start.5
  1.4 0.8 %pad_maximum_fusion = bf16[2,512,256]{2,1,0:T(8,128)(2,1)} fusion(bf16[1,512,256]{2,1,0:T(8,128)(2,1)S(1)} %get-tuple-element.46, bf16[1,512,256]{2,1,0:T(8,128)(2,1)S(1)} %get-tuple-element.47), kind=kLoop, calls=%fused_computation | loop fusion | flops 262144 | bytes 1048576 | tf_op jit(solution)/shard_map/stack | solution.py:384
  2.3 0.2 collective-permute-start.3
  2.5 0.9 %pad_maximum_fusion.1 = bf16[2,512,256]{2,1,0:T(8,128)(2,1)} fusion(bf16[1,512,256]{2,1,0:T(8,128)(2,1)S(1)} %get-tuple-element.45, bf16[1,512,256]{2,1,0:T(8,128)(2,1)S(1)} %get-tuple-element.48), kind=kLoop, calls=%fused_computation.1 | loop fusion | flops 262144 | bytes 1048576 | tf_op jit(solution)/shard_map/stack | solution.py:384
  3.3 1.3 %collective-permute-start.13 = (bf16[2,512,256]{2,1,0:T(8,128)(2,1)}, bf16[2,512,256]{2,1,0:T(8,128)(2,1)}, u32[]{:S(2)}, u32[]{:S(2)}) collective-permute-start(bf16[2,512,256]{2,1,0:T(8,128)(2,1)} %pad_maximum_fusion.1), channel_id=1, source_target_pairs={{0,1},{1,0},{2,3},{3,2},{4,5},{5,4},{6,7},{7,6},{8,9},{9,8},{10,11... | collective-permute-start | bytes 1572872 | tf_op jit(solution)/shard_map/ppermute | solution.py:384
  4.6 0.1 fusion
  4.7 2.4 %collective-permute-start.2 = (bf16[256,256]{1,0:T(8,128)(2,1)S(1)}, bf16[256,256]{1,0:T(8,128)(2,1)S(1)}, u32[]{:S(2)}, u32[]{:S(2)}) collective-permute-start(bf16[256,256]{1,0:T(8,128)(2,1)S(1)} %get-tuple-element.40), channel_id=1, source_target_pairs={{0,12},{4,8},{8,4},{12,0},{1,13},{5,9},{9,5},{13,1},{2,14},{6,10},... | collective-permute-start | bytes 393224 | tf_op jit(solution)/shard_map/ppermute | solution.py:389
  7.1 0.3 collective-permute-start.1
  7.4 0.2 collective-permute-start
  7.6 4.0 %collective-permute-done.2.q_3 = bf16[256,256]{1,0:T(8,128)(2,1)S(1)} collective-permute-done((bf16[256,256]{1,0:T(8,128)(2,1)S(1)}, bf16[256,256]{1,0:T(8,128)(2,1)S(1)}, u32[]{:S(2)}, u32[]{:S(2)}) %collective-permute-start.2) | collective-permute-done | bytes 131104 | tf_op jit(solution)/shard_map/ppermute | solution.py:389
  11.6 1.3 %collective-permute-start.12 = (bf16[256,256]{1,0:T(8,128)(2,1)S(1)}, bf16[256,256]{1,0:T(8,128)(2,1)S(1)}, u32[]{:S(2)}, u32[]{:S(2)}) collective-permute-start(bf16[256,256]{1,0:T(8,128)(2,1)S(1)} %get-tuple-element.37), channel_id=1, source_target_pairs={{0,12},{4,8},{8,4},{12,0},{1,13},{5,9},{9,5},{13,1},{2,14},{6,10},... | collective-permute-start | bytes 393224 | tf_op jit(solution)/shard_map/ppermute | solution.py:389
  12.8 1.4 %collective-permute-done.1.q_2 = bf16[256,256]{1,0:T(8,128)(2,1)S(1)} collective-permute-done((bf16[256,256]{1,0:T(8,128)(2,1)S(1)}, bf16[256,256]{1,0:T(8,128)(2,1)S(1)}, u32[]{:S(2)}, u32[]{:S(2)}) %collective-permute-start.1) | collective-permute-done | bytes 131104 | tf_op jit(solution)/shard_map/ppermute | solution.py:389
  14.3 0.7 %collective-permute-start.11 = (bf16[256,256]{1,0:T(8,128)(2,1)S(1)}, bf16[256,256]{1,0:T(8,128)(2,1)S(1)}, u32[]{:S(2)}, u32[]{:S(2)}) collective-permute-start(bf16[256,256]{1,0:T(8,128)(2,1)S(1)} %get-tuple-element.38), channel_id=1, source_target_pairs={{0,8},{4,12},{8,0},{12,4},{1,9},{5,13},{9,1},{13,5},{2,10},{6,14},... | collective-permute-start | bytes 393224 | tf_op jit(solution)/shard_map/ppermute | solution.py:389
  15.0 0.0 collective-permute-done.q_1
  15.0 0.1 collective-permute-start.10
  15.1 0.3 collective-permute-done.3.got
  15.4 4.7 %attend.2 = (bf16[9,128,128]{2,1,0:T(8,128)(2,1)S(1)}, bf16[9,128,128]{2,1,0:T(8,128)(2,1)S(1)}, bf16[5,128,128]{2,1,0:T(8,128)(2,1)S(1)}, bf16[9,128,128]{2,1,0:T(8,128)(2,1)S(1)}) custom-call(s32[16,128]{1,0:T(8,128)S(1)} %bitcast.9, bf16[512,2048]{1,0:T(8,128)(2,1)S(1)} %copy-done, bf16[256,256]{1,0:T(8,128)(2,1)S(1)} %collective-permute-done.q_1, ...), custom_call_target="tpu_custom_call" | custom-call | flops 1073741824 | bytes 4194304 | tf_op jit(solution)/shard_map/attend/pallas_call | solution.py:239
  20.1 1.3 %collective-permute-start.5 = (bf16[5,128,128]{2,1,0:T(8,128)(2,1)S(1)}, bf16[5,128,128]{2,1,0:T(8,128)(2,1)S(1)}, u32[]{:S(2)}, u32[]{:S(2)}) collective-permute-start(bf16[5,128,128]{2,1,0:T(8,128)(2,1)S(1)} %get-tuple-element.23), channel_id=1, source_target_pairs={{3,2},{2,1},{7,6},{6,5},{11,10},{10,9},{15,14},{14,13},{19,18},{18... | collective-permute-start | bytes 491528 | tf_op jit(solution)/shard_map/ppermute | solution.py:402
  21.4 0.0 collective-permute-done.12.q_3
  21.4 0.7 %collective-permute-start.4 = (bf16[9,128,128]{2,1,0:T(8,128)(2,1)S(1)}, bf16[9,128,128]{2,1,0:T(8,128)(2,1)S(1)}, u32[]{:S(2)}, u32[]{:S(2)}) collective-permute-start(bf16[9,128,128]{2,1,0:T(8,128)(2,1)S(1)} %get-tuple-element.22), channel_id=1, source_target_pairs={{0,1},{1,2},{4,5},{5,6},{8,9},{9,10},{12,13},{13,14},{16,17},{17,1... | collective-permute-start | bytes 884744 | tf_op jit(solution)/shard_map/ppermute | solution.py:401
  22.1 0.0 collective-permute-done.11.q_2
  22.1 1.3 %collective-permute-start.6 = (bf16[9,128,128]{2,1,0:T(8,128)(2,1)S(1)}, bf16[9,128,128]{2,1,0:T(8,128)(2,1)S(1)}, u32[]{:S(2)}, u32[]{:S(2)}) collective-permute-start(bf16[9,128,128]{2,1,0:T(8,128)(2,1)S(1)} %get-tuple-element.24), channel_id=1, source_target_pairs={{1,3},{2,0},{5,7},{6,4},{9,11},{10,8},{13,15},{14,12},{17,19},{18,... | collective-permute-start | bytes 884744 | tf_op jit(solution)/shard_map/ppermute | solution.py:403
  23.4 0.0 collective-permute-done.10.q_1
  23.4 3.2 %collective-permute-done.13.got = bf16[2,512,256]{2,1,0:T(8,128)(2,1)} collective-permute-done((bf16[2,512,256]{2,1,0:T(8,128)(2,1)}, bf16[2,512,256]{2,1,0:T(8,128)(2,1)}, u32[]{:S(2)}, u32[]{:S(2)}) %collective-permute-start.13) | collective-permute-done | bytes 524320 | tf_op jit(solution)/shard_map/ppermute | solution.py:384
  26.6 4.8 %attend.3 = (bf16[9,128,128]{2,1,0:T(8,128)(2,1)S(1)}, bf16[9,128,128]{2,1,0:T(8,128)(2,1)S(1)}, bf16[5,128,128]{2,1,0:T(8,128)(2,1)S(1)}, bf16[9,128,128]{2,1,0:T(8,128)(2,1)S(1)}) custom-call(s32[16,128]{1,0:T(8,128)S(1)} %bitcast.10, bf16[512,2048]{1,0:T(8,128)(2,1)S(1)} %copy-done, bf16[256,256]{1,0:T(8,128)(2,1)S(1)} %collective-permute-done.10.q_1, ...), custom_call_target="tpu_custom_call" | custom-call | flops 1073741824 | bytes 4194304 | tf_op jit(solution)/shard_map/attend/pallas_call | solution.py:239
  31.5 0.7 %collective-permute-start.14 = (bf16[9,128,128]{2,1,0:T(8,128)(2,1)S(1)}, bf16[9,128,128]{2,1,0:T(8,128)(2,1)S(1)}, u32[]{:S(2)}, u32[]{:S(2)}) collective-permute-start(bf16[9,128,128]{2,1,0:T(8,128)(2,1)S(1)} %get-tuple-element.30), channel_id=1, source_target_pairs={{0,1},{1,2},{4,5},{5,6},{8,9},{9,10},{12,13},{13,14},{16,17},{17,1... | collective-permute-start | bytes 884744 | tf_op jit(solution)/shard_map/ppermute | solution.py:401
  32.1 1.3 %collective-permute-start.16 = (bf16[9,128,128]{2,1,0:T(8,128)(2,1)S(1)}, bf16[9,128,128]{2,1,0:T(8,128)(2,1)S(1)}, u32[]{:S(2)}, u32[]{:S(2)}) collective-permute-start(bf16[9,128,128]{2,1,0:T(8,128)(2,1)S(1)} %get-tuple-element.32), channel_id=1, source_target_pairs={{1,3},{2,0},{5,7},{6,4},{9,11},{10,8},{13,15},{14,12},{17,19},{18,... | collective-permute-start | bytes 884744 | tf_op jit(solution)/shard_map/ppermute | solution.py:403
  33.4 0.0 collective-permute-done.5.refs_2_
  33.5 7.3 %collective-permute-start.15 = (bf16[5,128,128]{2,1,0:T(8,128)(2,1)S(1)}, bf16[5,128,128]{2,1,0:T(8,128)(2,1)S(1)}, u32[]{:S(2)}, u32[]{:S(2)}) collective-permute-start(bf16[5,128,128]{2,1,0:T(8,128)(2,1)S(1)} %get-tuple-element.31), channel_id=1, source_target_pairs={{3,2},{2,1},{7,6},{6,5},{11,10},{10,9},{15,14},{14,13},{19,18},{18... | collective-permute-start | bytes 491528 | tf_op jit(solution)/shard_map/ppermute | solution.py:402
  40.8 0.0 collective-permute-done.4.refs_1_
  40.8 0.0 collective-permute-done.6.refs_3_
  40.8 1.5 %merge.2 = (bf16[128,256]{1,0:T(8,128)(2,1)S(1)}, bf16[128,256]{1,0:T(8,128)(2,1)S(1)}, bf16[128,256]{1,0:T(8,128)(2,1)S(1)}, bf16[128,256]{1,0:T(8,128)(2,1)S(1)}) custom-call(bf16[9,128,128]{2,1,0:T(8,128)(2,1)S(1)} %get-tuple-element.21.refs_0_, bf16[9,128,128]{2,1,0:T(8,128)(2,1)S(1)} %collective-permute-done.4.refs_1_, ...), custom_call_target="tpu_custom_call" | custom-call | flops 1048576 | bytes 4194304 | tf_op jit(solution)/shard_map/merge/pallas_call | solution.py:327
  42.3 4.2 %collective-permute-start.7 = (bf16[128,256]{1,0:T(8,128)(2,1)S(1)}, bf16[128,256]{1,0:T(8,128)(2,1)S(1)}, u32[]{:S(2)}, u32[]{:S(2)}) collective-permute-start(bf16[128,256]{1,0:T(8,128)(2,1)S(1)} %get-tuple-element.26), channel_id=1, source_target_pairs={{0,4},{4,0},{8,12},{12,8},{1,5},{5,1},{9,13},{13,9},{2,6},{6,2},{1... | collective-permute-start | bytes 196616 | tf_op jit(solution)/shard_map/ppermute | solution.py:406
  46.5 1.2 %collective-permute-start.8 = (bf16[128,256]{1,0:T(8,128)(2,1)S(1)}, bf16[128,256]{1,0:T(8,128)(2,1)S(1)}, u32[]{:S(2)}, u32[]{:S(2)}) collective-permute-start(bf16[128,256]{1,0:T(8,128)(2,1)S(1)} %get-tuple-element.27), channel_id=1, source_target_pairs={{0,8},{4,12},{8,0},{12,4},{1,9},{5,13},{9,1},{13,5},{2,10},{6,14},... | collective-permute-start | bytes 196616 | tf_op jit(solution)/shard_map/ppermute | solution.py:406
  47.7 1.0 %collective-permute-start.9 = (bf16[128,256]{1,0:T(8,128)(2,1)S(1)}, bf16[128,256]{1,0:T(8,128)(2,1)S(1)}, u32[]{:S(2)}, u32[]{:S(2)}) collective-permute-start(bf16[128,256]{1,0:T(8,128)(2,1)S(1)} %get-tuple-element.28), channel_id=1, source_target_pairs={{0,12},{4,8},{8,4},{12,0},{1,13},{5,9},{9,5},{13,1},{2,14},{6,10},... | collective-permute-start | bytes 196616 | tf_op jit(solution)/shard_map/ppermute | solution.py:406
  48.8 0.3 collective-permute-done.16.refs_3_
  49.1 1.5 %merge.3 = (bf16[128,256]{1,0:T(8,128)(2,1)S(1)}, bf16[128,256]{1,0:T(8,128)(2,1)S(1)}, bf16[128,256]{1,0:T(8,128)(2,1)S(1)}, bf16[128,256]{1,0:T(8,128)(2,1)S(1)}) custom-call(bf16[9,128,128]{2,1,0:T(8,128)(2,1)S(1)} %get-tuple-element.29.refs_0_, bf16[9,128,128]{2,1,0:T(8,128)(2,1)S(1)} %collective-permute-done.14.refs_1_, ...), custom_call_target="tpu_custom_call" | custom-call | flops 1048576 | bytes 4194304 | tf_op jit(solution)/shard_map/merge/pallas_call | solution.py:327
  50.6 0.6 copy-done.4
  51.2 4.2 %collective-permute-start.17 = (bf16[128,256]{1,0:T(8,128)(2,1)S(1)}, bf16[128,256]{1,0:T(8,128)(2,1)S(1)}, u32[]{:S(2)}, u32[]{:S(2)}) collective-permute-start(bf16[128,256]{1,0:T(8,128)(2,1)S(1)} %get-tuple-element.34), channel_id=1, source_target_pairs={{0,4},{4,0},{8,12},{12,8},{1,5},{5,1},{9,13},{13,9},{2,6},{6,2},{1... | collective-permute-start | bytes 196616 | tf_op jit(solution)/shard_map/ppermute | solution.py:406
  55.4 1.2 %collective-permute-start.18 = (bf16[128,256]{1,0:T(8,128)(2,1)S(1)}, bf16[128,256]{1,0:T(8,128)(2,1)S(1)}, u32[]{:S(2)}, u32[]{:S(2)}) collective-permute-start(bf16[128,256]{1,0:T(8,128)(2,1)S(1)} %get-tuple-element.35), channel_id=1, source_target_pairs={{0,8},{4,12},{8,0},{12,4},{1,9},{5,13},{9,1},{13,5},{2,10},{6,14},... | collective-permute-start | bytes 196616 | tf_op jit(solution)/shard_map/ppermute | solution.py:406
  56.6 0.4 collective-permute-start.19
  57.1 2.0 %collective-permute-done.18.refs_6_ = bf16[128,256]{1,0:T(8,128)(2,1)S(1)} collective-permute-done((bf16[128,256]{1,0:T(8,128)(2,1)S(1)}, bf16[128,256]{1,0:T(8,128)(2,1)S(1)}, u32[]{:S(2)}, u32[]{:S(2)}) %collective-permute-start.18) | collective-permute-done | bytes 65568 | tf_op jit(solution)/shard_map/ppermute | solution.py:406
  59.1 1.5 %collective-permute-done.19.refs_7_ = bf16[128,256]{1,0:T(8,128)(2,1)S(1)} collective-permute-done((bf16[128,256]{1,0:T(8,128)(2,1)S(1)}, bf16[128,256]{1,0:T(8,128)(2,1)S(1)}, u32[]{:S(2)}, u32[]{:S(2)}) %collective-permute-start.19) | collective-permute-done | bytes 65568 | tf_op jit(solution)/shard_map/ppermute | solution.py:406
  60.7 0.6 copy-done.11
  61.3 1.9 %assemble.1 = bf16[128,2048]{1,0:T(8,128)(2,1)} custom-call(bf16[128,256]{1,0:T(8,128)(2,1)} %copy-done.3, bf16[128,256]{1,0:T(8,128)(2,1)} %copy-done.6, bf16[128,256]{1,0:T(8,128)(2,1)} %copy-done.7, bf16[128,256]{1,0:T(8,128)(2,1)} %copy-done.8, bf16[128,256]{1,0:T(8,128)(2,1)} %copy-done.4, bf16[128,256]{1,0:T(8,128)(2,1)} %copy-done.9, ...), custom_call_target="tpu_custom_call" | custom-call | tf_op jit(solution)/shard_map/assemble/pallas_call | solution.py:358
  (25 shorter events, 0.1 us)
Async XLA Ops:
  0.0 4.6 %copy-start = (bf16[512,2048]{1,0:T(8,128)(2,1)S(1)}, bf16[512,2048]{1,0:T(8,128)(2,1)}, u32[]{:S(2)}) copy-start(bf16[512,2048]{1,0:T(8,128)(2,1)} %queries.3) | copy-start | bytes 6291460
  1.4 14.0 %copy-start.1 = (bf16[512,512]{1,0:T(8,128)(2,1)S(1)}, bf16[512,512]{1,0:T(8,128)(2,1)}, u32[]{:S(2)}) copy-start(bf16[512,512]{1,0:T(8,128)(2,1)} %keys.3) | copy-start | bytes 1572868
  1.4 14.0 %copy-start.2 = (bf16[512,512]{1,0:T(8,128)(2,1)S(1)}, bf16[512,512]{1,0:T(8,128)(2,1)}, u32[]{:S(2)}) copy-start(bf16[512,512]{1,0:T(8,128)(2,1)} %values.3) | copy-start | bytes 1572868
  1.4 14.0 %copy-start.5 = (s32[2048]{0:T(1024)S(1)}, s32[2048]{0:T(1024)}, u32[]{:S(2)}) copy-start(s32[2048]{0:T(1024)} %param.7) | copy-start | bytes 24580
  2.3 13.1 %collective-permute-start.3 = (bf16[2,512,256]{2,1,0:T(8,128)(2,1)}, bf16[2,512,256]{2,1,0:T(8,128)(2,1)}, u32[]{:S(2)}, u32[]{:S(2)}) collective-permute-start(bf16[2,512,256]{2,1,0:T(8,128)(2,1)} %pad_maximum_fusion), channel_id=1, source_target_pairs={{0,1},{1,0},{2,3},{3,2},{4,5},{5,4},{6,7},{7,6},{8,9},{9,8},{10,11... | collective-permute-start | bytes 1572872 | tf_op jit(solution)/shard_map/ppermute | solution.py:384
  3.3 23.3 %collective-permute-start.13 = (bf16[2,512,256]{2,1,0:T(8,128)(2,1)}, bf16[2,512,256]{2,1,0:T(8,128)(2,1)}, u32[]{:S(2)}, u32[]{:S(2)}) collective-permute-start(bf16[2,512,256]{2,1,0:T(8,128)(2,1)} %pad_maximum_fusion.1), channel_id=1, source_target_pairs={{0,1},{1,0},{2,3},{3,2},{4,5},{5,4},{6,7},{7,6},{8,9},{9,8},{10,11... | collective-permute-start | bytes 1572872 | tf_op jit(solution)/shard_map/ppermute | solution.py:384
  4.7 6.9 %collective-permute-start.2 = (bf16[256,256]{1,0:T(8,128)(2,1)S(1)}, bf16[256,256]{1,0:T(8,128)(2,1)S(1)}, u32[]{:S(2)}, u32[]{:S(2)}) collective-permute-start(bf16[256,256]{1,0:T(8,128)(2,1)S(1)} %get-tuple-element.40), channel_id=1, source_target_pairs={{0,12},{4,8},{8,4},{12,0},{1,13},{5,9},{9,5},{13,1},{2,14},{6,10},... | collective-permute-start | bytes 393224 | tf_op jit(solution)/shard_map/ppermute | solution.py:389
  7.1 7.2 %collective-permute-start.1 = (bf16[256,256]{1,0:T(8,128)(2,1)S(1)}, bf16[256,256]{1,0:T(8,128)(2,1)S(1)}, u32[]{:S(2)}, u32[]{:S(2)}) collective-permute-start(bf16[256,256]{1,0:T(8,128)(2,1)S(1)} %get-tuple-element.41), channel_id=1, source_target_pairs={{0,8},{4,12},{8,0},{12,4},{1,9},{5,13},{9,1},{13,5},{2,10},{6,14},... | collective-permute-start | bytes 393224 | tf_op jit(solution)/shard_map/ppermute | solution.py:389
  7.4 7.6 %collective-permute-start = (bf16[256,256]{1,0:T(8,128)(2,1)S(1)}, bf16[256,256]{1,0:T(8,128)(2,1)S(1)}, u32[]{:S(2)}, u32[]{:S(2)}) collective-permute-start(bf16[256,256]{1,0:T(8,128)(2,1)S(1)} %get-tuple-element.42), channel_id=1, source_target_pairs={{0,4},{4,0},{8,12},{12,8},{1,5},{5,1},{9,13},{13,9},{2,6},{6,2},{1... | collective-permute-start | bytes 393224 | tf_op jit(solution)/shard_map/ppermute | solution.py:389
  11.6 9.8 %collective-permute-start.12 = (bf16[256,256]{1,0:T(8,128)(2,1)S(1)}, bf16[256,256]{1,0:T(8,128)(2,1)S(1)}, u32[]{:S(2)}, u32[]{:S(2)}) collective-permute-start(bf16[256,256]{1,0:T(8,128)(2,1)S(1)} %get-tuple-element.37), channel_id=1, source_target_pairs={{0,12},{4,8},{8,4},{12,0},{1,13},{5,9},{9,5},{13,1},{2,14},{6,10},... | collective-permute-start | bytes 393224 | tf_op jit(solution)/shard_map/ppermute | solution.py:389
  14.3 7.8 %collective-permute-start.11 = (bf16[256,256]{1,0:T(8,128)(2,1)S(1)}, bf16[256,256]{1,0:T(8,128)(2,1)S(1)}, u32[]{:S(2)}, u32[]{:S(2)}) collective-permute-start(bf16[256,256]{1,0:T(8,128)(2,1)S(1)} %get-tuple-element.38), channel_id=1, source_target_pairs={{0,8},{4,12},{8,0},{12,4},{1,9},{5,13},{9,1},{13,5},{2,10},{6,14},... | collective-permute-start | bytes 393224 | tf_op jit(solution)/shard_map/ppermute | solution.py:389
  15.0 8.4 %collective-permute-start.10 = (bf16[256,256]{1,0:T(8,128)(2,1)S(1)}, bf16[256,256]{1,0:T(8,128)(2,1)S(1)}, u32[]{:S(2)}, u32[]{:S(2)}) collective-permute-start(bf16[256,256]{1,0:T(8,128)(2,1)S(1)} %get-tuple-element.39), channel_id=1, source_target_pairs={{0,4},{4,0},{8,12},{12,8},{1,5},{5,1},{9,13},{13,9},{2,6},{6,2},{1... | collective-permute-start | bytes 393224 | tf_op jit(solution)/shard_map/ppermute | solution.py:389
  20.1 13.4 %collective-permute-start.5 = (bf16[5,128,128]{2,1,0:T(8,128)(2,1)S(1)}, bf16[5,128,128]{2,1,0:T(8,128)(2,1)S(1)}, u32[]{:S(2)}, u32[]{:S(2)}) collective-permute-start(bf16[5,128,128]{2,1,0:T(8,128)(2,1)S(1)} %get-tuple-element.23), channel_id=1, source_target_pairs={{3,2},{2,1},{7,6},{6,5},{11,10},{10,9},{15,14},{14,13},{19,18},{18... | collective-permute-start | bytes 491528 | tf_op jit(solution)/shard_map/ppermute | solution.py:402
  21.4 19.3 %collective-permute-start.4 = (bf16[9,128,128]{2,1,0:T(8,128)(2,1)S(1)}, bf16[9,128,128]{2,1,0:T(8,128)(2,1)S(1)}, u32[]{:S(2)}, u32[]{:S(2)}) collective-permute-start(bf16[9,128,128]{2,1,0:T(8,128)(2,1)S(1)} %get-tuple-element.22), channel_id=1, source_target_pairs={{0,1},{1,2},{4,5},{5,6},{8,9},{9,10},{12,13},{13,14},{16,17},{17,1... | collective-permute-start | bytes 884744 | tf_op jit(solution)/shard_map/ppermute | solution.py:401
  22.1 18.7 %collective-permute-start.6 = (bf16[9,128,128]{2,1,0:T(8,128)(2,1)S(1)}, bf16[9,128,128]{2,1,0:T(8,128)(2,1)S(1)}, u32[]{:S(2)}, u32[]{:S(2)}) collective-permute-start(bf16[9,128,128]{2,1,0:T(8,128)(2,1)S(1)} %get-tuple-element.24), channel_id=1, source_target_pairs={{1,3},{2,0},{5,7},{6,4},{9,11},{10,8},{13,15},{14,12},{17,19},{18,... | collective-permute-start | bytes 884744 | tf_op jit(solution)/shard_map/ppermute | solution.py:403
  31.5 17.3 %collective-permute-start.14 = (bf16[9,128,128]{2,1,0:T(8,128)(2,1)S(1)}, bf16[9,128,128]{2,1,0:T(8,128)(2,1)S(1)}, u32[]{:S(2)}, u32[]{:S(2)}) collective-permute-start(bf16[9,128,128]{2,1,0:T(8,128)(2,1)S(1)} %get-tuple-element.30), channel_id=1, source_target_pairs={{0,1},{1,2},{4,5},{5,6},{8,9},{9,10},{12,13},{13,14},{16,17},{17,1... | collective-permute-start | bytes 884744 | tf_op jit(solution)/shard_map/ppermute | solution.py:401
  32.1 16.9 %collective-permute-start.16 = (bf16[9,128,128]{2,1,0:T(8,128)(2,1)S(1)}, bf16[9,128,128]{2,1,0:T(8,128)(2,1)S(1)}, u32[]{:S(2)}, u32[]{:S(2)}) collective-permute-start(bf16[9,128,128]{2,1,0:T(8,128)(2,1)S(1)} %get-tuple-element.32), channel_id=1, source_target_pairs={{1,3},{2,0},{5,7},{6,4},{9,11},{10,8},{13,15},{14,12},{17,19},{18,... | collective-permute-start | bytes 884744 | tf_op jit(solution)/shard_map/ppermute | solution.py:403
  33.5 14.3 %collective-permute-start.15 = (bf16[5,128,128]{2,1,0:T(8,128)(2,1)S(1)}, bf16[5,128,128]{2,1,0:T(8,128)(2,1)S(1)}, u32[]{:S(2)}, u32[]{:S(2)}) collective-permute-start(bf16[5,128,128]{2,1,0:T(8,128)(2,1)S(1)} %get-tuple-element.31), channel_id=1, source_target_pairs={{3,2},{2,1},{7,6},{6,5},{11,10},{10,9},{15,14},{14,13},{19,18},{18... | collective-permute-start | bytes 491528 | tf_op jit(solution)/shard_map/ppermute | solution.py:402
  42.3 8.3 %copy-start.3 = (bf16[128,256]{1,0:T(8,128)(2,1)}, bf16[128,256]{1,0:T(8,128)(2,1)S(1)}, u32[]{:S(2)}) copy-start(bf16[128,256]{1,0:T(8,128)(2,1)S(1)} %get-tuple-element.25.refs_0_) | copy-start | bytes 196612
  42.3 14.3 %collective-permute-start.7 = (bf16[128,256]{1,0:T(8,128)(2,1)S(1)}, bf16[128,256]{1,0:T(8,128)(2,1)S(1)}, u32[]{:S(2)}, u32[]{:S(2)}) collective-permute-start(bf16[128,256]{1,0:T(8,128)(2,1)S(1)} %get-tuple-element.26), channel_id=1, source_target_pairs={{0,4},{4,0},{8,12},{12,8},{1,5},{5,1},{9,13},{13,9},{2,6},{6,2},{1... | collective-permute-start | bytes 196616 | tf_op jit(solution)/shard_map/ppermute | solution.py:406
  46.5 10.6 %collective-permute-start.8 = (bf16[128,256]{1,0:T(8,128)(2,1)S(1)}, bf16[128,256]{1,0:T(8,128)(2,1)S(1)}, u32[]{:S(2)}, u32[]{:S(2)}) collective-permute-start(bf16[128,256]{1,0:T(8,128)(2,1)S(1)} %get-tuple-element.27), channel_id=1, source_target_pairs={{0,8},{4,12},{8,0},{12,4},{1,9},{5,13},{9,1},{13,5},{2,10},{6,14},... | collective-permute-start | bytes 196616 | tf_op jit(solution)/shard_map/ppermute | solution.py:406
  47.7 9.3 %collective-permute-start.9 = (bf16[128,256]{1,0:T(8,128)(2,1)S(1)}, bf16[128,256]{1,0:T(8,128)(2,1)S(1)}, u32[]{:S(2)}, u32[]{:S(2)}) collective-permute-start(bf16[128,256]{1,0:T(8,128)(2,1)S(1)} %get-tuple-element.28), channel_id=1, source_target_pairs={{0,12},{4,8},{8,4},{12,0},{1,13},{5,9},{9,5},{13,1},{2,14},{6,10},... | collective-permute-start | bytes 196616 | tf_op jit(solution)/shard_map/ppermute | solution.py:406
  50.6 0.6 copy-start.4
  51.2 5.9 %collective-permute-start.17 = (bf16[128,256]{1,0:T(8,128)(2,1)S(1)}, bf16[128,256]{1,0:T(8,128)(2,1)S(1)}, u32[]{:S(2)}, u32[]{:S(2)}) collective-permute-start(bf16[128,256]{1,0:T(8,128)(2,1)S(1)} %get-tuple-element.34), channel_id=1, source_target_pairs={{0,4},{4,0},{8,12},{12,8},{1,5},{5,1},{9,13},{13,9},{2,6},{6,2},{1... | collective-permute-start | bytes 196616 | tf_op jit(solution)/shard_map/ppermute | solution.py:406
  55.4 3.7 %collective-permute-start.18 = (bf16[128,256]{1,0:T(8,128)(2,1)S(1)}, bf16[128,256]{1,0:T(8,128)(2,1)S(1)}, u32[]{:S(2)}, u32[]{:S(2)}) collective-permute-start(bf16[128,256]{1,0:T(8,128)(2,1)S(1)} %get-tuple-element.35), channel_id=1, source_target_pairs={{0,8},{4,12},{8,0},{12,4},{1,9},{5,13},{9,1},{13,5},{2,10},{6,14},... | collective-permute-start | bytes 196616 | tf_op jit(solution)/shard_map/ppermute | solution.py:406
  56.6 4.0 %copy-start.6 = (bf16[128,256]{1,0:T(8,128)(2,1)}, bf16[128,256]{1,0:T(8,128)(2,1)S(1)}, u32[]{:S(2)}) copy-start(bf16[128,256]{1,0:T(8,128)(2,1)S(1)} %collective-permute-done.7.refs_1_) | copy-start | bytes 196612
  56.6 4.0 %collective-permute-start.19 = (bf16[128,256]{1,0:T(8,128)(2,1)S(1)}, bf16[128,256]{1,0:T(8,128)(2,1)S(1)}, u32[]{:S(2)}, u32[]{:S(2)}) collective-permute-start(bf16[128,256]{1,0:T(8,128)(2,1)S(1)} %get-tuple-element.36), channel_id=1, source_target_pairs={{0,12},{4,8},{8,4},{12,0},{1,13},{5,9},{9,5},{13,1},{2,14},{6,10},... | collective-permute-start | bytes 196616 | tf_op jit(solution)/shard_map/ppermute | solution.py:406
  57.0 3.6 %copy-start.7 = (bf16[128,256]{1,0:T(8,128)(2,1)}, bf16[128,256]{1,0:T(8,128)(2,1)S(1)}, u32[]{:S(2)}) copy-start(bf16[128,256]{1,0:T(8,128)(2,1)S(1)} %collective-permute-done.8.refs_2_) | copy-start | bytes 196612
  57.1 3.6 %copy-start.8 = (bf16[128,256]{1,0:T(8,128)(2,1)}, bf16[128,256]{1,0:T(8,128)(2,1)S(1)}, u32[]{:S(2)}) copy-start(bf16[128,256]{1,0:T(8,128)(2,1)S(1)} %collective-permute-done.9.refs_3_) | copy-start | bytes 196612
  57.1 3.6 %copy-start.9 = (bf16[128,256]{1,0:T(8,128)(2,1)}, bf16[128,256]{1,0:T(8,128)(2,1)S(1)}, u32[]{:S(2)}) copy-start(bf16[128,256]{1,0:T(8,128)(2,1)S(1)} %collective-permute-done.17.refs_5_) | copy-start | bytes 196612
  59.1 1.5 %copy-start.10 = (bf16[128,256]{1,0:T(8,128)(2,1)}, bf16[128,256]{1,0:T(8,128)(2,1)S(1)}, u32[]{:S(2)}) copy-start(bf16[128,256]{1,0:T(8,128)(2,1)S(1)} %collective-permute-done.18.refs_6_) | copy-start | bytes 196612
  60.6 0.6 copy-start.11

commit v2 on v0

--- a/solution.py
+++ b/solution.py
@@ -1,14 +1,18 @@
+import functools
 import math
 
 import jax
 import jax.numpy as jnp
 from jax import lax
+from jax.experimental import pallas as pl
+from jax.experimental.pallas import tpu as pltpu
 from jax.sharding import PartitionSpec as P
 
 HEAD_DIM = 128
-
-
+LANES = 128
 LOW_SCORE = -1e30
+ROW_TILE = 256
+ANY = pl.BlockSpec(memory_space=pl.ANY)
 
 
 def attend_half(q_rows, q_steps, keys_all, values_all, key_steps, block_keys):
@@ -66,7 +70,7 @@
     return final_state
 
 
-def on_device(queries, keys, values, step_of):
+def on_any(queries, keys, values, step_of):
     block_rows, width = queries.shape
     head_size = HEAD_DIM
     head_count = width // head_size
@@ -115,6 +119,210 @@
     result = result.astype(jnp.bfloat16)
     return result
 
+def pack_kernel(queries, keys, values, *refs):
+    outs, sem = refs[:6], refs[6]
+    column = lax.axis_index("pb")
+    z = lax.axis_index("ka")
+    copies = []
+    for d, out in zip((1, 2, 3), outs[:3]):
+        head = pl.ds(pl.multiple_of((z ^ d) * HEAD_DIM, HEAD_DIM), HEAD_DIM)
+        copies += [(keys.at[:, head], out.at[0]), (values.at[:, head], out.at[1])]
+    for d, out in zip((1, 2, 3), outs[3:]):
+        head = pl.ds(pl.multiple_of((column ^ d) * keys.shape[1] + z * HEAD_DIM, HEAD_DIM), HEAD_DIM)
+        copies.append((queries.at[:, head], out))
+    copies = [pltpu.make_async_copy(a, b, sem.at[i]) for i, (a, b) in enumerate(copies)]
+    for copy in copies:
+        copy.start()
+    for copy in copies:
+        copy.wait()
+
+
+def pack(queries, keys, values):
+    pair = jax.ShapeDtypeStruct((2, keys.shape[0], HEAD_DIM), keys.dtype)
+    head = jax.ShapeDtypeStruct((queries.shape[0], HEAD_DIM), queries.dtype)
+    return pl.pallas_call(
+        pack_kernel,
+        out_shape=[pair] * 3 + [head] * 3,
+        in_specs=[ANY] * 3,
+        out_specs=[pl.BlockSpec(memory_space=pltpu.VMEM)] * 6,
+        scratch_shapes=[pltpu.SemaphoreType.DMA((9,))],
+        name="pack",
+    )(queries, keys, values)
+
+
+def split_keys(start, length, late, held):
+    limit = min(start + ROW_TILE + LANES, length)
+    low, high = min(late * held, limit), min((late + 1) * held, limit)
+    early = [cut for cut in ((0, low), (high, limit)) if cut[0] < cut[1]]
+    return early, [(low, high)] if low < high else []
+
+
+def scores_of(q, start, cuts, base, k_buf, steps, columns):
+    q_steps = jnp.concatenate([columns[:, g:g + 1] for g in range(start // LANES, (start + ROW_TILE) // LANES)], axis=0)
+    found = []
+    for low, high in cuts:
+        scores = lax.dot_general(q, k_buf[low - base:high - base, :], (((1,), (1,)), ((), ())),
+                                 preferred_element_type=jnp.float32)
+        first = max(low, start)
+        if first < high:
+            k_steps = jnp.concatenate([steps[g:g + 1] for g in range(first // LANES, high // LANES)], axis=1)
+            seen = jnp.where(k_steps <= q_steps, scores[:, first - low:], LOW_SCORE)
+            scores = jnp.concatenate([scores[:, :first - low], seen], axis=1) if low < first else seen
+        found.append(scores)
+    return jnp.concatenate(found, axis=1) if len(found) > 1 else found[0]
+
+
+def weigh(weights, cuts, base, v_buf):
+    mixed = None
+    at = 0
+    for low, high in cuts:
+        part = lax.dot_general(weights[:, at:at + high - low], v_buf[low - base:high - base, :], (((1,), (0,)), ((), ())),
+                               preferred_element_type=jnp.float32)
+        mixed = part if mixed is None else mixed + part
+        at += high - low
+    return mixed
+
+
+def early_kernel(scale, steps_ref, queries, q_1, q_2, q_3, keys, values, got_1, got_2, sums, stats, q_buf, k_buf, v_buf, sem):
+    column = lax.axis_index("pb")
+    z = lax.axis_index("ka")
+    rows = queries.shape[0]
+    held = keys.shape[0]
+    length = k_buf.shape[0]
+    head = pl.ds(pl.multiple_of(z * HEAD_DIM, HEAD_DIM), HEAD_DIM)
+    query_head = pl.ds(pl.multiple_of(column * keys.shape[1] + z * HEAD_DIM, HEAD_DIM), HEAD_DIM)
+    left = pl.ds(0, HEAD_DIM)
+
+    def block(index, size):
+        return pl.ds(pl.multiple_of(index * size, size), size)
+
+    copies = [
+        (queries.at[:, query_head], q_buf.at[block(column, rows), :]),
+        (keys.at[:, head], k_buf.at[block(z, held), :]),
+        (values.at[:, head], v_buf.at[block(z, held), left]),
+    ]
+    copies += [(q, q_buf.at[block(column ^ d, rows), :]) for d, q in ((1, q_1), (2, q_2), (3, q_3))]
+    for d, got in ((1, got_1), (2, got_2)):
+        copies += [
+            (got.at[0], k_buf.at[block(z ^ d, held), :]),
+            (got.at[1], v_buf.at[block(z ^ d, held), left]),
+        ]
+    copies = [pltpu.make_async_copy(a, b, sem.at[i]) for i, (a, b) in enumerate(copies)]
+    for copy in copies:
+        copy.start()
+    v_buf[:, HEAD_DIM:] = jnp.ones((length, HEAD_DIM), jnp.bfloat16)
+    steps = steps_ref[...].astype(jnp.float32)
+    columns = jnp.transpose(steps)
+    lane = lax.broadcasted_iota(jnp.int32, (ROW_TILE, LANES), 1)
+    for copy in copies:
+        copy.wait()
+    for which in range(4):
+        @pl.when(z == which)
+        def _():
+            for start in range(0, length, ROW_TILE):
+                tile = slice(start, start + ROW_TILE)
+                cuts, _ = split_keys(start, length, which ^ 3, held)
+                if not cuts:
+                    continue
+                scores = scores_of(q_buf[tile, :], start, cuts, 0, k_buf, steps, columns)
+                top = jnp.max(scores, axis=1, keepdims=True) * scale
+                mixed = weigh(jnp.exp2(scores * scale - top).astype(jnp.bfloat16), cuts, 0, v_buf)
+                sums[tile, :] = mixed[:, :HEAD_DIM]
+                stats[tile, :] = jnp.where(lane < LANES // 2, top, mixed[:, HEAD_DIM:])
+
+
+def late_kernel(scale, steps_ref, q_buf, sums, stats, got, out, v_buf):
+    z = lax.axis_index("ka")
+    held = got.shape[1]
+    length = q_buf.shape[0]
+    v_buf[:, :HEAD_DIM] = got[1]
+    v_buf[:, HEAD_DIM:] = jnp.ones((held, HEAD_DIM), jnp.bfloat16)
+    steps = steps_ref[...].astype(jnp.float32)
+    columns = jnp.transpose(steps)
+    k_buf = got.at[0]
+    for which in range(4):
+        @pl.when(z == which)
+        def _():
+            late = which ^ 3
+            for start in range(0, length, ROW_TILE):
+                tile = slice(start, start + ROW_TILE)
+                early, cuts = split_keys(start, length, late, held)
+                if early:
+                    mixed = sums[tile, :]
+                    top, total = stats[tile, 0:1], stats[tile, LANES // 2:LANES // 2 + 1]
+                if cuts:
+                    scores = scores_of(q_buf[tile, :], start, cuts, late * held, k_buf, steps, columns)
+                    best = jnp.max(scores, axis=1, keepdims=True) * scale
+                    if early:
+                        best = jnp.maximum(best, top)
+                    added = weigh(jnp.exp2(scores * scale - best).astype(jnp.bfloat16), cuts, late * held, v_buf)
+                    if early:
+                        kept = jnp.exp2(top - best)
+                        mixed = mixed * kept + added[:, :HEAD_DIM]
+                        total = total * kept + added[:, HEAD_DIM:]
+                    else:
+                        mixed, total = added[:, :HEAD_DIM], added[:, HEAD_DIM:]
+                out[tile, :] = (mixed / total).astype(jnp.bfloat16)
+
+
+def attend(steps, queries, moved, keys, values, got):
+    length = steps.shape[0] * LANES
+    held = keys.shape[0]
+    exps = length * (length // 2 + LANES)
+    scale = math.log2(math.e) / math.sqrt(HEAD_DIM)
+    vmem = pl.BlockSpec(memory_space=pltpu.VMEM)
+    head = jax.ShapeDtypeStruct((length, HEAD_DIM), jnp.bfloat16)
+    held_sums = jax.ShapeDtypeStruct((length, HEAD_DIM), jnp.float32)
+    sums, stats, gathered = pl.pallas_call(
+        functools.partial(early_kernel, scale),
+        out_shape=[held_sums, held_sums, head],
+        in_specs=[vmem] + [ANY] * 8,
+        out_specs=[vmem] * 3,
+        scratch_shapes=[
+            pltpu.VMEM((length, HEAD_DIM), jnp.bfloat16),
+            pltpu.VMEM((length, 2 * HEAD_DIM), jnp.bfloat16),
+            pltpu.SemaphoreType.DMA((10,)),
+        ],
+        compiler_params=pltpu.CompilerParams(vmem_limit_bytes=40 << 20),
+        cost_estimate=pl.CostEstimate(flops=exps * 4 * HEAD_DIM, bytes_accessed=4 << 20, transcendentals=exps),
+        name="attend_early",
+    )(steps, queries, *moved, keys, values, *got[:2])
+    return pl.pallas_call(
+        functools.partial(late_kernel, scale),
+        out_shape=head,
+        in_specs=[vmem] * 5,
+        out_specs=vmem,
+        scratch_shapes=[pltpu.VMEM((held, 2 * HEAD_DIM), jnp.bfloat16)],
+        compiler_params=pltpu.CompilerParams(vmem_limit_bytes=40 << 20),
+        cost_estimate=pl.CostEstimate(flops=exps * HEAD_DIM, bytes_accessed=4 << 20, transcendentals=exps // 4),
+        name="attend_late",
+    )(steps, gathered, sums, stats, got[2])
+
+
+def one_head_each(queries, keys, values, step_of):
+    swaps = [[(i, i ^ d) for i in range(4)] for d in (1, 2, 3)]
+    packed = pack(queries, keys, values)
+    got = [lax.ppermute(piece, "ka", swap) for piece, swap in zip(packed[:3], swaps)]
+    moved = [lax.ppermute(piece, "pb", swap) for piece, swap in zip(packed[3:], swaps)]
+    done = attend(step_of.reshape(-1, LANES), queries, moved, keys, values, got)
+    rows = done.shape[0] // 16
+    pieces = lax.all_to_all(done.reshape(16, rows, HEAD_DIM), ("pb", "ka"), split_axis=0, concat_axis=0, tiled=True)
+    return jnp.transpose(pieces, (1, 0, 2)).reshape(rows, 16 * HEAD_DIM)
+
+
+def on_device(queries, keys, values, step_of):
+    rows = queries.shape[0]
+    held, block = keys.shape
+    square = (
+        lax.axis_size("pb") == 4
+        and lax.axis_size("ka") == 4
+        and held == rows == 4 * LANES
+        and block == 4 * HEAD_DIM
+    )
+    if square:
+        return one_head_each(queries, keys, values, step_of)
+    return on_any(queries, keys, values, step_of)
+
 
 def solution(mesh):
     placed = (

time: 305 us -> 57.9 us (0.19)
  the two profiles are of different devices: /device:TPU:2 before, /device:TPU:0 now
where the time goes in v2:
time: 57.9 us; the launch traced here: 57.8 us
  blocking collectives  22 us (38%)
  waiting for transfers between devices  17.2 us (30%)
  Pallas kernels  10.1 us (17%)
  starting transfers between devices  7.49 us (13%)
  local copies, waits for them, and re-layouts  0.88 us (2%)
    all_to_all x1, blocking collectives, one_head_each(): lax.all_to_all(done.reshape(16, rows, HEAD_DIM), ('pb', 'ka'), split_axis...  22 us
    ppermute x3, waiting for transfers between devices, one_head_each(): lax.ppermute(piece, 'ka', swap)  11.2 us
    ppermute x3, waiting for transfers between devices, one_head_each(): lax.ppermute(piece, 'pb', swap)  6.02 us
    pallas_call x1, Pallas kernels, attend(): pl.pallas_call(functools.partial(early_kernel, scale), out_shape=[held_su...  5.85 us
    ppermute x3, starting transfers between devices, one_head_each(): lax.ppermute(piece, 'ka', swap)  5.24 us
    pallas_call x1, Pallas kernels, pack(): pl.pallas_call(pack_kernel, out_shape=[pair] * 3 + [head] * 3, in_specs=[...  2.58 us
    ppermute x3, starting transfers between devices, one_head_each(): lax.ppermute(piece, 'pb', swap)  2.25 us
    pallas_call x1, Pallas kernels, attend(): pl.pallas_call(functools.partial(late_kernel, scale), out_shape=head, in_...  1.64 us
  transfers between devices with their start and end apart: 6, of which 4 were waited for; matrix products, arithmetic and copies ran while one was open for 0% of the time, Pallas kernels for 10%

profile of v2, /device:TPU:0, one launch (start us, length us, event | category | flops | bytes accessed | tf_op | source)
XLA Modules:
  0.0 57.8 jit_solution(17654259189672397257)
XLA Ops:
  0.0 0.0 copy-start.2
  0.0 0.0 copy-start.1
  0.0 0.0 copy-start
  0.0 0.0 copy-start.3
  0.0 2.6 %pack.1 = (bf16[2,512,128]{2,1,0:T(8,128)(2,1)}, bf16[2,512,128]{2,1,0:T(8,128)(2,1)}, bf16[2,512,128]{2,1,0:T(8,128)(2,1)}, bf16[512,128]{1,0:T(8,128)(2,1)}, b...) custom-call(bf16[512,2048]{1,0:T(8,128)(2,1)} %queries.3, bf16[512,512]{1,0:T(8,128)(2,1)} %keys.3, bf16[512,512]{1,0:T(8,128)(2,1)} %values.3), custom_call_target="tpu_custom_call" | custom-call | tf_op jit(solution)/shard_map/pack/pallas_call | solution.py:143
  2.6 0.5 collective-permute-start
  3.1 2.6 %collective-permute-start.3 = (bf16[2,512,128]{2,1,0:T(8,128)(2,1)}, bf16[2,512,128]{2,1,0:T(8,128)(2,1)S(1)}, u32[]{:S(2)}, u32[]{:S(2)}) collective-permute-start(bf16[2,512,128]{2,1,0:T(8,128)(2,1)} %get-tuple-element.17), channel_id=1, source_target_pairs={{0,1},{1,0},{2,3},{3,2},{4,5},{5,4},{6,7},{7,6},{8,9},{9,8},{10,11... | collective-permute-start | bytes 786440 | tf_op jit(solution)/shard_map/ppermute | solution.py:305
  5.8 2.6 %collective-permute-start.4 = (bf16[2,512,128]{2,1,0:T(8,128)(2,1)}, bf16[2,512,128]{2,1,0:T(8,128)(2,1)S(1)}, u32[]{:S(2)}, u32[]{:S(2)}) collective-permute-start(bf16[2,512,128]{2,1,0:T(8,128)(2,1)} %get-tuple-element.18), channel_id=1, source_target_pairs={{0,2},{1,3},{2,0},{3,1},{4,6},{5,7},{6,4},{7,5},{8,10},{9,11},{10,... | collective-permute-start | bytes 786440 | tf_op jit(solution)/shard_map/ppermute | solution.py:305
  8.4 0.0 collective-permute-start.5
  8.4 1.7 %collective-permute-start.1 = (bf16[512,128]{1,0:T(8,128)(2,1)}, bf16[512,128]{1,0:T(8,128)(2,1)S(1)}, u32[]{:S(2)}, u32[]{:S(2)}) collective-permute-start(bf16[512,128]{1,0:T(8,128)(2,1)} %get-tuple-element.15), channel_id=1, source_target_pairs={{0,8},{4,12},{8,0},{12,4},{1,9},{5,13},{9,1},{13,5},{2,10},{6,14},... | collective-permute-start | bytes 393224 | tf_op jit(solution)/shard_map/ppermute | solution.py:306
  10.1 0.0 collective-permute-done.q_1
  10.1 0.0 collective-permute-start.2
  10.1 4.3 %collective-permute-done.1.q_2 = bf16[512,128]{1,0:T(8,128)(2,1)S(1)} collective-permute-done((bf16[512,128]{1,0:T(8,128)(2,1)}, bf16[512,128]{1,0:T(8,128)(2,1)S(1)}, u32[]{:S(2)}, u32[]{:S(2)}) %collective-permute-start.1) | collective-permute-done | bytes 131104 | tf_op jit(solution)/shard_map/ppermute | solution.py:306
  14.4 1.7 %collective-permute-done.2.q_3 = bf16[512,128]{1,0:T(8,128)(2,1)S(1)} collective-permute-done((bf16[512,128]{1,0:T(8,128)(2,1)}, bf16[512,128]{1,0:T(8,128)(2,1)S(1)}, u32[]{:S(2)}, u32[]{:S(2)}) %collective-permute-start.2) | collective-permute-done | bytes 131104 | tf_op jit(solution)/shard_map/ppermute | solution.py:306
  16.1 2.0 %collective-permute-done.3.got_1 = bf16[2,512,128]{2,1,0:T(8,128)(2,1)S(1)} collective-permute-done((bf16[2,512,128]{2,1,0:T(8,128)(2,1)}, bf16[2,512,128]{2,1,0:T(8,128)(2,1)S(1)}, u32[]{:S(2)}, u32[]{:S(2)}) %collective-permute-start.3) | collective-permute-done | bytes 262176 | tf_op jit(solution)/shard_map/ppermute | solution.py:305
  18.1 9.3 %collective-permute-done.4.got_2 = bf16[2,512,128]{2,1,0:T(8,128)(2,1)S(1)} collective-permute-done((bf16[2,512,128]{2,1,0:T(8,128)(2,1)}, bf16[2,512,128]{2,1,0:T(8,128)(2,1)S(1)}, u32[]{:S(2)}, u32[]{:S(2)}) %collective-permute-start.4) | collective-permute-done | bytes 262176 | tf_op jit(solution)/shard_map/ppermute | solution.py:305
  27.3 0.0 copy-done.2
  27.3 0.0 copy-done.1
  27.3 0.0 copy-done
  27.3 0.0 copy-done.3
  27.3 5.9 %attend_early.1 = (f32[2048,128]{1,0:T(8,128)S(1)}, f32[2048,128]{1,0:T(8,128)S(1)}, bf16[2048,128]{1,0:T(8,128)(2,1)S(1)}) custom-call(s32[16,128]{1,0:T(8,128)S(1)} %bitcast.9, bf16[512,2048]{1,0:T(8,128)(2,1)S(1)} %copy-done, bf16[512,128]{1,0:T(8,128)(2,1)S(1)} %collective-permute-done.q_1, bf16[512,128]{1,0:T(8,128)(2,1)S(1)} %collective-permute-done.1.q_2, ...), custom_call_target="tpu_custom_call" | custom-call | flops 1207959552 | bytes 4194304 | tf_op jit(solution)/shard_map/attend_early/pallas_call | solution.py:276
  33.2 0.0 collective-permute-done.5.got
  33.2 1.6 %attend_late.1 = bf16[2048,128]{1,0:T(8,128)(2,1)S(1)} custom-call(s32[16,128]{1,0:T(8,128)S(1)} %bitcast.10, bf16[2048,128]{1,0:T(8,128)(2,1)S(1)} %get-tuple-element.19.q_buf, f32[2048,128]{1,0:T(8,128)S(1)} %get-tuple-element.20.sums, f32[2048,128]{1,0:T(8,128)S(1)} %get-tuple-element.21.stats, bf16[2,512,128]{2,1,0:T(8,128)(2,1)S(1)} %collective-permute-done.5.got), custom_call_target="tpu_custom_call" | custom-call | flops 301989888 | bytes 4194304 | tf_op jit(solution)/shard_map/attend_late/pallas_call | solution.py:290
  34.9 22.0 %all_to_all.5 = bf16[16,128,128]{2,1,0:T(8,128)(2,1)S(1)} all-to-all(bf16[16,128,128]{2,1,0:T(8,128)(2,1)S(1)} %bitcast.8), channel_id=1, replica_groups=mesh['groups'=2,'pb'=4,'ka'=4] {'pb','ka'}, dimensions={0} | all-to-all | bytes 1048576 | tf_op jit(solution)/shard_map/all_to_all | solution.py:309
  56.9 0.9 %copy_bitcast_fusion = bf16[128,2048]{1,0:T(8,128)(2,1)} fusion(bf16[16,128,128]{2,1,0:T(8,128)(2,1)S(1)} %all_to_all.5), kind=kLoop, calls=%fused_computation | loop fusion | bytes 1048576 | tf_op jit(solution)/shard_map/reshape | solution.py:310
Async XLA Ops:
  0.0 27.3 %copy-start.2 = (bf16[512,512]{1,0:T(8,128)(2,1)S(1)}, bf16[512,512]{1,0:T(8,128)(2,1)}, u32[]{:S(2)}) copy-start(bf16[512,512]{1,0:T(8,128)(2,1)} %values.3) | copy-start | bytes 1572868
  0.0 27.3 %copy-start.1 = (bf16[512,512]{1,0:T(8,128)(2,1)S(1)}, bf16[512,512]{1,0:T(8,128)(2,1)}, u32[]{:S(2)}) copy-start(bf16[512,512]{1,0:T(8,128)(2,1)} %keys.3) | copy-start | bytes 1572868
  0.0 27.3 %copy-start = (bf16[512,2048]{1,0:T(8,128)(2,1)S(1)}, bf16[512,2048]{1,0:T(8,128)(2,1)}, u32[]{:S(2)}) copy-start(bf16[512,2048]{1,0:T(8,128)(2,1)} %queries.3) | copy-start | bytes 6291460
  0.0 27.3 %copy-start.3 = (s32[2048]{0:T(1024)S(1)}, s32[2048]{0:T(1024)}, u32[]{:S(2)}) copy-start(s32[2048]{0:T(1024)} %param.7) | copy-start | bytes 24580
  2.6 7.5 %collective-permute-start = (bf16[512,128]{1,0:T(8,128)(2,1)}, bf16[512,128]{1,0:T(8,128)(2,1)S(1)}, u32[]{:S(2)}, u32[]{:S(2)}) collective-permute-start(bf16[512,128]{1,0:T(8,128)(2,1)} %get-tuple-element.14), channel_id=1, source_target_pairs={{0,4},{4,0},{8,12},{12,8},{1,5},{5,1},{9,13},{13,9},{2,6},{6,2},{1... | collective-permute-start | bytes 393224 | tf_op jit(solution)/shard_map/ppermute | solution.py:306
  3.1 14.9 %collective-permute-start.3 = (bf16[2,512,128]{2,1,0:T(8,128)(2,1)}, bf16[2,512,128]{2,1,0:T(8,128)(2,1)S(1)}, u32[]{:S(2)}, u32[]{:S(2)}) collective-permute-start(bf16[2,512,128]{2,1,0:T(8,128)(2,1)} %get-tuple-element.17), channel_id=1, source_target_pairs={{0,1},{1,0},{2,3},{3,2},{4,5},{5,4},{6,7},{7,6},{8,9},{9,8},{10,11... | collective-permute-start | bytes 786440 | tf_op jit(solution)/shard_map/ppermute | solution.py:305
  5.8 21.5 %collective-permute-start.4 = (bf16[2,512,128]{2,1,0:T(8,128)(2,1)}, bf16[2,512,128]{2,1,0:T(8,128)(2,1)S(1)}, u32[]{:S(2)}, u32[]{:S(2)}) collective-permute-start(bf16[2,512,128]{2,1,0:T(8,128)(2,1)} %get-tuple-element.18), channel_id=1, source_target_pairs={{0,2},{1,3},{2,0},{3,1},{4,6},{5,7},{6,4},{7,5},{8,10},{9,11},{10,... | collective-permute-start | bytes 786440 | tf_op jit(solution)/shard_map/ppermute | solution.py:305
  8.4 24.8 %collective-permute-start.5 = (bf16[2,512,128]{2,1,0:T(8,128)(2,1)}, bf16[2,512,128]{2,1,0:T(8,128)(2,1)S(1)}, u32[]{:S(2)}, u32[]{:S(2)}) collective-permute-start(bf16[2,512,128]{2,1,0:T(8,128)(2,1)} %get-tuple-element.22), channel_id=1, source_target_pairs={{0,3},{1,2},{2,1},{3,0},{4,7},{5,6},{6,5},{7,4},{8,11},{9,10},{10,... | collective-permute-start | bytes 786440 | tf_op jit(solution)/shard_map/ppermute | solution.py:305
  8.4 6.1 %collective-permute-start.1 = (bf16[512,128]{1,0:T(8,128)(2,1)}, bf16[512,128]{1,0:T(8,128)(2,1)S(1)}, u32[]{:S(2)}, u32[]{:S(2)}) collective-permute-start(bf16[512,128]{1,0:T(8,128)(2,1)} %get-tuple-element.15), channel_id=1, source_target_pairs={{0,8},{4,12},{8,0},{12,4},{1,9},{5,13},{9,1},{13,5},{2,10},{6,14},... | collective-permute-start | bytes 393224 | tf_op jit(solution)/shard_map/ppermute | solution.py:306
  10.1 6.0 %collective-permute-start.2 = (bf16[512,128]{1,0:T(8,128)(2,1)}, bf16[512,128]{1,0:T(8,128)(2,1)S(1)}, u32[]{:S(2)}, u32[]{:S(2)}) collective-permute-start(bf16[512,128]{1,0:T(8,128)(2,1)} %get-tuple-element.16), channel_id=1, source_target_pairs={{0,12},{4,8},{8,4},{12,0},{1,13},{5,9},{9,5},{13,1},{2,14},{6,10},... | collective-permute-start | bytes 393224 | tf_op jit(solution)/shard_map/ppermute | solution.py:306

commit v3 on v0

--- a/solution.py
+++ b/solution.py
@@ -1,14 +1,21 @@
+import functools
 import math
 
 import jax
 import jax.numpy as jnp
 from jax import lax
+from jax.experimental import pallas as pl
+from jax.experimental.pallas import tpu as pltpu
 from jax.sharding import PartitionSpec as P
 
 HEAD_DIM = 128
-
-
+LANES = 128
 LOW_SCORE = -1e30
+UNSEEN = -float(1 << 20)
+ROW_TILE = 256
+STATS = 16
+ANY = pl.BlockSpec(memory_space=pl.ANY)
+VMEM = pl.BlockSpec(memory_space=pltpu.VMEM)
 
 
 def attend_half(q_rows, q_steps, keys_all, values_all, key_steps, block_keys):
@@ -66,7 +73,7 @@
     return final_state
 
 
-def on_device(queries, keys, values, step_of):
+def on_any(queries, keys, values, step_of):
     block_rows, width = queries.shape
     head_size = HEAD_DIM
     head_count = width // head_size
@@ -115,6 +122,275 @@
     result = result.astype(jnp.bfloat16)
     return result
 
+def run_copies(pairs, sem):
+    copies = [pltpu.make_async_copy(a, b, sem.at[i]) for i, (a, b) in enumerate(pairs)]
+    for copy in copies:
+        copy.start()
+    return copies
+
+
+def aligned(index, size):
+    return pl.ds(pl.multiple_of(index * size, size), size)
+
+
+def pack_kernel(chunk, queries, keys, values, pair, to_1, to_2, to_3, sem):
+    column = lax.axis_index("pb")
+    half = lax.axis_index("ka") % 2
+    heads = keys.shape[1] // HEAD_DIM
+    theirs = aligned((1 - half) * 2 + chunk, HEAD_DIM)
+    pairs = [(keys.at[:, theirs], pair.at[0]), (values.at[:, theirs], pair.at[1])]
+    for d, to in ((1, to_1), (2, to_2), (3, to_3)):
+        pairs.append((queries.at[:, aligned((column ^ d) * heads + half * 2 + chunk, HEAD_DIM)], to))
+    for copy in run_copies(pairs, sem):
+        copy.wait()
+
+
+def pack(chunk, queries, keys, values):
+    pair = jax.ShapeDtypeStruct((2, keys.shape[0], HEAD_DIM), keys.dtype)
+    head = jax.ShapeDtypeStruct((queries.shape[0], HEAD_DIM), queries.dtype)
+    return pl.pallas_call(
+        functools.partial(pack_kernel, chunk),
+        out_shape=[pair] + [head] * 3,
+        in_specs=[pl.BlockSpec(memory_space=pltpu.HBM)] * 3,
+        out_specs=[VMEM] * 4,
+        scratch_shapes=[pltpu.SemaphoreType.DMA((5,))],
+        name="pack",
+    )(queries, keys, values)
+
+
+def attend_kernel(chunk, scale, steps_ref, queries, keys, values, q_1, q_2, q_3, got, own, to_1, to_2, to_3,
+                  q_buf, k_buf, v_buf, stats_buf, parts, sem, out_sem):
+    column = lax.axis_index("pb")
+    z = lax.axis_index("ka")
+    rows = queries.shape[0]
+    half_rows, sub = rows // 2, rows // 4
+    held = keys.shape[0]
+    pair = 2 * held
+    heads = keys.shape[1] // HEAD_DIM
+    upper, half = z // 2, z % 2
+    left = pl.ds(0, HEAD_DIM)
+    head = aligned(half * 2 + chunk, HEAD_DIM)
+
+    def place(block):
+        return (block + 4 - 2 * upper) % 4
+
+    pairs = [
+        (keys.at[:, head], k_buf.at[aligned(half, held), :]),
+        (got.at[0], k_buf.at[aligned(1 - half, held), :]),
+        (queries.at[:, aligned(column * heads + half * 2 + chunk, HEAD_DIM)], q_buf.at[place(column)]),
+    ]
+    pairs += [(q, q_buf.at[place(column ^ d)]) for d, q in ((1, q_1), (2, q_2), (3, q_3))]
+    pairs += [
+        (values.at[:, head], v_buf.at[aligned(half, held), left]),
+        (got.at[1], v_buf.at[aligned(1 - half, held), left]),
+    ]
+    copies = run_copies(pairs, sem)
+    v_buf[:, HEAD_DIM:] = jnp.ones((pair, HEAD_DIM), jnp.bfloat16)
+    steps = steps_ref[...].astype(jnp.float32)
+    columns = jnp.transpose(steps)
+    for copy in copies:
+        copy.wait()
+
+    def tile(slot, start, first_row, limit, masked_from, base, stats, size=half_rows):
+        scores = lax.dot_general(q_buf[slot, start:start + size, :], k_buf[:limit, :],
+                                 (((1,), (1,)), ((), ())), preferred_element_type=jnp.float32)
+        if masked_from < limit:
+            at = (first_row + start) // LANES
+            q_steps = jnp.concatenate([columns[:, g:g + 1] for g in range(at, at + size // LANES)], axis=0)
+            k_steps = jnp.concatenate([steps[g:g + 1] for g in range((base + masked_from) // LANES, (base + limit) // LANES)], axis=1)
+            seen = jnp.where(k_steps <= q_steps, scores[:, masked_from:], UNSEEN / scale)
+            scores = jnp.concatenate([scores[:, :masked_from], seen], axis=1) if masked_from else seen
+        top = jnp.max(scores, axis=1, keepdims=True) * scale
+        top = top.astype(jnp.bfloat16).astype(jnp.float32)
+        weights = jnp.exp2(scores * scale - top).astype(jnp.bfloat16)
+        mixed = lax.dot_general(weights, v_buf[:limit, :], (((1,), (0,)), ((), ())), preferred_element_type=jnp.float32)
+        total = mixed[:, HEAD_DIM:]
+        result = (mixed[:, :HEAD_DIM] / total).astype(jnp.bfloat16)
+        for j in range(0, size, sub):
+            parts[(start + j) // sub, slot * sub:(slot + 1) * sub, :] = result[j:j + sub]
+        high = total.astype(jnp.bfloat16).astype(jnp.float32)
+        lane = lax.broadcasted_iota(jnp.int32, (size, LANES), 1)
+        stats = jnp.where(lane == 3 * slot, top, stats)
+        stats = jnp.where(lane == 3 * slot + 1, high, stats)
+        return jnp.where(lane == 3 * slot + 2, total - high, stats)
+
+    def region(which, start):
+        base = which * pair
+        reach = start + half_rows + LANES
+        stats = jnp.zeros((half_rows, LANES), jnp.float32)
+        stats = tile(0, start, base, reach, start, base, stats)
+        stats = tile(1, start, base + held, min(held + reach, pair), held + start, base, stats)
+        if which == 0:
+            stats = tile(2, start, 0, pair, pair, base, stats)
+            stats = tile(3, start, 0, pair, pair, base, stats)
+        stats_buf[...] = stats
+        if which == 1 and start > 0:
+            stats_buf[sub:, :] = tile(3, start + sub, held, LANES, 0, base, stats[sub:], sub)
+        for j in range(2):
+            stats = jnp.transpose(stats_buf[j * sub:(j + 1) * sub, :])
+            parts[start // sub + j, 4 * sub:, :] = stats[:STATS].astype(jnp.bfloat16)
+
+    def send(outs):
+        copies = [pltpu.make_async_copy(parts.at[z ^ d], to, out_sem.at[d]) for d, to in outs]
+        for copy in copies:
+            copy.start()
+        return copies
+
+    for which in range(2):
+        @pl.when(upper == which)
+        def _():
+            region(which, (1 - which) * half_rows)
+
+    sent = send(((3, to_3), (2, to_2)))
+    for which in range(2):
+        @pl.when(upper == which)
+        def _():
+            region(which, which * half_rows)
+
+    for copy in sent + send(((1, to_1), (0, own))):
+        copy.wait()
+
+
+def attend(chunk, steps, queries, keys, values, ready):
+    rows = queries.shape[0]
+    held = keys.shape[0]
+    part = jax.ShapeDtypeStruct((rows + STATS, LANES), jnp.bfloat16)
+    exps = 4 * rows * 2 * held
+    return pl.pallas_call(
+        functools.partial(attend_kernel, chunk, math.log2(math.e) / math.sqrt(HEAD_DIM)),
+        out_shape=[part] * 4,
+        in_specs=[VMEM] + [ANY] * 7,
+        out_specs=[ANY] * 4,
+        scratch_shapes=[
+            pltpu.VMEM((4, rows, HEAD_DIM), jnp.bfloat16),
+            pltpu.VMEM((2 * held, HEAD_DIM), jnp.bfloat16),
+            pltpu.VMEM((2 * held, 2 * HEAD_DIM), jnp.bfloat16),
+            pltpu.VMEM((rows // 2, LANES), jnp.float32),
+            pltpu.VMEM((4,) + part.shape, jnp.bfloat16),
+            pltpu.SemaphoreType.DMA((8,)),
+            pltpu.SemaphoreType.DMA((4,)),
+        ],
+        compiler_params=pltpu.CompilerParams(vmem_limit_bytes=24 << 20),
+        cost_estimate=pl.CostEstimate(flops=exps * 4 * HEAD_DIM, bytes_accessed=4 << 20, transcendentals=exps),
+        name="attend",
+    )(steps, queries, keys, values, *ready)
+
+
+def merge_kernel(own, from_1, from_2, from_3, out_0, out_1, out_2, out_3, held, result, sem):
+    column = lax.axis_index("pb")
+    z = lax.axis_index("ka")
+    sub = result.shape[2]
+    for copy in run_copies([(a, held.at[z ^ d]) for d, a in enumerate((own, from_1, from_2, from_3))], sem):
+        copy.wait()
+    stats = [jnp.transpose(held[s, 4 * sub:, :].astype(jnp.float32)) for s in range(4)]
+
+    def part(s, slot):
+        return held[s, slot * sub:(slot + 1) * sub, :]
+
+    def merge_block(block, half):
+        parts = ((half, block), (2 + half, (block + 2) % 4))
+        tops = [stats[s][:, 3 * slot:3 * slot + 1] for s, slot in parts]
+        totals = [stats[s][:, 3 * slot + 1:3 * slot + 2] + stats[s][:, 3 * slot + 2:3 * slot + 3] for s, slot in parts]
+        best = jnp.maximum(*tops)
+        shares = [total * jnp.exp2(top - best) for top, total in zip(tops, totals)]
+        share = shares[0] / (shares[0] + shares[1])
+        a, b = [part(s, slot).astype(jnp.float32) for s, slot in parts]
+        result[block, half] = (a * share + b * (1.0 - share)).astype(jnp.bfloat16)
+
+    for half in range(2):
+        result[0, half] = part(half, 0)
+        merge_block(2, half)
+        merge_block(3, half)
+
+    @pl.when(z < 3)
+    def _():
+        for half in range(2):
+            result[1, half] = part(half, 1)
+
+    @pl.when(z == 3)
+    def _():
+        for half in range(2):
+            merge_block(1, half)
+
+    outs = ((3, out_3), (2, out_2), (1, out_1), (0, out_0))
+    for copy in run_copies([(result.at[column ^ d], out) for d, out in outs], sem):
+        copy.wait()
+
+
+def merge(parts):
+    sub = (parts[0].shape[0] - STATS) // 4
+    block = jax.ShapeDtypeStruct((2, sub, HEAD_DIM), jnp.bfloat16)
+    return pl.pallas_call(
+        merge_kernel,
+        out_shape=[block] * 4,
+        in_specs=[ANY] * 4,
+        out_specs=[ANY] * 4,
+        scratch_shapes=[
+            pltpu.VMEM((4,) + parts[0].shape, jnp.bfloat16),
+            pltpu.VMEM((4,) + block.shape, jnp.bfloat16),
+            pltpu.SemaphoreType.DMA((4,)),
+        ],
+        compiler_params=pltpu.CompilerParams(vmem_limit_bytes=4 << 20),
+        cost_estimate=pl.CostEstimate(flops=1 << 10, bytes_accessed=1 << 10, transcendentals=0),
+        name="merge",
+    )(*parts)
+
+
+def assemble_kernel(*refs):
+    pieces, (out, held, sem) = refs[:-3], refs[-3:]
+    column = lax.axis_index("pb")
+    pairs = []
+    for i, piece in enumerate(pieces):
+        chunk, d = i // 4, i % 4
+        pairs += [(piece.at[half], held.at[(column ^ d) * 4 + 2 * half + chunk]) for half in range(2)]
+    for copy in run_copies(pairs, sem):
+        copy.wait()
+    for head in range(held.shape[0]):
+        out[:, head * HEAD_DIM:(head + 1) * HEAD_DIM] = held[head]
+
+
+def assemble(pieces):
+    sub = pieces[0].shape[1]
+    return pl.pallas_call(
+        assemble_kernel,
+        out_shape=jax.ShapeDtypeStruct((sub, 16 * HEAD_DIM), jnp.bfloat16),
+        in_specs=[ANY] * 8,
+        out_specs=VMEM,
+        scratch_shapes=[pltpu.VMEM((16, sub, HEAD_DIM), jnp.bfloat16), pltpu.SemaphoreType.DMA((16,))],
+        compiler_params=pltpu.CompilerParams(vmem_limit_bytes=4 << 20),
+        name="assemble",
+    )(*pieces)
+
+
+def by_pairs(queries, keys, values, step_of):
+    steps = step_of.reshape(-1, LANES)
+    swaps = [[(i, i ^ d) for i in range(4)] for d in range(4)]
+    ready = []
+    for chunk in range(2):
+        pair, *sent = pack(chunk, queries, keys, values)
+        got = lax.ppermute(pair, "ka", swaps[1])
+        ready.append([lax.ppermute(piece, "pb", swap) for piece, swap in zip(sent, swaps[1:])] + [got])
+    pieces = []
+    for chunk in range(2):
+        own, *parts = attend(chunk, steps, queries, keys, values, ready[chunk])
+        blocks = merge([own] + [lax.ppermute(part, "ka", swap) for part, swap in zip(parts, swaps[1:])])
+        pieces += [blocks[0]] + [lax.ppermute(piece, "pb", swap) for piece, swap in zip(blocks[1:], swaps[1:])]
+    return assemble(pieces)
+
+
+def on_device(queries, keys, values, step_of):
+    rows = queries.shape[0]
+    held, block = keys.shape
+    square = (
+        lax.axis_size("pb") == 4
+        and lax.axis_size("ka") == 4
+        and held == rows == 4 * LANES
+        and block == 4 * HEAD_DIM
+    )
+    if square:
+        return by_pairs(queries, keys, values, step_of)
+    return on_any(queries, keys, values, step_of)
+
 
 def solution(mesh):
     placed = (

time: 305 us -> 55.9 us (0.18)
  the two profiles are of different devices: /device:TPU:2 before, /device:TPU:0 now
where the time goes in v3:
time: 55.9 us; the launch traced here: 55.8 us
  starting transfers between devices  21.2 us (38%)
  Pallas kernels  20.7 us (37%)
  waiting for transfers between devices  13.4 us (24%)
    pallas_call x2, Pallas kernels, attend(): pl.pallas_call(functools.partial(attend_kernel, chunk, math.log2(math.e)...  11.5 us
    ppermute x12, starting transfers between devices, by_pairs(): lax.ppermute(piece, 'pb', swap)  8.96 us
    ppermute x6, starting transfers between devices, by_pairs(): lax.ppermute(part, 'ka', swap)  8.9 us
    ppermute x6, waiting for transfers between devices, by_pairs(): lax.ppermute(part, 'ka', swap)  7.04 us
    ppermute x12, waiting for transfers between devices, by_pairs(): lax.ppermute(piece, 'pb', swap)  6.4 us
    pallas_call x2, Pallas kernels, pack(): pl.pallas_call(functools.partial(pack_kernel, chunk), out_shape=[pair] +...  4.1 us
    pallas_call x2, Pallas kernels, merge(): pl.pallas_call(merge_kernel, out_shape=[block] * 4, in_specs=[ANY] * 4, o...  3.4 us
    ppermute x2, starting transfers between devices, by_pairs(): got = lax.ppermute(pair, 'ka', swaps[1])  3.38 us
  transfers between devices with their start and end apart: 20, of which 5 were waited for; matrix products, arithmetic and copies ran while one was open for 0% of the time, Pallas kernels for 30%

profile of v3, /device:TPU:0, one launch (start us, length us, event | category | flops | bytes accessed | tf_op | source)
XLA Modules:
  0.0 55.8 jit_solution(14796441970943583252)
XLA Ops:
  0.0 2.0 %pack.2 = (bf16[2,512,128]{2,1,0:T(8,128)(2,1)}, bf16[512,128]{1,0:T(8,128)(2,1)}, bf16[512,128]{1,0:T(8,128)(2,1)}, bf16[512,128]{1,0:T(8,128)(2,1)}) custom-call(bf16[512,2048]{1,0:T(8,128)(2,1)} %queries.7, bf16[512,512]{1,0:T(8,128)(2,1)} %keys.7, bf16[512,512]{1,0:T(8,128)(2,1)} %values.7), custom_call_target="tpu_custom_call" | custom-call | tf_op jit(solution)/shard_map/pack/pallas_call | solution.py:151
  2.1 0.0 copy-start
  2.1 0.0 copy-start.1
  2.1 0.0 copy-start.2
  2.1 0.0 copy-start.3
  2.1 3.1 %collective-permute-start.3 = (bf16[2,512,128]{2,1,0:T(8,128)(2,1)}, bf16[2,512,128]{2,1,0:T(8,128)(2,1)S(1)}, u32[]{:S(2)}, u32[]{:S(2)}) collective-permute-start(bf16[2,512,128]{2,1,0:T(8,128)(2,1)} %get-tuple-element.32), channel_id=1, source_target_pairs={{0,1},{1,0},{2,3},{3,2},{4,5},{5,4},{6,7},{7,6},{8,9},{9,8},{10,11... | collective-permute-start | bytes 786440 | tf_op jit(solution)/shard_map/ppermute | solution.py:371
  5.2 0.0 collective-permute-start
  5.2 1.5 %collective-permute-start.1 = (bf16[512,128]{1,0:T(8,128)(2,1)}, bf16[512,128]{1,0:T(8,128)(2,1)}, u32[]{:S(2)}, u32[]{:S(2)}) collective-permute-start(bf16[512,128]{1,0:T(8,128)(2,1)} %get-tuple-element.30), channel_id=1, source_target_pairs={{0,8},{4,12},{8,0},{12,4},{1,9},{5,13},{9,1},{13,5},{2,10},{6,14},... | collective-permute-start | bytes 393224 | tf_op jit(solution)/shard_map/ppermute | solution.py:372
  6.7 0.4 collective-permute-start.2
  7.1 2.0 %pack.3 = (bf16[2,512,128]{2,1,0:T(8,128)(2,1)}, bf16[512,128]{1,0:T(8,128)(2,1)}, bf16[512,128]{1,0:T(8,128)(2,1)}, bf16[512,128]{1,0:T(8,128)(2,1)}) custom-call(bf16[512,2048]{1,0:T(8,128)(2,1)} %queries.7, bf16[512,512]{1,0:T(8,128)(2,1)} %keys.7, bf16[512,512]{1,0:T(8,128)(2,1)} %values.7), custom_call_target="tpu_custom_call" | custom-call | tf_op jit(solution)/shard_map/pack/pallas_call | solution.py:151
  9.1 0.3 collective-permute-start.13
  9.4 0.0 collective-permute-done.q_1
  9.4 0.1 collective-permute-start.10
  9.6 2.3 %collective-permute-done.1.q_2 = bf16[512,128]{1,0:T(8,128)(2,1)} collective-permute-done((bf16[512,128]{1,0:T(8,128)(2,1)}, bf16[512,128]{1,0:T(8,128)(2,1)}, u32[]{:S(2)}, u32[]{:S(2)}) %collective-permute-start.1) | collective-permute-done | bytes 131104 | tf_op jit(solution)/shard_map/ppermute | solution.py:372
  11.8 1.5 %collective-permute-start.11 = (bf16[512,128]{1,0:T(8,128)(2,1)}, bf16[512,128]{1,0:T(8,128)(2,1)S(1)}, u32[]{:S(2)}, u32[]{:S(2)}) collective-permute-start(bf16[512,128]{1,0:T(8,128)(2,1)} %get-tuple-element.42), channel_id=1, source_target_pairs={{0,8},{4,12},{8,0},{12,4},{1,9},{5,13},{9,1},{13,5},{2,10},{6,14},... | collective-permute-start | bytes 393224 | tf_op jit(solution)/shard_map/ppermute | solution.py:372
  13.3 0.5 collective-permute-done.2.q_3
  13.8 1.6 %collective-permute-start.12 = (bf16[512,128]{1,0:T(8,128)(2,1)}, bf16[512,128]{1,0:T(8,128)(2,1)S(1)}, u32[]{:S(2)}, u32[]{:S(2)}) collective-permute-start(bf16[512,128]{1,0:T(8,128)(2,1)} %get-tuple-element.43), channel_id=1, source_target_pairs={{0,12},{4,8},{8,4},{12,0},{1,13},{5,9},{9,5},{13,1},{2,14},{6,10},... | collective-permute-start | bytes 393224 | tf_op jit(solution)/shard_map/ppermute | solution.py:372
  15.4 0.0 collective-permute-done.3.got
  15.5 5.9 %attend.2 = (bf16[528,128]{1,0:T(8,128)(2,1)S(1)}, bf16[528,128]{1,0:T(8,128)(2,1)S(1)}, bf16[528,128]{1,0:T(8,128)(2,1)S(1)}, bf16[528,128]{1,0:T(8,128)(2,1)S(1)}) custom-call(s32[16,128]{1,0:T(8,128)S(1)} %bitcast.1, bf16[512,2048]{1,0:T(8,128)(2,1)S(1)} %copy-done, bf16[512,512]{1,0:T(8,128)(2,1)S(1)} %copy-done.1, bf16[512,512]{1,0:T(8,128)(2,1)S(1)} %copy-done.2, ...), custom_call_target="tpu_custom_call" | custom-call | flops 1073741824 | bytes 4194304 | tf_op jit(solution)/shard_map/attend/pallas_call | solution.py:259
  21.4 0.4 collective-permute-start.4
  21.8 0.0 collective-permute-done.10.q_1
  21.8 1.6 %collective-permute-start.5 = (bf16[528,128]{1,0:T(8,128)(2,1)S(1)}, bf16[528,128]{1,0:T(8,128)(2,1)S(1)}, u32[]{:S(2)}, u32[]{:S(2)}) collective-permute-start(bf16[528,128]{1,0:T(8,128)(2,1)S(1)} %get-tuple-element.35), channel_id=1, source_target_pairs={{0,2},{1,3},{2,0},{3,1},{4,6},{5,7},{6,4},{7,5},{8,10},{9,11},{10,... | collective-permute-start | bytes 405512 | tf_op jit(solution)/shard_map/ppermute | solution.py:376
  23.4 0.0 collective-permute-done.11.q_2
  23.4 2.4 %collective-permute-start.6 = (bf16[528,128]{1,0:T(8,128)(2,1)S(1)}, bf16[528,128]{1,0:T(8,128)(2,1)S(1)}, u32[]{:S(2)}, u32[]{:S(2)}) collective-permute-start(bf16[528,128]{1,0:T(8,128)(2,1)S(1)} %get-tuple-element.36), channel_id=1, source_target_pairs={{0,3},{1,2},{2,1},{3,0},{4,7},{5,6},{6,5},{7,4},{8,11},{9,10},{10,... | collective-permute-start | bytes 405512 | tf_op jit(solution)/shard_map/ppermute | solution.py:376
  25.9 0.0 collective-permute-done.12.q_3
  25.9 0.0 collective-permute-done.13.got
  25.9 5.6 %attend.3 = (bf16[528,128]{1,0:T(8,128)(2,1)S(1)}, bf16[528,128]{1,0:T(8,128)(2,1)S(1)}, bf16[528,128]{1,0:T(8,128)(2,1)S(1)}, bf16[528,128]{1,0:T(8,128)(2,1)S(1)}) custom-call(s32[16,128]{1,0:T(8,128)S(1)} %bitcast.2, bf16[512,2048]{1,0:T(8,128)(2,1)S(1)} %copy-done, bf16[512,512]{1,0:T(8,128)(2,1)S(1)} %copy-done.1, bf16[512,512]{1,0:T(8,128)(2,1)S(1)} %copy-done.2, ...), custom_call_target="tpu_custom_call" | custom-call | flops 1073741824 | bytes 4194304 | tf_op jit(solution)/shard_map/attend/pallas_call | solution.py:259
  31.5 0.1 collective-permute-start.14
  31.5 1.0 %collective-permute-start.15 = (bf16[528,128]{1,0:T(8,128)(2,1)S(1)}, bf16[528,128]{1,0:T(8,128)(2,1)S(1)}, u32[]{:S(2)}, u32[]{:S(2)}) collective-permute-start(bf16[528,128]{1,0:T(8,128)(2,1)S(1)} %get-tuple-element.47), channel_id=1, source_target_pairs={{0,2},{1,3},{2,0},{3,1},{4,6},{5,7},{6,4},{7,5},{8,10},{9,11},{10,... | collective-permute-start | bytes 405512 | tf_op jit(solution)/shard_map/ppermute | solution.py:376
  32.5 0.0 collective-permute-done.4.from_1
  32.5 3.4 %collective-permute-start.16 = (bf16[528,128]{1,0:T(8,128)(2,1)S(1)}, bf16[528,128]{1,0:T(8,128)(2,1)S(1)}, u32[]{:S(2)}, u32[]{:S(2)}) collective-permute-start(bf16[528,128]{1,0:T(8,128)(2,1)S(1)} %get-tuple-element.48), channel_id=1, source_target_pairs={{0,3},{1,2},{2,1},{3,0},{4,7},{5,6},{6,5},{7,4},{8,11},{9,10},{10,... | collective-permute-start | bytes 405512 | tf_op jit(solution)/shard_map/ppermute | solution.py:376
  35.9 0.0 collective-permute-done.5.from_2
  35.9 1.7 %merge.2 = (bf16[2,128,128]{2,1,0:T(8,128)(2,1)S(1)}, bf16[2,128,128]{2,1,0:T(8,128)(2,1)S(1)}, bf16[2,128,128]{2,1,0:T(8,128)(2,1)S(1)}, bf16[2,128,128]{2,1,0:T(8,128)(2,1)S(1)}) custom-call(bf16[528,128]{1,0:T(8,128)(2,1)S(1)} %get-tuple-element.33.own, bf16[528,128]{1,0:T(8,128)(2,1)S(1)} %collective-permute-done.4.from_1, ...), custom_call_target="tpu_custom_call" | custom-call | flops 1024 | bytes 1024 | tf_op jit(solution)/shard_map/merge/pallas_call | solution.py:323
  37.6 0.1 collective-permute-start.7
  37.7 0.6 %collective-permute-start.8 = (bf16[2,128,128]{2,1,0:T(8,128)(2,1)S(1)}, bf16[2,128,128]{2,1,0:T(8,128)(2,1)S(1)}, u32[]{:S(2)}, u32[]{:S(2)}) collective-permute-start(bf16[2,128,128]{2,1,0:T(8,128)(2,1)S(1)} %get-tuple-element.39), channel_id=1, source_target_pairs={{0,8},{4,12},{8,0},{12,4},{1,9},{5,13},{9,1},{13,5},{2,10},{6,14},... | collective-permute-start | bytes 196616 | tf_op jit(solution)/shard_map/ppermute | solution.py:377
  38.3 1.3 %collective-permute-start.9 = (bf16[2,128,128]{2,1,0:T(8,128)(2,1)S(1)}, bf16[2,128,128]{2,1,0:T(8,128)(2,1)S(1)}, u32[]{:S(2)}, u32[]{:S(2)}) collective-permute-start(bf16[2,128,128]{2,1,0:T(8,128)(2,1)S(1)} %get-tuple-element.40), channel_id=1, source_target_pairs={{0,12},{4,8},{8,4},{12,0},{1,13},{5,9},{9,5},{13,1},{2,14},{6,10},... | collective-permute-start | bytes 196616 | tf_op jit(solution)/shard_map/ppermute | solution.py:377
  39.6 7.0 %collective-permute-done.15.from_2 = bf16[528,128]{1,0:T(8,128)(2,1)S(1)} collective-permute-done((bf16[528,128]{1,0:T(8,128)(2,1)S(1)}, bf16[528,128]{1,0:T(8,128)(2,1)S(1)}, u32[]{:S(2)}, u32[]{:S(2)}) %collective-permute-start.15) | collective-permute-done | bytes 135200 | tf_op jit(solution)/shard_map/ppermute | solution.py:376
  46.6 0.0 collective-permute-done.16.from_3
  46.6 1.7 %merge.3 = (bf16[2,128,128]{2,1,0:T(8,128)(2,1)S(1)}, bf16[2,128,128]{2,1,0:T(8,128)(2,1)S(1)}, bf16[2,128,128]{2,1,0:T(8,128)(2,1)S(1)}, bf16[2,128,128]{2,1,0:T(8,128)(2,1)S(1)}) custom-call(bf16[528,128]{1,0:T(8,128)(2,1)S(1)} %get-tuple-element.45.own, bf16[528,128]{1,0:T(8,128)(2,1)S(1)} %collective-permute-done.14.from_1, ...), custom_call_target="tpu_custom_call" | custom-call | flops 1024 | bytes 1024 | tf_op jit(solution)/shard_map/merge/pallas_call | solution.py:323
  48.3 0.1 collective-permute-start.17
  48.4 0.3 collective-permute-start.18
  48.7 1.5 %collective-permute-start.19 = (bf16[2,128,128]{2,1,0:T(8,128)(2,1)S(1)}, bf16[2,128,128]{2,1,0:T(8,128)(2,1)S(1)}, u32[]{:S(2)}, u32[]{:S(2)}) collective-permute-start(bf16[2,128,128]{2,1,0:T(8,128)(2,1)S(1)} %get-tuple-element.52), channel_id=1, source_target_pairs={{0,12},{4,8},{8,4},{12,0},{1,13},{5,9},{9,5},{13,1},{2,14},{6,10},... | collective-permute-start | bytes 196616 | tf_op jit(solution)/shard_map/ppermute | solution.py:377
  50.3 0.0 collective-permute-done.8.refs_2_
  50.3 0.0 collective-permute-done.9.refs_3_
  50.3 0.0 collective-permute-done.17.refs_5_
  50.3 3.1 %collective-permute-done.18.refs_6_ = bf16[2,128,128]{2,1,0:T(8,128)(2,1)S(1)} collective-permute-done((bf16[2,128,128]{2,1,0:T(8,128)(2,1)S(1)}, bf16[2,128,128]{2,1,0:T(8,128)(2,1)S(1)}, u32[]{:S(2)}, u32[]{:S(2)}) %collective-permute-start.18) | collective-permute-done | bytes 65568 | tf_op jit(solution)/shard_map/ppermute | solution.py:377
  53.3 0.5 collective-permute-done.19.refs_7_
  53.8 1.7 %assemble.1 = bf16[128,2048]{1,0:T(8,128)(2,1)} custom-call(bf16[2,128,128]{2,1,0:T(8,128)(2,1)S(1)} %get-tuple-element.37.refs_0_, bf16[2,128,128]{2,1,0:T(8,128)(2,1)S(1)} %collective-permute-done.7.refs_1_, bf16[2,128,128]{2,1,0:T(8,128)(2,1)S(1)} %collective-permute-done.8.refs_2_, bf16[2,128,128]{2,1,0:T(8,128)(2,1)S(1)} %collective-permute-done.9.refs_3_, ...), custom_call_target="tpu_custom_call" | custom-call | tf_op jit(solution)/shard_map/assemble/pallas_call | solution.py:354
  (7 shorter events, 0.0 us)
Async XLA Ops:
  2.1 13.4 %copy-start = (bf16[512,2048]{1,0:T(8,128)(2,1)S(1)}, bf16[512,2048]{1,0:T(8,128)(2,1)}, u32[]{:S(2)}) copy-start(bf16[512,2048]{1,0:T(8,128)(2,1)} %queries.7) | copy-start | bytes 6291460
  2.1 13.4 %copy-start.1 = (bf16[512,512]{1,0:T(8,128)(2,1)S(1)}, bf16[512,512]{1,0:T(8,128)(2,1)}, u32[]{:S(2)}) copy-start(bf16[512,512]{1,0:T(8,128)(2,1)} %keys.7) | copy-start | bytes 1572868
  2.1 13.4 %copy-start.2 = (bf16[512,512]{1,0:T(8,128)(2,1)S(1)}, bf16[512,512]{1,0:T(8,128)(2,1)}, u32[]{:S(2)}) copy-start(bf16[512,512]{1,0:T(8,128)(2,1)} %values.7) | copy-start | bytes 1572868
  2.1 13.4 %copy-start.3 = (s32[2048]{0:T(1024)S(1)}, s32[2048]{0:T(1024)}, u32[]{:S(2)}) copy-start(s32[2048]{0:T(1024)} %param.7) | copy-start | bytes 24580
  2.1 13.3 %collective-permute-start.3 = (bf16[2,512,128]{2,1,0:T(8,128)(2,1)}, bf16[2,512,128]{2,1,0:T(8,128)(2,1)S(1)}, u32[]{:S(2)}, u32[]{:S(2)}) collective-permute-start(bf16[2,512,128]{2,1,0:T(8,128)(2,1)} %get-tuple-element.32), channel_id=1, source_target_pairs={{0,1},{1,0},{2,3},{3,2},{4,5},{5,4},{6,7},{7,6},{8,9},{9,8},{10,11... | collective-permute-start | bytes 786440 | tf_op jit(solution)/shard_map/ppermute | solution.py:371
  5.2 4.2 %collective-permute-start = (bf16[512,128]{1,0:T(8,128)(2,1)}, bf16[512,128]{1,0:T(8,128)(2,1)S(1)}, u32[]{:S(2)}, u32[]{:S(2)}) collective-permute-start(bf16[512,128]{1,0:T(8,128)(2,1)} %get-tuple-element.29), channel_id=1, source_target_pairs={{0,4},{4,0},{8,12},{12,8},{1,5},{5,1},{9,13},{13,9},{2,6},{6,2},{1... | collective-permute-start | bytes 393224 | tf_op jit(solution)/shard_map/ppermute | solution.py:372
  5.2 6.6 %collective-permute-start.1 = (bf16[512,128]{1,0:T(8,128)(2,1)}, bf16[512,128]{1,0:T(8,128)(2,1)}, u32[]{:S(2)}, u32[]{:S(2)}) collective-permute-start(bf16[512,128]{1,0:T(8,128)(2,1)} %get-tuple-element.30), channel_id=1, source_target_pairs={{0,8},{4,12},{8,0},{12,4},{1,9},{5,13},{9,1},{13,5},{2,10},{6,14},... | collective-permute-start | bytes 393224 | tf_op jit(solution)/shard_map/ppermute | solution.py:372
  6.7 7.2 %collective-permute-start.2 = (bf16[512,128]{1,0:T(8,128)(2,1)}, bf16[512,128]{1,0:T(8,128)(2,1)}, u32[]{:S(2)}, u32[]{:S(2)}) collective-permute-start(bf16[512,128]{1,0:T(8,128)(2,1)} %get-tuple-element.31), channel_id=1, source_target_pairs={{0,12},{4,8},{8,4},{12,0},{1,13},{5,9},{9,5},{13,1},{2,14},{6,10},... | collective-permute-start | bytes 393224 | tf_op jit(solution)/shard_map/ppermute | solution.py:372
  9.1 16.7 %collective-permute-start.13 = (bf16[2,512,128]{2,1,0:T(8,128)(2,1)}, bf16[2,512,128]{2,1,0:T(8,128)(2,1)S(1)}, u32[]{:S(2)}, u32[]{:S(2)}) collective-permute-start(bf16[2,512,128]{2,1,0:T(8,128)(2,1)} %get-tuple-element.44), channel_id=1, source_target_pairs={{0,1},{1,0},{2,3},{3,2},{4,5},{5,4},{6,7},{7,6},{8,9},{9,8},{10,11... | collective-permute-start | bytes 786440 | tf_op jit(solution)/shard_map/ppermute | solution.py:371
  9.4 12.4 %collective-permute-start.10 = (bf16[512,128]{1,0:T(8,128)(2,1)}, bf16[512,128]{1,0:T(8,128)(2,1)S(1)}, u32[]{:S(2)}, u32[]{:S(2)}) collective-permute-start(bf16[512,128]{1,0:T(8,128)(2,1)} %get-tuple-element.41), channel_id=1, source_target_pairs={{0,4},{4,0},{8,12},{12,8},{1,5},{5,1},{9,13},{13,9},{2,6},{6,2},{1... | collective-permute-start | bytes 393224 | tf_op jit(solution)/shard_map/ppermute | solution.py:372
  11.8 11.6 %collective-permute-start.11 = (bf16[512,128]{1,0:T(8,128)(2,1)}, bf16[512,128]{1,0:T(8,128)(2,1)S(1)}, u32[]{:S(2)}, u32[]{:S(2)}) collective-permute-start(bf16[512,128]{1,0:T(8,128)(2,1)} %get-tuple-element.42), channel_id=1, source_target_pairs={{0,8},{4,12},{8,0},{12,4},{1,9},{5,13},{9,1},{13,5},{2,10},{6,14},... | collective-permute-start | bytes 393224 | tf_op jit(solution)/shard_map/ppermute | solution.py:372
  13.8 12.0 %collective-permute-start.12 = (bf16[512,128]{1,0:T(8,128)(2,1)}, bf16[512,128]{1,0:T(8,128)(2,1)S(1)}, u32[]{:S(2)}, u32[]{:S(2)}) collective-permute-start(bf16[512,128]{1,0:T(8,128)(2,1)} %get-tuple-element.43), channel_id=1, source_target_pairs={{0,12},{4,8},{8,4},{12,0},{1,13},{5,9},{9,5},{13,1},{2,14},{6,10},... | collective-permute-start | bytes 393224 | tf_op jit(solution)/shard_map/ppermute | solution.py:372
  21.4 11.1 %collective-permute-start.4 = (bf16[528,128]{1,0:T(8,128)(2,1)S(1)}, bf16[528,128]{1,0:T(8,128)(2,1)S(1)}, u32[]{:S(2)}, u32[]{:S(2)}) collective-permute-start(bf16[528,128]{1,0:T(8,128)(2,1)S(1)} %get-tuple-element.34), channel_id=1, source_target_pairs={{0,1},{1,0},{2,3},{3,2},{4,5},{5,4},{6,7},{7,6},{8,9},{9,8},{10,11... | collective-permute-start | bytes 405512 | tf_op jit(solution)/shard_map/ppermute | solution.py:376
  21.8 14.1 %collective-permute-start.5 = (bf16[528,128]{1,0:T(8,128)(2,1)S(1)}, bf16[528,128]{1,0:T(8,128)(2,1)S(1)}, u32[]{:S(2)}, u32[]{:S(2)}) collective-permute-start(bf16[528,128]{1,0:T(8,128)(2,1)S(1)} %get-tuple-element.35), channel_id=1, source_target_pairs={{0,2},{1,3},{2,0},{3,1},{4,6},{5,7},{6,4},{7,5},{8,10},{9,11},{10,... | collective-permute-start | bytes 405512 | tf_op jit(solution)/shard_map/ppermute | solution.py:376
  23.4 12.5 %collective-permute-start.6 = (bf16[528,128]{1,0:T(8,128)(2,1)S(1)}, bf16[528,128]{1,0:T(8,128)(2,1)S(1)}, u32[]{:S(2)}, u32[]{:S(2)}) collective-permute-start(bf16[528,128]{1,0:T(8,128)(2,1)S(1)} %get-tuple-element.36), channel_id=1, source_target_pairs={{0,3},{1,2},{2,1},{3,0},{4,7},{5,6},{6,5},{7,4},{8,11},{9,10},{10,... | collective-permute-start | bytes 405512 | tf_op jit(solution)/shard_map/ppermute | solution.py:376
  31.5 6.9 %collective-permute-start.14 = (bf16[528,128]{1,0:T(8,128)(2,1)S(1)}, bf16[528,128]{1,0:T(8,128)(2,1)S(1)}, u32[]{:S(2)}, u32[]{:S(2)}) collective-permute-start(bf16[528,128]{1,0:T(8,128)(2,1)S(1)} %get-tuple-element.46), channel_id=1, source_target_pairs={{0,1},{1,0},{2,3},{3,2},{4,5},{5,4},{6,7},{7,6},{8,9},{9,8},{10,11... | collective-permute-start | bytes 405512 | tf_op jit(solution)/shard_map/ppermute | solution.py:376
  31.5 15.1 %collective-permute-start.15 = (bf16[528,128]{1,0:T(8,128)(2,1)S(1)}, bf16[528,128]{1,0:T(8,128)(2,1)S(1)}, u32[]{:S(2)}, u32[]{:S(2)}) collective-permute-start(bf16[528,128]{1,0:T(8,128)(2,1)S(1)} %get-tuple-element.47), channel_id=1, source_target_pairs={{0,2},{1,3},{2,0},{3,1},{4,6},{5,7},{6,4},{7,5},{8,10},{9,11},{10,... | collective-permute-start | bytes 405512 | tf_op jit(solution)/shard_map/ppermute | solution.py:376
  32.5 14.1 %collective-permute-start.16 = (bf16[528,128]{1,0:T(8,128)(2,1)S(1)}, bf16[528,128]{1,0:T(8,128)(2,1)S(1)}, u32[]{:S(2)}, u32[]{:S(2)}) collective-permute-start(bf16[528,128]{1,0:T(8,128)(2,1)S(1)} %get-tuple-element.48), channel_id=1, source_target_pairs={{0,3},{1,2},{2,1},{3,0},{4,7},{5,6},{6,5},{7,4},{8,11},{9,10},{10,... | collective-permute-start | bytes 405512 | tf_op jit(solution)/shard_map/ppermute | solution.py:376
  37.6 11.1 %collective-permute-start.7 = (bf16[2,128,128]{2,1,0:T(8,128)(2,1)S(1)}, bf16[2,128,128]{2,1,0:T(8,128)(2,1)S(1)}, u32[]{:S(2)}, u32[]{:S(2)}) collective-permute-start(bf16[2,128,128]{2,1,0:T(8,128)(2,1)S(1)} %get-tuple-element.38), channel_id=1, source_target_pairs={{0,4},{4,0},{8,12},{12,8},{1,5},{5,1},{9,13},{13,9},{2,6},{6,2},{1... | collective-permute-start | bytes 196616 | tf_op jit(solution)/shard_map/ppermute | solution.py:377
  37.7 12.5 %collective-permute-start.8 = (bf16[2,128,128]{2,1,0:T(8,128)(2,1)S(1)}, bf16[2,128,128]{2,1,0:T(8,128)(2,1)S(1)}, u32[]{:S(2)}, u32[]{:S(2)}) collective-permute-start(bf16[2,128,128]{2,1,0:T(8,128)(2,1)S(1)} %get-tuple-element.39), channel_id=1, source_target_pairs={{0,8},{4,12},{8,0},{12,4},{1,9},{5,13},{9,1},{13,5},{2,10},{6,14},... | collective-permute-start | bytes 196616 | tf_op jit(solution)/shard_map/ppermute | solution.py:377
  38.3 11.9 %collective-permute-start.9 = (bf16[2,128,128]{2,1,0:T(8,128)(2,1)S(1)}, bf16[2,128,128]{2,1,0:T(8,128)(2,1)S(1)}, u32[]{:S(2)}, u32[]{:S(2)}) collective-permute-start(bf16[2,128,128]{2,1,0:T(8,128)(2,1)S(1)} %get-tuple-element.40), channel_id=1, source_target_pairs={{0,12},{4,8},{8,4},{12,0},{1,13},{5,9},{9,5},{13,1},{2,14},{6,10},... | collective-permute-start | bytes 196616 | tf_op jit(solution)/shard_map/ppermute | solution.py:377
  48.3 2.0 %collective-permute-start.17 = (bf16[2,128,128]{2,1,0:T(8,128)(2,1)S(1)}, bf16[2,128,128]{2,1,0:T(8,128)(2,1)S(1)}, u32[]{:S(2)}, u32[]{:S(2)}) collective-permute-start(bf16[2,128,128]{2,1,0:T(8,128)(2,1)S(1)} %get-tuple-element.50), channel_id=1, source_target_pairs={{0,4},{4,0},{8,12},{12,8},{1,5},{5,1},{9,13},{13,9},{2,6},{6,2},{1... | collective-permute-start | bytes 196616 | tf_op jit(solution)/shard_map/ppermute | solution.py:377
  48.4 5.0 %collective-permute-start.18 = (bf16[2,128,128]{2,1,0:T(8,128)(2,1)S(1)}, bf16[2,128,128]{2,1,0:T(8,128)(2,1)S(1)}, u32[]{:S(2)}, u32[]{:S(2)}) collective-permute-start(bf16[2,128,128]{2,1,0:T(8,128)(2,1)S(1)} %get-tuple-element.51), channel_id=1, source_target_pairs={{0,8},{4,12},{8,0},{12,4},{1,9},{5,13},{9,1},{13,5},{2,10},{6,14},... | collective-permute-start | bytes 196616 | tf_op jit(solution)/shard_map/ppermute | solution.py:377
  48.7 5.1 %collective-permute-start.19 = (bf16[2,128,128]{2,1,0:T(8,128)(2,1)S(1)}, bf16[2,128,128]{2,1,0:T(8,128)(2,1)S(1)}, u32[]{:S(2)}, u32[]{:S(2)}) collective-permute-start(bf16[2,128,128]{2,1,0:T(8,128)(2,1)S(1)} %get-tuple-element.52), channel_id=1, source_target_pairs={{0,12},{4,8},{8,4},{12,0},{1,13},{5,9},{9,5},{13,1},{2,14},{6,10},... | collective-permute-start | bytes 196616 | tf_op jit(solution)/shard_map/ppermute | solution.py:377

commit v4 on v3

v4 whole, which is shorter than its diff:
```python
import functools
import math

import jax
import jax.numpy as jnp
from jax import lax
from jax.experimental import pallas as pl
from jax.experimental.pallas import tpu as pltpu
from jax.sharding import PartitionSpec as P

HEAD_DIM = 128
LANES = 128
LOW_SCORE = -1e30
UNSEEN = -float(1 << 20)
ROW_TILE = 256
STATS = 16
ANY = pl.BlockSpec(memory_space=pl.ANY)
VMEM = pl.BlockSpec(memory_space=pltpu.VMEM)


def attend_half(q_rows, q_steps, keys_all, values_all, key_steps, block_keys):
    row_count, width = q_rows.shape
    head_size = HEAD_DIM
    head_count = width // head_size
    key_count = keys_all.shape[0]
    block_count = key_count // block_keys
    factor_scale = 1.0 / math.sqrt(head_size)
    q_heads = q_rows.reshape(row_count, head_count, head_size)
    blocks = (
        keys_all.reshape(block_count, block_keys, head_count, head_size),
        values_all.reshape(block_count, block_keys, head_count, head_size),
        key_steps.reshape(block_count, block_keys),
    )
    last_step = q_steps[row_count - 1]

    def compute(carry, key_block, value_block, step_block):
        run_max, run_sum, run_out = carry
        scores = (
            jnp.einsum("rhd,khd->hkr", q_heads, key_block, preferred_element_type=jnp.float32)
            * factor_scale
        )
        visible = step_block[None, :, None] <= q_steps[None, None, :]
        masked = jnp.where(visible, scores, LOW_SCORE)
        new_max = jnp.maximum(run_max, jnp.max(masked, axis=1))
        weights = jnp.where(visible, jnp.exp(masked - new_max[:, None, :]), 0.0)
        rescale = jnp.exp(run_max - new_max)
        new_sum = run_sum * rescale + jnp.sum(weights, axis=1)
        update = jnp.einsum(
            "hkr,khd->rhd",
            weights.astype(jnp.bfloat16),
            value_block,
            preferred_element_type=jnp.float32,
        )
        new_out = run_out * jnp.transpose(rescale)[:, :, None] + update
        return (new_max, new_sum, new_out)

    def visit(carry, block):
        key_block, value_block, step_block = block
        result = lax.cond(
            step_block[0] <= last_step,
            lambda state: compute(state, key_block, value_block, step_block),
            lambda state: state,
            carry,
        )
        return (result, None)

    initial = (
        jnp.full((head_count, row_count), LOW_SCORE, jnp.float32),
        jnp.zeros((head_count, row_count), jnp.float32),
        jnp.zeros((row_count, head_count, head_size), jnp.float32),
    )
    final_state, unused = lax.scan(visit, initial, blocks)
    return final_state


def on_any(queries, keys, values, step_of):
    block_rows, width = queries.shape
    head_size = HEAD_DIM
    head_count = width // head_size
    key_parts = lax.axis_size("ka")
    query_index = lax.axis_index("pb")
    key_index = lax.axis_index("ka")
    shard_rows = block_rows // key_parts
    half_rows = block_rows // 2
    key_count = keys.shape[0]
    first_steps = lax.dynamic_slice_in_dim(step_of, query_index * block_rows, half_rows)
    second_steps = lax.dynamic_slice_in_dim(
        step_of, query_index * block_rows + half_rows, half_rows
    )
    keys_mine, values_mine = (keys, values)
    key_steps = lax.dynamic_slice_in_dim(step_of, key_index * key_count, key_count)
    keys_all, values_all = (
        lax.all_gather(keys_mine, "pb", axis=1, tiled=True),
        lax.all_gather(values_mine, "pb", axis=1, tiled=True),
    )
    block_keys = math.gcd(64, key_count)
    first_state = attend_half(
        queries[:half_rows], first_steps, keys_all, values_all, key_steps, block_keys
    )
    second_state = attend_half(
        queries[half_rows:], second_steps, keys_all, values_all, key_steps, block_keys
    )
    row_max = jnp.concatenate([first_state[0], second_state[0]], axis=1)
    row_sum = jnp.concatenate([first_state[1], second_state[1]], axis=1)
    row_out = jnp.concatenate([first_state[2], second_state[2]], axis=0)
    sent = (
        jnp.transpose(row_max)[:, None, :],
        jnp.transpose(row_sum)[:, None, :],
        row_out.reshape(block_rows, 1, width),
    )
    got_max, got_sum, got_out = (
        lax.all_to_all(sent[0], "ka", split_axis=0, concat_axis=1, tiled=True),
        lax.all_to_all(sent[1], "ka", split_axis=0, concat_axis=1, tiled=True),
        lax.all_to_all(sent[2], "ka", split_axis=0, concat_axis=1, tiled=True),
    )
    best = jnp.max(got_max, axis=1, keepdims=True)
    weight = jnp.exp(got_max - best)
    total = jnp.sum(got_sum * weight, axis=1)
    shares = weight / total[:, None, :]
    pieces = got_out.reshape(shard_rows, key_parts, head_count, head_size) * shares[:, :, :, None]
    result = jnp.sum(pieces, axis=1).reshape(shard_rows, width)
    result = result.astype(jnp.bfloat16)
    return result

def run_copies(pairs, sem):
    copies = [pltpu.make_async_copy(a, b, sem.at[i]) for i, (a, b) in enumerate(pairs)]
    for copy in copies:
        copy.start()
    return copies


def aligned(index, size):
    return pl.ds(pl.multiple_of(index * size, size), size)


def region_of(z, far):
    return 1 - z // 2 if far else z // 2


def pack_kernel(batches, queries, keys, values, *refs):
    outs, sem = refs[:-1], refs[-1]
    column = lax.axis_index("pb")
    z = lax.axis_index("ka")
    half = z % 2
    heads = keys.shape[1] // HEAD_DIM
    count = queries.shape[0] // 2
    pairs = []
    for chunk, to in enumerate(outs[:2]):
        theirs = aligned((1 - half) * 2 + chunk, HEAD_DIM)
        pairs += [(keys.at[:, theirs], to.at[0]), (values.at[:, theirs], to.at[1])]
    for b, batch in enumerate(batches):
        for i, (chunk, far) in enumerate(batch):
            for d, to in zip((1, 2, 3), outs[2 + 3 * b:]):
                cut = (aligned(region_of(z, far), count), aligned((column ^ d) * heads + half * 2 + chunk, HEAD_DIM))
                pairs.append((queries.at[cut], to.at[pl.ds(i * count, count), :]))
    for copy in run_copies(pairs, sem):
        copy.wait()


def pack(batches, queries, keys, values):
    pair = jax.ShapeDtypeStruct((2, keys.shape[0], HEAD_DIM), keys.dtype)
    rows = [jax.ShapeDtypeStruct((len(batch) * queries.shape[0] // 2, HEAD_DIM), queries.dtype) for batch in batches]
    return pl.pallas_call(
        functools.partial(pack_kernel, batches),
        out_shape=[pair] * 2 + sum([[shape] * 3 for shape in rows], []),
        in_specs=[ANY] * 3,
        out_specs=[VMEM] * (2 + 3 * len(batches)),
        scratch_shapes=[pltpu.SemaphoreType.DMA((4 + 3 * sum(map(len, batches)),))],
        name="pack",
    )(queries, keys, values)


def attend_kernel(shapes, skip, waits, scale, steps_ref, queries, keys, values, *refs):
    refs = refs[waits:]
    chunks = sorted({chunk for chunk, _ in shapes})
    count = len(shapes)
    moved, got = refs[:3], refs[3:3 + len(chunks)]
    outs = refs[3 + len(chunks):3 + len(chunks) + 2 * count]
    q_buf, k_buf, v_buf, stats_buf, parts, sem, out_sem = refs[3 + len(chunks) + 2 * count:]
    column = lax.axis_index("pb")
    z = lax.axis_index("ka")
    half_rows = queries.shape[0] // 2
    sub = half_rows // 2
    held = keys.shape[0]
    pair = 2 * held
    heads = keys.shape[1] // HEAD_DIM
    upper, half = z // 2, z % 2
    left = pl.ds(0, HEAD_DIM)

    def place(block):
        return (block + 4 - 2 * upper) % 4

    pairs = []
    for i, chunk in enumerate(chunks):
        head = aligned(half * 2 + chunk, HEAD_DIM)
        pairs += [
            (keys.at[:, head], k_buf.at[i, aligned(half, held), :]),
            (got[i].at[0], k_buf.at[i, aligned(1 - half, held), :]),
            (values.at[:, head], v_buf.at[i, aligned(half, held), left]),
            (got[i].at[1], v_buf.at[i, aligned(1 - half, held), left]),
        ]
    for i, (chunk, far) in enumerate(shapes):
        cut = (aligned(region_of(z, far), half_rows), aligned(column * heads + half * 2 + chunk, HEAD_DIM))
        pairs.append((queries.at[cut], q_buf.at[i, place(column)]))
        for d, q in zip((1, 2, 3), moved):
            pairs.append((q.at[pl.ds((skip + i) * half_rows, half_rows), :], q_buf.at[i, place(column ^ d)]))
    copies = run_copies(pairs, sem)
    v_buf[:, :, HEAD_DIM:] = jnp.ones((len(chunks), pair, HEAD_DIM), jnp.bfloat16)
    steps = steps_ref[...].astype(jnp.float32)
    columns = jnp.transpose(steps)
    for copy in copies:
        copy.wait()

    def region(i, which):
        chunk, far = shapes[i]
        kv = chunks.index(chunk)
        start = half_rows if far == (which == 0) else 0
        base = which * pair

        def tile(slot, first_row, limit, masked_from, stats, first=0, size=half_rows):
            scores = lax.dot_general(q_buf[i, slot, first:first + size, :], k_buf[kv, :limit, :],
                                     (((1,), (1,)), ((), ())), preferred_element_type=jnp.float32)
            if masked_from < limit:
                at = (first_row + first) // LANES
                q_steps = jnp.concatenate([columns[:, g:g + 1] for g in range(at, at + size // LANES)], axis=0)
                k_steps = jnp.concatenate(
                    [steps[g:g + 1] for g in range((base + masked_from) // LANES, (base + limit) // LANES)], axis=1)
                seen = jnp.where(k_steps <= q_steps, scores[:, masked_from:], UNSEEN / scale)
                scores = jnp.concatenate([scores[:, :masked_from], seen], axis=1) if masked_from else seen
            top = jnp.max(scores, axis=1, keepdims=True) * scale
            top = top.astype(jnp.bfloat16).astype(jnp.float32)
            weights = jnp.exp2(scores * scale - top).astype(jnp.bfloat16)
            mixed = lax.dot_general(weights, v_buf[kv, :limit, :], (((1,), (0,)), ((), ())), preferred_element_type=jnp.float32)
            total = mixed[:, HEAD_DIM:]
            result = (mixed[:, :HEAD_DIM] / total).astype(jnp.bfloat16)
            for j in range(0, size, sub):
                parts[i, (first + j) // sub, slot * sub:(slot + 1) * sub, :] = result[j:j + sub]
            high = total.astype(jnp.bfloat16).astype(jnp.float32)
            lane = lax.broadcasted_iota(jnp.int32, (size, LANES), 1)
            stats = jnp.where(lane == 3 * slot, top, stats)
            stats = jnp.where(lane == 3 * slot + 1, high, stats)
            return jnp.where(lane == 3 * slot + 2, total - high, stats)

        reach = start + half_rows + LANES
        stats = jnp.zeros((half_rows, LANES), jnp.float32)
        stats = tile(0, base + start, reach, start, stats)
        stats = tile(1, base + held + start, min(held + reach, pair), held + start, stats)
        if which == 0:
            stats = tile(2, 0, pair, pair, stats)
            stats = tile(3, 0, pair, pair, stats)
        stats_buf[...] = stats
        if which == 1 and not far:
            stats_buf[sub:, :] = tile(3, held + start, LANES, 0, stats[sub:], sub, sub)
        for j in range(2):
            stats = jnp.transpose(stats_buf[j * sub:(j + 1) * sub, :])
            parts[i, j, 4 * sub:, :] = stats[:STATS].astype(jnp.bfloat16)

    sent = []
    for i in range(count):
        for which in range(2):
            pl.when(upper == which)(functools.partial(region, i, which))
        for j, place_in_pair in enumerate((half, 1 - half)):
            copy = pltpu.make_async_copy(parts.at[i, place_in_pair], outs[2 * i + j], out_sem.at[2 * i + j])
            copy.start()
            sent.append(copy)
    for copy in sent:
        copy.wait()


def attend(shapes, skip, steps, queries, keys, values, moved, got, after=()):
    chunks = len({chunk for chunk, _ in shapes})
    count = len(shapes)
    rows = queries.shape[0]
    held = keys.shape[0]
    part = jax.ShapeDtypeStruct((rows + STATS, LANES), jnp.bfloat16)
    return pl.pallas_call(
        functools.partial(attend_kernel, shapes, skip, len(after), math.log2(math.e) / math.sqrt(HEAD_DIM)),
        out_shape=[part] * (2 * count),
        in_specs=[VMEM] + [ANY] * (6 + chunks + len(after)),
        out_specs=[ANY] * (2 * count),
        scratch_shapes=[
            pltpu.VMEM((count, 4, rows // 2, HEAD_DIM), jnp.bfloat16),
            pltpu.VMEM((chunks, 2 * held, HEAD_DIM), jnp.bfloat16),
            pltpu.VMEM((chunks, 2 * held, 2 * HEAD_DIM), jnp.bfloat16),
            pltpu.VMEM((rows // 2, LANES), jnp.float32),
            pltpu.VMEM((count, 2) + part.shape, jnp.bfloat16),
            pltpu.SemaphoreType.DMA((4 * chunks + 4 * count,)),
            pltpu.SemaphoreType.DMA((2 * count,)),
        ],
        compiler_params=pltpu.CompilerParams(vmem_limit_bytes=24 << 20),
        cost_estimate=pl.CostEstimate(flops=1 << 10, bytes_accessed=1 << 10, transcendentals=0),
        name="attend_far" if shapes[0][1] else "attend_near",
    )(steps, queries, keys, values, *after, *moved, *got)


def collect_kernel(a, b, out, sem):
    for copy in run_copies([(a, out.at[0]), (b, out.at[1])], sem):
        copy.wait()


def collect(a, b):
    return pl.pallas_call(
        collect_kernel,
        out_shape=jax.ShapeDtypeStruct((2,) + a.shape, a.dtype),
        in_specs=[ANY] * 2,
        out_specs=ANY,
        scratch_shapes=[pltpu.SemaphoreType.DMA((2,))],
        compiler_params=pltpu.CompilerParams(vmem_limit_bytes=4 << 20),
        cost_estimate=pl.CostEstimate(flops=1 << 30, bytes_accessed=32 << 20, transcendentals=0),
        name="collect",
    )(a, b)


def merge_kernel(waits, *refs):
    own, from_1, *far = refs[waits:-7]
    (out_0, out_1, out_2, out_3, held, result, sem) = refs[-7:]
    if len(far) == 1:
        far = (far[0].at[0], far[0].at[1])
    column = lax.axis_index("pb")
    z = lax.axis_index("ka")
    sub = result.shape[2]
    for copy in run_copies([(a, held.at[z ^ d]) for d, a in enumerate((own, from_1) + tuple(far))], sem):
        copy.wait()
    stats = [jnp.transpose(held[s, 4 * sub:, :].astype(jnp.float32)) for s in range(4)]

    def part(s, slot):
        return held[s, slot * sub:(slot + 1) * sub, :]

    def merge_block(block, half):
        parts = ((half, block), (2 + half, (block + 2) % 4))
        tops = [stats[s][:, 3 * slot:3 * slot + 1] for s, slot in parts]
        totals = [stats[s][:, 3 * slot + 1:3 * slot + 2] + stats[s][:, 3 * slot + 2:3 * slot + 3] for s, slot in parts]
        best = jnp.maximum(*tops)
        shares = [total * jnp.exp2(top - best) for top, total in zip(tops, totals)]
        share = shares[0] / (shares[0] + shares[1])
        a, b = [part(s, slot).astype(jnp.float32) for s, slot in parts]
        result[block, half] = (a * share + b * (1.0 - share)).astype(jnp.bfloat16)

    for half in range(2):
        result[0, half] = part(half, 0)
        merge_block(2, half)
        merge_block(3, half)

    @pl.when(z < 3)
    def _():
        for half in range(2):
            result[1, half] = part(half, 1)

    @pl.when(z == 3)
    def _():
        for half in range(2):
            merge_block(1, half)

    outs = ((3, out_3), (2, out_2), (1, out_1), (0, out_0))
    for copy in run_copies([(result.at[column ^ d], out) for d, out in outs], sem):
        copy.wait()


def merge(parts, after=()):
    sub = (parts[0].shape[0] - STATS) // 4
    block = jax.ShapeDtypeStruct((2, sub, HEAD_DIM), jnp.bfloat16)
    return pl.pallas_call(
        functools.partial(merge_kernel, len(after)),
        out_shape=[block] * 4,
        in_specs=[ANY] * (len(after) + len(parts)),
        out_specs=[ANY] * 4,
        scratch_shapes=[
            pltpu.VMEM((4,) + parts[0].shape, jnp.bfloat16),
            pltpu.VMEM((4,) + block.shape, jnp.bfloat16),
            pltpu.SemaphoreType.DMA((4,)),
        ],
        compiler_params=pltpu.CompilerParams(vmem_limit_bytes=4 << 20),
        cost_estimate=pl.CostEstimate(flops=1 << 10, bytes_accessed=1 << 10, transcendentals=0),
        name="merge",
    )(*after, *parts)


def assemble_kernel(chunk, *refs):
    pieces, (out, sem) = refs[-6:-2], refs[-2:]
    column = lax.axis_index("pb")
    pairs = []
    for d, piece in enumerate(pieces):
        for half in range(2):
            pairs.append((piece.at[half], out.at[:, aligned((column ^ d) * 4 + 2 * half + chunk, HEAD_DIM)]))
    for copy in run_copies(pairs, sem):
        copy.wait()


def assemble(chunk, pieces, begun=()):
    sub = pieces[0].shape[1]
    return pl.pallas_call(
        functools.partial(assemble_kernel, chunk),
        out_shape=jax.ShapeDtypeStruct((sub, 16 * HEAD_DIM), jnp.bfloat16),
        in_specs=[ANY] * (4 + len(begun)),
        out_specs=ANY,
        scratch_shapes=[pltpu.SemaphoreType.DMA((8,))],
        input_output_aliases={0: 0} if begun else {},
        compiler_params=pltpu.CompilerParams(vmem_limit_bytes=4 << 20),
        cost_estimate=pl.CostEstimate(flops=1 << 30, bytes_accessed=32 << 20, transcendentals=0),
        name="assemble",
    )(*begun, *pieces)


def by_pairs(queries, keys, values, step_of):
    steps = step_of.reshape(-1, LANES)
    swaps = [[(i, i ^ d) for i in range(4)] for d in range(4)]

    def travel(sent, axis):
        return [lax.ppermute(piece, axis, swap) for piece, swap in zip(sent, swaps[1:])]

    order = ((0, True), (0, False), (1, True), (1, False))
    packed = pack((order[:1], order[1:]), queries, keys, values)
    got = travel(packed[:1], "ka"), travel(packed[1:2], "ka")
    moved = travel(packed[2:5], "pb"), travel(packed[5:], "pb")
    parts = []
    for i, (chunk, far) in enumerate(order):
        after = [parts[-1][0]] if parts else []
        parts.append(attend((order[i],), max(i - 1, 0), steps, queries, keys, values, moved[min(i, 1)], got[chunk], after))
    far = [collect(lax.ppermute(same, "ka", swaps[2]), lax.ppermute(cross, "ka", swaps[3])) for same, cross in parts[::2]]
    result = ()
    blocks = ()
    for chunk, (own, beside) in enumerate(parts[1::2]):
        blocks = merge([own, lax.ppermute(beside, "ka", swaps[1]), far[chunk]], blocks[:1])
        result = (assemble(chunk, [blocks[0]] + travel(blocks[1:], "pb"), result),)
    return result[0]


def on_device(queries, keys, values, step_of):
    rows = queries.shape[0]
    held, block = keys.shape
    square = (
        lax.axis_size("pb") == 4
        and lax.axis_size("ka") == 4
        and held == rows == 4 * LANES
        and block == 4 * HEAD_DIM
    )
    if square:
        return by_pairs(queries, keys, values, step_of)
    return on_any(queries, keys, values, step_of)


def solution(mesh):
    placed = (
        P(("groups", "pb"), None),
        P(("groups", "ka"), "pb"),
        P(("groups", "ka"), "pb"),
        P("groups"),
    )
    return jax.shard_map(
        on_device,
        mesh=mesh,
        in_specs=placed,
        out_specs=P(("groups", "pb", "ka"), None),
        check_vma=False,
    )
```

time: 55.9 us -> 51.7 us (0.925)
  waiting for transfers between devices: 13.4 us -> 10.4 us
  starting transfers between devices: 21.2 us -> 20.6 us
    ppermute x20, waiting for transfers between devices: 13.4 us -> 10.4 us  [the longest x14 6.42 us: travel(): lax.ppermute(piece, axis, swap)]
    ppermute x20, starting transfers between devices: 21.2 us -> 20.6 us  [the longest x14 12.2 us: travel(): lax.ppermute(piece, axis, swap)]
    pallas_call x7 -> x11, Pallas kernels: 20.7 us -> 20.3 us  [the longest x4 11.9 us: attend(): pl.pallas_call(functools.partial(attend_kernel, shapes, skip, len(after),...]
  transfers between devices with their start and end apart: 20 -> 20, of which waited for: 5 -> 6; matrix products, arithmetic and copies ran while one was open for 0% -> 0% of each run, Pallas kernels for 30% -> 33%
where the time goes in v4:
time: 51.7 us; the launch traced here: 51.6 us
  starting transfers between devices  20.6 us (40%)
  Pallas kernels  20.3 us (39%)
  waiting for transfers between devices  10.4 us (20%)
    ppermute x14, starting transfers between devices, travel(): lax.ppermute(piece, axis, swap)  12.2 us
    pallas_call x4, Pallas kernels, attend(): pl.pallas_call(functools.partial(attend_kernel, shapes, skip, len(after),...  11.9 us
    ppermute x14, waiting for transfers between devices, travel(): lax.ppermute(piece, axis, swap)  6.42 us
    ppermute x2, starting transfers between devices, by_pairs(): lax.ppermute(cross, 'ka', swaps[3])  6.06 us
    ppermute x2, waiting for transfers between devices, by_pairs(): lax.ppermute(same, 'ka', swaps[2])  3.61 us
    pallas_call x2, Pallas kernels, merge(): pl.pallas_call(functools.partial(merge_kernel, len(after)), out_shape=[bl...  3.41 us
    pallas_call x1, Pallas kernels, pack(): pl.pallas_call(functools.partial(pack_kernel, batches), out_shape=[pair]...  2.69 us
    ppermute x2, starting transfers between devices, by_pairs(): lax.ppermute(beside, 'ka', swaps[1])  1.89 us
  transfers between devices with their start and end apart: 20, of which 6 were waited for; matrix products, arithmetic and copies ran while one was open for 0% of the time, Pallas kernels for 33%

profile of v4, /device:TPU:0, one launch (start us, length us, event | category | flops | bytes accessed | tf_op | source)
XLA Modules:
  0.0 51.6 jit_solution(14662379619124001629)
XLA Ops:
  0.0 2.7 %pack.1 = (bf16[2,512,128]{2,1,0:T(8,128)(2,1)}, bf16[2,512,128]{2,1,0:T(8,128)(2,1)}, bf16[256,128]{1,0:T(8,128)(2,1)}, bf16[256,128]{1,0:T(8,128)(2,1)}, bf16[...) custom-call(bf16[512,2048]{1,0:T(8,128)(2,1)} %queries.9, ...), custom_call_target="tpu_custom_call" | custom-call | tf_op jit(solution)/shard_map/pack/pallas_call | solution.py:163
  2.7 3.1 %collective-permute-start.3 = (bf16[2,512,128]{2,1,0:T(8,128)(2,1)}, bf16[2,512,128]{2,1,0:T(8,128)(2,1)S(1)}, u32[]{:S(2)}, u32[]{:S(2)}) collective-permute-start(bf16[2,512,128]{2,1,0:T(8,128)(2,1)} %get-tuple-element.32), channel_id=1, source_target_pairs={{0,1},{1,0},{2,3},{3,2},{4,5},{5,4},{6,7},{7,6},{8,9},{9,8},{10,11... | collective-permute-start | bytes 786440 | tf_op jit(solution)/shard_map/ppermute | solution.py:409
  5.8 0.0 collective-permute-start
  5.8 0.5 collective-permute-start.4
  6.3 1.5 %collective-permute-start.1 = (bf16[256,128]{1,0:T(8,128)(2,1)}, bf16[256,128]{1,0:T(8,128)(2,1)S(1)}, u32[]{:S(2)}, u32[]{:S(2)}) collective-permute-start(bf16[256,128]{1,0:T(8,128)(2,1)} %get-tuple-element.30), channel_id=1, source_target_pairs={{0,8},{4,12},{8,0},{12,4},{1,9},{5,13},{9,1},{13,5},{2,10},{6,14},... | collective-permute-start | bytes 196616 | tf_op jit(solution)/shard_map/ppermute | solution.py:409
  7.8 0.0 collective-permute-start.2
  7.8 0.0 collective-permute-done.refs_0_
  7.8 0.5 collective-permute-start.13
  8.3 2.5 %collective-permute-done.1.refs_1_ = bf16[256,128]{1,0:T(8,128)(2,1)S(1)} collective-permute-done((bf16[256,128]{1,0:T(8,128)(2,1)}, bf16[256,128]{1,0:T(8,128)(2,1)S(1)}, u32[]{:S(2)}, u32[]{:S(2)}) %collective-permute-start.1) | collective-permute-done | bytes 65568 | tf_op jit(solution)/shard_map/ppermute | solution.py:409
  10.8 2.2 %collective-permute-start.5 = (bf16[768,128]{1,0:T(8,128)(2,1)}, bf16[768,128]{1,0:T(8,128)(2,1)S(1)}, u32[]{:S(2)}, u32[]{:S(2)}) collective-permute-start(bf16[768,128]{1,0:T(8,128)(2,1)} %get-tuple-element.35), channel_id=1, source_target_pairs={{0,8},{4,12},{8,0},{12,4},{1,9},{5,13},{9,1},{13,5},{2,10},{6,14},... | collective-permute-start | bytes 589832 | tf_op jit(solution)/shard_map/ppermute | solution.py:409
  13.0 0.0 collective-permute-done.2.refs_2_
  13.0 0.4 collective-permute-start.6
  13.4 0.0 collective-permute-done.3.refs_3_.refs_4_
  13.4 3.0 %attend_far.2 = (bf16[528,128]{1,0:T(8,128)(2,1)S(1)}, bf16[528,128]{1,0:T(8,128)(2,1)S(1)}) custom-call(s32[16,128]{1,0:T(8,128)S(1)} %bitcast.1, bf16[512,2048]{1,0:T(8,128)(2,1)S(1)} %copy-done, bf16[512,512]{1,0:T(8,128)(2,1)S(1)} %copy-done.1, bf16[512,512]{1,0:T(8,128)(2,1)S(1)} %copy-done.2, bf16[256,128]{1,0:T(8,128)(2,1)S(1)} %collective-permute-done.refs_0_, ...), custom_call_target="tpu_custom_call" | custom-call | flops 1024 | bytes 1024 | tf_op jit(solution)/shard_map/attend_far/pallas_call | solution.py:276
  16.4 3.4 %collective-permute-start.9 = (bf16[528,128]{1,0:T(8,128)(2,1)S(1)}, bf16[528,128]{1,0:T(8,128)(2,1)S(1)}, u32[]{:S(2)}, u32[]{:S(2)}) collective-permute-start(bf16[528,128]{1,0:T(8,128)(2,1)S(1)} %get-tuple-element.39), channel_id=1, source_target_pairs={{0,3},{1,2},{2,1},{3,0},{4,7},{5,6},{6,5},{7,4},{8,11},{9,10},{10,... | collective-permute-start | bytes 405512 | tf_op jit(solution)/shard_map/ppermute | solution.py:419
  19.7 0.0 collective-permute-done.4.refs_1_
  19.8 0.0 collective-permute-start.8
  19.8 0.0 collective-permute-done.5.refs_2_
  19.8 0.7 %collective-permute-done.6.refs_3_ = bf16[768,128]{1,0:T(8,128)(2,1)S(1)} collective-permute-done((bf16[768,128]{1,0:T(8,128)(2,1)}, bf16[768,128]{1,0:T(8,128)(2,1)S(1)}, u32[]{:S(2)}, u32[]{:S(2)}) %collective-permute-start.6) | collective-permute-done | bytes 196640 | tf_op jit(solution)/shard_map/ppermute | solution.py:409
  20.4 2.9 %attend_near.2 = (bf16[528,128]{1,0:T(8,128)(2,1)S(1)}, bf16[528,128]{1,0:T(8,128)(2,1)S(1)}) custom-call(s32[16,128]{1,0:T(8,128)S(1)} %bitcast.2, bf16[512,2048]{1,0:T(8,128)(2,1)S(1)} %copy-done, bf16[512,512]{1,0:T(8,128)(2,1)S(1)} %copy-done.1, bf16[512,512]{1,0:T(8,128)(2,1)S(1)} %copy-done.2, bf16[528,128]{1,0:T(8,128)(2,1)S(1)} %get-tuple-element.33.refs_0_, ...), custom_call_target="tpu_custom_call" | custom-call | flops 1024 | bytes 1024 | tf_op jit(solution)/shard_map/attend_near/pallas_call | solution.py:276
  23.4 0.5 collective-permute-start.7
  23.9 0.0 collective-permute-done.13.refs_4_
  23.9 2.9 %attend_far.3 = (bf16[528,128]{1,0:T(8,128)(2,1)S(1)}, bf16[528,128]{1,0:T(8,128)(2,1)S(1)}) custom-call(s32[16,128]{1,0:T(8,128)S(1)} %bitcast.3, bf16[512,2048]{1,0:T(8,128)(2,1)S(1)} %copy-done, bf16[512,512]{1,0:T(8,128)(2,1)S(1)} %copy-done.1, bf16[512,512]{1,0:T(8,128)(2,1)S(1)} %copy-done.2, bf16[528,128]{1,0:T(8,128)(2,1)S(1)} %get-tuple-element.37.refs_0_, ...), custom_call_target="tpu_custom_call" | custom-call | flops 1024 | bytes 1024 | tf_op jit(solution)/shard_map/attend_far/pallas_call | solution.py:276
  26.8 2.7 %collective-permute-start.16 = (bf16[528,128]{1,0:T(8,128)(2,1)S(1)}, bf16[528,128]{1,0:T(8,128)(2,1)S(1)}, u32[]{:S(2)}, u32[]{:S(2)}) collective-permute-start(bf16[528,128]{1,0:T(8,128)(2,1)S(1)} %get-tuple-element.48), channel_id=1, source_target_pairs={{0,3},{1,2},{2,1},{3,0},{4,7},{5,6},{6,5},{7,4},{8,11},{9,10},{10,... | collective-permute-start | bytes 405512 | tf_op jit(solution)/shard_map/ppermute | solution.py:419
  29.5 0.4 collective-permute-start.15
  29.9 3.1 %attend_near.3 = (bf16[528,128]{1,0:T(8,128)(2,1)S(1)}, bf16[528,128]{1,0:T(8,128)(2,1)S(1)}) custom-call(s32[16,128]{1,0:T(8,128)S(1)} %bitcast.4, bf16[512,2048]{1,0:T(8,128)(2,1)S(1)} %copy-done, bf16[512,512]{1,0:T(8,128)(2,1)S(1)} %copy-done.1, bf16[512,512]{1,0:T(8,128)(2,1)S(1)} %copy-done.2, bf16[528,128]{1,0:T(8,128)(2,1)S(1)} %get-tuple-element.45.refs_0_, ...), custom_call_target="tpu_custom_call" | custom-call | flops 1024 | bytes 1024 | tf_op jit(solution)/shard_map/attend_near/pallas_call | solution.py:276
  33.0 0.0 collective-permute-done.9.b
  33.1 1.4 %collective-permute-start.14 = (bf16[528,128]{1,0:T(8,128)(2,1)S(1)}, bf16[528,128]{1,0:T(8,128)(2,1)S(1)}, u32[]{:S(2)}, u32[]{:S(2)}) collective-permute-start(bf16[528,128]{1,0:T(8,128)(2,1)S(1)} %get-tuple-element.47), channel_id=1, source_target_pairs={{0,1},{1,0},{2,3},{3,2},{4,5},{5,4},{6,7},{7,6},{8,9},{9,8},{10,11... | collective-permute-start | bytes 405512 | tf_op jit(solution)/shard_map/ppermute | solution.py:423
  34.5 0.3 collect.2.refs_2_
  34.8 0.3 collective-permute-done.7.refs_1_
  35.1 1.7 %merge.2 = (bf16[2,128,128]{2,1,0:T(8,128)(2,1)S(1)}, bf16[2,128,128]{2,1,0:T(8,128)(2,1)S(1)}, bf16[2,128,128]{2,1,0:T(8,128)(2,1)S(1)}, bf16[2,128,128]{2,1,0:T(8,128)(2,1)S(1)}) custom-call(bf16[528,128]{1,0:T(8,128)(2,1)S(1)} %get-tuple-element.37.refs_0_, bf16[528,128]{1,0:T(8,128)(2,1)S(1)} %collective-permute-done.7.refs_1_, ...), custom_call_target="tpu_custom_call" | custom-call | flops 1024 | bytes 1024 | tf_op jit(solution)/shard_map/merge/pallas_call | solution.py:362
  36.8 0.1 collective-permute-start.10
  36.9 1.5 %collective-permute-start.11 = (bf16[2,128,128]{2,1,0:T(8,128)(2,1)S(1)}, bf16[2,128,128]{2,1,0:T(8,128)(2,1)S(1)}, u32[]{:S(2)}, u32[]{:S(2)}) collective-permute-start(bf16[2,128,128]{2,1,0:T(8,128)(2,1)S(1)} %get-tuple-element.42), channel_id=1, source_target_pairs={{0,8},{4,12},{8,0},{12,4},{1,9},{5,13},{9,1},{13,5},{2,10},{6,14},... | collective-permute-start | bytes 196616 | tf_op jit(solution)/shard_map/ppermute | solution.py:409
  38.4 0.3 collective-permute-start.12
  38.8 3.6 %collective-permute-done.15.a = bf16[528,128]{1,0:T(8,128)(2,1)S(1)} collective-permute-done((bf16[528,128]{1,0:T(8,128)(2,1)S(1)}, bf16[528,128]{1,0:T(8,128)(2,1)S(1)}, u32[]{:S(2)}, u32[]{:S(2)}) %collective-permute-start.15) | collective-permute-done | bytes 135200 | tf_op jit(solution)/shard_map/ppermute | solution.py:419
  42.4 0.3 collect.3.refs_3_
  42.7 0.0 collective-permute-done.14.refs_2_
  42.7 1.7 %merge.3 = (bf16[2,128,128]{2,1,0:T(8,128)(2,1)S(1)}, bf16[2,128,128]{2,1,0:T(8,128)(2,1)S(1)}, bf16[2,128,128]{2,1,0:T(8,128)(2,1)S(1)}, bf16[2,128,128]{2,1,0:T(8,128)(2,1)S(1)}) custom-call(bf16[2,128,128]{2,1,0:T(8,128)(2,1)S(1)} %get-tuple-element.40.refs_0_, bf16[528,128]{1,0:T(8,128)(2,1)S(1)} %get-tuple-element.46.refs_1_, ...), custom_call_target="tpu_custom_call" | custom-call | flops 1024 | bytes 1024 | tf_op jit(solution)/shard_map/merge/pallas_call | solution.py:362
  44.5 0.1 collective-permute-start.17
  44.6 2.0 %collective-permute-start.18 = (bf16[2,128,128]{2,1,0:T(8,128)(2,1)S(1)}, bf16[2,128,128]{2,1,0:T(8,128)(2,1)S(1)}, u32[]{:S(2)}, u32[]{:S(2)}) collective-permute-start(bf16[2,128,128]{2,1,0:T(8,128)(2,1)S(1)} %get-tuple-element.51), channel_id=1, source_target_pairs={{0,8},{4,12},{8,0},{12,4},{1,9},{5,13},{9,1},{13,5},{2,10},{6,14},... | collective-permute-start | bytes 196616 | tf_op jit(solution)/shard_map/ppermute | solution.py:409
  46.6 0.0 collective-permute-done.10.refs_1_
  46.6 0.1 collective-permute-start.19
  46.7 0.0 collective-permute-done.11.refs_2_
  46.7 0.0 collective-permute-done.12.refs_3_
  46.7 0.8 %assemble.2.refs_0_ = bf16[128,2048]{1,0:T(8,128)(2,1)} custom-call(bf16[2,128,128]{2,1,0:T(8,128)(2,1)S(1)} %get-tuple-element.40.refs_0_, bf16[2,128,128]{2,1,0:T(8,128)(2,1)S(1)} %collective-permute-done.10.refs_1_, bf16[2,128,128]{2,1,0:T(8,128)(2,1)S(1)} %collective-permute-done.11.refs_2_, bf16[2,128,128]{2,1,0:T(8,128)(2,1)S(1)} %collective-permute-done.12.refs_3_), custom_call_target="tpu_custom_call" | custom-call | flops 1073741824 | bytes 33554432 | tf_op jit(solution)/shard_map/assemble/pallas_call | solution.py:391
  47.4 1.8 %collective-permute-done.18.refs_3_ = bf16[2,128,128]{2,1,0:T(8,128)(2,1)S(1)} collective-permute-done((bf16[2,128,128]{2,1,0:T(8,128)(2,1)S(1)}, bf16[2,128,128]{2,1,0:T(8,128)(2,1)S(1)}, u32[]{:S(2)}, u32[]{:S(2)}) %collective-permute-start.18) | collective-permute-done | bytes 65568 | tf_op jit(solution)/shard_map/ppermute | solution.py:409
  49.3 1.4 %collective-permute-done.19.refs_4_ = bf16[2,128,128]{2,1,0:T(8,128)(2,1)S(1)} collective-permute-done((bf16[2,128,128]{2,1,0:T(8,128)(2,1)S(1)}, bf16[2,128,128]{2,1,0:T(8,128)(2,1)S(1)}, u32[]{:S(2)}, u32[]{:S(2)}) %collective-permute-start.19) | collective-permute-done | bytes 65568 | tf_op jit(solution)/shard_map/ppermute | solution.py:409
  50.6 0.8 %assemble.3 = bf16[128,2048]{1,0:T(8,128)(2,1)} custom-call(bf16[128,2048]{1,0:T(8,128)(2,1)} %assemble.2.refs_0_, bf16[2,128,128]{2,1,0:T(8,128)(2,1)S(1)} %get-tuple-element.49.refs_1_, bf16[2,128,128]{2,1,0:T(8,128)(2,1)S(1)} %collective-permute-done.17.refs_2_, ...), custom_call_target="tpu_custom_call", output_to_operand_aliasing={{}: (0, {})} | custom-call | flops 1073741824 | bytes 33554432 | tf_op jit(solution)/shard_map/assemble/pallas_call | solution.py:391
  (11 shorter events, 0.0 us)
Async XLA Ops:
  0.0 13.4 %copy-start.2 = (bf16[512,512]{1,0:T(8,128)(2,1)S(1)}, bf16[512,512]{1,0:T(8,128)(2,1)}, u32[]{:S(2)}) copy-start(bf16[512,512]{1,0:T(8,128)(2,1)} %values.9) | copy-start | bytes 1572868
  0.0 13.4 %copy-start.1 = (bf16[512,512]{1,0:T(8,128)(2,1)S(1)}, bf16[512,512]{1,0:T(8,128)(2,1)}, u32[]{:S(2)}) copy-start(bf16[512,512]{1,0:T(8,128)(2,1)} %keys.9) | copy-start | bytes 1572868
  0.0 13.4 %copy-start = (bf16[512,2048]{1,0:T(8,128)(2,1)S(1)}, bf16[512,2048]{1,0:T(8,128)(2,1)}, u32[]{:S(2)}) copy-start(bf16[512,2048]{1,0:T(8,128)(2,1)} %queries.9) | copy-start | bytes 6291460
  0.0 13.4 %copy-start.3 = (s32[2048]{0:T(1024)S(1)}, s32[2048]{0:T(1024)}, u32[]{:S(2)}) copy-start(s32[2048]{0:T(1024)} %param.7) | copy-start | bytes 24580
  2.7 10.7 %collective-permute-start.3 = (bf16[2,512,128]{2,1,0:T(8,128)(2,1)}, bf16[2,512,128]{2,1,0:T(8,128)(2,1)S(1)}, u32[]{:S(2)}, u32[]{:S(2)}) collective-permute-start(bf16[2,512,128]{2,1,0:T(8,128)(2,1)} %get-tuple-element.32), channel_id=1, source_target_pairs={{0,1},{1,0},{2,3},{3,2},{4,5},{5,4},{6,7},{7,6},{8,9},{9,8},{10,11... | collective-permute-start | bytes 786440 | tf_op jit(solution)/shard_map/ppermute | solution.py:409
  5.8 2.0 %collective-permute-start = (bf16[256,128]{1,0:T(8,128)(2,1)}, bf16[256,128]{1,0:T(8,128)(2,1)S(1)}, u32[]{:S(2)}, u32[]{:S(2)}) collective-permute-start(bf16[256,128]{1,0:T(8,128)(2,1)} %get-tuple-element.29), channel_id=1, source_target_pairs={{0,4},{4,0},{8,12},{12,8},{1,5},{5,1},{9,13},{13,9},{2,6},{6,2},{1... | collective-permute-start | bytes 196616 | tf_op jit(solution)/shard_map/ppermute | solution.py:409
  5.8 13.9 %collective-permute-start.4 = (bf16[768,128]{1,0:T(8,128)(2,1)}, bf16[768,128]{1,0:T(8,128)(2,1)S(1)}, u32[]{:S(2)}, u32[]{:S(2)}) collective-permute-start(bf16[768,128]{1,0:T(8,128)(2,1)} %get-tuple-element.34), channel_id=1, source_target_pairs={{0,4},{4,0},{8,12},{12,8},{1,5},{5,1},{9,13},{13,9},{2,6},{6,2},{1... | collective-permute-start | bytes 589832 | tf_op jit(solution)/shard_map/ppermute | solution.py:409
  6.3 4.5 %collective-permute-start.1 = (bf16[256,128]{1,0:T(8,128)(2,1)}, bf16[256,128]{1,0:T(8,128)(2,1)S(1)}, u32[]{:S(2)}, u32[]{:S(2)}) collective-permute-start(bf16[256,128]{1,0:T(8,128)(2,1)} %get-tuple-element.30), channel_id=1, source_target_pairs={{0,8},{4,12},{8,0},{12,4},{1,9},{5,13},{9,1},{13,5},{2,10},{6,14},... | collective-permute-start | bytes 196616 | tf_op jit(solution)/shard_map/ppermute | solution.py:409
  7.8 5.1 %collective-permute-start.2 = (bf16[256,128]{1,0:T(8,128)(2,1)}, bf16[256,128]{1,0:T(8,128)(2,1)S(1)}, u32[]{:S(2)}, u32[]{:S(2)}) collective-permute-start(bf16[256,128]{1,0:T(8,128)(2,1)} %get-tuple-element.31), channel_id=1, source_target_pairs={{0,12},{4,8},{8,4},{12,0},{1,13},{5,9},{9,5},{13,1},{2,14},{6,10},... | collective-permute-start | bytes 196616 | tf_op jit(solution)/shard_map/ppermute | solution.py:409
  7.8 16.0 %collective-permute-start.13 = (bf16[2,512,128]{2,1,0:T(8,128)(2,1)}, bf16[2,512,128]{2,1,0:T(8,128)(2,1)S(1)}, u32[]{:S(2)}, u32[]{:S(2)}) collective-permute-start(bf16[2,512,128]{2,1,0:T(8,128)(2,1)} %get-tuple-element.44), channel_id=1, source_target_pairs={{0,1},{1,0},{2,3},{3,2},{4,5},{5,4},{6,7},{7,6},{8,9},{9,8},{10,11... | collective-permute-start | bytes 786440 | tf_op jit(solution)/shard_map/ppermute | solution.py:409
  10.8 9.0 %collective-permute-start.5 = (bf16[768,128]{1,0:T(8,128)(2,1)}, bf16[768,128]{1,0:T(8,128)(2,1)S(1)}, u32[]{:S(2)}, u32[]{:S(2)}) collective-permute-start(bf16[768,128]{1,0:T(8,128)(2,1)} %get-tuple-element.35), channel_id=1, source_target_pairs={{0,8},{4,12},{8,0},{12,4},{1,9},{5,13},{9,1},{13,5},{2,10},{6,14},... | collective-permute-start | bytes 589832 | tf_op jit(solution)/shard_map/ppermute | solution.py:409
  13.0 7.5 %collective-permute-start.6 = (bf16[768,128]{1,0:T(8,128)(2,1)}, bf16[768,128]{1,0:T(8,128)(2,1)S(1)}, u32[]{:S(2)}, u32[]{:S(2)}) collective-permute-start(bf16[768,128]{1,0:T(8,128)(2,1)} %get-tuple-element.36), channel_id=1, source_target_pairs={{0,12},{4,8},{8,4},{12,0},{1,13},{5,9},{9,5},{13,1},{2,14},{6,10},... | collective-permute-start | bytes 589832 | tf_op jit(solution)/shard_map/ppermute | solution.py:409
  16.4 16.7 %collective-permute-start.9 = (bf16[528,128]{1,0:T(8,128)(2,1)S(1)}, bf16[528,128]{1,0:T(8,128)(2,1)S(1)}, u32[]{:S(2)}, u32[]{:S(2)}) collective-permute-start(bf16[528,128]{1,0:T(8,128)(2,1)S(1)} %get-tuple-element.39), channel_id=1, source_target_pairs={{0,3},{1,2},{2,1},{3,0},{4,7},{5,6},{6,5},{7,4},{8,11},{9,10},{10,... | collective-permute-start | bytes 405512 | tf_op jit(solution)/shard_map/ppermute | solution.py:419
  19.8 14.7 %collective-permute-start.8 = (bf16[528,128]{1,0:T(8,128)(2,1)S(1)}, bf16[528,128]{1,0:T(8,128)(2,1)S(1)}, u32[]{:S(2)}, u32[]{:S(2)}) collective-permute-start(bf16[528,128]{1,0:T(8,128)(2,1)S(1)} %get-tuple-element.33.refs_0_), channel_id=1, source_target_pairs={{0,2},{1,3},{2,0},{3,1},{4,6},{5,7},{6,4},{7,5},{8,10},{9,11},{10,... | collective-permute-start | bytes 405512 | tf_op jit(solution)/shard_map/ppermute | solution.py:419
  23.4 11.8 %collective-permute-start.7 = (bf16[528,128]{1,0:T(8,128)(2,1)S(1)}, bf16[528,128]{1,0:T(8,128)(2,1)S(1)}, u32[]{:S(2)}, u32[]{:S(2)}) collective-permute-start(bf16[528,128]{1,0:T(8,128)(2,1)S(1)} %get-tuple-element.38), channel_id=1, source_target_pairs={{0,1},{1,0},{2,3},{3,2},{4,5},{5,4},{6,7},{7,6},{8,9},{9,8},{10,11... | collective-permute-start | bytes 405512 | tf_op jit(solution)/shard_map/ppermute | solution.py:423
  26.8 11.6 %collective-permute-start.16 = (bf16[528,128]{1,0:T(8,128)(2,1)S(1)}, bf16[528,128]{1,0:T(8,128)(2,1)S(1)}, u32[]{:S(2)}, u32[]{:S(2)}) collective-permute-start(bf16[528,128]{1,0:T(8,128)(2,1)S(1)} %get-tuple-element.48), channel_id=1, source_target_pairs={{0,3},{1,2},{2,1},{3,0},{4,7},{5,6},{6,5},{7,4},{8,11},{9,10},{10,... | collective-permute-start | bytes 405512 | tf_op jit(solution)/shard_map/ppermute | solution.py:419
  29.5 12.9 %collective-permute-start.15 = (bf16[528,128]{1,0:T(8,128)(2,1)S(1)}, bf16[528,128]{1,0:T(8,128)(2,1)S(1)}, u32[]{:S(2)}, u32[]{:S(2)}) collective-permute-start(bf16[528,128]{1,0:T(8,128)(2,1)S(1)} %get-tuple-element.45.refs_0_), channel_id=1, source_target_pairs={{0,2},{1,3},{2,0},{3,1},{4,6},{5,7},{6,4},{7,5},{8,10},{9,11},{10,... | collective-permute-start | bytes 405512 | tf_op jit(solution)/shard_map/ppermute | solution.py:419
  33.1 9.7 %collective-permute-start.14 = (bf16[528,128]{1,0:T(8,128)(2,1)S(1)}, bf16[528,128]{1,0:T(8,128)(2,1)S(1)}, u32[]{:S(2)}, u32[]{:S(2)}) collective-permute-start(bf16[528,128]{1,0:T(8,128)(2,1)S(1)} %get-tuple-element.47), channel_id=1, source_target_pairs={{0,1},{1,0},{2,3},{3,2},{4,5},{5,4},{6,7},{7,6},{8,9},{9,8},{10,11... | collective-permute-start | bytes 405512 | tf_op jit(solution)/shard_map/ppermute | solution.py:423
  36.8 9.8 %collective-permute-start.10 = (bf16[2,128,128]{2,1,0:T(8,128)(2,1)S(1)}, bf16[2,128,128]{2,1,0:T(8,128)(2,1)S(1)}, u32[]{:S(2)}, u32[]{:S(2)}) collective-permute-start(bf16[2,128,128]{2,1,0:T(8,128)(2,1)S(1)} %get-tuple-element.41), channel_id=1, source_target_pairs={{0,4},{4,0},{8,12},{12,8},{1,5},{5,1},{9,13},{13,9},{2,6},{6,2},{1... | collective-permute-start | bytes 196616 | tf_op jit(solution)/shard_map/ppermute | solution.py:409
  36.9 9.8 %collective-permute-start.11 = (bf16[2,128,128]{2,1,0:T(8,128)(2,1)S(1)}, bf16[2,128,128]{2,1,0:T(8,128)(2,1)S(1)}, u32[]{:S(2)}, u32[]{:S(2)}) collective-permute-start(bf16[2,128,128]{2,1,0:T(8,128)(2,1)S(1)} %get-tuple-element.42), channel_id=1, source_target_pairs={{0,8},{4,12},{8,0},{12,4},{1,9},{5,13},{9,1},{13,5},{2,10},{6,14},... | collective-permute-start | bytes 196616 | tf_op jit(solution)/shard_map/ppermute | solution.py:409
  38.4 8.2 %collective-permute-start.12 = (bf16[2,128,128]{2,1,0:T(8,128)(2,1)S(1)}, bf16[2,128,128]{2,1,0:T(8,128)(2,1)S(1)}, u32[]{:S(2)}, u32[]{:S(2)}) collective-permute-start(bf16[2,128,128]{2,1,0:T(8,128)(2,1)S(1)} %get-tuple-element.43), channel_id=1, source_target_pairs={{0,12},{4,8},{8,4},{12,0},{1,13},{5,9},{9,5},{13,1},{2,14},{6,10},... | collective-permute-start | bytes 196616 | tf_op jit(solution)/shard_map/ppermute | solution.py:409
  44.5 3.0 %collective-permute-start.17 = (bf16[2,128,128]{2,1,0:T(8,128)(2,1)S(1)}, bf16[2,128,128]{2,1,0:T(8,128)(2,1)S(1)}, u32[]{:S(2)}, u32[]{:S(2)}) collective-permute-start(bf16[2,128,128]{2,1,0:T(8,128)(2,1)S(1)} %get-tuple-element.50), channel_id=1, source_target_pairs={{0,4},{4,0},{8,12},{12,8},{1,5},{5,1},{9,13},{13,9},{2,6},{6,2},{1... | collective-permute-start | bytes 196616 | tf_op jit(solution)/shard_map/ppermute | solution.py:409
  44.6 4.7 %collective-permute-start.18 = (bf16[2,128,128]{2,1,0:T(8,128)(2,1)S(1)}, bf16[2,128,128]{2,1,0:T(8,128)(2,1)S(1)}, u32[]{:S(2)}, u32[]{:S(2)}) collective-permute-start(bf16[2,128,128]{2,1,0:T(8,128)(2,1)S(1)} %get-tuple-element.51), channel_id=1, source_target_pairs={{0,8},{4,12},{8,0},{12,4},{1,9},{5,13},{9,1},{13,5},{2,10},{6,14},... | collective-permute-start | bytes 196616 | tf_op jit(solution)/shard_map/ppermute | solution.py:409
  46.6 4.0 %collective-permute-start.19 = (bf16[2,128,128]{2,1,0:T(8,128)(2,1)S(1)}, bf16[2,128,128]{2,1,0:T(8,128)(2,1)S(1)}, u32[]{:S(2)}, u32[]{:S(2)}) collective-permute-start(bf16[2,128,128]{2,1,0:T(8,128)(2,1)S(1)} %get-tuple-element.52), channel_id=1, source_target_pairs={{0,12},{4,8},{8,4},{12,0},{1,13},{5,9},{9,5},{13,1},{2,14},{6,10},... | collective-permute-start | bytes 196616 | tf_op jit(solution)/shard_map/ppermute | solution.py:409

commit v5 on v4

--- a/solution.py
+++ b/solution.py
@@ -170,56 +170,42 @@
     )(queries, keys, values)
 
 
-def attend_kernel(shapes, skip, waits, scale, steps_ref, queries, keys, values, *refs):
-    refs = refs[waits:]
-    chunks = sorted({chunk for chunk, _ in shapes})
-    count = len(shapes)
-    moved, got = refs[:3], refs[3:3 + len(chunks)]
-    outs = refs[3 + len(chunks):3 + len(chunks) + 2 * count]
-    q_buf, k_buf, v_buf, stats_buf, parts, sem, out_sem = refs[3 + len(chunks) + 2 * count:]
+def attend_kernel(chunk, far, skip, waits, scale, steps_ref, queries, keys, values, *refs):
+    *moved, got, same, cross, q_buf, k_buf, v_buf = refs[waits:]
     column = lax.axis_index("pb")
     z = lax.axis_index("ka")
-    half_rows = queries.shape[0] // 2
+    half_rows = q_buf.shape[1]
     sub = half_rows // 2
     held = keys.shape[0]
     pair = 2 * held
-    heads = keys.shape[1] // HEAD_DIM
-    upper, half = z // 2, z % 2
-    left = pl.ds(0, HEAD_DIM)
-
-    def place(block):
-        return (block + 4 - 2 * upper) % 4
-
-    pairs = []
-    for i, chunk in enumerate(chunks):
-        head = aligned(half * 2 + chunk, HEAD_DIM)
-        pairs += [
-            (keys.at[:, head], k_buf.at[i, aligned(half, held), :]),
-            (got[i].at[0], k_buf.at[i, aligned(1 - half, held), :]),
-            (values.at[:, head], v_buf.at[i, aligned(half, held), left]),
-            (got[i].at[1], v_buf.at[i, aligned(1 - half, held), left]),
-        ]
-    for i, (chunk, far) in enumerate(shapes):
-        cut = (aligned(region_of(z, far), half_rows), aligned(column * heads + half * 2 + chunk, HEAD_DIM))
-        pairs.append((queries.at[cut], q_buf.at[i, place(column)]))
+
+    def sort_queries(mine):
         for d, q in zip((1, 2, 3), moved):
-            pairs.append((q.at[pl.ds((skip + i) * half_rows, half_rows), :], q_buf.at[i, place(column ^ d)]))
-    copies = run_copies(pairs, sem)
-    v_buf[:, :, HEAD_DIM:] = jnp.ones((len(chunks), pair, HEAD_DIM), jnp.bfloat16)
-    steps = steps_ref[...].astype(jnp.float32)
-    columns = jnp.transpose(steps)
-    for copy in copies:
-        copy.wait()
-
-    def region(i, which):
-        chunk, far = shapes[i]
-        kv = chunks.index(chunk)
-        start = half_rows if far == (which == 0) else 0
-        base = which * pair
+            q_buf[mine ^ d] = q[skip * half_rows:(skip + 1) * half_rows, :]
+
+    def work(which):
+        upper, half = which // 2, which % 2
+        start = half_rows if far == (upper == 0) else 0
+        base = upper * pair
+        outs = (same, cross) if half == 0 else (cross, same)
+
+        def own_queries(mine):
+            at = (mine * 4 + half * 2 + chunk) * HEAD_DIM
+            q_buf[mine] = queries[start:start + half_rows, at:at + HEAD_DIM]
+
+        for mine in range(4):
+            pl.when(column == mine)(functools.partial(own_queries, mine))
+        head = slice((half * 2 + chunk) * HEAD_DIM, (half * 2 + chunk + 1) * HEAD_DIM)
+        for buf, own, theirs in ((k_buf, keys, got.at[0]), (v_buf, values, got.at[1])):
+            buf[half * held:(half + 1) * held, :HEAD_DIM] = own[:, head]
+            buf[(1 - half) * held:(2 - half) * held, :HEAD_DIM] = theirs[...]
+        v_buf[:, HEAD_DIM:] = jnp.ones((pair, HEAD_DIM), jnp.bfloat16)
+        steps = steps_ref[...].astype(jnp.float32)
+        columns = jnp.transpose(steps)
 
         def tile(slot, first_row, limit, masked_from, stats, first=0, size=half_rows):
-            scores = lax.dot_general(q_buf[i, slot, first:first + size, :], k_buf[kv, :limit, :],
-                                     (((1,), (1,)), ((), ())), preferred_element_type=jnp.float32)
+            q = q_buf[(slot + 2 * upper) % 4, first:first + size, :]
+            scores = lax.dot_general(q, k_buf[:limit, :], (((1,), (1,)), ((), ())), preferred_element_type=jnp.float32)
             if masked_from < limit:
                 at = (first_row + first) // LANES
                 q_steps = jnp.concatenate([columns[:, g:g + 1] for g in range(at, at + size // LANES)], axis=0)
@@ -230,11 +216,11 @@
             top = jnp.max(scores, axis=1, keepdims=True) * scale
             top = top.astype(jnp.bfloat16).astype(jnp.float32)
             weights = jnp.exp2(scores * scale - top).astype(jnp.bfloat16)
-            mixed = lax.dot_general(weights, v_buf[kv, :limit, :], (((1,), (0,)), ((), ())), preferred_element_type=jnp.float32)
+            mixed = lax.dot_general(weights, v_buf[:limit, :], (((1,), (0,)), ((), ())), preferred_element_type=jnp.float32)
             total = mixed[:, HEAD_DIM:]
             result = (mixed[:, :HEAD_DIM] / total).astype(jnp.bfloat16)
             for j in range(0, size, sub):
-                parts[i, (first + j) // sub, slot * sub:(slot + 1) * sub, :] = result[j:j + sub]
+                outs[(first + j) // sub][slot * sub:(slot + 1) * sub, :] = result[j:j + sub]
             high = total.astype(jnp.bfloat16).astype(jnp.float32)
             lane = lax.broadcasted_iota(jnp.int32, (size, LANES), 1)
             stats = jnp.where(lane == 3 * slot, top, stats)
@@ -245,51 +231,37 @@
         stats = jnp.zeros((half_rows, LANES), jnp.float32)
         stats = tile(0, base + start, reach, start, stats)
         stats = tile(1, base + held + start, min(held + reach, pair), held + start, stats)
-        if which == 0:
+        if upper == 0:
             stats = tile(2, 0, pair, pair, stats)
             stats = tile(3, 0, pair, pair, stats)
-        stats_buf[...] = stats
-        if which == 1 and not far:
-            stats_buf[sub:, :] = tile(3, held + start, LANES, 0, stats[sub:], sub, sub)
-        for j in range(2):
-            stats = jnp.transpose(stats_buf[j * sub:(j + 1) * sub, :])
-            parts[i, j, 4 * sub:, :] = stats[:STATS].astype(jnp.bfloat16)
-
-    sent = []
-    for i in range(count):
-        for which in range(2):
-            pl.when(upper == which)(functools.partial(region, i, which))
-        for j, place_in_pair in enumerate((half, 1 - half)):
-            copy = pltpu.make_async_copy(parts.at[i, place_in_pair], outs[2 * i + j], out_sem.at[2 * i + j])
-            copy.start()
-            sent.append(copy)
-    for copy in sent:
-        copy.wait()
-
-
-def attend(shapes, skip, steps, queries, keys, values, moved, got, after=()):
-    chunks = len({chunk for chunk, _ in shapes})
-    count = len(shapes)
-    rows = queries.shape[0]
+        stats = [stats[:sub], stats[sub:]]
+        if upper == 1 and not far:
+            stats[1] = tile(3, held + start, LANES, 0, stats[1], sub, sub)
+        for out, of in zip(outs, stats):
+            out[4 * sub:, :] = jnp.transpose(of)[:STATS].astype(jnp.bfloat16)
+
+    for which in range(4):
+        pl.when(column == which)(functools.partial(sort_queries, which))
+    for which in range(4):
+        pl.when(z == which)(functools.partial(work, which))
+
+
+def attend(chunk, far, skip, steps, queries, keys, values, moved, got, after=()):
     held = keys.shape[0]
-    part = jax.ShapeDtypeStruct((rows + STATS, LANES), jnp.bfloat16)
+    part = jax.ShapeDtypeStruct((held + STATS, LANES), jnp.bfloat16)
     return pl.pallas_call(
-        functools.partial(attend_kernel, shapes, skip, len(after), math.log2(math.e) / math.sqrt(HEAD_DIM)),
-        out_shape=[part] * (2 * count),
-        in_specs=[VMEM] + [ANY] * (6 + chunks + len(after)),
-        out_specs=[ANY] * (2 * count),
+        functools.partial(attend_kernel, chunk, far, skip, len(after), math.log2(math.e) / math.sqrt(HEAD_DIM)),
+        out_shape=[part] * 2,
+        in_specs=[VMEM] * 4 + [ANY] * len(after) + [VMEM] * 4,
+        out_specs=[VMEM] * 2,
         scratch_shapes=[
-            pltpu.VMEM((count, 4, rows // 2, HEAD_DIM), jnp.bfloat16),
-            pltpu.VMEM((chunks, 2 * held, HEAD_DIM), jnp.bfloat16),
-            pltpu.VMEM((chunks, 2 * held, 2 * HEAD_DIM), jnp.bfloat16),
-            pltpu.VMEM((rows // 2, LANES), jnp.float32),
-            pltpu.VMEM((count, 2) + part.shape, jnp.bfloat16),
-            pltpu.SemaphoreType.DMA((4 * chunks + 4 * count,)),
-            pltpu.SemaphoreType.DMA((2 * count,)),
+            pltpu.VMEM((4, held // 2, HEAD_DIM), jnp.bfloat16),
+            pltpu.VMEM((2 * held, HEAD_DIM), jnp.bfloat16),
+            pltpu.VMEM((2 * held, 2 * HEAD_DIM), jnp.bfloat16),
         ],
         compiler_params=pltpu.CompilerParams(vmem_limit_bytes=24 << 20),
         cost_estimate=pl.CostEstimate(flops=1 << 10, bytes_accessed=1 << 10, transcendentals=0),
-        name="attend_far" if shapes[0][1] else "attend_near",
+        name="attend_far" if far else "attend_near",
     )(steps, queries, keys, values, *after, *moved, *got)
 
 
@@ -312,48 +284,42 @@
 
 
 def merge_kernel(waits, *refs):
-    own, from_1, *far = refs[waits:-7]
-    (out_0, out_1, out_2, out_3, held, result, sem) = refs[-7:]
-    if len(far) == 1:
-        far = (far[0].at[0], far[0].at[1])
+    own, from_1, far = refs[waits:waits + 3]
+    outs, result = refs[waits + 3:-1], refs[-1]
     column = lax.axis_index("pb")
     z = lax.axis_index("ka")
     sub = result.shape[2]
-    for copy in run_copies([(a, held.at[z ^ d]) for d, a in enumerate((own, from_1) + tuple(far))], sem):
-        copy.wait()
-    stats = [jnp.transpose(held[s, 4 * sub:, :].astype(jnp.float32)) for s in range(4)]
-
-    def part(s, slot):
-        return held[s, slot * sub:(slot + 1) * sub, :]
-
-    def merge_block(block, half):
-        parts = ((half, block), (2 + half, (block + 2) % 4))
-        tops = [stats[s][:, 3 * slot:3 * slot + 1] for s, slot in parts]
-        totals = [stats[s][:, 3 * slot + 1:3 * slot + 2] + stats[s][:, 3 * slot + 2:3 * slot + 3] for s, slot in parts]
-        best = jnp.maximum(*tops)
-        shares = [total * jnp.exp2(top - best) for top, total in zip(tops, totals)]
-        share = shares[0] / (shares[0] + shares[1])
-        a, b = [part(s, slot).astype(jnp.float32) for s, slot in parts]
-        result[block, half] = (a * share + b * (1.0 - share)).astype(jnp.bfloat16)
-
-    for half in range(2):
-        result[0, half] = part(half, 0)
-        merge_block(2, half)
-        merge_block(3, half)
-
-    @pl.when(z < 3)
-    def _():
+    arrived = (own, from_1, far.at[0], far.at[1])
+
+    def merge_at(which):
+        held = [arrived[which ^ s] for s in range(4)]
+        stats = [jnp.transpose(held[s][4 * sub:, :].astype(jnp.float32)) for s in range(4)]
+
+        def part(s, slot):
+            return held[s][slot * sub:(slot + 1) * sub, :]
+
         for half in range(2):
-            result[1, half] = part(half, 1)
-
-    @pl.when(z == 3)
-    def _():
-        for half in range(2):
-            merge_block(1, half)
-
-    outs = ((3, out_3), (2, out_2), (1, out_1), (0, out_0))
-    for copy in run_copies([(result.at[column ^ d], out) for d, out in outs], sem):
-        copy.wait()
+            for block in range(4):
+                if block == 0 or block == 1 and which < 3:
+                    result[block, half] = part(half, block)
+                    continue
+                parts = ((half, block), (2 + half, (block + 2) % 4))
+                tops = [stats[s][:, 3 * slot:3 * slot + 1] for s, slot in parts]
+                totals = [stats[s][:, 3 * slot + 1:3 * slot + 2] + stats[s][:, 3 * slot + 2:3 * slot + 3] for s, slot in parts]
+                best = jnp.maximum(*tops)
+                shares = [total * jnp.exp2(top - best) for top, total in zip(tops, totals)]
+                share = shares[0] / (shares[0] + shares[1])
+                a, b = [part(s, slot).astype(jnp.float32) for s, slot in parts]
+                result[block, half] = (a * share + b * (1.0 - share)).astype(jnp.bfloat16)
+
+    def sort_at(which):
+        for d, out in enumerate(outs):
+            out[...] = result[which ^ d]
+
+    for which in range(4):
+        pl.when(z == which)(functools.partial(merge_at, which))
+    for which in range(4):
+        pl.when(column == which)(functools.partial(sort_at, which))
 
 
 def merge(parts, after=()):
@@ -362,14 +328,10 @@
     return pl.pallas_call(
         functools.partial(merge_kernel, len(after)),
         out_shape=[block] * 4,
-        in_specs=[ANY] * (len(after) + len(parts)),
-        out_specs=[ANY] * 4,
-        scratch_shapes=[
-            pltpu.VMEM((4,) + parts[0].shape, jnp.bfloat16),
-            pltpu.VMEM((4,) + block.shape, jnp.bfloat16),
-            pltpu.SemaphoreType.DMA((4,)),
-        ],
-        compiler_params=pltpu.CompilerParams(vmem_limit_bytes=4 << 20),
+        in_specs=[ANY] * len(after) + [VMEM] * len(parts),
+        out_specs=[VMEM] * 4,
+        scratch_shapes=[pltpu.VMEM((4,) + block.shape, jnp.bfloat16)],
+        compiler_params=pltpu.CompilerParams(vmem_limit_bytes=6 << 20),
         cost_estimate=pl.CostEstimate(flops=1 << 10, bytes_accessed=1 << 10, transcendentals=0),
         name="merge",
     )(*after, *parts)
@@ -415,7 +377,7 @@
     parts = []
     for i, (chunk, far) in enumerate(order):
         after = [parts[-1][0]] if parts else []
-        parts.append(attend((order[i],), max(i - 1, 0), steps, queries, keys, values, moved[min(i, 1)], got[chunk], after))
+        parts.append(attend(chunk, far, max(i - 1, 0), steps, queries, keys, values, moved[min(i, 1)], got[chunk], after))
     far = [collect(lax.ppermute(same, "ka", swaps[2]), lax.ppermute(cross, "ka", swaps[3])) for same, cross in parts[::2]]
     result = ()
     blocks = ()

time: 51.7 us -> 49.7 us (0.961)
  Pallas kernels: 20.3 us -> 14.5 us
  waiting for transfers between devices: 10.4 us -> 14.3 us
    pallas_call x4, Pallas kernels: 11.9 us -> 8.02 us  [attend(): pl.pallas_call(functools.partial(attend_kernel, chunk, far, skip, len(aft...]
    ppermute x2, waiting for transfers between devices: 3.61 us -> 6.87 us  [by_pairs(): lax.ppermute(same, 'ka', swaps[2])]
    pallas_call x2, Pallas kernels: 3.41 us -> 1.6 us  [merge(): pl.pallas_call(functools.partial(merge_kernel, len(after)), out_shape=[bl...]
    ppermute x14, waiting for transfers between devices: 6.42 us -> 7.4 us  [travel(): lax.ppermute(piece, axis, swap)]
  transfers between devices with their start and end apart: 20 -> 20, of which waited for: 6 -> 6; matrix products, arithmetic and copies ran while one was open for 0% -> 0% of each run, Pallas kernels for 33% -> 22%
where the time goes in v5:
time: 49.7 us; the launch traced here: 49.5 us
  starting transfers between devices  20.4 us (41%)
  Pallas kernels  14.5 us (29%)
  waiting for transfers between devices  14.3 us (29%)
    ppermute x14, starting transfers between devices, travel(): lax.ppermute(piece, axis, swap)  12.2 us
    pallas_call x4, Pallas kernels, attend(): pl.pallas_call(functools.partial(attend_kernel, chunk, far, skip, len(aft...  8.02 us
    ppermute x14, waiting for transfers between devices, travel(): lax.ppermute(piece, axis, swap)  7.4 us
    ppermute x2, waiting for transfers between devices, by_pairs(): lax.ppermute(same, 'ka', swaps[2])  6.87 us
    ppermute x2, starting transfers between devices, by_pairs(): lax.ppermute(cross, 'ka', swaps[3])  6.14 us
    pallas_call x1, Pallas kernels, pack(): pl.pallas_call(functools.partial(pack_kernel, batches), out_shape=[pair]...  2.69 us
    ppermute x2, starting transfers between devices, by_pairs(): lax.ppermute(beside, 'ka', swaps[1])  1.64 us
    pallas_call x2, Pallas kernels, merge(): pl.pallas_call(functools.partial(merge_kernel, len(after)), out_shape=[bl...  1.6 us
  transfers between devices with their start and end apart: 20, of which 6 were waited for; matrix products, arithmetic and copies ran while one was open for 0% of the time, Pallas kernels for 22%

profile of v5, /device:TPU:0, one launch (start us, length us, event | category | flops | bytes accessed | tf_op | source)
XLA Modules:
  0.0 49.5 jit_solution(1799525576617672397)
XLA Ops:
  0.0 2.7 %pack.1 = (bf16[2,512,128]{2,1,0:T(8,128)(2,1)}, bf16[2,512,128]{2,1,0:T(8,128)(2,1)}, bf16[256,128]{1,0:T(8,128)(2,1)}, bf16[256,128]{1,0:T(8,128)(2,1)}, bf16[...) custom-call(bf16[512,2048]{1,0:T(8,128)(2,1)} %queries.9, ...), custom_call_target="tpu_custom_call" | custom-call | tf_op jit(solution)/shard_map/pack/pallas_call | solution.py:163
  2.7 3.1 %collective-permute-start.3 = (bf16[2,512,128]{2,1,0:T(8,128)(2,1)}, bf16[2,512,128]{2,1,0:T(8,128)(2,1)S(1)}, u32[]{:S(2)}, u32[]{:S(2)}) collective-permute-start(bf16[2,512,128]{2,1,0:T(8,128)(2,1)} %get-tuple-element.32), channel_id=1, source_target_pairs={{0,1},{1,0},{2,3},{3,2},{4,5},{5,4},{6,7},{7,6},{8,9},{9,8},{10,11... | collective-permute-start | bytes 786440 | tf_op jit(solution)/shard_map/ppermute | solution.py:371
  5.8 0.0 collective-permute-start
  5.8 0.5 %collective-permute-start.4 = (bf16[768,128]{1,0:T(8,128)(2,1)}, bf16[768,128]{1,0:T(8,128)(2,1)S(1)}, u32[]{:S(2)}, u32[]{:S(2)}) collective-permute-start(bf16[768,128]{1,0:T(8,128)(2,1)} %get-tuple-element.34), channel_id=1, source_target_pairs={{0,4},{4,0},{8,12},{12,8},{1,5},{5,1},{9,13},{13,9},{2,6},{6,2},{1... | collective-permute-start | bytes 589832 | tf_op jit(solution)/shard_map/ppermute | solution.py:371
  6.3 1.5 %collective-permute-start.1 = (bf16[256,128]{1,0:T(8,128)(2,1)}, bf16[256,128]{1,0:T(8,128)(2,1)S(1)}, u32[]{:S(2)}, u32[]{:S(2)}) collective-permute-start(bf16[256,128]{1,0:T(8,128)(2,1)} %get-tuple-element.30), channel_id=1, source_target_pairs={{0,8},{4,12},{8,0},{12,4},{1,9},{5,13},{9,1},{13,5},{2,10},{6,14},... | collective-permute-start | bytes 196616 | tf_op jit(solution)/shard_map/ppermute | solution.py:371
  7.8 0.0 collective-permute-start.2
  7.8 0.0 collective-permute-done.refs_0_
  7.8 0.5 collective-permute-start.13
  8.3 2.5 %collective-permute-done.1.refs_1_ = bf16[256,128]{1,0:T(8,128)(2,1)S(1)} collective-permute-done((bf16[256,128]{1,0:T(8,128)(2,1)}, bf16[256,128]{1,0:T(8,128)(2,1)S(1)}, u32[]{:S(2)}, u32[]{:S(2)}) %collective-permute-start.1) | collective-permute-done | bytes 65568 | tf_op jit(solution)/shard_map/ppermute | solution.py:371
  10.8 2.2 %collective-permute-start.5 = (bf16[768,128]{1,0:T(8,128)(2,1)}, bf16[768,128]{1,0:T(8,128)(2,1)S(1)}, u32[]{:S(2)}, u32[]{:S(2)}) collective-permute-start(bf16[768,128]{1,0:T(8,128)(2,1)} %get-tuple-element.35), channel_id=1, source_target_pairs={{0,8},{4,12},{8,0},{12,4},{1,9},{5,13},{9,1},{13,5},{2,10},{6,14},... | collective-permute-start | bytes 589832 | tf_op jit(solution)/shard_map/ppermute | solution.py:371
  13.0 0.0 collective-permute-done.2.refs_2_
  13.0 0.4 collective-permute-start.6
  13.4 0.0 collective-permute-done.3.refs_3_.refs_4_
  13.4 2.0 %attend_far.2 = (bf16[528,128]{1,0:T(8,128)(2,1)S(1)}, bf16[528,128]{1,0:T(8,128)(2,1)S(1)}) custom-call(s32[16,128]{1,0:T(8,128)S(1)} %bitcast.1, bf16[512,2048]{1,0:T(8,128)(2,1)S(1)} %copy-done, bf16[512,512]{1,0:T(8,128)(2,1)S(1)} %copy-done.1, bf16[512,512]{1,0:T(8,128)(2,1)S(1)} %copy-done.2, bf16[256,128]{1,0:T(8,128)(2,1)S(1)} %collective-permute-done.refs_0_, ...), custom_call_target="tpu_custom_call" | custom-call | flops 1024 | bytes 1024 | tf_op jit(solution)/shard_map/attend_far/pallas_call | solution.py:252
  15.4 3.4 %collective-permute-start.9 = (bf16[528,128]{1,0:T(8,128)(2,1)S(1)}, bf16[528,128]{1,0:T(8,128)(2,1)S(1)}, u32[]{:S(2)}, u32[]{:S(2)}) collective-permute-start(bf16[528,128]{1,0:T(8,128)(2,1)S(1)} %get-tuple-element.39), channel_id=1, source_target_pairs={{0,3},{1,2},{2,1},{3,0},{4,7},{5,6},{6,5},{7,4},{8,11},{9,10},{10,... | collective-permute-start | bytes 405512 | tf_op jit(solution)/shard_map/ppermute | solution.py:381
  18.7 0.0 collective-permute-done.4.refs_1_
  18.7 0.0 collective-permute-start.8
  18.7 1.7 %collective-permute-done.6.refs_3_ = bf16[768,128]{1,0:T(8,128)(2,1)S(1)} collective-permute-done((bf16[768,128]{1,0:T(8,128)(2,1)}, bf16[768,128]{1,0:T(8,128)(2,1)S(1)}, u32[]{:S(2)}, u32[]{:S(2)}) %collective-permute-start.6) | collective-permute-done | bytes 196640 | tf_op jit(solution)/shard_map/ppermute | solution.py:371
  20.4 2.1 %attend_near.2 = (bf16[528,128]{1,0:T(8,128)(2,1)S(1)}, bf16[528,128]{1,0:T(8,128)(2,1)S(1)}) custom-call(s32[16,128]{1,0:T(8,128)S(1)} %bitcast.2, bf16[512,2048]{1,0:T(8,128)(2,1)S(1)} %copy-done, bf16[512,512]{1,0:T(8,128)(2,1)S(1)} %copy-done.1, bf16[512,512]{1,0:T(8,128)(2,1)S(1)} %copy-done.2, bf16[528,128]{1,0:T(8,128)(2,1)S(1)} %get-tuple-element.33.refs_0_, ...), custom_call_target="tpu_custom_call" | custom-call | flops 1024 | bytes 1024 | tf_op jit(solution)/shard_map/attend_near/pallas_call | solution.py:252
  22.6 0.4 collective-permute-start.7
  22.9 0.0 collective-permute-done.13.refs_4_
  22.9 2.0 %attend_far.3 = (bf16[528,128]{1,0:T(8,128)(2,1)S(1)}, bf16[528,128]{1,0:T(8,128)(2,1)S(1)}) custom-call(s32[16,128]{1,0:T(8,128)S(1)} %bitcast.3, bf16[512,2048]{1,0:T(8,128)(2,1)S(1)} %copy-done, bf16[512,512]{1,0:T(8,128)(2,1)S(1)} %copy-done.1, bf16[512,512]{1,0:T(8,128)(2,1)S(1)} %copy-done.2, bf16[528,128]{1,0:T(8,128)(2,1)S(1)} %get-tuple-element.37.refs_0_, ...), custom_call_target="tpu_custom_call" | custom-call | flops 1024 | bytes 1024 | tf_op jit(solution)/shard_map/attend_far/pallas_call | solution.py:252
  24.9 2.8 %collective-permute-start.16 = (bf16[528,128]{1,0:T(8,128)(2,1)S(1)}, bf16[528,128]{1,0:T(8,128)(2,1)S(1)}, u32[]{:S(2)}, u32[]{:S(2)}) collective-permute-start(bf16[528,128]{1,0:T(8,128)(2,1)S(1)} %get-tuple-element.48), channel_id=1, source_target_pairs={{0,3},{1,2},{2,1},{3,0},{4,7},{5,6},{6,5},{7,4},{8,11},{9,10},{10,... | collective-permute-start | bytes 405512 | tf_op jit(solution)/shard_map/ppermute | solution.py:381
  27.7 0.4 collective-permute-start.15
  28.1 2.0 %attend_near.3 = (bf16[528,128]{1,0:T(8,128)(2,1)S(1)}, bf16[528,128]{1,0:T(8,128)(2,1)S(1)}) custom-call(s32[16,128]{1,0:T(8,128)S(1)} %bitcast.4, bf16[512,2048]{1,0:T(8,128)(2,1)S(1)} %copy-done, bf16[512,512]{1,0:T(8,128)(2,1)S(1)} %copy-done.1, bf16[512,512]{1,0:T(8,128)(2,1)S(1)} %copy-done.2, bf16[528,128]{1,0:T(8,128)(2,1)S(1)} %get-tuple-element.45.refs_0_, ...), custom_call_target="tpu_custom_call" | custom-call | flops 1024 | bytes 1024 | tf_op jit(solution)/shard_map/attend_near/pallas_call | solution.py:252
  30.1 1.3 %collective-permute-start.14 = (bf16[528,128]{1,0:T(8,128)(2,1)S(1)}, bf16[528,128]{1,0:T(8,128)(2,1)S(1)}, u32[]{:S(2)}, u32[]{:S(2)}) collective-permute-start(bf16[528,128]{1,0:T(8,128)(2,1)S(1)} %get-tuple-element.47), channel_id=1, source_target_pairs={{0,1},{1,0},{2,3},{3,2},{4,5},{5,4},{6,7},{7,6},{8,9},{9,8},{10,11... | collective-permute-start | bytes 405512 | tf_op jit(solution)/shard_map/ppermute | solution.py:385
  31.4 5.2 %collective-permute-done.8.a = bf16[528,128]{1,0:T(8,128)(2,1)S(1)} collective-permute-done((bf16[528,128]{1,0:T(8,128)(2,1)S(1)}, bf16[528,128]{1,0:T(8,128)(2,1)S(1)}, u32[]{:S(2)}, u32[]{:S(2)}) %collective-permute-start.8) | collective-permute-done | bytes 135200 | tf_op jit(solution)/shard_map/ppermute | solution.py:381
  36.6 0.3 collect.2.refs_2_
  36.9 0.0 collective-permute-done.7.refs_1_
  36.9 0.9 %merge.2 = (bf16[2,128,128]{2,1,0:T(8,128)(2,1)S(1)}, bf16[2,128,128]{2,1,0:T(8,128)(2,1)S(1)}, bf16[2,128,128]{2,1,0:T(8,128)(2,1)S(1)}, bf16[2,128,128]{2,1,0:T(8,128)(2,1)S(1)}) custom-call(bf16[528,128]{1,0:T(8,128)(2,1)S(1)} %get-tuple-element.37.refs_0_, bf16[528,128]{1,0:T(8,128)(2,1)S(1)} %collective-permute-done.7.refs_1_, ...), custom_call_target="tpu_custom_call" | custom-call | flops 1024 | bytes 1024 | tf_op jit(solution)/shard_map/merge/pallas_call | solution.py:328
  37.9 0.1 collective-permute-start.10
  37.9 2.0 %collective-permute-start.11 = (bf16[2,128,128]{2,1,0:T(8,128)(2,1)S(1)}, bf16[2,128,128]{2,1,0:T(8,128)(2,1)S(1)}, u32[]{:S(2)}, u32[]{:S(2)}) collective-permute-start(bf16[2,128,128]{2,1,0:T(8,128)(2,1)S(1)} %get-tuple-element.42), channel_id=1, source_target_pairs={{0,8},{4,12},{8,0},{12,4},{1,9},{5,13},{9,1},{13,5},{2,10},{6,14},... | collective-permute-start | bytes 196616 | tf_op jit(solution)/shard_map/ppermute | solution.py:371
  39.9 0.0 collective-permute-done.16.b
  39.9 0.1 collective-permute-start.12
  40.0 1.6 %collective-permute-done.15.a = bf16[528,128]{1,0:T(8,128)(2,1)S(1)} collective-permute-done((bf16[528,128]{1,0:T(8,128)(2,1)S(1)}, bf16[528,128]{1,0:T(8,128)(2,1)S(1)}, u32[]{:S(2)}, u32[]{:S(2)}) %collective-permute-start.15) | collective-permute-done | bytes 135200 | tf_op jit(solution)/shard_map/ppermute | solution.py:381
  41.7 0.3 collect.3.refs_3_
  42.0 0.0 collective-permute-done.14.refs_2_
  42.0 0.7 %merge.3 = (bf16[2,128,128]{2,1,0:T(8,128)(2,1)S(1)}, bf16[2,128,128]{2,1,0:T(8,128)(2,1)S(1)}, bf16[2,128,128]{2,1,0:T(8,128)(2,1)S(1)}, bf16[2,128,128]{2,1,0:T(8,128)(2,1)S(1)}) custom-call(bf16[2,128,128]{2,1,0:T(8,128)(2,1)S(1)} %get-tuple-element.40.refs_0_, bf16[528,128]{1,0:T(8,128)(2,1)S(1)} %get-tuple-element.46.refs_1_, ...), custom_call_target="tpu_custom_call" | custom-call | flops 1024 | bytes 1024 | tf_op jit(solution)/shard_map/merge/pallas_call | solution.py:328
  42.7 0.1 collective-permute-start.17
  42.8 1.8 %collective-permute-start.18 = (bf16[2,128,128]{2,1,0:T(8,128)(2,1)S(1)}, bf16[2,128,128]{2,1,0:T(8,128)(2,1)S(1)}, u32[]{:S(2)}, u32[]{:S(2)}) collective-permute-start(bf16[2,128,128]{2,1,0:T(8,128)(2,1)S(1)} %get-tuple-element.51), channel_id=1, source_target_pairs={{0,8},{4,12},{8,0},{12,4},{1,9},{5,13},{9,1},{13,5},{2,10},{6,14},... | collective-permute-start | bytes 196616 | tf_op jit(solution)/shard_map/ppermute | solution.py:371
  44.6 0.0 collective-permute-done.10.refs_1_
  44.6 0.1 collective-permute-start.19
  44.7 0.0 collective-permute-done.11.refs_2_
  44.7 0.8 %assemble.2.refs_0_ = bf16[128,2048]{1,0:T(8,128)(2,1)} custom-call(bf16[2,128,128]{2,1,0:T(8,128)(2,1)S(1)} %get-tuple-element.40.refs_0_, bf16[2,128,128]{2,1,0:T(8,128)(2,1)S(1)} %collective-permute-done.10.refs_1_, bf16[2,128,128]{2,1,0:T(8,128)(2,1)S(1)} %collective-permute-done.11.refs_2_, bf16[2,128,128]{2,1,0:T(8,128)(2,1)S(1)} %collective-permute-done.12.refs_3_), custom_call_target="tpu_custom_call" | custom-call | flops 1073741824 | bytes 33554432 | tf_op jit(solution)/shard_map/assemble/pallas_call | solution.py:353
  45.4 0.0 collective-permute-done.17.refs_2_
  45.4 1.9 %collective-permute-done.18.refs_3_ = bf16[2,128,128]{2,1,0:T(8,128)(2,1)S(1)} collective-permute-done((bf16[2,128,128]{2,1,0:T(8,128)(2,1)S(1)}, bf16[2,128,128]{2,1,0:T(8,128)(2,1)S(1)}, u32[]{:S(2)}, u32[]{:S(2)}) %collective-permute-start.18) | collective-permute-done | bytes 65568 | tf_op jit(solution)/shard_map/ppermute | solution.py:371
  47.3 1.3 %collective-permute-done.19.refs_4_ = bf16[2,128,128]{2,1,0:T(8,128)(2,1)S(1)} collective-permute-done((bf16[2,128,128]{2,1,0:T(8,128)(2,1)S(1)}, bf16[2,128,128]{2,1,0:T(8,128)(2,1)S(1)}, u32[]{:S(2)}, u32[]{:S(2)}) %collective-permute-start.19) | collective-permute-done | bytes 65568 | tf_op jit(solution)/shard_map/ppermute | solution.py:371
  48.6 0.8 %assemble.3 = bf16[128,2048]{1,0:T(8,128)(2,1)} custom-call(bf16[128,2048]{1,0:T(8,128)(2,1)} %assemble.2.refs_0_, bf16[2,128,128]{2,1,0:T(8,128)(2,1)S(1)} %get-tuple-element.49.refs_1_, bf16[2,128,128]{2,1,0:T(8,128)(2,1)S(1)} %collective-permute-done.17.refs_2_, ...), custom_call_target="tpu_custom_call", output_to_operand_aliasing={{}: (0, {})} | custom-call | flops 1073741824 | bytes 33554432 | tf_op jit(solution)/shard_map/assemble/pallas_call | solution.py:353
  (11 shorter events, 0.0 us)
Async XLA Ops:
  0.0 13.4 %copy-start.2 = (bf16[512,512]{1,0:T(8,128)(2,1)S(1)}, bf16[512,512]{1,0:T(8,128)(2,1)}, u32[]{:S(2)}) copy-start(bf16[512,512]{1,0:T(8,128)(2,1)} %values.9) | copy-start | bytes 1572868
  0.0 13.4 %copy-start.1 = (bf16[512,512]{1,0:T(8,128)(2,1)S(1)}, bf16[512,512]{1,0:T(8,128)(2,1)}, u32[]{:S(2)}) copy-start(bf16[512,512]{1,0:T(8,128)(2,1)} %keys.9) | copy-start | bytes 1572868
  0.0 13.4 %copy-start = (bf16[512,2048]{1,0:T(8,128)(2,1)S(1)}, bf16[512,2048]{1,0:T(8,128)(2,1)}, u32[]{:S(2)}) copy-start(bf16[512,2048]{1,0:T(8,128)(2,1)} %queries.9) | copy-start | bytes 6291460
  0.0 13.4 %copy-start.3 = (s32[2048]{0:T(1024)S(1)}, s32[2048]{0:T(1024)}, u32[]{:S(2)}) copy-start(s32[2048]{0:T(1024)} %param.7) | copy-start | bytes 24580
  2.7 10.7 %collective-permute-start.3 = (bf16[2,512,128]{2,1,0:T(8,128)(2,1)}, bf16[2,512,128]{2,1,0:T(8,128)(2,1)S(1)}, u32[]{:S(2)}, u32[]{:S(2)}) collective-permute-start(bf16[2,512,128]{2,1,0:T(8,128)(2,1)} %get-tuple-element.32), channel_id=1, source_target_pairs={{0,1},{1,0},{2,3},{3,2},{4,5},{5,4},{6,7},{7,6},{8,9},{9,8},{10,11... | collective-permute-start | bytes 786440 | tf_op jit(solution)/shard_map/ppermute | solution.py:371
  5.8 2.0 %collective-permute-start = (bf16[256,128]{1,0:T(8,128)(2,1)}, bf16[256,128]{1,0:T(8,128)(2,1)S(1)}, u32[]{:S(2)}, u32[]{:S(2)}) collective-permute-start(bf16[256,128]{1,0:T(8,128)(2,1)} %get-tuple-element.29), channel_id=1, source_target_pairs={{0,4},{4,0},{8,12},{12,8},{1,5},{5,1},{9,13},{13,9},{2,6},{6,2},{1... | collective-permute-start | bytes 196616 | tf_op jit(solution)/shard_map/ppermute | solution.py:371
  5.8 12.9 %collective-permute-start.4 = (bf16[768,128]{1,0:T(8,128)(2,1)}, bf16[768,128]{1,0:T(8,128)(2,1)S(1)}, u32[]{:S(2)}, u32[]{:S(2)}) collective-permute-start(bf16[768,128]{1,0:T(8,128)(2,1)} %get-tuple-element.34), channel_id=1, source_target_pairs={{0,4},{4,0},{8,12},{12,8},{1,5},{5,1},{9,13},{13,9},{2,6},{6,2},{1... | collective-permute-start | bytes 589832 | tf_op jit(solution)/shard_map/ppermute | solution.py:371
  6.3 4.5 %collective-permute-start.1 = (bf16[256,128]{1,0:T(8,128)(2,1)}, bf16[256,128]{1,0:T(8,128)(2,1)S(1)}, u32[]{:S(2)}, u32[]{:S(2)}) collective-permute-start(bf16[256,128]{1,0:T(8,128)(2,1)} %get-tuple-element.30), channel_id=1, source_target_pairs={{0,8},{4,12},{8,0},{12,4},{1,9},{5,13},{9,1},{13,5},{2,10},{6,14},... | collective-permute-start | bytes 196616 | tf_op jit(solution)/shard_map/ppermute | solution.py:371
  7.8 5.1 %collective-permute-start.2 = (bf16[256,128]{1,0:T(8,128)(2,1)}, bf16[256,128]{1,0:T(8,128)(2,1)S(1)}, u32[]{:S(2)}, u32[]{:S(2)}) collective-permute-start(bf16[256,128]{1,0:T(8,128)(2,1)} %get-tuple-element.31), channel_id=1, source_target_pairs={{0,12},{4,8},{8,4},{12,0},{1,13},{5,9},{9,5},{13,1},{2,14},{6,10},... | collective-permute-start | bytes 196616 | tf_op jit(solution)/shard_map/ppermute | solution.py:371
  7.8 15.1 %collective-permute-start.13 = (bf16[2,512,128]{2,1,0:T(8,128)(2,1)}, bf16[2,512,128]{2,1,0:T(8,128)(2,1)S(1)}, u32[]{:S(2)}, u32[]{:S(2)}) collective-permute-start(bf16[2,512,128]{2,1,0:T(8,128)(2,1)} %get-tuple-element.44), channel_id=1, source_target_pairs={{0,1},{1,0},{2,3},{3,2},{4,5},{5,4},{6,7},{7,6},{8,9},{9,8},{10,11... | collective-permute-start | bytes 786440 | tf_op jit(solution)/shard_map/ppermute | solution.py:371
  10.8 7.9 %collective-permute-start.5 = (bf16[768,128]{1,0:T(8,128)(2,1)}, bf16[768,128]{1,0:T(8,128)(2,1)S(1)}, u32[]{:S(2)}, u32[]{:S(2)}) collective-permute-start(bf16[768,128]{1,0:T(8,128)(2,1)} %get-tuple-element.35), channel_id=1, source_target_pairs={{0,8},{4,12},{8,0},{12,4},{1,9},{5,13},{9,1},{13,5},{2,10},{6,14},... | collective-permute-start | bytes 589832 | tf_op jit(solution)/shard_map/ppermute | solution.py:371
  13.0 7.5 %collective-permute-start.6 = (bf16[768,128]{1,0:T(8,128)(2,1)}, bf16[768,128]{1,0:T(8,128)(2,1)S(1)}, u32[]{:S(2)}, u32[]{:S(2)}) collective-permute-start(bf16[768,128]{1,0:T(8,128)(2,1)} %get-tuple-element.36), channel_id=1, source_target_pairs={{0,12},{4,8},{8,4},{12,0},{1,13},{5,9},{9,5},{13,1},{2,14},{6,10},... | collective-permute-start | bytes 589832 | tf_op jit(solution)/shard_map/ppermute | solution.py:371
  15.4 14.7 %collective-permute-start.9 = (bf16[528,128]{1,0:T(8,128)(2,1)S(1)}, bf16[528,128]{1,0:T(8,128)(2,1)S(1)}, u32[]{:S(2)}, u32[]{:S(2)}) collective-permute-start(bf16[528,128]{1,0:T(8,128)(2,1)S(1)} %get-tuple-element.39), channel_id=1, source_target_pairs={{0,3},{1,2},{2,1},{3,0},{4,7},{5,6},{6,5},{7,4},{8,11},{9,10},{10,... | collective-permute-start | bytes 405512 | tf_op jit(solution)/shard_map/ppermute | solution.py:381
  18.7 17.8 %collective-permute-start.8 = (bf16[528,128]{1,0:T(8,128)(2,1)S(1)}, bf16[528,128]{1,0:T(8,128)(2,1)S(1)}, u32[]{:S(2)}, u32[]{:S(2)}) collective-permute-start(bf16[528,128]{1,0:T(8,128)(2,1)S(1)} %get-tuple-element.33.refs_0_), channel_id=1, source_target_pairs={{0,2},{1,3},{2,0},{3,1},{4,6},{5,7},{6,4},{7,5},{8,10},{9,11},{10,... | collective-permute-start | bytes 405512 | tf_op jit(solution)/shard_map/ppermute | solution.py:381
  22.6 14.4 %collective-permute-start.7 = (bf16[528,128]{1,0:T(8,128)(2,1)S(1)}, bf16[528,128]{1,0:T(8,128)(2,1)S(1)}, u32[]{:S(2)}, u32[]{:S(2)}) collective-permute-start(bf16[528,128]{1,0:T(8,128)(2,1)S(1)} %get-tuple-element.38), channel_id=1, source_target_pairs={{0,1},{1,0},{2,3},{3,2},{4,5},{5,4},{6,7},{7,6},{8,9},{9,8},{10,11... | collective-permute-start | bytes 405512 | tf_op jit(solution)/shard_map/ppermute | solution.py:385
  24.9 15.0 %collective-permute-start.16 = (bf16[528,128]{1,0:T(8,128)(2,1)S(1)}, bf16[528,128]{1,0:T(8,128)(2,1)S(1)}, u32[]{:S(2)}, u32[]{:S(2)}) collective-permute-start(bf16[528,128]{1,0:T(8,128)(2,1)S(1)} %get-tuple-element.48), channel_id=1, source_target_pairs={{0,3},{1,2},{2,1},{3,0},{4,7},{5,6},{6,5},{7,4},{8,11},{9,10},{10,... | collective-permute-start | bytes 405512 | tf_op jit(solution)/shard_map/ppermute | solution.py:381
  27.7 14.0 %collective-permute-start.15 = (bf16[528,128]{1,0:T(8,128)(2,1)S(1)}, bf16[528,128]{1,0:T(8,128)(2,1)S(1)}, u32[]{:S(2)}, u32[]{:S(2)}) collective-permute-start(bf16[528,128]{1,0:T(8,128)(2,1)S(1)} %get-tuple-element.45.refs_0_), channel_id=1, source_target_pairs={{0,2},{1,3},{2,0},{3,1},{4,6},{5,7},{6,4},{7,5},{8,10},{9,11},{10,... | collective-permute-start | bytes 405512 | tf_op jit(solution)/shard_map/ppermute | solution.py:381
  30.1 11.9 %collective-permute-start.14 = (bf16[528,128]{1,0:T(8,128)(2,1)S(1)}, bf16[528,128]{1,0:T(8,128)(2,1)S(1)}, u32[]{:S(2)}, u32[]{:S(2)}) collective-permute-start(bf16[528,128]{1,0:T(8,128)(2,1)S(1)} %get-tuple-element.47), channel_id=1, source_target_pairs={{0,1},{1,0},{2,3},{3,2},{4,5},{5,4},{6,7},{7,6},{8,9},{9,8},{10,11... | collective-permute-start | bytes 405512 | tf_op jit(solution)/shard_map/ppermute | solution.py:385
  37.9 6.7 %collective-permute-start.10 = (bf16[2,128,128]{2,1,0:T(8,128)(2,1)S(1)}, bf16[2,128,128]{2,1,0:T(8,128)(2,1)S(1)}, u32[]{:S(2)}, u32[]{:S(2)}) collective-permute-start(bf16[2,128,128]{2,1,0:T(8,128)(2,1)S(1)} %get-tuple-element.41), channel_id=1, source_target_pairs={{0,4},{4,0},{8,12},{12,8},{1,5},{5,1},{9,13},{13,9},{2,6},{6,2},{1... | collective-permute-start | bytes 196616 | tf_op jit(solution)/shard_map/ppermute | solution.py:371
  37.9 6.7 %collective-permute-start.11 = (bf16[2,128,128]{2,1,0:T(8,128)(2,1)S(1)}, bf16[2,128,128]{2,1,0:T(8,128)(2,1)S(1)}, u32[]{:S(2)}, u32[]{:S(2)}) collective-permute-start(bf16[2,128,128]{2,1,0:T(8,128)(2,1)S(1)} %get-tuple-element.42), channel_id=1, source_target_pairs={{0,8},{4,12},{8,0},{12,4},{1,9},{5,13},{9,1},{13,5},{2,10},{6,14},... | collective-permute-start | bytes 196616 | tf_op jit(solution)/shard_map/ppermute | solution.py:371
  39.9 4.7 %collective-permute-start.12 = (bf16[2,128,128]{2,1,0:T(8,128)(2,1)S(1)}, bf16[2,128,128]{2,1,0:T(8,128)(2,1)S(1)}, u32[]{:S(2)}, u32[]{:S(2)}) collective-permute-start(bf16[2,128,128]{2,1,0:T(8,128)(2,1)S(1)} %get-tuple-element.43), channel_id=1, source_target_pairs={{0,12},{4,8},{8,4},{12,0},{1,13},{5,9},{9,5},{13,1},{2,14},{6,10},... | collective-permute-start | bytes 196616 | tf_op jit(solution)/shard_map/ppermute | solution.py:371
  42.7 2.7 %collective-permute-start.17 = (bf16[2,128,128]{2,1,0:T(8,128)(2,1)S(1)}, bf16[2,128,128]{2,1,0:T(8,128)(2,1)S(1)}, u32[]{:S(2)}, u32[]{:S(2)}) collective-permute-start(bf16[2,128,128]{2,1,0:T(8,128)(2,1)S(1)} %get-tuple-element.50), channel_id=1, source_target_pairs={{0,4},{4,0},{8,12},{12,8},{1,5},{5,1},{9,13},{13,9},{2,6},{6,2},{1... | collective-permute-start | bytes 196616 | tf_op jit(solution)/shard_map/ppermute | solution.py:371
  42.8 4.5 %collective-permute-start.18 = (bf16[2,128,128]{2,1,0:T(8,128)(2,1)S(1)}, bf16[2,128,128]{2,1,0:T(8,128)(2,1)S(1)}, u32[]{:S(2)}, u32[]{:S(2)}) collective-permute-start(bf16[2,128,128]{2,1,0:T(8,128)(2,1)S(1)} %get-tuple-element.51), channel_id=1, source_target_pairs={{0,8},{4,12},{8,0},{12,4},{1,9},{5,13},{9,1},{13,5},{2,10},{6,14},... | collective-permute-start | bytes 196616 | tf_op jit(solution)/shard_map/ppermute | solution.py:371
  44.6 4.0 %collective-permute-start.19 = (bf16[2,128,128]{2,1,0:T(8,128)(2,1)S(1)}, bf16[2,128,128]{2,1,0:T(8,128)(2,1)S(1)}, u32[]{:S(2)}, u32[]{:S(2)}) collective-permute-start(bf16[2,128,128]{2,1,0:T(8,128)(2,1)S(1)} %get-tuple-element.52), channel_id=1, source_target_pairs={{0,12},{4,8},{8,4},{12,0},{1,13},{5,9},{9,5},{13,1},{2,14},{6,10},... | collective-permute-start | bytes 196616 | tf_op jit(solution)/shard_map/ppermute | solution.py:371

commit v6 on v5

--- a/solution.py
+++ b/solution.py
@@ -12,8 +12,8 @@
 LANES = 128
 LOW_SCORE = -1e30
 UNSEEN = -float(1 << 20)
-ROW_TILE = 256
 STATS = 16
+PACK_VMEM = 419 << 17
 ANY = pl.BlockSpec(memory_space=pl.ANY)
 VMEM = pl.BlockSpec(memory_space=pltpu.VMEM)
 
@@ -137,40 +137,40 @@
     return 1 - z // 2 if far else z // 2
 
 
-def pack_kernel(batches, queries, keys, values, *refs):
-    outs, sem = refs[:-1], refs[-1]
+def pack_kernel(chunks, batches, waits, queries, keys, values, *refs):
+    outs, sem = refs[waits:-1], refs[-1]
     column = lax.axis_index("pb")
     z = lax.axis_index("ka")
     half = z % 2
     heads = keys.shape[1] // HEAD_DIM
     count = queries.shape[0] // 2
     pairs = []
-    for chunk, to in enumerate(outs[:2]):
+    for chunk, to in zip(chunks, outs):
         theirs = aligned((1 - half) * 2 + chunk, HEAD_DIM)
         pairs += [(keys.at[:, theirs], to.at[0]), (values.at[:, theirs], to.at[1])]
-    for b, batch in enumerate(batches):
+    for (d, batch), to in zip(batches, outs[len(chunks):]):
         for i, (chunk, far) in enumerate(batch):
-            for d, to in zip((1, 2, 3), outs[2 + 3 * b:]):
-                cut = (aligned(region_of(z, far), count), aligned((column ^ d) * heads + half * 2 + chunk, HEAD_DIM))
-                pairs.append((queries.at[cut], to.at[pl.ds(i * count, count), :]))
+            cut = (aligned(region_of(z, far), count), aligned((column ^ d) * heads + half * 2 + chunk, HEAD_DIM))
+            pairs.append((queries.at[cut], to.at[pl.ds(i * count, count), :]))
     for copy in run_copies(pairs, sem):
         copy.wait()
 
 
-def pack(batches, queries, keys, values):
+def pack(chunks, batches, queries, keys, values, after=()):
     pair = jax.ShapeDtypeStruct((2, keys.shape[0], HEAD_DIM), keys.dtype)
-    rows = [jax.ShapeDtypeStruct((len(batch) * queries.shape[0] // 2, HEAD_DIM), queries.dtype) for batch in batches]
+    rows = [jax.ShapeDtypeStruct((len(batch) * queries.shape[0] // 2, HEAD_DIM), queries.dtype) for _, batch in batches]
     return pl.pallas_call(
-        functools.partial(pack_kernel, batches),
-        out_shape=[pair] * 2 + sum([[shape] * 3 for shape in rows], []),
-        in_specs=[ANY] * 3,
-        out_specs=[VMEM] * (2 + 3 * len(batches)),
-        scratch_shapes=[pltpu.SemaphoreType.DMA((4 + 3 * sum(map(len, batches)),))],
+        functools.partial(pack_kernel, chunks, batches, len(after)),
+        out_shape=[pair] * len(chunks) + rows,
+        in_specs=[ANY] * (3 + len(after)),
+        out_specs=[ANY] * (len(chunks) + len(batches)),
+        scratch_shapes=[pltpu.SemaphoreType.DMA((2 * len(chunks) + sum(len(batch) for _, batch in batches),))],
+        compiler_params=pltpu.CompilerParams(vmem_limit_bytes=PACK_VMEM),
         name="pack",
-    )(queries, keys, values)
-
-
-def attend_kernel(chunk, far, skip, waits, scale, steps_ref, queries, keys, values, *refs):
+    )(queries, keys, values, *after)
+
+
+def attend_kernel(chunk, far, skips, waits, scale, steps_ref, queries, keys, values, *refs):
     *moved, got, same, cross, q_buf, k_buf, v_buf = refs[waits:]
     column = lax.axis_index("pb")
     z = lax.axis_index("ka")
@@ -180,7 +180,7 @@
     pair = 2 * held
 
     def sort_queries(mine):
-        for d, q in zip((1, 2, 3), moved):
+        for d, skip, q in zip((1, 2, 3), skips, moved):
             q_buf[mine ^ d] = q[skip * half_rows:(skip + 1) * half_rows, :]
 
     def work(which):
@@ -246,11 +246,11 @@
         pl.when(z == which)(functools.partial(work, which))
 
 
-def attend(chunk, far, skip, steps, queries, keys, values, moved, got, after=()):
+def attend(chunk, far, skips, steps, queries, keys, values, moved, got, after=()):
     held = keys.shape[0]
     part = jax.ShapeDtypeStruct((held + STATS, LANES), jnp.bfloat16)
     return pl.pallas_call(
-        functools.partial(attend_kernel, chunk, far, skip, len(after), math.log2(math.e) / math.sqrt(HEAD_DIM)),
+        functools.partial(attend_kernel, chunk, far, skips, len(after), math.log2(math.e) / math.sqrt(HEAD_DIM)),
         out_shape=[part] * 2,
         in_specs=[VMEM] * 4 + [ANY] * len(after) + [VMEM] * 4,
         out_specs=[VMEM] * 2,
@@ -371,13 +371,16 @@
         return [lax.ppermute(piece, axis, swap) for piece, swap in zip(sent, swaps[1:])]
 
     order = ((0, True), (0, False), (1, True), (1, False))
-    packed = pack((order[:1], order[1:]), queries, keys, values)
+    batches = ((1, order), (2, order[:1]), (3, order[:1]), (2, order[1:]), (3, order[1:]))
+    packed = pack((0, 1), batches, queries, keys, values)
     got = travel(packed[:1], "ka"), travel(packed[1:2], "ka")
-    moved = travel(packed[2:5], "pb"), travel(packed[5:], "pb")
+    all_1, *others = [lax.ppermute(piece, "pb", swaps[d]) for piece, (d, _) in zip(packed[2:], batches)]
+    first, rest = others[:2], others[2:]
     parts = []
     for i, (chunk, far) in enumerate(order):
         after = [parts[-1][0]] if parts else []
-        parts.append(attend(chunk, far, max(i - 1, 0), steps, queries, keys, values, moved[min(i, 1)], got[chunk], after))
+        arrived, skips = ([all_1, *first], (0, 0, 0)) if i == 0 else ([all_1, *rest], (i, i - 1, i - 1))
+        parts.append(attend(chunk, far, skips, steps, queries, keys, values, arrived, got[chunk], after))
     far = [collect(lax.ppermute(same, "ka", swaps[2]), lax.ppermute(cross, "ka", swaps[3])) for same, cross in parts[::2]]
     result = ()
     blocks = ()

time: 49.7 us -> 48.6 us (0.978)
  Pallas kernels: 14.5 us -> 13.5 us
    ppermute x14 -> x8, starting transfers between devices: 12.2 us -> 6.93 us  [travel(): lax.ppermute(piece, axis, swap)]
    ppermute x0 -> x5, starting transfers between devices: none -> 4.64 us  [by_pairs(): lax.ppermute(piece, 'pb', swaps[d])]
    ppermute x14 -> x8, waiting for transfers between devices: 7.4 us -> 3.25 us  [travel(): lax.ppermute(piece, axis, swap)]
    ppermute x0 -> x5, waiting for transfers between devices: none -> 3.38 us  [by_pairs(): lax.ppermute(piece, 'pb', swaps[d])]
    ppermute x2, waiting for transfers between devices: 6.87 us -> 8 us  [by_pairs(): lax.ppermute(same, 'ka', swaps[2])]
    pallas_call x5, Pallas kernels: 10.7 us -> 9.67 us  [the longest x4 8.03 us: attend(): pl.pallas_call(functools.partial(attend_kernel, chunk, far, skips, len(af...]
  transfers between devices with their start and end apart: 20 -> 19, of which waited for: 6 -> 7; matrix products, arithmetic and copies ran while one was open for 0% -> 0% of each run, Pallas kernels for 22% -> 23%
where the time goes in v6:
time: 48.6 us; the launch traced here: 48.4 us
  starting transfers between devices  20 us (41%)
  waiting for transfers between devices  14.6 us (30%)
  Pallas kernels  13.5 us (28%)
    pallas_call x4, Pallas kernels, attend(): pl.pallas_call(functools.partial(attend_kernel, chunk, far, skips, len(af...  8.03 us
    ppermute x2, waiting for transfers between devices, by_pairs(): lax.ppermute(same, 'ka', swaps[2])  8 us
    ppermute x8, starting transfers between devices, travel(): lax.ppermute(piece, axis, swap)  6.93 us
    ppermute x2, starting transfers between devices, by_pairs(): lax.ppermute(cross, 'ka', swaps[3])  6.18 us
    ppermute x5, starting transfers between devices, by_pairs(): lax.ppermute(piece, 'pb', swaps[d])  4.64 us
    ppermute x5, waiting for transfers between devices, by_pairs(): lax.ppermute(piece, 'pb', swaps[d])  3.38 us
    ppermute x8, waiting for transfers between devices, travel(): lax.ppermute(piece, axis, swap)  3.25 us
    ppermute x2, starting transfers between devices, by_pairs(): lax.ppermute(beside, 'ka', swaps[1])  1.78 us
  transfers between devices with their start and end apart: 19, of which 7 were waited for; matrix products, arithmetic and copies ran while one was open for 0% of the time, Pallas kernels for 23%

profile of v6, /device:TPU:0, one launch (start us, length us, event | category | flops | bytes accessed | tf_op | source)
XLA Modules:
  0.0 48.4 jit_solution(16662876544629969468)
XLA Ops:
  0.0 1.6 %pack.1 = (bf16[2,512,128]{2,1,0:T(8,128)(2,1)S(1)}, bf16[2,512,128]{2,1,0:T(8,128)(2,1)S(1)}, bf16[1024,128]{1,0:T(8,128)(2,1)S(1)}, bf16[256,128]{1,0:T(8,128)...) custom-call(bf16[512,2048]{1,0:T(8,128)(2,1)} %queries.9, ...), custom_call_target="tpu_custom_call" | custom-call | tf_op jit(solution)/shard_map/pack/pallas_call | solution.py:162
  1.7 0.5 %collective-permute-start = (bf16[1024,128]{1,0:T(8,128)(2,1)S(1)}, bf16[1024,128]{1,0:T(8,128)(2,1)S(1)}, u32[]{:S(2)}, u32[]{:S(2)}) collective-permute-start(bf16[1024,128]{1,0:T(8,128)(2,1)S(1)} %get-tuple-element.28), channel_id=1, source_target_pairs={{0,4},{4,0},{8,12},{12,8},{1,5},{5,1},{9,13},{13,9},{2,6},{6,2},{1... | collective-permute-start | bytes 786440 | tf_op jit(solution)/shard_map/ppermute | solution.py:377
  2.2 2.6 %collective-permute-start.3 = (bf16[2,512,128]{2,1,0:T(8,128)(2,1)S(1)}, bf16[2,512,128]{2,1,0:T(8,128)(2,1)S(1)}, u32[]{:S(2)}, u32[]{:S(2)}) collective-permute-start(bf16[2,512,128]{2,1,0:T(8,128)(2,1)S(1)} %get-tuple-element.31), channel_id=1, source_target_pairs={{0,1},{1,0},{2,3},{3,2},{4,5},{5,4},{6,7},{7,6},{8,9},{9,8},{10,11... | collective-permute-start | bytes 786440 | tf_op jit(solution)/shard_map/ppermute | solution.py:371
  4.8 1.5 %collective-permute-start.1 = (bf16[256,128]{1,0:T(8,128)(2,1)S(1)}, bf16[256,128]{1,0:T(8,128)(2,1)S(1)}, u32[]{:S(2)}, u32[]{:S(2)}) collective-permute-start(bf16[256,128]{1,0:T(8,128)(2,1)S(1)} %get-tuple-element.29), channel_id=1, source_target_pairs={{0,8},{4,12},{8,0},{12,4},{1,9},{5,13},{9,1},{13,5},{2,10},{6,14},... | collective-permute-start | bytes 196616 | tf_op jit(solution)/shard_map/ppermute | solution.py:377
  6.3 0.0 collective-permute-start.2
  6.4 0.4 collective-permute-start.12
  6.8 2.3 %collective-permute-done.1.refs_1_ = bf16[256,128]{1,0:T(8,128)(2,1)S(1)} collective-permute-done((bf16[256,128]{1,0:T(8,128)(2,1)S(1)}, bf16[256,128]{1,0:T(8,128)(2,1)S(1)}, u32[]{:S(2)}, u32[]{:S(2)}) %collective-permute-start.1) | collective-permute-done | bytes 65568 | tf_op jit(solution)/shard_map/ppermute | solution.py:377
  9.1 2.2 %collective-permute-start.4 = (bf16[768,128]{1,0:T(8,128)(2,1)S(1)}, bf16[768,128]{1,0:T(8,128)(2,1)S(1)}, u32[]{:S(2)}, u32[]{:S(2)}) collective-permute-start(bf16[768,128]{1,0:T(8,128)(2,1)S(1)} %get-tuple-element.33), channel_id=1, source_target_pairs={{0,8},{4,12},{8,0},{12,4},{1,9},{5,13},{9,1},{13,5},{2,10},{6,14},... | collective-permute-start | bytes 589832 | tf_op jit(solution)/shard_map/ppermute | solution.py:377
  11.3 0.0 collective-permute-done.2.refs_2_
  11.3 0.4 collective-permute-start.5
  11.7 0.0 collective-permute-done.refs_0_.refs_1_
  11.7 0.3 collective-permute-done.3.refs_3_.refs_4_
  12.0 2.0 %attend_far.2 = (bf16[528,128]{1,0:T(8,128)(2,1)S(1)}, bf16[528,128]{1,0:T(8,128)(2,1)S(1)}) custom-call(s32[16,128]{1,0:T(8,128)S(1)} %bitcast.1, bf16[512,2048]{1,0:T(8,128)(2,1)S(1)} %copy-done, bf16[512,512]{1,0:T(8,128)(2,1)S(1)} %copy-done.1, bf16[512,512]{1,0:T(8,128)(2,1)S(1)} %copy-done.2, ...), custom_call_target="tpu_custom_call" | custom-call | flops 1024 | bytes 1024 | tf_op jit(solution)/shard_map/attend_far/pallas_call | solution.py:252
  14.0 3.5 %collective-permute-start.8 = (bf16[528,128]{1,0:T(8,128)(2,1)S(1)}, bf16[528,128]{1,0:T(8,128)(2,1)S(1)}, u32[]{:S(2)}, u32[]{:S(2)}) collective-permute-start(bf16[528,128]{1,0:T(8,128)(2,1)S(1)} %get-tuple-element.37), channel_id=1, source_target_pairs={{0,3},{1,2},{2,1},{3,0},{4,7},{5,6},{6,5},{7,4},{8,11},{9,10},{10,... | collective-permute-start | bytes 405512 | tf_op jit(solution)/shard_map/ppermute | solution.py:384
  17.5 0.0 collective-permute-start.7
  17.5 0.0 collective-permute-done.4.refs_2_
  17.5 1.0 %collective-permute-done.5.refs_3_ = bf16[768,128]{1,0:T(8,128)(2,1)S(1)} collective-permute-done((bf16[768,128]{1,0:T(8,128)(2,1)S(1)}, bf16[768,128]{1,0:T(8,128)(2,1)S(1)}, u32[]{:S(2)}, u32[]{:S(2)}) %collective-permute-start.5) | collective-permute-done | bytes 196640 | tf_op jit(solution)/shard_map/ppermute | solution.py:377
  18.5 2.1 %attend_near.2 = (bf16[528,128]{1,0:T(8,128)(2,1)S(1)}, bf16[528,128]{1,0:T(8,128)(2,1)S(1)}) custom-call(s32[16,128]{1,0:T(8,128)S(1)} %bitcast.2, bf16[512,2048]{1,0:T(8,128)(2,1)S(1)} %copy-done, bf16[512,512]{1,0:T(8,128)(2,1)S(1)} %copy-done.1, bf16[512,512]{1,0:T(8,128)(2,1)S(1)} %copy-done.2, bf16[528,128]{1,0:T(8,128)(2,1)S(1)} %get-tuple-element.32.refs_0_, ...), custom_call_target="tpu_custom_call" | custom-call | flops 1024 | bytes 1024 | tf_op jit(solution)/shard_map/attend_near/pallas_call | solution.py:252
  20.7 0.4 collective-permute-start.6
  21.1 0.0 collective-permute-done.12.refs_4_
  21.1 2.0 %attend_far.3 = (bf16[528,128]{1,0:T(8,128)(2,1)S(1)}, bf16[528,128]{1,0:T(8,128)(2,1)S(1)}) custom-call(s32[16,128]{1,0:T(8,128)S(1)} %bitcast.3, bf16[512,2048]{1,0:T(8,128)(2,1)S(1)} %copy-done, bf16[512,512]{1,0:T(8,128)(2,1)S(1)} %copy-done.1, bf16[512,512]{1,0:T(8,128)(2,1)S(1)} %copy-done.2, bf16[528,128]{1,0:T(8,128)(2,1)S(1)} %get-tuple-element.35.refs_0_, ...), custom_call_target="tpu_custom_call" | custom-call | flops 1024 | bytes 1024 | tf_op jit(solution)/shard_map/attend_far/pallas_call | solution.py:252
  23.1 2.7 %collective-permute-start.15 = (bf16[528,128]{1,0:T(8,128)(2,1)S(1)}, bf16[528,128]{1,0:T(8,128)(2,1)S(1)}, u32[]{:S(2)}, u32[]{:S(2)}) collective-permute-start(bf16[528,128]{1,0:T(8,128)(2,1)S(1)} %get-tuple-element.46), channel_id=1, source_target_pairs={{0,3},{1,2},{2,1},{3,0},{4,7},{5,6},{6,5},{7,4},{8,11},{9,10},{10,... | collective-permute-start | bytes 405512 | tf_op jit(solution)/shard_map/ppermute | solution.py:384
  25.8 0.5 collective-permute-start.14
  26.2 2.0 %attend_near.3 = (bf16[528,128]{1,0:T(8,128)(2,1)S(1)}, bf16[528,128]{1,0:T(8,128)(2,1)S(1)}) custom-call(s32[16,128]{1,0:T(8,128)S(1)} %bitcast.4, bf16[512,2048]{1,0:T(8,128)(2,1)S(1)} %copy-done, bf16[512,512]{1,0:T(8,128)(2,1)S(1)} %copy-done.1, bf16[512,512]{1,0:T(8,128)(2,1)S(1)} %copy-done.2, bf16[528,128]{1,0:T(8,128)(2,1)S(1)} %get-tuple-element.43.refs_0_, ...), custom_call_target="tpu_custom_call" | custom-call | flops 1024 | bytes 1024 | tf_op jit(solution)/shard_map/attend_near/pallas_call | solution.py:252
  28.2 0.0 collective-permute-done.8.b
  28.2 1.3 %collective-permute-start.13 = (bf16[528,128]{1,0:T(8,128)(2,1)S(1)}, bf16[528,128]{1,0:T(8,128)(2,1)S(1)}, u32[]{:S(2)}, u32[]{:S(2)}) collective-permute-start(bf16[528,128]{1,0:T(8,128)(2,1)S(1)} %get-tuple-element.45), channel_id=1, source_target_pairs={{0,1},{1,0},{2,3},{3,2},{4,5},{5,4},{6,7},{7,6},{8,9},{9,8},{10,11... | collective-permute-start | bytes 405512 | tf_op jit(solution)/shard_map/ppermute | solution.py:388
  29.5 6.4 %collective-permute-done.7.a = bf16[528,128]{1,0:T(8,128)(2,1)S(1)} collective-permute-done((bf16[528,128]{1,0:T(8,128)(2,1)S(1)}, bf16[528,128]{1,0:T(8,128)(2,1)S(1)}, u32[]{:S(2)}, u32[]{:S(2)}) %collective-permute-start.7) | collective-permute-done | bytes 135200 | tf_op jit(solution)/shard_map/ppermute | solution.py:384
  35.9 0.3 collect.2.refs_2_
  36.3 0.0 collective-permute-done.6.refs_1_
  36.3 0.9 %merge.2 = (bf16[2,128,128]{2,1,0:T(8,128)(2,1)S(1)}, bf16[2,128,128]{2,1,0:T(8,128)(2,1)S(1)}, bf16[2,128,128]{2,1,0:T(8,128)(2,1)S(1)}, bf16[2,128,128]{2,1,0:T(8,128)(2,1)S(1)}) custom-call(bf16[528,128]{1,0:T(8,128)(2,1)S(1)} %get-tuple-element.35.refs_0_, bf16[528,128]{1,0:T(8,128)(2,1)S(1)} %collective-permute-done.6.refs_1_, ...), custom_call_target="tpu_custom_call" | custom-call | flops 1024 | bytes 1024 | tf_op jit(solution)/shard_map/merge/pallas_call | solution.py:328
  37.2 0.1 collective-permute-start.9
  37.3 1.5 %collective-permute-start.10 = (bf16[2,128,128]{2,1,0:T(8,128)(2,1)S(1)}, bf16[2,128,128]{2,1,0:T(8,128)(2,1)S(1)}, u32[]{:S(2)}, u32[]{:S(2)}) collective-permute-start(bf16[2,128,128]{2,1,0:T(8,128)(2,1)S(1)} %get-tuple-element.40), channel_id=1, source_target_pairs={{0,8},{4,12},{8,0},{12,4},{1,9},{5,13},{9,1},{13,5},{2,10},{6,14},... | collective-permute-start | bytes 196616 | tf_op jit(solution)/shard_map/ppermute | solution.py:371
  38.8 0.0 collective-permute-done.15.b
  38.8 0.4 collective-permute-start.11
  39.1 1.6 %collective-permute-done.14.a = bf16[528,128]{1,0:T(8,128)(2,1)S(1)} collective-permute-done((bf16[528,128]{1,0:T(8,128)(2,1)S(1)}, bf16[528,128]{1,0:T(8,128)(2,1)S(1)}, u32[]{:S(2)}, u32[]{:S(2)}) %collective-permute-start.14) | collective-permute-done | bytes 135200 | tf_op jit(solution)/shard_map/ppermute | solution.py:384
  40.8 0.3 collect.3.refs_3_
  41.1 0.0 collective-permute-done.13.refs_2_
  41.1 0.7 %merge.3 = (bf16[2,128,128]{2,1,0:T(8,128)(2,1)S(1)}, bf16[2,128,128]{2,1,0:T(8,128)(2,1)S(1)}, bf16[2,128,128]{2,1,0:T(8,128)(2,1)S(1)}, bf16[2,128,128]{2,1,0:T(8,128)(2,1)S(1)}) custom-call(bf16[2,128,128]{2,1,0:T(8,128)(2,1)S(1)} %get-tuple-element.38.refs_0_, bf16[528,128]{1,0:T(8,128)(2,1)S(1)} %get-tuple-element.44.refs_1_, ...), custom_call_target="tpu_custom_call" | custom-call | flops 1024 | bytes 1024 | tf_op jit(solution)/shard_map/merge/pallas_call | solution.py:328
  41.8 0.1 collective-permute-start.16
  41.9 1.5 %collective-permute-start.17 = (bf16[2,128,128]{2,1,0:T(8,128)(2,1)S(1)}, bf16[2,128,128]{2,1,0:T(8,128)(2,1)S(1)}, u32[]{:S(2)}, u32[]{:S(2)}) collective-permute-start(bf16[2,128,128]{2,1,0:T(8,128)(2,1)S(1)} %get-tuple-element.49), channel_id=1, source_target_pairs={{0,8},{4,12},{8,0},{12,4},{1,9},{5,13},{9,1},{13,5},{2,10},{6,14},... | collective-permute-start | bytes 196616 | tf_op jit(solution)/shard_map/ppermute | solution.py:371
  43.4 0.0 collective-permute-done.9.refs_1_
  43.4 0.4 collective-permute-start.18
  43.8 0.0 collective-permute-done.10.refs_2_
  43.8 0.8 %assemble.2.refs_0_ = bf16[128,2048]{1,0:T(8,128)(2,1)} custom-call(bf16[2,128,128]{2,1,0:T(8,128)(2,1)S(1)} %get-tuple-element.38.refs_0_, bf16[2,128,128]{2,1,0:T(8,128)(2,1)S(1)} %collective-permute-done.9.refs_1_, bf16[2,128,128]{2,1,0:T(8,128)(2,1)S(1)} %collective-permute-done.10.refs_2_, bf16[2,128,128]{2,1,0:T(8,128)(2,1)S(1)} %collective-permute-done.11.refs_3_), custom_call_target="tpu_custom_call" | custom-call | flops 1073741824 | bytes 33554432 | tf_op jit(solution)/shard_map/assemble/pallas_call | solution.py:353
  44.5 0.0 collective-permute-done.16.refs_2_
  44.5 1.9 %collective-permute-done.17.refs_3_ = bf16[2,128,128]{2,1,0:T(8,128)(2,1)S(1)} collective-permute-done((bf16[2,128,128]{2,1,0:T(8,128)(2,1)S(1)}, bf16[2,128,128]{2,1,0:T(8,128)(2,1)S(1)}, u32[]{:S(2)}, u32[]{:S(2)}) %collective-permute-start.17) | collective-permute-done | bytes 65568 | tf_op jit(solution)/shard_map/ppermute | solution.py:371
  46.4 1.0 %collective-permute-done.18.refs_4_ = bf16[2,128,128]{2,1,0:T(8,128)(2,1)S(1)} collective-permute-done((bf16[2,128,128]{2,1,0:T(8,128)(2,1)S(1)}, bf16[2,128,128]{2,1,0:T(8,128)(2,1)S(1)}, u32[]{:S(2)}, u32[]{:S(2)}) %collective-permute-start.18) | collective-permute-done | bytes 65568 | tf_op jit(solution)/shard_map/ppermute | solution.py:371
  47.5 0.8 %assemble.3 = bf16[128,2048]{1,0:T(8,128)(2,1)} custom-call(bf16[128,2048]{1,0:T(8,128)(2,1)} %assemble.2.refs_0_, bf16[2,128,128]{2,1,0:T(8,128)(2,1)S(1)} %get-tuple-element.47.refs_1_, bf16[2,128,128]{2,1,0:T(8,128)(2,1)S(1)} %collective-permute-done.16.refs_2_, ...), custom_call_target="tpu_custom_call", output_to_operand_aliasing={{}: (0, {})} | custom-call | flops 1073741824 | bytes 33554432 | tf_op jit(solution)/shard_map/assemble/pallas_call | solution.py:353
  (9 shorter events, 0.0 us)
Async XLA Ops:
  0.0 12.0 %copy-start.2 = (bf16[512,512]{1,0:T(8,128)(2,1)S(1)}, bf16[512,512]{1,0:T(8,128)(2,1)}, u32[]{:S(2)}) copy-start(bf16[512,512]{1,0:T(8,128)(2,1)} %values.9) | copy-start | bytes 1572868
  0.0 12.0 %copy-start.1 = (bf16[512,512]{1,0:T(8,128)(2,1)S(1)}, bf16[512,512]{1,0:T(8,128)(2,1)}, u32[]{:S(2)}) copy-start(bf16[512,512]{1,0:T(8,128)(2,1)} %keys.9) | copy-start | bytes 1572868
  0.0 12.0 %copy-start = (bf16[512,2048]{1,0:T(8,128)(2,1)S(1)}, bf16[512,2048]{1,0:T(8,128)(2,1)}, u32[]{:S(2)}) copy-start(bf16[512,2048]{1,0:T(8,128)(2,1)} %queries.9) | copy-start | bytes 6291460
  0.0 12.0 %copy-start.3 = (s32[2048]{0:T(1024)S(1)}, s32[2048]{0:T(1024)}, u32[]{:S(2)}) copy-start(s32[2048]{0:T(1024)} %param.7) | copy-start | bytes 24580
  1.7 10.0 %collective-permute-start = (bf16[1024,128]{1,0:T(8,128)(2,1)S(1)}, bf16[1024,128]{1,0:T(8,128)(2,1)S(1)}, u32[]{:S(2)}, u32[]{:S(2)}) collective-permute-start(bf16[1024,128]{1,0:T(8,128)(2,1)S(1)} %get-tuple-element.28), channel_id=1, source_target_pairs={{0,4},{4,0},{8,12},{12,8},{1,5},{5,1},{9,13},{13,9},{2,6},{6,2},{1... | collective-permute-start | bytes 786440 | tf_op jit(solution)/shard_map/ppermute | solution.py:377
  2.2 9.8 %collective-permute-start.3 = (bf16[2,512,128]{2,1,0:T(8,128)(2,1)S(1)}, bf16[2,512,128]{2,1,0:T(8,128)(2,1)S(1)}, u32[]{:S(2)}, u32[]{:S(2)}) collective-permute-start(bf16[2,512,128]{2,1,0:T(8,128)(2,1)S(1)} %get-tuple-element.31), channel_id=1, source_target_pairs={{0,1},{1,0},{2,3},{3,2},{4,5},{5,4},{6,7},{7,6},{8,9},{9,8},{10,11... | collective-permute-start | bytes 786440 | tf_op jit(solution)/shard_map/ppermute | solution.py:371
  4.8 4.3 %collective-permute-start.1 = (bf16[256,128]{1,0:T(8,128)(2,1)S(1)}, bf16[256,128]{1,0:T(8,128)(2,1)S(1)}, u32[]{:S(2)}, u32[]{:S(2)}) collective-permute-start(bf16[256,128]{1,0:T(8,128)(2,1)S(1)} %get-tuple-element.29), channel_id=1, source_target_pairs={{0,8},{4,12},{8,0},{12,4},{1,9},{5,13},{9,1},{13,5},{2,10},{6,14},... | collective-permute-start | bytes 196616 | tf_op jit(solution)/shard_map/ppermute | solution.py:377
  6.3 4.9 %collective-permute-start.2 = (bf16[256,128]{1,0:T(8,128)(2,1)S(1)}, bf16[256,128]{1,0:T(8,128)(2,1)S(1)}, u32[]{:S(2)}, u32[]{:S(2)}) collective-permute-start(bf16[256,128]{1,0:T(8,128)(2,1)S(1)} %get-tuple-element.30), channel_id=1, source_target_pairs={{0,12},{4,8},{8,4},{12,0},{1,13},{5,9},{9,5},{13,1},{2,14},{6,10},... | collective-permute-start | bytes 196616 | tf_op jit(solution)/shard_map/ppermute | solution.py:377
  6.4 14.7 %collective-permute-start.12 = (bf16[2,512,128]{2,1,0:T(8,128)(2,1)S(1)}, bf16[2,512,128]{2,1,0:T(8,128)(2,1)S(1)}, u32[]{:S(2)}, u32[]{:S(2)}) collective-permute-start(bf16[2,512,128]{2,1,0:T(8,128)(2,1)S(1)} %get-tuple-element.42), channel_id=1, source_target_pairs={{0,1},{1,0},{2,3},{3,2},{4,5},{5,4},{6,7},{7,6},{8,9},{9,8},{10,11... | collective-permute-start | bytes 786440 | tf_op jit(solution)/shard_map/ppermute | solution.py:371
  9.1 8.4 %collective-permute-start.4 = (bf16[768,128]{1,0:T(8,128)(2,1)S(1)}, bf16[768,128]{1,0:T(8,128)(2,1)S(1)}, u32[]{:S(2)}, u32[]{:S(2)}) collective-permute-start(bf16[768,128]{1,0:T(8,128)(2,1)S(1)} %get-tuple-element.33), channel_id=1, source_target_pairs={{0,8},{4,12},{8,0},{12,4},{1,9},{5,13},{9,1},{13,5},{2,10},{6,14},... | collective-permute-start | bytes 589832 | tf_op jit(solution)/shard_map/ppermute | solution.py:377
  11.3 7.3 %collective-permute-start.5 = (bf16[768,128]{1,0:T(8,128)(2,1)S(1)}, bf16[768,128]{1,0:T(8,128)(2,1)S(1)}, u32[]{:S(2)}, u32[]{:S(2)}) collective-permute-start(bf16[768,128]{1,0:T(8,128)(2,1)S(1)} %get-tuple-element.34), channel_id=1, source_target_pairs={{0,12},{4,8},{8,4},{12,0},{1,13},{5,9},{9,5},{13,1},{2,14},{6,10},... | collective-permute-start | bytes 589832 | tf_op jit(solution)/shard_map/ppermute | solution.py:377
  14.0 14.2 %collective-permute-start.8 = (bf16[528,128]{1,0:T(8,128)(2,1)S(1)}, bf16[528,128]{1,0:T(8,128)(2,1)S(1)}, u32[]{:S(2)}, u32[]{:S(2)}) collective-permute-start(bf16[528,128]{1,0:T(8,128)(2,1)S(1)} %get-tuple-element.37), channel_id=1, source_target_pairs={{0,3},{1,2},{2,1},{3,0},{4,7},{5,6},{6,5},{7,4},{8,11},{9,10},{10,... | collective-permute-start | bytes 405512 | tf_op jit(solution)/shard_map/ppermute | solution.py:384
  17.5 18.4 %collective-permute-start.7 = (bf16[528,128]{1,0:T(8,128)(2,1)S(1)}, bf16[528,128]{1,0:T(8,128)(2,1)S(1)}, u32[]{:S(2)}, u32[]{:S(2)}) collective-permute-start(bf16[528,128]{1,0:T(8,128)(2,1)S(1)} %get-tuple-element.32.refs_0_), channel_id=1, source_target_pairs={{0,2},{1,3},{2,0},{3,1},{4,6},{5,7},{6,4},{7,5},{8,10},{9,11},{10,... | collective-permute-start | bytes 405512 | tf_op jit(solution)/shard_map/ppermute | solution.py:384
  20.7 15.6 %collective-permute-start.6 = (bf16[528,128]{1,0:T(8,128)(2,1)S(1)}, bf16[528,128]{1,0:T(8,128)(2,1)S(1)}, u32[]{:S(2)}, u32[]{:S(2)}) collective-permute-start(bf16[528,128]{1,0:T(8,128)(2,1)S(1)} %get-tuple-element.36), channel_id=1, source_target_pairs={{0,1},{1,0},{2,3},{3,2},{4,5},{5,4},{6,7},{7,6},{8,9},{9,8},{10,11... | collective-permute-start | bytes 405512 | tf_op jit(solution)/shard_map/ppermute | solution.py:388
  23.1 15.7 %collective-permute-start.15 = (bf16[528,128]{1,0:T(8,128)(2,1)S(1)}, bf16[528,128]{1,0:T(8,128)(2,1)S(1)}, u32[]{:S(2)}, u32[]{:S(2)}) collective-permute-start(bf16[528,128]{1,0:T(8,128)(2,1)S(1)} %get-tuple-element.46), channel_id=1, source_target_pairs={{0,3},{1,2},{2,1},{3,0},{4,7},{5,6},{6,5},{7,4},{8,11},{9,10},{10,... | collective-permute-start | bytes 405512 | tf_op jit(solution)/shard_map/ppermute | solution.py:384
  25.8 15.0 %collective-permute-start.14 = (bf16[528,128]{1,0:T(8,128)(2,1)S(1)}, bf16[528,128]{1,0:T(8,128)(2,1)S(1)}, u32[]{:S(2)}, u32[]{:S(2)}) collective-permute-start(bf16[528,128]{1,0:T(8,128)(2,1)S(1)} %get-tuple-element.43.refs_0_), channel_id=1, source_target_pairs={{0,2},{1,3},{2,0},{3,1},{4,6},{5,7},{6,4},{7,5},{8,10},{9,11},{10,... | collective-permute-start | bytes 405512 | tf_op jit(solution)/shard_map/ppermute | solution.py:384
  28.2 12.9 %collective-permute-start.13 = (bf16[528,128]{1,0:T(8,128)(2,1)S(1)}, bf16[528,128]{1,0:T(8,128)(2,1)S(1)}, u32[]{:S(2)}, u32[]{:S(2)}) collective-permute-start(bf16[528,128]{1,0:T(8,128)(2,1)S(1)} %get-tuple-element.45), channel_id=1, source_target_pairs={{0,1},{1,0},{2,3},{3,2},{4,5},{5,4},{6,7},{7,6},{8,9},{9,8},{10,11... | collective-permute-start | bytes 405512 | tf_op jit(solution)/shard_map/ppermute | solution.py:388
  37.2 6.2 %collective-permute-start.9 = (bf16[2,128,128]{2,1,0:T(8,128)(2,1)S(1)}, bf16[2,128,128]{2,1,0:T(8,128)(2,1)S(1)}, u32[]{:S(2)}, u32[]{:S(2)}) collective-permute-start(bf16[2,128,128]{2,1,0:T(8,128)(2,1)S(1)} %get-tuple-element.39), channel_id=1, source_target_pairs={{0,4},{4,0},{8,12},{12,8},{1,5},{5,1},{9,13},{13,9},{2,6},{6,2},{1... | collective-permute-start | bytes 196616 | tf_op jit(solution)/shard_map/ppermute | solution.py:371
  37.3 6.5 %collective-permute-start.10 = (bf16[2,128,128]{2,1,0:T(8,128)(2,1)S(1)}, bf16[2,128,128]{2,1,0:T(8,128)(2,1)S(1)}, u32[]{:S(2)}, u32[]{:S(2)}) collective-permute-start(bf16[2,128,128]{2,1,0:T(8,128)(2,1)S(1)} %get-tuple-element.40), channel_id=1, source_target_pairs={{0,8},{4,12},{8,0},{12,4},{1,9},{5,13},{9,1},{13,5},{2,10},{6,14},... | collective-permute-start | bytes 196616 | tf_op jit(solution)/shard_map/ppermute | solution.py:371
  38.8 5.0 %collective-permute-start.11 = (bf16[2,128,128]{2,1,0:T(8,128)(2,1)S(1)}, bf16[2,128,128]{2,1,0:T(8,128)(2,1)S(1)}, u32[]{:S(2)}, u32[]{:S(2)}) collective-permute-start(bf16[2,128,128]{2,1,0:T(8,128)(2,1)S(1)} %get-tuple-element.41), channel_id=1, source_target_pairs={{0,12},{4,8},{8,4},{12,0},{1,13},{5,9},{9,5},{13,1},{2,14},{6,10},... | collective-permute-start | bytes 196616 | tf_op jit(solution)/shard_map/ppermute | solution.py:371
  41.8 2.7 %collective-permute-start.16 = (bf16[2,128,128]{2,1,0:T(8,128)(2,1)S(1)}, bf16[2,128,128]{2,1,0:T(8,128)(2,1)S(1)}, u32[]{:S(2)}, u32[]{:S(2)}) collective-permute-start(bf16[2,128,128]{2,1,0:T(8,128)(2,1)S(1)} %get-tuple-element.48), channel_id=1, source_target_pairs={{0,4},{4,0},{8,12},{12,8},{1,5},{5,1},{9,13},{13,9},{2,6},{6,2},{1... | collective-permute-start | bytes 196616 | tf_op jit(solution)/shard_map/ppermute | solution.py:371
  41.9 4.5 %collective-permute-start.17 = (bf16[2,128,128]{2,1,0:T(8,128)(2,1)S(1)}, bf16[2,128,128]{2,1,0:T(8,128)(2,1)S(1)}, u32[]{:S(2)}, u32[]{:S(2)}) collective-permute-start(bf16[2,128,128]{2,1,0:T(8,128)(2,1)S(1)} %get-tuple-element.49), channel_id=1, source_target_pairs={{0,8},{4,12},{8,0},{12,4},{1,9},{5,13},{9,1},{13,5},{2,10},{6,14},... | collective-permute-start | bytes 196616 | tf_op jit(solution)/shard_map/ppermute | solution.py:371
  43.4 4.1 %collective-permute-start.18 = (bf16[2,128,128]{2,1,0:T(8,128)(2,1)S(1)}, bf16[2,128,128]{2,1,0:T(8,128)(2,1)S(1)}, u32[]{:S(2)}, u32[]{:S(2)}) collective-permute-start(bf16[2,128,128]{2,1,0:T(8,128)(2,1)S(1)} %get-tuple-element.50), channel_id=1, source_target_pairs={{0,12},{4,8},{8,4},{12,0},{1,13},{5,9},{9,5},{13,1},{2,14},{6,10},... | collective-permute-start | bytes 196616 | tf_op jit(solution)/shard_map/ppermute | solution.py:371

commit v7 on v6

--- a/solution.py
+++ b/solution.py
@@ -170,28 +170,29 @@
     )(queries, keys, values, *after)
 
 
-def attend_kernel(chunk, far, skips, waits, scale, steps_ref, queries, keys, values, *refs):
-    *moved, got, same, cross, q_buf, k_buf, v_buf = refs[waits:]
+def attend_kernel(chunk, fars, skips, waits, scale, steps_ref, queries, keys, values, *refs):
+    moved, got, results, (q_buf, k_buf, v_buf) = refs[waits:waits + 3], refs[waits + 3], refs[waits + 4:-3], refs[-3:]
     column = lax.axis_index("pb")
     z = lax.axis_index("ka")
-    half_rows = q_buf.shape[1]
+    half_rows = q_buf.shape[2]
     sub = half_rows // 2
     held = keys.shape[0]
     pair = 2 * held
 
     def sort_queries(mine):
         for d, skip, q in zip((1, 2, 3), skips, moved):
-            q_buf[mine ^ d] = q[skip * half_rows:(skip + 1) * half_rows, :]
+            for i in range(len(fars)):
+                q_buf[i, mine ^ d] = q[(skip + i) * half_rows:(skip + i + 1) * half_rows, :]
 
     def work(which):
         upper, half = which // 2, which % 2
-        start = half_rows if far == (upper == 0) else 0
         base = upper * pair
-        outs = (same, cross) if half == 0 else (cross, same)
+        starts = [half_rows if far == (upper == 0) else 0 for far in fars]
 
         def own_queries(mine):
             at = (mine * 4 + half * 2 + chunk) * HEAD_DIM
-            q_buf[mine] = queries[start:start + half_rows, at:at + HEAD_DIM]
+            for i, start in enumerate(starts):
+                q_buf[i, mine] = queries[start:start + half_rows, at:at + HEAD_DIM]
 
         for mine in range(4):
             pl.when(column == mine)(functools.partial(own_queries, mine))
@@ -203,8 +204,8 @@
         steps = steps_ref[...].astype(jnp.float32)
         columns = jnp.transpose(steps)
 
-        def tile(slot, first_row, limit, masked_from, stats, first=0, size=half_rows):
-            q = q_buf[(slot + 2 * upper) % 4, first:first + size, :]
+        def tile(i, slot, first_row, limit, masked_from, stats, first=0, size=half_rows):
+            q = q_buf[i, (slot + 2 * upper) % 4, first:first + size, :]
             scores = lax.dot_general(q, k_buf[:limit, :], (((1,), (1,)), ((), ())), preferred_element_type=jnp.float32)
             if masked_from < limit:
                 at = (first_row + first) // LANES
@@ -220,25 +221,26 @@
             total = mixed[:, HEAD_DIM:]
             result = (mixed[:, :HEAD_DIM] / total).astype(jnp.bfloat16)
             for j in range(0, size, sub):
-                outs[(first + j) // sub][slot * sub:(slot + 1) * sub, :] = result[j:j + sub]
+                results[2 * i + ((first + j) // sub ^ half)][slot * sub:(slot + 1) * sub, :] = result[j:j + sub]
             high = total.astype(jnp.bfloat16).astype(jnp.float32)
             lane = lax.broadcasted_iota(jnp.int32, (size, LANES), 1)
             stats = jnp.where(lane == 3 * slot, top, stats)
             stats = jnp.where(lane == 3 * slot + 1, high, stats)
             return jnp.where(lane == 3 * slot + 2, total - high, stats)
 
-        reach = start + half_rows + LANES
-        stats = jnp.zeros((half_rows, LANES), jnp.float32)
-        stats = tile(0, base + start, reach, start, stats)
-        stats = tile(1, base + held + start, min(held + reach, pair), held + start, stats)
-        if upper == 0:
-            stats = tile(2, 0, pair, pair, stats)
-            stats = tile(3, 0, pair, pair, stats)
-        stats = [stats[:sub], stats[sub:]]
-        if upper == 1 and not far:
-            stats[1] = tile(3, held + start, LANES, 0, stats[1], sub, sub)
-        for out, of in zip(outs, stats):
-            out[4 * sub:, :] = jnp.transpose(of)[:STATS].astype(jnp.bfloat16)
+        for i, (far, start) in enumerate(zip(fars, starts)):
+            reach = start + half_rows + LANES
+            stats = jnp.zeros((half_rows, LANES), jnp.float32)
+            stats = tile(i, 0, base + start, reach, start, stats)
+            stats = tile(i, 1, base + held + start, min(held + reach, pair), held + start, stats)
+            if upper == 0:
+                stats = tile(i, 2, 0, pair, pair, stats)
+                stats = tile(i, 3, 0, pair, pair, stats)
+            stats = [stats[:sub], stats[sub:]]
+            if upper == 1 and not far:
+                stats[1] = tile(i, 3, held + start, LANES, 0, stats[1], sub, sub)
+            for j, of in enumerate(stats):
+                results[2 * i + (j ^ half)][4 * sub:, :] = jnp.transpose(of)[:STATS].astype(jnp.bfloat16)
 
     for which in range(4):
         pl.when(column == which)(functools.partial(sort_queries, which))
@@ -246,50 +248,46 @@
         pl.when(z == which)(functools.partial(work, which))
 
 
-def attend(chunk, far, skips, steps, queries, keys, values, moved, got, after=()):
+def attend(chunk, fars, skips, steps, queries, keys, values, moved, got, after=()):
     held = keys.shape[0]
     part = jax.ShapeDtypeStruct((held + STATS, LANES), jnp.bfloat16)
     return pl.pallas_call(
-        functools.partial(attend_kernel, chunk, far, skips, len(after), math.log2(math.e) / math.sqrt(HEAD_DIM)),
-        out_shape=[part] * 2,
+        functools.partial(attend_kernel, chunk, fars, skips, len(after), math.log2(math.e) / math.sqrt(HEAD_DIM)),
+        out_shape=[part] * (2 * len(fars)),
         in_specs=[VMEM] * 4 + [ANY] * len(after) + [VMEM] * 4,
-        out_specs=[VMEM] * 2,
+        out_specs=[VMEM] * (2 * len(fars)),
         scratch_shapes=[
-            pltpu.VMEM((4, held // 2, HEAD_DIM), jnp.bfloat16),
+            pltpu.VMEM((len(fars), 4, held // 2, HEAD_DIM), jnp.bfloat16),
             pltpu.VMEM((2 * held, HEAD_DIM), jnp.bfloat16),
             pltpu.VMEM((2 * held, 2 * HEAD_DIM), jnp.bfloat16),
         ],
         compiler_params=pltpu.CompilerParams(vmem_limit_bytes=24 << 20),
         cost_estimate=pl.CostEstimate(flops=1 << 10, bytes_accessed=1 << 10, transcendentals=0),
-        name="attend_far" if far else "attend_near",
+        name="attend_far" if fars == (True,) else "attend",
     )(steps, queries, keys, values, *after, *moved, *got)
 
 
-def collect_kernel(a, b, out, sem):
-    for copy in run_copies([(a, out.at[0]), (b, out.at[1])], sem):
-        copy.wait()
-
-
-def collect(a, b):
+def mark_kernel(a, b, out):
+    out[...] = jnp.zeros(out.shape, out.dtype)
+
+
+def mark(a, b):
     return pl.pallas_call(
-        collect_kernel,
-        out_shape=jax.ShapeDtypeStruct((2,) + a.shape, a.dtype),
+        mark_kernel,
+        out_shape=jax.ShapeDtypeStruct((8, LANES), jnp.float32),
         in_specs=[ANY] * 2,
-        out_specs=ANY,
-        scratch_shapes=[pltpu.SemaphoreType.DMA((2,))],
+        out_specs=VMEM,
         compiler_params=pltpu.CompilerParams(vmem_limit_bytes=4 << 20),
         cost_estimate=pl.CostEstimate(flops=1 << 30, bytes_accessed=32 << 20, transcendentals=0),
-        name="collect",
+        name="mark",
     )(a, b)
 
 
 def merge_kernel(waits, *refs):
-    own, from_1, far = refs[waits:waits + 3]
-    outs, result = refs[waits + 3:-1], refs[-1]
+    arrived, outs, result = refs[waits:-5], refs[-5:-1], refs[-1]
     column = lax.axis_index("pb")
     z = lax.axis_index("ka")
     sub = result.shape[2]
-    arrived = (own, from_1, far.at[0], far.at[1])
 
     def merge_at(which):
         held = [arrived[which ^ s] for s in range(4)]
@@ -376,16 +374,19 @@
     got = travel(packed[:1], "ka"), travel(packed[1:2], "ka")
     all_1, *others = [lax.ppermute(piece, "pb", swaps[d]) for piece, (d, _) in zip(packed[2:], batches)]
     first, rest = others[:2], others[2:]
-    parts = []
-    for i, (chunk, far) in enumerate(order):
-        after = [parts[-1][0]] if parts else []
-        arrived, skips = ([all_1, *first], (0, 0, 0)) if i == 0 else ([all_1, *rest], (i, i - 1, i - 1))
-        parts.append(attend(chunk, far, skips, steps, queries, keys, values, arrived, got[chunk], after))
-    far = [collect(lax.ppermute(same, "ka", swaps[2]), lax.ppermute(cross, "ka", swaps[3])) for same, cross in parts[::2]]
+    def work(chunk, fars, arrived, skips, after):
+        parts = attend(chunk, fars, skips, steps, queries, keys, values, arrived, got[chunk], after)
+        return [parts[i:i + 2] for i in range(0, len(parts), 2)]
+
+    parts = work(0, (True,), [all_1, *first], (0, 0, 0), [])
+    parts += work(0, (False,), [all_1, *rest], (1, 0, 0), [parts[-1][0]])
+    parts += work(1, (True, False), [all_1, *rest], (2, 1, 1), [parts[-1][0]])
+    far = [[lax.ppermute(same, "ka", swaps[2]), lax.ppermute(cross, "ka", swaps[3])] for same, cross in parts[::2]]
+    marks = [mark(*far[0])]
     result = ()
     blocks = ()
     for chunk, (own, beside) in enumerate(parts[1::2]):
-        blocks = merge([own, lax.ppermute(beside, "ka", swaps[1]), far[chunk]], blocks[:1])
+        blocks = merge([own, lax.ppermute(beside, "ka", swaps[1]), *far[chunk]], [*blocks[:1], *marks[chunk:chunk + 1]])
         result = (assemble(chunk, [blocks[0]] + travel(blocks[1:], "pb"), result),)
     return result[0]
 

time: 48.6 us -> 46.7 us (0.961)
  starting transfers between devices: 20 us -> 18.6 us
  Pallas kernels: 13.5 us -> 12.2 us
  waiting for transfers between devices: 14.6 us -> 15.4 us
    ppermute x2, waiting for transfers between devices: 0.01 us -> 4.28 us  [by_pairs(): lax.ppermute(beside, 'ka', swaps[1])]
    ppermute x2, waiting for transfers between devices: 8 us -> 4.58 us  [by_pairs(): lax.ppermute(same, 'ka', swaps[2])]
    ppermute x8, starting transfers between devices: 6.93 us -> 5.63 us  [travel(): lax.ppermute(piece, axis, swap)]
    pallas_call x6 -> x4, Pallas kernels: 8.7 us -> 7.44 us  [the longest x3 7.44 us: attend(): pl.pallas_call(functools.partial(attend_kernel, chunk, fars, skips, len(a...]
    ppermute x2, starting transfers between devices: 6.18 us -> 5.02 us  [by_pairs(): lax.ppermute(cross, 'ka', swaps[3])]
    ppermute x2, starting transfers between devices: 0.46 us -> 1.21 us  [by_pairs(): lax.ppermute(same, 'ka', swaps[2])]
  transfers between devices with their start and end apart: 19 -> 19, of which waited for: 7 -> 9; matrix products, arithmetic and copies ran while one was open for 0% -> 0% of each run, Pallas kernels for 23% -> 21%
where the time goes in v7:
time: 46.7 us; the launch traced here: 46.5 us
  starting transfers between devices  18.6 us (40%)
  waiting for transfers between devices  15.4 us (33%)
  Pallas kernels  12.2 us (26%)
    pallas_call x3, Pallas kernels, attend(): pl.pallas_call(functools.partial(attend_kernel, chunk, fars, skips, len(a...  7.44 us
    ppermute x8, starting transfers between devices, travel(): lax.ppermute(piece, axis, swap)  5.63 us
    ppermute x2, starting transfers between devices, by_pairs(): lax.ppermute(cross, 'ka', swaps[3])  5.02 us
    ppermute x5, starting transfers between devices, by_pairs(): lax.ppermute(piece, 'pb', swaps[d])  4.64 us
    ppermute x2, waiting for transfers between devices, by_pairs(): lax.ppermute(same, 'ka', swaps[2])  4.58 us
    ppermute x2, waiting for transfers between devices, by_pairs(): lax.ppermute(beside, 'ka', swaps[1])  4.28 us
    ppermute x5, waiting for transfers between devices, by_pairs(): lax.ppermute(piece, 'pb', swaps[d])  3.37 us
    ppermute x8, waiting for transfers between devices, travel(): lax.ppermute(piece, axis, swap)  3.13 us
  transfers between devices with their start and end apart: 19, of which 9 were waited for; matrix products, arithmetic and copies ran while one was open for 0% of the time, Pallas kernels for 21%

profile of v7, /device:TPU:0, one launch (start us, length us, event | category | flops | bytes accessed | tf_op | source)
XLA Modules:
  0.0 46.5 jit_solution(12815753516660463920)
XLA Ops:
  0.0 1.6 %pack.1 = (bf16[2,512,128]{2,1,0:T(8,128)(2,1)S(1)}, bf16[2,512,128]{2,1,0:T(8,128)(2,1)S(1)}, bf16[1024,128]{1,0:T(8,128)(2,1)S(1)}, bf16[256,128]{1,0:T(8,128)...) custom-call(bf16[512,2048]{1,0:T(8,128)(2,1)} %queries.7, ...), custom_call_target="tpu_custom_call" | custom-call | tf_op jit(solution)/shard_map/pack/pallas_call | solution.py:162
  1.7 0.5 %collective-permute-start = (bf16[1024,128]{1,0:T(8,128)(2,1)S(1)}, bf16[1024,128]{1,0:T(8,128)(2,1)S(1)}, u32[]{:S(2)}, u32[]{:S(2)}) collective-permute-start(bf16[1024,128]{1,0:T(8,128)(2,1)S(1)} %get-tuple-element.28), channel_id=1, source_target_pairs={{0,4},{4,0},{8,12},{12,8},{1,5},{5,1},{9,13},{13,9},{2,6},{6,2},{1... | collective-permute-start | bytes 786440 | tf_op jit(solution)/shard_map/ppermute | solution.py:375
  2.2 2.6 %collective-permute-start.3 = (bf16[2,512,128]{2,1,0:T(8,128)(2,1)S(1)}, bf16[2,512,128]{2,1,0:T(8,128)(2,1)S(1)}, u32[]{:S(2)}, u32[]{:S(2)}) collective-permute-start(bf16[2,512,128]{2,1,0:T(8,128)(2,1)S(1)} %get-tuple-element.31), channel_id=1, source_target_pairs={{0,1},{1,0},{2,3},{3,2},{4,5},{5,4},{6,7},{7,6},{8,9},{9,8},{10,11... | collective-permute-start | bytes 786440 | tf_op jit(solution)/shard_map/ppermute | solution.py:369
  4.8 1.5 %collective-permute-start.1 = (bf16[256,128]{1,0:T(8,128)(2,1)S(1)}, bf16[256,128]{1,0:T(8,128)(2,1)S(1)}, u32[]{:S(2)}, u32[]{:S(2)}) collective-permute-start(bf16[256,128]{1,0:T(8,128)(2,1)S(1)} %get-tuple-element.29), channel_id=1, source_target_pairs={{0,8},{4,12},{8,0},{12,4},{1,9},{5,13},{9,1},{13,5},{2,10},{6,14},... | collective-permute-start | bytes 196616 | tf_op jit(solution)/shard_map/ppermute | solution.py:375
  6.3 0.0 collective-permute-start.2
  6.4 0.4 collective-permute-start.12
  6.8 2.3 %collective-permute-done.1.refs_1_ = bf16[256,128]{1,0:T(8,128)(2,1)S(1)} collective-permute-done((bf16[256,128]{1,0:T(8,128)(2,1)S(1)}, bf16[256,128]{1,0:T(8,128)(2,1)S(1)}, u32[]{:S(2)}, u32[]{:S(2)}) %collective-permute-start.1) | collective-permute-done | bytes 65568 | tf_op jit(solution)/shard_map/ppermute | solution.py:375
  9.1 2.2 %collective-permute-start.6 = (bf16[768,128]{1,0:T(8,128)(2,1)S(1)}, bf16[768,128]{1,0:T(8,128)(2,1)S(1)}, u32[]{:S(2)}, u32[]{:S(2)}) collective-permute-start(bf16[768,128]{1,0:T(8,128)(2,1)S(1)} %get-tuple-element.34), channel_id=1, source_target_pairs={{0,8},{4,12},{8,0},{12,4},{1,9},{5,13},{9,1},{13,5},{2,10},{6,14},... | collective-permute-start | bytes 589832 | tf_op jit(solution)/shard_map/ppermute | solution.py:375
  11.3 0.0 collective-permute-done.2.refs_2_
  11.3 0.4 collective-permute-start.7
  11.7 0.0 collective-permute-done.refs_0_.refs_1_
  11.7 0.3 collective-permute-done.3.refs_3_.refs_4_
  12.0 0.0 copy-done.2
  12.0 0.0 copy-done.1
  12.0 2.0 %attend_far.1 = (bf16[528,128]{1,0:T(8,128)(2,1)S(1)}, bf16[528,128]{1,0:T(8,128)(2,1)S(1)}) custom-call(s32[16,128]{1,0:T(8,128)S(1)} %bitcast.1, bf16[512,2048]{1,0:T(8,128)(2,1)S(1)} %copy-done, bf16[512,512]{1,0:T(8,128)(2,1)S(1)} %copy-done.1, bf16[512,512]{1,0:T(8,128)(2,1)S(1)} %copy-done.2, ...), custom_call_target="tpu_custom_call" | custom-call | flops 1024 | bytes 1024 | tf_op jit(solution)/shard_map/attend_far/pallas_call | solution.py:254
  14.0 3.5 %collective-permute-start.5 = (bf16[528,128]{1,0:T(8,128)(2,1)S(1)}, bf16[528,128]{1,0:T(8,128)(2,1)S(1)}, u32[]{:S(2)}, u32[]{:S(2)}) collective-permute-start(bf16[528,128]{1,0:T(8,128)(2,1)S(1)} %get-tuple-element.33), channel_id=1, source_target_pairs={{0,3},{1,2},{2,1},{3,0},{4,7},{5,6},{6,5},{7,4},{8,11},{9,10},{10,... | collective-permute-start | bytes 405512 | tf_op jit(solution)/shard_map/ppermute | solution.py:384
  17.5 0.0 collective-permute-start.4
  17.5 0.0 collective-permute-done.6.refs_2_
  17.5 1.0 %collective-permute-done.7.refs_3_ = bf16[768,128]{1,0:T(8,128)(2,1)S(1)} collective-permute-done((bf16[768,128]{1,0:T(8,128)(2,1)S(1)}, bf16[768,128]{1,0:T(8,128)(2,1)S(1)}, u32[]{:S(2)}, u32[]{:S(2)}) %collective-permute-start.7) | collective-permute-done | bytes 196640 | tf_op jit(solution)/shard_map/ppermute | solution.py:375
  18.5 2.1 %attend.2 = (bf16[528,128]{1,0:T(8,128)(2,1)S(1)}, bf16[528,128]{1,0:T(8,128)(2,1)S(1)}) custom-call(s32[16,128]{1,0:T(8,128)S(1)} %bitcast.2, bf16[512,2048]{1,0:T(8,128)(2,1)S(1)} %copy-done, bf16[512,512]{1,0:T(8,128)(2,1)S(1)} %copy-done.1, bf16[512,512]{1,0:T(8,128)(2,1)S(1)} %copy-done.2, bf16[528,128]{1,0:T(8,128)(2,1)S(1)} %get-tuple-element.32.refs_0_, ...), custom_call_target="tpu_custom_call" | custom-call | flops 1024 | bytes 1024 | tf_op jit(solution)/shard_map/attend/pallas_call | solution.py:254
  20.7 0.4 collective-permute-start.8
  21.1 0.0 collective-permute-done.12.refs_4_
  21.1 3.3 %attend.3 = (bf16[528,128]{1,0:T(8,128)(2,1)S(1)}, bf16[528,128]{1,0:T(8,128)(2,1)S(1)}, bf16[528,128]{1,0:T(8,128)(2,1)S(1)}, bf16[528,128]{1,0:T(8,128)(2,1)S(1)}) custom-call(s32[16,128]{1,0:T(8,128)S(1)} %bitcast.3, bf16[512,2048]{1,0:T(8,128)(2,1)S(1)} %copy-done, bf16[512,512]{1,0:T(8,128)(2,1)S(1)} %copy-done.1, bf16[512,512]{1,0:T(8,128)(2,1)S(1)} %copy-done.2, ...), custom_call_target="tpu_custom_call" | custom-call | flops 1024 | bytes 1024 | tf_op jit(solution)/shard_map/attend/pallas_call | solution.py:254
  24.4 1.7 %collective-permute-start.13 = (bf16[528,128]{1,0:T(8,128)(2,1)S(1)}, bf16[528,128]{1,0:T(8,128)(2,1)S(1)}, u32[]{:S(2)}, u32[]{:S(2)}) collective-permute-start(bf16[528,128]{1,0:T(8,128)(2,1)S(1)} %get-tuple-element.44), channel_id=1, source_target_pairs={{0,1},{1,0},{2,3},{3,2},{4,5},{5,4},{6,7},{7,6},{8,9},{9,8},{10,11... | collective-permute-start | bytes 405512 | tf_op jit(solution)/shard_map/ppermute | solution.py:389
  26.1 1.2 %collective-permute-start.14 = (bf16[528,128]{1,0:T(8,128)(2,1)S(1)}, bf16[528,128]{1,0:T(8,128)(2,1)S(1)}, u32[]{:S(2)}, u32[]{:S(2)}) collective-permute-start(bf16[528,128]{1,0:T(8,128)(2,1)S(1)} %get-tuple-element.45), channel_id=1, source_target_pairs={{0,2},{1,3},{2,0},{3,1},{4,6},{5,7},{6,4},{7,5},{8,10},{9,11},{10,... | collective-permute-start | bytes 405512 | tf_op jit(solution)/shard_map/ppermute | solution.py:384
  27.3 0.0 collective-permute-done.5.b.refs_4_
  27.4 1.5 %collective-permute-start.15 = (bf16[528,128]{1,0:T(8,128)(2,1)S(1)}, bf16[528,128]{1,0:T(8,128)(2,1)S(1)}, u32[]{:S(2)}, u32[]{:S(2)}) collective-permute-start(bf16[528,128]{1,0:T(8,128)(2,1)S(1)} %get-tuple-element.46), channel_id=1, source_target_pairs={{0,3},{1,2},{2,1},{3,0},{4,7},{5,6},{6,5},{7,4},{8,11},{9,10},{10,... | collective-permute-start | bytes 405512 | tf_op jit(solution)/shard_map/ppermute | solution.py:384
  28.9 0.4 collective-permute-done.4.a.refs_3_
  29.2 2.7 %collective-permute-done.8.refs_2_ = bf16[528,128]{1,0:T(8,128)(2,1)S(1)} collective-permute-done((bf16[528,128]{1,0:T(8,128)(2,1)S(1)}, bf16[528,128]{1,0:T(8,128)(2,1)S(1)}, u32[]{:S(2)}, u32[]{:S(2)}) %collective-permute-start.8) | collective-permute-done | bytes 135200 | tf_op jit(solution)/shard_map/ppermute | solution.py:389
  31.9 0.9 %merge.2 = (bf16[2,128,128]{2,1,0:T(8,128)(2,1)S(1)}, bf16[2,128,128]{2,1,0:T(8,128)(2,1)S(1)}, bf16[2,128,128]{2,1,0:T(8,128)(2,1)S(1)}, bf16[2,128,128]{2,1,0:T(8,128)(2,1)S(1)}) custom-call(f32[8,128]{1,0:T(8,128)S(1)} %mark.1.refs_0_, bf16[528,128]{1,0:T(8,128)(2,1)S(1)} %get-tuple-element.36.refs_1_.refs_0_, ...), custom_call_target="tpu_custom_call" | custom-call | flops 1024 | bytes 1024 | tf_op jit(solution)/shard_map/merge/pallas_call | solution.py:326
  32.8 0.1 collective-permute-start.9
  32.9 0.1 collective-permute-start.10
  33.0 1.6 %collective-permute-done.13.refs_2_ = bf16[528,128]{1,0:T(8,128)(2,1)S(1)} collective-permute-done((bf16[528,128]{1,0:T(8,128)(2,1)S(1)}, bf16[528,128]{1,0:T(8,128)(2,1)S(1)}, u32[]{:S(2)}, u32[]{:S(2)}) %collective-permute-start.13) | collective-permute-done | bytes 135200 | tf_op jit(solution)/shard_map/ppermute | solution.py:389
  34.6 0.5 %collective-permute-start.11 = (bf16[2,128,128]{2,1,0:T(8,128)(2,1)S(1)}, bf16[2,128,128]{2,1,0:T(8,128)(2,1)S(1)}, u32[]{:S(2)}, u32[]{:S(2)}) collective-permute-start(bf16[2,128,128]{2,1,0:T(8,128)(2,1)S(1)} %get-tuple-element.41), channel_id=1, source_target_pairs={{0,12},{4,8},{8,4},{12,0},{1,13},{5,9},{9,5},{13,1},{2,14},{6,10},... | collective-permute-start | bytes 196616 | tf_op jit(solution)/shard_map/ppermute | solution.py:369
  35.1 4.2 %collective-permute-done.14.refs_3_ = bf16[528,128]{1,0:T(8,128)(2,1)S(1)} collective-permute-done((bf16[528,128]{1,0:T(8,128)(2,1)S(1)}, bf16[528,128]{1,0:T(8,128)(2,1)S(1)}, u32[]{:S(2)}, u32[]{:S(2)}) %collective-permute-start.14) | collective-permute-done | bytes 135200 | tf_op jit(solution)/shard_map/ppermute | solution.py:384
  39.3 0.0 collective-permute-done.15.refs_4_
  39.3 0.7 %merge.3 = (bf16[2,128,128]{2,1,0:T(8,128)(2,1)S(1)}, bf16[2,128,128]{2,1,0:T(8,128)(2,1)S(1)}, bf16[2,128,128]{2,1,0:T(8,128)(2,1)S(1)}, bf16[2,128,128]{2,1,0:T(8,128)(2,1)S(1)}) custom-call(bf16[2,128,128]{2,1,0:T(8,128)(2,1)S(1)} %get-tuple-element.38.refs_0_, bf16[528,128]{1,0:T(8,128)(2,1)S(1)} %get-tuple-element.43.refs_1_, ...), custom_call_target="tpu_custom_call" | custom-call | flops 1024 | bytes 1024 | tf_op jit(solution)/shard_map/merge/pallas_call | solution.py:326
  40.0 0.1 collective-permute-start.16
  40.1 0.5 collective-permute-start.17
  40.5 0.0 collective-permute-done.9.refs_1_
  40.5 1.4 %collective-permute-start.18 = (bf16[2,128,128]{2,1,0:T(8,128)(2,1)S(1)}, bf16[2,128,128]{2,1,0:T(8,128)(2,1)S(1)}, u32[]{:S(2)}, u32[]{:S(2)}) collective-permute-start(bf16[2,128,128]{2,1,0:T(8,128)(2,1)S(1)} %get-tuple-element.50), channel_id=1, source_target_pairs={{0,12},{4,8},{8,4},{12,0},{1,13},{5,9},{9,5},{13,1},{2,14},{6,10},... | collective-permute-start | bytes 196616 | tf_op jit(solution)/shard_map/ppermute | solution.py:369
  41.9 0.0 collective-permute-done.10.refs_2_
  41.9 0.0 collective-permute-done.11.refs_3_
  41.9 0.8 %assemble.2.refs_0_ = bf16[128,2048]{1,0:T(8,128)(2,1)} custom-call(bf16[2,128,128]{2,1,0:T(8,128)(2,1)S(1)} %get-tuple-element.38.refs_0_, bf16[2,128,128]{2,1,0:T(8,128)(2,1)S(1)} %collective-permute-done.9.refs_1_, bf16[2,128,128]{2,1,0:T(8,128)(2,1)S(1)} %collective-permute-done.10.refs_2_, bf16[2,128,128]{2,1,0:T(8,128)(2,1)S(1)} %collective-permute-done.11.refs_3_), custom_call_target="tpu_custom_call" | custom-call | flops 1073741824 | bytes 33554432 | tf_op jit(solution)/shard_map/assemble/pallas_call | solution.py:351
  42.7 0.0 collective-permute-done.16.refs_2_
  42.7 2.3 %collective-permute-done.17.refs_3_ = bf16[2,128,128]{2,1,0:T(8,128)(2,1)S(1)} collective-permute-done((bf16[2,128,128]{2,1,0:T(8,128)(2,1)S(1)}, bf16[2,128,128]{2,1,0:T(8,128)(2,1)S(1)}, u32[]{:S(2)}, u32[]{:S(2)}) %collective-permute-start.17) | collective-permute-done | bytes 65568 | tf_op jit(solution)/shard_map/ppermute | solution.py:369
  45.0 0.5 %collective-permute-done.18.refs_4_ = bf16[2,128,128]{2,1,0:T(8,128)(2,1)S(1)} collective-permute-done((bf16[2,128,128]{2,1,0:T(8,128)(2,1)S(1)}, bf16[2,128,128]{2,1,0:T(8,128)(2,1)S(1)}, u32[]{:S(2)}, u32[]{:S(2)}) %collective-permute-start.18) | collective-permute-done | bytes 65568 | tf_op jit(solution)/shard_map/ppermute | solution.py:369
  45.5 0.8 %assemble.3 = bf16[128,2048]{1,0:T(8,128)(2,1)} custom-call(bf16[128,2048]{1,0:T(8,128)(2,1)} %assemble.2.refs_0_, bf16[2,128,128]{2,1,0:T(8,128)(2,1)S(1)} %get-tuple-element.47.refs_1_, bf16[2,128,128]{2,1,0:T(8,128)(2,1)S(1)} %collective-permute-done.16.refs_2_, ...), custom_call_target="tpu_custom_call", output_to_operand_aliasing={{}: (0, {})} | custom-call | flops 1073741824 | bytes 33554432 | tf_op jit(solution)/shard_map/assemble/pallas_call | solution.py:351
  (7 shorter events, 0.0 us)
Async XLA Ops:
  0.0 12.0 %copy-start.2 = (bf16[512,512]{1,0:T(8,128)(2,1)S(1)}, bf16[512,512]{1,0:T(8,128)(2,1)}, u32[]{:S(2)}) copy-start(bf16[512,512]{1,0:T(8,128)(2,1)} %values.7) | copy-start | bytes 1572868
  0.0 12.0 %copy-start.1 = (bf16[512,512]{1,0:T(8,128)(2,1)S(1)}, bf16[512,512]{1,0:T(8,128)(2,1)}, u32[]{:S(2)}) copy-start(bf16[512,512]{1,0:T(8,128)(2,1)} %keys.7) | copy-start | bytes 1572868
  0.0 12.0 %copy-start = (bf16[512,2048]{1,0:T(8,128)(2,1)S(1)}, bf16[512,2048]{1,0:T(8,128)(2,1)}, u32[]{:S(2)}) copy-start(bf16[512,2048]{1,0:T(8,128)(2,1)} %queries.7) | copy-start | bytes 6291460
  0.0 12.0 %copy-start.3 = (s32[2048]{0:T(1024)S(1)}, s32[2048]{0:T(1024)}, u32[]{:S(2)}) copy-start(s32[2048]{0:T(1024)} %param.7) | copy-start | bytes 24580
  1.7 10.0 %collective-permute-start = (bf16[1024,128]{1,0:T(8,128)(2,1)S(1)}, bf16[1024,128]{1,0:T(8,128)(2,1)S(1)}, u32[]{:S(2)}, u32[]{:S(2)}) collective-permute-start(bf16[1024,128]{1,0:T(8,128)(2,1)S(1)} %get-tuple-element.28), channel_id=1, source_target_pairs={{0,4},{4,0},{8,12},{12,8},{1,5},{5,1},{9,13},{13,9},{2,6},{6,2},{1... | collective-permute-start | bytes 786440 | tf_op jit(solution)/shard_map/ppermute | solution.py:375
  2.2 9.8 %collective-permute-start.3 = (bf16[2,512,128]{2,1,0:T(8,128)(2,1)S(1)}, bf16[2,512,128]{2,1,0:T(8,128)(2,1)S(1)}, u32[]{:S(2)}, u32[]{:S(2)}) collective-permute-start(bf16[2,512,128]{2,1,0:T(8,128)(2,1)S(1)} %get-tuple-element.31), channel_id=1, source_target_pairs={{0,1},{1,0},{2,3},{3,2},{4,5},{5,4},{6,7},{7,6},{8,9},{9,8},{10,11... | collective-permute-start | bytes 786440 | tf_op jit(solution)/shard_map/ppermute | solution.py:369
  4.8 4.3 %collective-permute-start.1 = (bf16[256,128]{1,0:T(8,128)(2,1)S(1)}, bf16[256,128]{1,0:T(8,128)(2,1)S(1)}, u32[]{:S(2)}, u32[]{:S(2)}) collective-permute-start(bf16[256,128]{1,0:T(8,128)(2,1)S(1)} %get-tuple-element.29), channel_id=1, source_target_pairs={{0,8},{4,12},{8,0},{12,4},{1,9},{5,13},{9,1},{13,5},{2,10},{6,14},... | collective-permute-start | bytes 196616 | tf_op jit(solution)/shard_map/ppermute | solution.py:375
  6.3 4.9 %collective-permute-start.2 = (bf16[256,128]{1,0:T(8,128)(2,1)S(1)}, bf16[256,128]{1,0:T(8,128)(2,1)S(1)}, u32[]{:S(2)}, u32[]{:S(2)}) collective-permute-start(bf16[256,128]{1,0:T(8,128)(2,1)S(1)} %get-tuple-element.30), channel_id=1, source_target_pairs={{0,12},{4,8},{8,4},{12,0},{1,13},{5,9},{9,5},{13,1},{2,14},{6,10},... | collective-permute-start | bytes 196616 | tf_op jit(solution)/shard_map/ppermute | solution.py:375
  6.4 14.7 %collective-permute-start.12 = (bf16[2,512,128]{2,1,0:T(8,128)(2,1)S(1)}, bf16[2,512,128]{2,1,0:T(8,128)(2,1)S(1)}, u32[]{:S(2)}, u32[]{:S(2)}) collective-permute-start(bf16[2,512,128]{2,1,0:T(8,128)(2,1)S(1)} %get-tuple-element.42), channel_id=1, source_target_pairs={{0,1},{1,0},{2,3},{3,2},{4,5},{5,4},{6,7},{7,6},{8,9},{9,8},{10,11... | collective-permute-start | bytes 786440 | tf_op jit(solution)/shard_map/ppermute | solution.py:369
  9.1 8.4 %collective-permute-start.6 = (bf16[768,128]{1,0:T(8,128)(2,1)S(1)}, bf16[768,128]{1,0:T(8,128)(2,1)S(1)}, u32[]{:S(2)}, u32[]{:S(2)}) collective-permute-start(bf16[768,128]{1,0:T(8,128)(2,1)S(1)} %get-tuple-element.34), channel_id=1, source_target_pairs={{0,8},{4,12},{8,0},{12,4},{1,9},{5,13},{9,1},{13,5},{2,10},{6,14},... | collective-permute-start | bytes 589832 | tf_op jit(solution)/shard_map/ppermute | solution.py:375
  11.3 7.3 %collective-permute-start.7 = (bf16[768,128]{1,0:T(8,128)(2,1)S(1)}, bf16[768,128]{1,0:T(8,128)(2,1)S(1)}, u32[]{:S(2)}, u32[]{:S(2)}) collective-permute-start(bf16[768,128]{1,0:T(8,128)(2,1)S(1)} %get-tuple-element.35), channel_id=1, source_target_pairs={{0,12},{4,8},{8,4},{12,0},{1,13},{5,9},{9,5},{13,1},{2,14},{6,10},... | collective-permute-start | bytes 589832 | tf_op jit(solution)/shard_map/ppermute | solution.py:375
  14.0 13.3 %collective-permute-start.5 = (bf16[528,128]{1,0:T(8,128)(2,1)S(1)}, bf16[528,128]{1,0:T(8,128)(2,1)S(1)}, u32[]{:S(2)}, u32[]{:S(2)}) collective-permute-start(bf16[528,128]{1,0:T(8,128)(2,1)S(1)} %get-tuple-element.33), channel_id=1, source_target_pairs={{0,3},{1,2},{2,1},{3,0},{4,7},{5,6},{6,5},{7,4},{8,11},{9,10},{10,... | collective-permute-start | bytes 405512 | tf_op jit(solution)/shard_map/ppermute | solution.py:384
  17.5 11.8 %collective-permute-start.4 = (bf16[528,128]{1,0:T(8,128)(2,1)S(1)}, bf16[528,128]{1,0:T(8,128)(2,1)S(1)}, u32[]{:S(2)}, u32[]{:S(2)}) collective-permute-start(bf16[528,128]{1,0:T(8,128)(2,1)S(1)} %get-tuple-element.32.refs_0_), channel_id=1, source_target_pairs={{0,2},{1,3},{2,0},{3,1},{4,6},{5,7},{6,4},{7,5},{8,10},{9,11},{10,... | collective-permute-start | bytes 405512 | tf_op jit(solution)/shard_map/ppermute | solution.py:384
  20.7 11.2 %collective-permute-start.8 = (bf16[528,128]{1,0:T(8,128)(2,1)S(1)}, bf16[528,128]{1,0:T(8,128)(2,1)S(1)}, u32[]{:S(2)}, u32[]{:S(2)}) collective-permute-start(bf16[528,128]{1,0:T(8,128)(2,1)S(1)} %get-tuple-element.37), channel_id=1, source_target_pairs={{0,1},{1,0},{2,3},{3,2},{4,5},{5,4},{6,7},{7,6},{8,9},{9,8},{10,11... | collective-permute-start | bytes 405512 | tf_op jit(solution)/shard_map/ppermute | solution.py:389
  24.4 10.1 %collective-permute-start.13 = (bf16[528,128]{1,0:T(8,128)(2,1)S(1)}, bf16[528,128]{1,0:T(8,128)(2,1)S(1)}, u32[]{:S(2)}, u32[]{:S(2)}) collective-permute-start(bf16[528,128]{1,0:T(8,128)(2,1)S(1)} %get-tuple-element.44), channel_id=1, source_target_pairs={{0,1},{1,0},{2,3},{3,2},{4,5},{5,4},{6,7},{7,6},{8,9},{9,8},{10,11... | collective-permute-start | bytes 405512 | tf_op jit(solution)/shard_map/ppermute | solution.py:389
  26.1 13.2 %collective-permute-start.14 = (bf16[528,128]{1,0:T(8,128)(2,1)S(1)}, bf16[528,128]{1,0:T(8,128)(2,1)S(1)}, u32[]{:S(2)}, u32[]{:S(2)}) collective-permute-start(bf16[528,128]{1,0:T(8,128)(2,1)S(1)} %get-tuple-element.45), channel_id=1, source_target_pairs={{0,2},{1,3},{2,0},{3,1},{4,6},{5,7},{6,4},{7,5},{8,10},{9,11},{10,... | collective-permute-start | bytes 405512 | tf_op jit(solution)/shard_map/ppermute | solution.py:384
  27.4 12.0 %collective-permute-start.15 = (bf16[528,128]{1,0:T(8,128)(2,1)S(1)}, bf16[528,128]{1,0:T(8,128)(2,1)S(1)}, u32[]{:S(2)}, u32[]{:S(2)}) collective-permute-start(bf16[528,128]{1,0:T(8,128)(2,1)S(1)} %get-tuple-element.46), channel_id=1, source_target_pairs={{0,3},{1,2},{2,1},{3,0},{4,7},{5,6},{6,5},{7,4},{8,11},{9,10},{10,... | collective-permute-start | bytes 405512 | tf_op jit(solution)/shard_map/ppermute | solution.py:384
  32.8 7.7 %collective-permute-start.9 = (bf16[2,128,128]{2,1,0:T(8,128)(2,1)S(1)}, bf16[2,128,128]{2,1,0:T(8,128)(2,1)S(1)}, u32[]{:S(2)}, u32[]{:S(2)}) collective-permute-start(bf16[2,128,128]{2,1,0:T(8,128)(2,1)S(1)} %get-tuple-element.39), channel_id=1, source_target_pairs={{0,4},{4,0},{8,12},{12,8},{1,5},{5,1},{9,13},{13,9},{2,6},{6,2},{1... | collective-permute-start | bytes 196616 | tf_op jit(solution)/shard_map/ppermute | solution.py:369
  32.9 9.0 %collective-permute-start.10 = (bf16[2,128,128]{2,1,0:T(8,128)(2,1)S(1)}, bf16[2,128,128]{2,1,0:T(8,128)(2,1)S(1)}, u32[]{:S(2)}, u32[]{:S(2)}) collective-permute-start(bf16[2,128,128]{2,1,0:T(8,128)(2,1)S(1)} %get-tuple-element.40), channel_id=1, source_target_pairs={{0,8},{4,12},{8,0},{12,4},{1,9},{5,13},{9,1},{13,5},{2,10},{6,14},... | collective-permute-start | bytes 196616 | tf_op jit(solution)/shard_map/ppermute | solution.py:369
  34.6 7.4 %collective-permute-start.11 = (bf16[2,128,128]{2,1,0:T(8,128)(2,1)S(1)}, bf16[2,128,128]{2,1,0:T(8,128)(2,1)S(1)}, u32[]{:S(2)}, u32[]{:S(2)}) collective-permute-start(bf16[2,128,128]{2,1,0:T(8,128)(2,1)S(1)} %get-tuple-element.41), channel_id=1, source_target_pairs={{0,12},{4,8},{8,4},{12,0},{1,13},{5,9},{9,5},{13,1},{2,14},{6,10},... | collective-permute-start | bytes 196616 | tf_op jit(solution)/shard_map/ppermute | solution.py:369
  40.0 2.7 %collective-permute-start.16 = (bf16[2,128,128]{2,1,0:T(8,128)(2,1)S(1)}, bf16[2,128,128]{2,1,0:T(8,128)(2,1)S(1)}, u32[]{:S(2)}, u32[]{:S(2)}) collective-permute-start(bf16[2,128,128]{2,1,0:T(8,128)(2,1)S(1)} %get-tuple-element.48), channel_id=1, source_target_pairs={{0,4},{4,0},{8,12},{12,8},{1,5},{5,1},{9,13},{13,9},{2,6},{6,2},{1... | collective-permute-start | bytes 196616 | tf_op jit(solution)/shard_map/ppermute | solution.py:369
  40.1 5.0 %collective-permute-start.17 = (bf16[2,128,128]{2,1,0:T(8,128)(2,1)S(1)}, bf16[2,128,128]{2,1,0:T(8,128)(2,1)S(1)}, u32[]{:S(2)}, u32[]{:S(2)}) collective-permute-start(bf16[2,128,128]{2,1,0:T(8,128)(2,1)S(1)} %get-tuple-element.49), channel_id=1, source_target_pairs={{0,8},{4,12},{8,0},{12,4},{1,9},{5,13},{9,1},{13,5},{2,10},{6,14},... | collective-permute-start | bytes 196616 | tf_op jit(solution)/shard_map/ppermute | solution.py:369
  40.5 5.0 %collective-permute-start.18 = (bf16[2,128,128]{2,1,0:T(8,128)(2,1)S(1)}, bf16[2,128,128]{2,1,0:T(8,128)(2,1)S(1)}, u32[]{:S(2)}, u32[]{:S(2)}) collective-permute-start(bf16[2,128,128]{2,1,0:T(8,128)(2,1)S(1)} %get-tuple-element.50), channel_id=1, source_target_pairs={{0,12},{4,8},{8,4},{12,0},{1,13},{5,9},{9,5},{13,1},{2,14},{6,10},... | collective-permute-start | bytes 196616 | tf_op jit(solution)/shard_map/ppermute | solution.py:369

commit v8 on v7

--- a/solution.py
+++ b/solution.py
@@ -170,8 +170,11 @@
     )(queries, keys, values, *after)
 
 
-def attend_kernel(chunk, fars, skips, waits, scale, steps_ref, queries, keys, values, *refs):
-    moved, got, results, (q_buf, k_buf, v_buf) = refs[waits:waits + 3], refs[waits + 3], refs[waits + 4:-3], refs[-3:]
+def attend_kernel(shapes, skips, waits, scale, steps_ref, queries, keys, values, *refs):
+    chunks = sorted({chunk for chunk, _ in shapes})
+    refs = refs[waits:]
+    moved, got, results = refs[:3], refs[3:3 + len(chunks)], refs[3 + len(chunks):-3]
+    q_buf, k_buf, v_buf = refs[-3:]
     column = lax.axis_index("pb")
     z = lax.axis_index("ka")
     half_rows = q_buf.shape[2]
@@ -181,32 +184,34 @@
 
     def sort_queries(mine):
         for d, skip, q in zip((1, 2, 3), skips, moved):
-            for i in range(len(fars)):
+            for i in range(len(shapes)):
                 q_buf[i, mine ^ d] = q[(skip + i) * half_rows:(skip + i + 1) * half_rows, :]
 
     def work(which):
         upper, half = which // 2, which % 2
         base = upper * pair
-        starts = [half_rows if far == (upper == 0) else 0 for far in fars]
+        starts = [half_rows if far == (upper == 0) else 0 for _, far in shapes]
 
         def own_queries(mine):
-            at = (mine * 4 + half * 2 + chunk) * HEAD_DIM
-            for i, start in enumerate(starts):
+            for i, ((chunk, _), start) in enumerate(zip(shapes, starts)):
+                at = (mine * 4 + half * 2 + chunk) * HEAD_DIM
                 q_buf[i, mine] = queries[start:start + half_rows, at:at + HEAD_DIM]
 
         for mine in range(4):
             pl.when(column == mine)(functools.partial(own_queries, mine))
-        head = slice((half * 2 + chunk) * HEAD_DIM, (half * 2 + chunk + 1) * HEAD_DIM)
-        for buf, own, theirs in ((k_buf, keys, got.at[0]), (v_buf, values, got.at[1])):
-            buf[half * held:(half + 1) * held, :HEAD_DIM] = own[:, head]
-            buf[(1 - half) * held:(2 - half) * held, :HEAD_DIM] = theirs[...]
-        v_buf[:, HEAD_DIM:] = jnp.ones((pair, HEAD_DIM), jnp.bfloat16)
+        for kv, chunk in enumerate(chunks):
+            head = slice((half * 2 + chunk) * HEAD_DIM, (half * 2 + chunk + 1) * HEAD_DIM)
+            for buf, own, theirs in ((k_buf, keys, got[kv].at[0]), (v_buf, values, got[kv].at[1])):
+                buf[kv, half * held:(half + 1) * held, :HEAD_DIM] = own[:, head]
+                buf[kv, (1 - half) * held:(2 - half) * held, :HEAD_DIM] = theirs[...]
+            v_buf[kv, :, HEAD_DIM:] = jnp.ones((pair, HEAD_DIM), jnp.bfloat16)
         steps = steps_ref[...].astype(jnp.float32)
         columns = jnp.transpose(steps)
 
         def tile(i, slot, first_row, limit, masked_from, stats, first=0, size=half_rows):
             q = q_buf[i, (slot + 2 * upper) % 4, first:first + size, :]
-            scores = lax.dot_general(q, k_buf[:limit, :], (((1,), (1,)), ((), ())), preferred_element_type=jnp.float32)
+            kv = chunks.index(shapes[i][0])
+            scores = lax.dot_general(q, k_buf[kv, :limit, :], (((1,), (1,)), ((), ())), preferred_element_type=jnp.float32)
             if masked_from < limit:
                 at = (first_row + first) // LANES
                 q_steps = jnp.concatenate([columns[:, g:g + 1] for g in range(at, at + size // LANES)], axis=0)
@@ -217,7 +222,7 @@
             top = jnp.max(scores, axis=1, keepdims=True) * scale
             top = top.astype(jnp.bfloat16).astype(jnp.float32)
             weights = jnp.exp2(scores * scale - top).astype(jnp.bfloat16)
-            mixed = lax.dot_general(weights, v_buf[:limit, :], (((1,), (0,)), ((), ())), preferred_element_type=jnp.float32)
+            mixed = lax.dot_general(weights, v_buf[kv, :limit, :], (((1,), (0,)), ((), ())), preferred_element_type=jnp.float32)
             total = mixed[:, HEAD_DIM:]
             result = (mixed[:, :HEAD_DIM] / total).astype(jnp.bfloat16)
             for j in range(0, size, sub):
@@ -228,7 +233,7 @@
             stats = jnp.where(lane == 3 * slot + 1, high, stats)
             return jnp.where(lane == 3 * slot + 2, total - high, stats)
 
-        for i, (far, start) in enumerate(zip(fars, starts)):
+        for i, ((_, far), start) in enumerate(zip(shapes, starts)):
             reach = start + half_rows + LANES
             stats = jnp.zeros((half_rows, LANES), jnp.float32)
             stats = tile(i, 0, base + start, reach, start, stats)
@@ -248,22 +253,22 @@
         pl.when(z == which)(functools.partial(work, which))
 
 
-def attend(chunk, fars, skips, steps, queries, keys, values, moved, got, after=()):
+def attend(shapes, skips, steps, queries, keys, values, moved, got, after=()):
     held = keys.shape[0]
     part = jax.ShapeDtypeStruct((held + STATS, LANES), jnp.bfloat16)
     return pl.pallas_call(
-        functools.partial(attend_kernel, chunk, fars, skips, len(after), math.log2(math.e) / math.sqrt(HEAD_DIM)),
-        out_shape=[part] * (2 * len(fars)),
-        in_specs=[VMEM] * 4 + [ANY] * len(after) + [VMEM] * 4,
-        out_specs=[VMEM] * (2 * len(fars)),
+        functools.partial(attend_kernel, shapes, skips, len(after), math.log2(math.e) / math.sqrt(HEAD_DIM)),
+        out_shape=[part] * (2 * len(shapes)),
+        in_specs=[VMEM] * 4 + [ANY] * len(after) + [VMEM] * (3 + len(got)),
+        out_specs=[VMEM] * (2 * len(shapes)),
         scratch_shapes=[
-            pltpu.VMEM((len(fars), 4, held // 2, HEAD_DIM), jnp.bfloat16),
-            pltpu.VMEM((2 * held, HEAD_DIM), jnp.bfloat16),
-            pltpu.VMEM((2 * held, 2 * HEAD_DIM), jnp.bfloat16),
+            pltpu.VMEM((len(shapes), 4, held // 2, HEAD_DIM), jnp.bfloat16),
+            pltpu.VMEM((len(got), 2 * held, HEAD_DIM), jnp.bfloat16),
+            pltpu.VMEM((len(got), 2 * held, 2 * HEAD_DIM), jnp.bfloat16),
         ],
         compiler_params=pltpu.CompilerParams(vmem_limit_bytes=24 << 20),
         cost_estimate=pl.CostEstimate(flops=1 << 10, bytes_accessed=1 << 10, transcendentals=0),
-        name="attend_far" if fars == (True,) else "attend",
+        name="attend_first" if len(shapes) == 1 else "attend_rest",
     )(steps, queries, keys, values, *after, *moved, *got)
 
 
@@ -278,7 +283,7 @@
         in_specs=[ANY] * 2,
         out_specs=VMEM,
         compiler_params=pltpu.CompilerParams(vmem_limit_bytes=4 << 20),
-        cost_estimate=pl.CostEstimate(flops=1 << 30, bytes_accessed=32 << 20, transcendentals=0),
+        cost_estimate=pl.CostEstimate(flops=1 << 34, bytes_accessed=512 << 20, transcendentals=0),
         name="mark",
     )(a, b)
 
@@ -374,13 +379,13 @@
     got = travel(packed[:1], "ka"), travel(packed[1:2], "ka")
     all_1, *others = [lax.ppermute(piece, "pb", swaps[d]) for piece, (d, _) in zip(packed[2:], batches)]
     first, rest = others[:2], others[2:]
-    def work(chunk, fars, arrived, skips, after):
-        parts = attend(chunk, fars, skips, steps, queries, keys, values, arrived, got[chunk], after)
+    def work(shapes, arrived, skips, got, after=()):
+        parts = attend(shapes, skips, steps, queries, keys, values, arrived, got, after)
         return [parts[i:i + 2] for i in range(0, len(parts), 2)]
 
-    parts = work(0, (True,), [all_1, *first], (0, 0, 0), [])
-    parts += work(0, (False,), [all_1, *rest], (1, 0, 0), [parts[-1][0]])
-    parts += work(1, (True, False), [all_1, *rest], (2, 1, 1), [parts[-1][0]])
+    got = [pair for pairs in got for pair in pairs]
+    parts = work(order[:1], [all_1, *first], (0, 0, 0), got[:1])
+    parts += work(order[1:], [all_1, *rest], (1, 0, 0), got, parts[0][:1])
     far = [[lax.ppermute(same, "ka", swaps[2]), lax.ppermute(cross, "ka", swaps[3])] for same, cross in parts[::2]]
     marks = [mark(*far[0])]
     result = ()

time: 46.7 us -> 46.7 us (level)
  starting transfers between devices: 18.6 us -> 22.6 us
  waiting for transfers between devices: 15.4 us -> 12.3 us
  Pallas kernels: 12.2 us -> 11.4 us
    ppermute x8, starting transfers between devices: 5.63 us -> 8.35 us  [travel(): lax.ppermute(piece, axis, swap)]
    ppermute x2, waiting for transfers between devices: 4.58 us -> 2.11 us  [by_pairs(): lax.ppermute(same, 'ka', swaps[2])]
    ppermute x2, starting transfers between devices: 1.21 us -> 2.88 us  [by_pairs(): lax.ppermute(same, 'ka', swaps[2])]
    ppermute x5, waiting for transfers between devices: 3.37 us -> 2.5 us  [by_pairs(): lax.ppermute(piece, 'pb', swaps[d])]
    ppermute x8, waiting for transfers between devices: 3.13 us -> 3.83 us  [travel(): lax.ppermute(piece, axis, swap)]
    pallas_call x3 -> x2, Pallas kernels: 7.44 us -> 6.88 us  [attend(): pl.pallas_call(functools.partial(attend_kernel, shapes, skips, len(after)...]
  transfers between devices with their start and end apart: 19 -> 19, of which waited for: 9 -> 10; matrix products, arithmetic and copies ran while one was open for 0% -> 0% of each run, Pallas kernels for 21% -> 19%
where the time goes in v8:
time: 46.7 us; the launch traced here: 46.6 us
  starting transfers between devices  22.6 us (48%)
  waiting for transfers between devices  12.3 us (26%)
  Pallas kernels  11.4 us (24%)
    ppermute x8, starting transfers between devices, travel(): lax.ppermute(piece, axis, swap)  8.35 us
    pallas_call x2, Pallas kernels, attend(): pl.pallas_call(functools.partial(attend_kernel, shapes, skips, len(after)...  6.88 us
    ppermute x5, starting transfers between devices, by_pairs(): lax.ppermute(piece, 'pb', swaps[d])  4.64 us
    ppermute x2, starting transfers between devices, by_pairs(): lax.ppermute(cross, 'ka', swaps[3])  4.62 us
    ppermute x2, waiting for transfers between devices, by_pairs(): lax.ppermute(beside, 'ka', swaps[1])  3.86 us
    ppermute x8, waiting for transfers between devices, travel(): lax.ppermute(piece, axis, swap)  3.83 us
    ppermute x2, starting transfers between devices, by_pairs(): lax.ppermute(same, 'ka', swaps[2])  2.88 us
    ppermute x5, waiting for transfers between devices, by_pairs(): lax.ppermute(piece, 'pb', swaps[d])  2.5 us
  transfers between devices with their start and end apart: 19, of which 10 were waited for; matrix products, arithmetic and copies ran while one was open for 0% of the time, Pallas kernels for 19%

profile of v8, /device:TPU:0, one launch (start us, length us, event | category | flops | bytes accessed | tf_op | source)
XLA Modules:
  0.0 46.6 jit_solution(17752896429619234929)
XLA Ops:
  0.0 1.6 %pack.1 = (bf16[2,512,128]{2,1,0:T(8,128)(2,1)S(1)}, bf16[2,512,128]{2,1,0:T(8,128)(2,1)S(1)}, bf16[1024,128]{1,0:T(8,128)(2,1)S(1)}, bf16[256,128]{1,0:T(8,128)...) custom-call(bf16[512,2048]{1,0:T(8,128)(2,1)} %queries.5, ...), custom_call_target="tpu_custom_call" | custom-call | tf_op jit(solution)/shard_map/pack/pallas_call | solution.py:162
  1.7 0.5 %collective-permute-start = (bf16[1024,128]{1,0:T(8,128)(2,1)S(1)}, bf16[1024,128]{1,0:T(8,128)(2,1)S(1)}, u32[]{:S(2)}, u32[]{:S(2)}) collective-permute-start(bf16[1024,128]{1,0:T(8,128)(2,1)S(1)} %get-tuple-element.28), channel_id=1, source_target_pairs={{0,4},{4,0},{8,12},{12,8},{1,5},{5,1},{9,13},{13,9},{2,6},{6,2},{1... | collective-permute-start | bytes 786440 | tf_op jit(solution)/shard_map/ppermute | solution.py:380
  2.2 2.6 %collective-permute-start.3 = (bf16[2,512,128]{2,1,0:T(8,128)(2,1)S(1)}, bf16[2,512,128]{2,1,0:T(8,128)(2,1)S(1)}, u32[]{:S(2)}, u32[]{:S(2)}) collective-permute-start(bf16[2,512,128]{2,1,0:T(8,128)(2,1)S(1)} %get-tuple-element.31), channel_id=1, source_target_pairs={{0,1},{1,0},{2,3},{3,2},{4,5},{5,4},{6,7},{7,6},{8,9},{9,8},{10,11... | collective-permute-start | bytes 786440 | tf_op jit(solution)/shard_map/ppermute | solution.py:374
  4.8 1.5 %collective-permute-start.1 = (bf16[256,128]{1,0:T(8,128)(2,1)S(1)}, bf16[256,128]{1,0:T(8,128)(2,1)S(1)}, u32[]{:S(2)}, u32[]{:S(2)}) collective-permute-start(bf16[256,128]{1,0:T(8,128)(2,1)S(1)} %get-tuple-element.29), channel_id=1, source_target_pairs={{0,8},{4,12},{8,0},{12,4},{1,9},{5,13},{9,1},{13,5},{2,10},{6,14},... | collective-permute-start | bytes 196616 | tf_op jit(solution)/shard_map/ppermute | solution.py:380
  6.3 0.0 collective-permute-start.2
  6.4 0.4 collective-permute-start.8
  6.8 2.3 %collective-permute-done.1.refs_1_ = bf16[256,128]{1,0:T(8,128)(2,1)S(1)} collective-permute-done((bf16[256,128]{1,0:T(8,128)(2,1)S(1)}, bf16[256,128]{1,0:T(8,128)(2,1)S(1)}, u32[]{:S(2)}, u32[]{:S(2)}) %collective-permute-start.1) | collective-permute-done | bytes 65568 | tf_op jit(solution)/shard_map/ppermute | solution.py:380
  9.1 2.2 %collective-permute-start.6 = (bf16[768,128]{1,0:T(8,128)(2,1)S(1)}, bf16[768,128]{1,0:T(8,128)(2,1)S(1)}, u32[]{:S(2)}, u32[]{:S(2)}) collective-permute-start(bf16[768,128]{1,0:T(8,128)(2,1)S(1)} %get-tuple-element.34), channel_id=1, source_target_pairs={{0,8},{4,12},{8,0},{12,4},{1,9},{5,13},{9,1},{13,5},{2,10},{6,14},... | collective-permute-start | bytes 589832 | tf_op jit(solution)/shard_map/ppermute | solution.py:380
  11.3 0.0 collective-permute-done.2.refs_2_
  11.3 0.4 collective-permute-start.7
  11.7 0.0 collective-permute-done.refs_0_.refs_1_
  11.7 0.3 collective-permute-done.3.refs_3_.refs_4_
  12.0 0.0 copy-done
  12.0 0.0 copy-done.1
  12.0 0.0 copy-done.2
  12.0 2.0 %attend_first.1 = (bf16[528,128]{1,0:T(8,128)(2,1)S(1)}, bf16[528,128]{1,0:T(8,128)(2,1)S(1)}) custom-call(s32[16,128]{1,0:T(8,128)S(1)} %bitcast.1, bf16[512,2048]{1,0:T(8,128)(2,1)S(1)} %copy-done, bf16[512,512]{1,0:T(8,128)(2,1)S(1)} %copy-done.1, bf16[512,512]{1,0:T(8,128)(2,1)S(1)} %copy-done.2, ...), custom_call_target="tpu_custom_call" | custom-call | flops 1024 | bytes 1024 | tf_op jit(solution)/shard_map/attend_first/pallas_call | solution.py:259
  14.0 2.5 %collective-permute-start.4 = (bf16[528,128]{1,0:T(8,128)(2,1)S(1)}, bf16[528,128]{1,0:T(8,128)(2,1)S(1)}, u32[]{:S(2)}, u32[]{:S(2)}) collective-permute-start(bf16[528,128]{1,0:T(8,128)(2,1)S(1)} %get-tuple-element.32.refs_0_), channel_id=1, source_target_pairs={{0,2},{1,3},{2,0},{3,1},{4,6},{5,7},{6,4},{7,5},{8,10},{9,11},{10,... | collective-permute-start | bytes 405512 | tf_op jit(solution)/shard_map/ppermute | solution.py:389
  16.5 1.9 %collective-permute-start.5 = (bf16[528,128]{1,0:T(8,128)(2,1)S(1)}, bf16[528,128]{1,0:T(8,128)(2,1)S(1)}, u32[]{:S(2)}, u32[]{:S(2)}) collective-permute-start(bf16[528,128]{1,0:T(8,128)(2,1)S(1)} %get-tuple-element.33), channel_id=1, source_target_pairs={{0,3},{1,2},{2,1},{3,0},{4,7},{5,6},{6,5},{7,4},{8,11},{9,10},{10,... | collective-permute-start | bytes 405512 | tf_op jit(solution)/shard_map/ppermute | solution.py:389
  18.4 0.0 collective-permute-done.6.refs_2_
  18.4 0.2 collective-permute-done.7.refs_3_
  18.5 0.7 %collective-permute-done.8.refs_5_ = bf16[2,512,128]{2,1,0:T(8,128)(2,1)S(1)} collective-permute-done((bf16[2,512,128]{2,1,0:T(8,128)(2,1)S(1)}, bf16[2,512,128]{2,1,0:T(8,128)(2,1)S(1)}, u32[]{:S(2)}, u32[]{:S(2)}) %collective-permute-start.8) | collective-permute-done | bytes 262176 | tf_op jit(solution)/shard_map/ppermute | solution.py:374
  19.2 4.9 %attend_rest.1 = (bf16[528,128]{1,0:T(8,128)(2,1)S(1)}, bf16[528,128]{1,0:T(8,128)(2,1)S(1)}, bf16[528,128]{1,0:T(8,128)(2,1)S(1)}, bf16[528,128]{1,0:T(8,128)(2...) custom-call(s32[16,128]{1,0:T(8,128)S(1)} %bitcast.2, bf16[512,2048]{1,0:T(8,128)(2,1)S(1)} %copy-done, ...), custom_call_target="tpu_custom_call" | custom-call | flops 1024 | bytes 1024 | tf_op jit(solution)/shard_map/attend_rest/pallas_call | solution.py:259
  24.1 0.6 %collective-permute-start.9 = (bf16[528,128]{1,0:T(8,128)(2,1)S(1)}, bf16[528,128]{1,0:T(8,128)(2,1)S(1)}, u32[]{:S(2)}, u32[]{:S(2)}) collective-permute-start(bf16[528,128]{1,0:T(8,128)(2,1)S(1)} %get-tuple-element.38), channel_id=1, source_target_pairs={{0,1},{1,0},{2,3},{3,2},{4,5},{5,4},{6,7},{7,6},{8,9},{9,8},{10,11... | collective-permute-start | bytes 405512 | tf_op jit(solution)/shard_map/ppermute | solution.py:394
  24.7 1.5 %collective-permute-start.13 = (bf16[528,128]{1,0:T(8,128)(2,1)S(1)}, bf16[528,128]{1,0:T(8,128)(2,1)S(1)}, u32[]{:S(2)}, u32[]{:S(2)}) collective-permute-start(bf16[528,128]{1,0:T(8,128)(2,1)S(1)} %get-tuple-element.44), channel_id=1, source_target_pairs={{0,1},{1,0},{2,3},{3,2},{4,5},{5,4},{6,7},{7,6},{8,9},{9,8},{10,11... | collective-permute-start | bytes 405512 | tf_op jit(solution)/shard_map/ppermute | solution.py:394
  26.2 0.4 collective-permute-start.14
  26.6 0.4 collective-permute-done.4.a.refs_3_
  27.0 2.7 %collective-permute-start.15 = (bf16[528,128]{1,0:T(8,128)(2,1)S(1)}, bf16[528,128]{1,0:T(8,128)(2,1)S(1)}, u32[]{:S(2)}, u32[]{:S(2)}) collective-permute-start(bf16[528,128]{1,0:T(8,128)(2,1)S(1)} %get-tuple-element.46), channel_id=1, source_target_pairs={{0,3},{1,2},{2,1},{3,0},{4,7},{5,6},{6,5},{7,4},{8,11},{9,10},{10,... | collective-permute-start | bytes 405512 | tf_op jit(solution)/shard_map/ppermute | solution.py:389
  29.8 0.0 collective-permute-done.5.b.refs_4_
  29.8 3.6 %collective-permute-done.9.refs_2_ = bf16[528,128]{1,0:T(8,128)(2,1)S(1)} collective-permute-done((bf16[528,128]{1,0:T(8,128)(2,1)S(1)}, bf16[528,128]{1,0:T(8,128)(2,1)S(1)}, u32[]{:S(2)}, u32[]{:S(2)}) %collective-permute-start.9) | collective-permute-done | bytes 135200 | tf_op jit(solution)/shard_map/ppermute | solution.py:394
  33.4 0.7 %merge.2 = (bf16[2,128,128]{2,1,0:T(8,128)(2,1)S(1)}, bf16[2,128,128]{2,1,0:T(8,128)(2,1)S(1)}, bf16[2,128,128]{2,1,0:T(8,128)(2,1)S(1)}, bf16[2,128,128]{2,1,0:T(8,128)(2,1)S(1)}) custom-call(f32[8,128]{1,0:T(8,128)S(1)} %mark.1.refs_0_, bf16[528,128]{1,0:T(8,128)(2,1)S(1)} %get-tuple-element.37.refs_1_, ...), custom_call_target="tpu_custom_call" | custom-call | flops 1024 | bytes 1024 | tf_op jit(solution)/shard_map/merge/pallas_call | solution.py:331
  34.1 0.1 collective-permute-start.10
  34.1 1.4 %collective-permute-start.11 = (bf16[2,128,128]{2,1,0:T(8,128)(2,1)S(1)}, bf16[2,128,128]{2,1,0:T(8,128)(2,1)S(1)}, u32[]{:S(2)}, u32[]{:S(2)}) collective-permute-start(bf16[2,128,128]{2,1,0:T(8,128)(2,1)S(1)} %get-tuple-element.41), channel_id=1, source_target_pairs={{0,8},{4,12},{8,0},{12,4},{1,9},{5,13},{9,1},{13,5},{2,10},{6,14},... | collective-permute-start | bytes 196616 | tf_op jit(solution)/shard_map/ppermute | solution.py:374
  35.5 0.3 collective-permute-done.13.refs_2_
  35.8 1.9 %collective-permute-start.12 = (bf16[2,128,128]{2,1,0:T(8,128)(2,1)S(1)}, bf16[2,128,128]{2,1,0:T(8,128)(2,1)S(1)}, u32[]{:S(2)}, u32[]{:S(2)}) collective-permute-start(bf16[2,128,128]{2,1,0:T(8,128)(2,1)S(1)} %get-tuple-element.42), channel_id=1, source_target_pairs={{0,12},{4,8},{8,4},{12,0},{1,13},{5,9},{9,5},{13,1},{2,14},{6,10},... | collective-permute-start | bytes 196616 | tf_op jit(solution)/shard_map/ppermute | solution.py:374
  37.7 1.7 %collective-permute-done.14.refs_3_ = bf16[528,128]{1,0:T(8,128)(2,1)S(1)} collective-permute-done((bf16[528,128]{1,0:T(8,128)(2,1)S(1)}, bf16[528,128]{1,0:T(8,128)(2,1)S(1)}, u32[]{:S(2)}, u32[]{:S(2)}) %collective-permute-start.14) | collective-permute-done | bytes 135200 | tf_op jit(solution)/shard_map/ppermute | solution.py:389
  39.4 0.0 collective-permute-done.15.refs_4_
  39.4 0.7 %merge.3 = (bf16[2,128,128]{2,1,0:T(8,128)(2,1)S(1)}, bf16[2,128,128]{2,1,0:T(8,128)(2,1)S(1)}, bf16[2,128,128]{2,1,0:T(8,128)(2,1)S(1)}, bf16[2,128,128]{2,1,0:T(8,128)(2,1)S(1)}) custom-call(bf16[2,128,128]{2,1,0:T(8,128)(2,1)S(1)} %get-tuple-element.39.refs_0_, bf16[528,128]{1,0:T(8,128)(2,1)S(1)} %get-tuple-element.43.refs_1_, ...), custom_call_target="tpu_custom_call" | custom-call | flops 1024 | bytes 1024 | tf_op jit(solution)/shard_map/merge/pallas_call | solution.py:331
  40.1 0.1 collective-permute-start.16
  40.2 0.7 %collective-permute-start.17 = (bf16[2,128,128]{2,1,0:T(8,128)(2,1)S(1)}, bf16[2,128,128]{2,1,0:T(8,128)(2,1)S(1)}, u32[]{:S(2)}, u32[]{:S(2)}) collective-permute-start(bf16[2,128,128]{2,1,0:T(8,128)(2,1)S(1)} %get-tuple-element.49), channel_id=1, source_target_pairs={{0,8},{4,12},{8,0},{12,4},{1,9},{5,13},{9,1},{13,5},{2,10},{6,14},... | collective-permute-start | bytes 196616 | tf_op jit(solution)/shard_map/ppermute | solution.py:374
  40.9 0.0 collective-permute-done.10.refs_1_
  40.9 1.1 %collective-permute-start.18 = (bf16[2,128,128]{2,1,0:T(8,128)(2,1)S(1)}, bf16[2,128,128]{2,1,0:T(8,128)(2,1)S(1)}, u32[]{:S(2)}, u32[]{:S(2)}) collective-permute-start(bf16[2,128,128]{2,1,0:T(8,128)(2,1)S(1)} %get-tuple-element.50), channel_id=1, source_target_pairs={{0,12},{4,8},{8,4},{12,0},{1,13},{5,9},{9,5},{13,1},{2,14},{6,10},... | collective-permute-start | bytes 196616 | tf_op jit(solution)/shard_map/ppermute | solution.py:374
  42.0 0.0 collective-permute-done.11.refs_2_
  42.1 0.0 collective-permute-done.12.refs_3_
  42.1 0.8 %assemble.2.refs_0_ = bf16[128,2048]{1,0:T(8,128)(2,1)} custom-call(bf16[2,128,128]{2,1,0:T(8,128)(2,1)S(1)} %get-tuple-element.39.refs_0_, bf16[2,128,128]{2,1,0:T(8,128)(2,1)S(1)} %collective-permute-done.10.refs_1_, bf16[2,128,128]{2,1,0:T(8,128)(2,1)S(1)} %collective-permute-done.11.refs_2_, bf16[2,128,128]{2,1,0:T(8,128)(2,1)S(1)} %collective-permute-done.12.refs_3_), custom_call_target="tpu_custom_call" | custom-call | flops 1073741824 | bytes 33554432 | tf_op jit(solution)/shard_map/assemble/pallas_call | solution.py:356
  42.8 0.0 collective-permute-done.16.refs_2_
  42.8 2.3 %collective-permute-done.17.refs_3_ = bf16[2,128,128]{2,1,0:T(8,128)(2,1)S(1)} collective-permute-done((bf16[2,128,128]{2,1,0:T(8,128)(2,1)S(1)}, bf16[2,128,128]{2,1,0:T(8,128)(2,1)S(1)}, u32[]{:S(2)}, u32[]{:S(2)}) %collective-permute-start.17) | collective-permute-done | bytes 65568 | tf_op jit(solution)/shard_map/ppermute | solution.py:374
  45.1 0.5 %collective-permute-done.18.refs_4_ = bf16[2,128,128]{2,1,0:T(8,128)(2,1)S(1)} collective-permute-done((bf16[2,128,128]{2,1,0:T(8,128)(2,1)S(1)}, bf16[2,128,128]{2,1,0:T(8,128)(2,1)S(1)}, u32[]{:S(2)}, u32[]{:S(2)}) %collective-permute-start.18) | collective-permute-done | bytes 65568 | tf_op jit(solution)/shard_map/ppermute | solution.py:374
  45.6 0.8 %assemble.3 = bf16[128,2048]{1,0:T(8,128)(2,1)} custom-call(bf16[128,2048]{1,0:T(8,128)(2,1)} %assemble.2.refs_0_, bf16[2,128,128]{2,1,0:T(8,128)(2,1)S(1)} %get-tuple-element.47.refs_1_, bf16[2,128,128]{2,1,0:T(8,128)(2,1)S(1)} %collective-permute-done.16.refs_2_, ...), custom_call_target="tpu_custom_call", output_to_operand_aliasing={{}: (0, {})} | custom-call | flops 1073741824 | bytes 33554432 | tf_op jit(solution)/shard_map/assemble/pallas_call | solution.py:356
  (6 shorter events, 0.0 us)
Async XLA Ops:
  0.0 12.0 %copy-start = (bf16[512,2048]{1,0:T(8,128)(2,1)S(1)}, bf16[512,2048]{1,0:T(8,128)(2,1)}, u32[]{:S(2)}) copy-start(bf16[512,2048]{1,0:T(8,128)(2,1)} %queries.5) | copy-start | bytes 6291460
  0.0 12.0 %copy-start.1 = (bf16[512,512]{1,0:T(8,128)(2,1)S(1)}, bf16[512,512]{1,0:T(8,128)(2,1)}, u32[]{:S(2)}) copy-start(bf16[512,512]{1,0:T(8,128)(2,1)} %keys.5) | copy-start | bytes 1572868
  0.0 12.0 %copy-start.2 = (bf16[512,512]{1,0:T(8,128)(2,1)S(1)}, bf16[512,512]{1,0:T(8,128)(2,1)}, u32[]{:S(2)}) copy-start(bf16[512,512]{1,0:T(8,128)(2,1)} %values.5) | copy-start | bytes 1572868
  0.0 12.0 %copy-start.3 = (s32[2048]{0:T(1024)S(1)}, s32[2048]{0:T(1024)}, u32[]{:S(2)}) copy-start(s32[2048]{0:T(1024)} %param.7) | copy-start | bytes 24580
  1.7 10.0 %collective-permute-start = (bf16[1024,128]{1,0:T(8,128)(2,1)S(1)}, bf16[1024,128]{1,0:T(8,128)(2,1)S(1)}, u32[]{:S(2)}, u32[]{:S(2)}) collective-permute-start(bf16[1024,128]{1,0:T(8,128)(2,1)S(1)} %get-tuple-element.28), channel_id=1, source_target_pairs={{0,4},{4,0},{8,12},{12,8},{1,5},{5,1},{9,13},{13,9},{2,6},{6,2},{1... | collective-permute-start | bytes 786440 | tf_op jit(solution)/shard_map/ppermute | solution.py:380
  2.2 9.8 %collective-permute-start.3 = (bf16[2,512,128]{2,1,0:T(8,128)(2,1)S(1)}, bf16[2,512,128]{2,1,0:T(8,128)(2,1)S(1)}, u32[]{:S(2)}, u32[]{:S(2)}) collective-permute-start(bf16[2,512,128]{2,1,0:T(8,128)(2,1)S(1)} %get-tuple-element.31), channel_id=1, source_target_pairs={{0,1},{1,0},{2,3},{3,2},{4,5},{5,4},{6,7},{7,6},{8,9},{9,8},{10,11... | collective-permute-start | bytes 786440 | tf_op jit(solution)/shard_map/ppermute | solution.py:374
  4.8 4.3 %collective-permute-start.1 = (bf16[256,128]{1,0:T(8,128)(2,1)S(1)}, bf16[256,128]{1,0:T(8,128)(2,1)S(1)}, u32[]{:S(2)}, u32[]{:S(2)}) collective-permute-start(bf16[256,128]{1,0:T(8,128)(2,1)S(1)} %get-tuple-element.29), channel_id=1, source_target_pairs={{0,8},{4,12},{8,0},{12,4},{1,9},{5,13},{9,1},{13,5},{2,10},{6,14},... | collective-permute-start | bytes 196616 | tf_op jit(solution)/shard_map/ppermute | solution.py:380
  6.3 4.9 %collective-permute-start.2 = (bf16[256,128]{1,0:T(8,128)(2,1)S(1)}, bf16[256,128]{1,0:T(8,128)(2,1)S(1)}, u32[]{:S(2)}, u32[]{:S(2)}) collective-permute-start(bf16[256,128]{1,0:T(8,128)(2,1)S(1)} %get-tuple-element.30), channel_id=1, source_target_pairs={{0,12},{4,8},{8,4},{12,0},{1,13},{5,9},{9,5},{13,1},{2,14},{6,10},... | collective-permute-start | bytes 196616 | tf_op jit(solution)/shard_map/ppermute | solution.py:380
  6.4 12.9 %collective-permute-start.8 = (bf16[2,512,128]{2,1,0:T(8,128)(2,1)S(1)}, bf16[2,512,128]{2,1,0:T(8,128)(2,1)S(1)}, u32[]{:S(2)}, u32[]{:S(2)}) collective-permute-start(bf16[2,512,128]{2,1,0:T(8,128)(2,1)S(1)} %get-tuple-element.36), channel_id=1, source_target_pairs={{0,1},{1,0},{2,3},{3,2},{4,5},{5,4},{6,7},{7,6},{8,9},{9,8},{10,11... | collective-permute-start | bytes 786440 | tf_op jit(solution)/shard_map/ppermute | solution.py:374
  9.1 9.2 %collective-permute-start.6 = (bf16[768,128]{1,0:T(8,128)(2,1)S(1)}, bf16[768,128]{1,0:T(8,128)(2,1)S(1)}, u32[]{:S(2)}, u32[]{:S(2)}) collective-permute-start(bf16[768,128]{1,0:T(8,128)(2,1)S(1)} %get-tuple-element.34), channel_id=1, source_target_pairs={{0,8},{4,12},{8,0},{12,4},{1,9},{5,13},{9,1},{13,5},{2,10},{6,14},... | collective-permute-start | bytes 589832 | tf_op jit(solution)/shard_map/ppermute | solution.py:380
  11.3 7.3 %collective-permute-start.7 = (bf16[768,128]{1,0:T(8,128)(2,1)S(1)}, bf16[768,128]{1,0:T(8,128)(2,1)S(1)}, u32[]{:S(2)}, u32[]{:S(2)}) collective-permute-start(bf16[768,128]{1,0:T(8,128)(2,1)S(1)} %get-tuple-element.35), channel_id=1, source_target_pairs={{0,12},{4,8},{8,4},{12,0},{1,13},{5,9},{9,5},{13,1},{2,14},{6,10},... | collective-permute-start | bytes 589832 | tf_op jit(solution)/shard_map/ppermute | solution.py:380
  14.0 13.0 %collective-permute-start.4 = (bf16[528,128]{1,0:T(8,128)(2,1)S(1)}, bf16[528,128]{1,0:T(8,128)(2,1)S(1)}, u32[]{:S(2)}, u32[]{:S(2)}) collective-permute-start(bf16[528,128]{1,0:T(8,128)(2,1)S(1)} %get-tuple-element.32.refs_0_), channel_id=1, source_target_pairs={{0,2},{1,3},{2,0},{3,1},{4,6},{5,7},{6,4},{7,5},{8,10},{9,11},{10,... | collective-permute-start | bytes 405512 | tf_op jit(solution)/shard_map/ppermute | solution.py:389
  16.5 13.3 %collective-permute-start.5 = (bf16[528,128]{1,0:T(8,128)(2,1)S(1)}, bf16[528,128]{1,0:T(8,128)(2,1)S(1)}, u32[]{:S(2)}, u32[]{:S(2)}) collective-permute-start(bf16[528,128]{1,0:T(8,128)(2,1)S(1)} %get-tuple-element.33), channel_id=1, source_target_pairs={{0,3},{1,2},{2,1},{3,0},{4,7},{5,6},{6,5},{7,4},{8,11},{9,10},{10,... | collective-permute-start | bytes 405512 | tf_op jit(solution)/shard_map/ppermute | solution.py:389
  24.1 9.2 %collective-permute-start.9 = (bf16[528,128]{1,0:T(8,128)(2,1)S(1)}, bf16[528,128]{1,0:T(8,128)(2,1)S(1)}, u32[]{:S(2)}, u32[]{:S(2)}) collective-permute-start(bf16[528,128]{1,0:T(8,128)(2,1)S(1)} %get-tuple-element.38), channel_id=1, source_target_pairs={{0,1},{1,0},{2,3},{3,2},{4,5},{5,4},{6,7},{7,6},{8,9},{9,8},{10,11... | collective-permute-start | bytes 405512 | tf_op jit(solution)/shard_map/ppermute | solution.py:394
  24.7 11.0 %collective-permute-start.13 = (bf16[528,128]{1,0:T(8,128)(2,1)S(1)}, bf16[528,128]{1,0:T(8,128)(2,1)S(1)}, u32[]{:S(2)}, u32[]{:S(2)}) collective-permute-start(bf16[528,128]{1,0:T(8,128)(2,1)S(1)} %get-tuple-element.44), channel_id=1, source_target_pairs={{0,1},{1,0},{2,3},{3,2},{4,5},{5,4},{6,7},{7,6},{8,9},{9,8},{10,11... | collective-permute-start | bytes 405512 | tf_op jit(solution)/shard_map/ppermute | solution.py:394
  26.2 13.2 %collective-permute-start.14 = (bf16[528,128]{1,0:T(8,128)(2,1)S(1)}, bf16[528,128]{1,0:T(8,128)(2,1)S(1)}, u32[]{:S(2)}, u32[]{:S(2)}) collective-permute-start(bf16[528,128]{1,0:T(8,128)(2,1)S(1)} %get-tuple-element.45), channel_id=1, source_target_pairs={{0,2},{1,3},{2,0},{3,1},{4,6},{5,7},{6,4},{7,5},{8,10},{9,11},{10,... | collective-permute-start | bytes 405512 | tf_op jit(solution)/shard_map/ppermute | solution.py:389
  27.0 12.4 %collective-permute-start.15 = (bf16[528,128]{1,0:T(8,128)(2,1)S(1)}, bf16[528,128]{1,0:T(8,128)(2,1)S(1)}, u32[]{:S(2)}, u32[]{:S(2)}) collective-permute-start(bf16[528,128]{1,0:T(8,128)(2,1)S(1)} %get-tuple-element.46), channel_id=1, source_target_pairs={{0,3},{1,2},{2,1},{3,0},{4,7},{5,6},{6,5},{7,4},{8,11},{9,10},{10,... | collective-permute-start | bytes 405512 | tf_op jit(solution)/shard_map/ppermute | solution.py:389
  34.1 6.8 %collective-permute-start.10 = (bf16[2,128,128]{2,1,0:T(8,128)(2,1)S(1)}, bf16[2,128,128]{2,1,0:T(8,128)(2,1)S(1)}, u32[]{:S(2)}, u32[]{:S(2)}) collective-permute-start(bf16[2,128,128]{2,1,0:T(8,128)(2,1)S(1)} %get-tuple-element.40), channel_id=1, source_target_pairs={{0,4},{4,0},{8,12},{12,8},{1,5},{5,1},{9,13},{13,9},{2,6},{6,2},{1... | collective-permute-start | bytes 196616 | tf_op jit(solution)/shard_map/ppermute | solution.py:374
  34.1 7.9 %collective-permute-start.11 = (bf16[2,128,128]{2,1,0:T(8,128)(2,1)S(1)}, bf16[2,128,128]{2,1,0:T(8,128)(2,1)S(1)}, u32[]{:S(2)}, u32[]{:S(2)}) collective-permute-start(bf16[2,128,128]{2,1,0:T(8,128)(2,1)S(1)} %get-tuple-element.41), channel_id=1, source_target_pairs={{0,8},{4,12},{8,0},{12,4},{1,9},{5,13},{9,1},{13,5},{2,10},{6,14},... | collective-permute-start | bytes 196616 | tf_op jit(solution)/shard_map/ppermute | solution.py:374
  35.8 6.3 %collective-permute-start.12 = (bf16[2,128,128]{2,1,0:T(8,128)(2,1)S(1)}, bf16[2,128,128]{2,1,0:T(8,128)(2,1)S(1)}, u32[]{:S(2)}, u32[]{:S(2)}) collective-permute-start(bf16[2,128,128]{2,1,0:T(8,128)(2,1)S(1)} %get-tuple-element.42), channel_id=1, source_target_pairs={{0,12},{4,8},{8,4},{12,0},{1,13},{5,9},{9,5},{13,1},{2,14},{6,10},... | collective-permute-start | bytes 196616 | tf_op jit(solution)/shard_map/ppermute | solution.py:374
  40.1 2.7 %collective-permute-start.16 = (bf16[2,128,128]{2,1,0:T(8,128)(2,1)S(1)}, bf16[2,128,128]{2,1,0:T(8,128)(2,1)S(1)}, u32[]{:S(2)}, u32[]{:S(2)}) collective-permute-start(bf16[2,128,128]{2,1,0:T(8,128)(2,1)S(1)} %get-tuple-element.48), channel_id=1, source_target_pairs={{0,4},{4,0},{8,12},{12,8},{1,5},{5,1},{9,13},{13,9},{2,6},{6,2},{1... | collective-permute-start | bytes 196616 | tf_op jit(solution)/shard_map/ppermute | solution.py:374
  40.2 5.0 %collective-permute-start.17 = (bf16[2,128,128]{2,1,0:T(8,128)(2,1)S(1)}, bf16[2,128,128]{2,1,0:T(8,128)(2,1)S(1)}, u32[]{:S(2)}, u32[]{:S(2)}) collective-permute-start(bf16[2,128,128]{2,1,0:T(8,128)(2,1)S(1)} %get-tuple-element.49), channel_id=1, source_target_pairs={{0,8},{4,12},{8,0},{12,4},{1,9},{5,13},{9,1},{13,5},{2,10},{6,14},... | collective-permute-start | bytes 196616 | tf_op jit(solution)/shard_map/ppermute | solution.py:374
  40.9 4.7 %collective-permute-start.18 = (bf16[2,128,128]{2,1,0:T(8,128)(2,1)S(1)}, bf16[2,128,128]{2,1,0:T(8,128)(2,1)S(1)}, u32[]{:S(2)}, u32[]{:S(2)}) collective-permute-start(bf16[2,128,128]{2,1,0:T(8,128)(2,1)S(1)} %get-tuple-element.50), channel_id=1, source_target_pairs={{0,12},{4,8},{8,4},{12,0},{1,13},{5,9},{9,5},{13,1},{2,14},{6,10},... | collective-permute-start | bytes 196616 | tf_op jit(solution)/shard_map/ppermute | solution.py:374

commit v9 on v7

--- a/solution.py
+++ b/solution.py
@@ -339,7 +339,7 @@
     pieces, (out, sem) = refs[-6:-2], refs[-2:]
     column = lax.axis_index("pb")
     pairs = []
-    for d, piece in enumerate(pieces):
+    for d, piece in zip((3, 2, 1, 0), pieces):
         for half in range(2):
             pairs.append((piece.at[half], out.at[:, aligned((column ^ d) * 4 + 2 * half + chunk, HEAD_DIM)]))
     for copy in run_copies(pairs, sem):
@@ -387,7 +387,8 @@
     blocks = ()
     for chunk, (own, beside) in enumerate(parts[1::2]):
         blocks = merge([own, lax.ppermute(beside, "ka", swaps[1]), *far[chunk]], [*blocks[:1], *marks[chunk:chunk + 1]])
-        result = (assemble(chunk, [blocks[0]] + travel(blocks[1:], "pb"), result),)
+        others = [lax.ppermute(blocks[d], "pb", swaps[d]) for d in (3, 2, 1)]
+        result = (assemble(chunk, others + [blocks[0]], result),)
     return result[0]
 
 

time: 46.7 us -> 46.2 us (0.989)
    ppermute x8 -> x2, waiting for transfers between devices: 3.13 us -> 0.31 us  [travel(): lax.ppermute(piece, axis, swap)]
    ppermute x8 -> x2, starting transfers between devices: 5.63 us -> 3.06 us  [travel(): lax.ppermute(piece, axis, swap)]
    ppermute x0 -> x6, waiting for transfers between devices: none -> 2.37 us  [by_pairs(): others = [lax.ppermute(blocks[d], 'pb', swaps[d]) for d in (3, 2, 1)]]
    ppermute x0 -> x6, starting transfers between devices: none -> 2.24 us  [by_pairs(): others = [lax.ppermute(blocks[d], 'pb', swaps[d]) for d in (3, 2, 1)]]
where the time goes in v9:
time: 46.2 us; the launch traced here: 46 us
  starting transfers between devices  18.3 us (40%)
  waiting for transfers between devices  15.2 us (33%)
  Pallas kernels  12.2 us (26%)
    pallas_call x3, Pallas kernels, attend(): pl.pallas_call(functools.partial(attend_kernel, chunk, fars, skips, len(a...  7.44 us
    ppermute x2, starting transfers between devices, by_pairs(): lax.ppermute(cross, 'ka', swaps[3])  5.02 us
    ppermute x2, waiting for transfers between devices, by_pairs(): lax.ppermute(same, 'ka', swaps[2])  4.9 us
    ppermute x5, starting transfers between devices, by_pairs(): lax.ppermute(piece, 'pb', swaps[d])  4.64 us
    ppermute x2, waiting for transfers between devices, by_pairs(): lax.ppermute(beside, 'ka', swaps[1])  4.28 us
    ppermute x5, waiting for transfers between devices, by_pairs(): lax.ppermute(piece, 'pb', swaps[d])  3.37 us
    ppermute x2, starting transfers between devices, travel(): lax.ppermute(piece, axis, swap)  3.06 us
    ppermute x6, waiting for transfers between devices, by_pairs(): others = [lax.ppermute(blocks[d], 'pb', swaps[d]) for d in (3, 2, 1)]  2.37 us
  transfers between devices with their start and end apart: 19, of which 9 were waited for; matrix products, arithmetic and copies ran while one was open for 0% of the time, Pallas kernels for 21%

profile of v9, /device:TPU:0, one launch (start us, length us, event | category | flops | bytes accessed | tf_op | source)
XLA Modules:
  0.0 46.0 jit_solution(10383135081222660167)
XLA Ops:
  0.0 1.6 %pack.1 = (bf16[2,512,128]{2,1,0:T(8,128)(2,1)S(1)}, bf16[2,512,128]{2,1,0:T(8,128)(2,1)S(1)}, bf16[1024,128]{1,0:T(8,128)(2,1)S(1)}, bf16[256,128]{1,0:T(8,128)...) custom-call(bf16[512,2048]{1,0:T(8,128)(2,1)} %queries.7, ...), custom_call_target="tpu_custom_call" | custom-call | tf_op jit(solution)/shard_map/pack/pallas_call | solution.py:162
  1.7 0.5 %collective-permute-start = (bf16[1024,128]{1,0:T(8,128)(2,1)S(1)}, bf16[1024,128]{1,0:T(8,128)(2,1)S(1)}, u32[]{:S(2)}, u32[]{:S(2)}) collective-permute-start(bf16[1024,128]{1,0:T(8,128)(2,1)S(1)} %get-tuple-element.28), channel_id=1, source_target_pairs={{0,4},{4,0},{8,12},{12,8},{1,5},{5,1},{9,13},{13,9},{2,6},{6,2},{1... | collective-permute-start | bytes 786440 | tf_op jit(solution)/shard_map/ppermute | solution.py:375
  2.2 2.6 %collective-permute-start.3 = (bf16[2,512,128]{2,1,0:T(8,128)(2,1)S(1)}, bf16[2,512,128]{2,1,0:T(8,128)(2,1)S(1)}, u32[]{:S(2)}, u32[]{:S(2)}) collective-permute-start(bf16[2,512,128]{2,1,0:T(8,128)(2,1)S(1)} %get-tuple-element.31), channel_id=1, source_target_pairs={{0,1},{1,0},{2,3},{3,2},{4,5},{5,4},{6,7},{7,6},{8,9},{9,8},{10,11... | collective-permute-start | bytes 786440 | tf_op jit(solution)/shard_map/ppermute | solution.py:369
  4.8 1.5 %collective-permute-start.1 = (bf16[256,128]{1,0:T(8,128)(2,1)S(1)}, bf16[256,128]{1,0:T(8,128)(2,1)S(1)}, u32[]{:S(2)}, u32[]{:S(2)}) collective-permute-start(bf16[256,128]{1,0:T(8,128)(2,1)S(1)} %get-tuple-element.29), channel_id=1, source_target_pairs={{0,8},{4,12},{8,0},{12,4},{1,9},{5,13},{9,1},{13,5},{2,10},{6,14},... | collective-permute-start | bytes 196616 | tf_op jit(solution)/shard_map/ppermute | solution.py:375
  6.3 0.0 collective-permute-start.2
  6.4 0.4 collective-permute-start.12
  6.8 2.3 %collective-permute-done.1.refs_1_ = bf16[256,128]{1,0:T(8,128)(2,1)S(1)} collective-permute-done((bf16[256,128]{1,0:T(8,128)(2,1)S(1)}, bf16[256,128]{1,0:T(8,128)(2,1)S(1)}, u32[]{:S(2)}, u32[]{:S(2)}) %collective-permute-start.1) | collective-permute-done | bytes 65568 | tf_op jit(solution)/shard_map/ppermute | solution.py:375
  9.1 2.2 %collective-permute-start.6 = (bf16[768,128]{1,0:T(8,128)(2,1)S(1)}, bf16[768,128]{1,0:T(8,128)(2,1)S(1)}, u32[]{:S(2)}, u32[]{:S(2)}) collective-permute-start(bf16[768,128]{1,0:T(8,128)(2,1)S(1)} %get-tuple-element.34), channel_id=1, source_target_pairs={{0,8},{4,12},{8,0},{12,4},{1,9},{5,13},{9,1},{13,5},{2,10},{6,14},... | collective-permute-start | bytes 589832 | tf_op jit(solution)/shard_map/ppermute | solution.py:375
  11.3 0.0 collective-permute-done.2.refs_2_
  11.3 0.4 collective-permute-start.7
  11.7 0.0 collective-permute-done.refs_0_.refs_1_
  11.7 0.3 collective-permute-done.3.refs_3_.refs_4_
  12.0 0.0 copy-done
  12.0 0.0 copy-done.3
  12.0 2.0 %attend_far.1 = (bf16[528,128]{1,0:T(8,128)(2,1)S(1)}, bf16[528,128]{1,0:T(8,128)(2,1)S(1)}) custom-call(s32[16,128]{1,0:T(8,128)S(1)} %bitcast.1, bf16[512,2048]{1,0:T(8,128)(2,1)S(1)} %copy-done, bf16[512,512]{1,0:T(8,128)(2,1)S(1)} %copy-done.1, bf16[512,512]{1,0:T(8,128)(2,1)S(1)} %copy-done.2, ...), custom_call_target="tpu_custom_call" | custom-call | flops 1024 | bytes 1024 | tf_op jit(solution)/shard_map/attend_far/pallas_call | solution.py:254
  14.0 3.5 %collective-permute-start.5 = (bf16[528,128]{1,0:T(8,128)(2,1)S(1)}, bf16[528,128]{1,0:T(8,128)(2,1)S(1)}, u32[]{:S(2)}, u32[]{:S(2)}) collective-permute-start(bf16[528,128]{1,0:T(8,128)(2,1)S(1)} %get-tuple-element.33), channel_id=1, source_target_pairs={{0,3},{1,2},{2,1},{3,0},{4,7},{5,6},{6,5},{7,4},{8,11},{9,10},{10,... | collective-permute-start | bytes 405512 | tf_op jit(solution)/shard_map/ppermute | solution.py:384
  17.5 0.0 collective-permute-start.4
  17.5 0.0 collective-permute-done.6.refs_2_
  17.5 1.0 %collective-permute-done.7.refs_3_ = bf16[768,128]{1,0:T(8,128)(2,1)S(1)} collective-permute-done((bf16[768,128]{1,0:T(8,128)(2,1)S(1)}, bf16[768,128]{1,0:T(8,128)(2,1)S(1)}, u32[]{:S(2)}, u32[]{:S(2)}) %collective-permute-start.7) | collective-permute-done | bytes 196640 | tf_op jit(solution)/shard_map/ppermute | solution.py:375
  18.5 2.1 %attend.2 = (bf16[528,128]{1,0:T(8,128)(2,1)S(1)}, bf16[528,128]{1,0:T(8,128)(2,1)S(1)}) custom-call(s32[16,128]{1,0:T(8,128)S(1)} %bitcast.2, bf16[512,2048]{1,0:T(8,128)(2,1)S(1)} %copy-done, bf16[512,512]{1,0:T(8,128)(2,1)S(1)} %copy-done.1, bf16[512,512]{1,0:T(8,128)(2,1)S(1)} %copy-done.2, bf16[528,128]{1,0:T(8,128)(2,1)S(1)} %get-tuple-element.32.refs_0_, ...), custom_call_target="tpu_custom_call" | custom-call | flops 1024 | bytes 1024 | tf_op jit(solution)/shard_map/attend/pallas_call | solution.py:254
  20.7 0.4 collective-permute-start.8
  21.1 0.0 collective-permute-done.12.refs_4_
  21.1 3.3 %attend.3 = (bf16[528,128]{1,0:T(8,128)(2,1)S(1)}, bf16[528,128]{1,0:T(8,128)(2,1)S(1)}, bf16[528,128]{1,0:T(8,128)(2,1)S(1)}, bf16[528,128]{1,0:T(8,128)(2,1)S(1)}) custom-call(s32[16,128]{1,0:T(8,128)S(1)} %bitcast.3, bf16[512,2048]{1,0:T(8,128)(2,1)S(1)} %copy-done, bf16[512,512]{1,0:T(8,128)(2,1)S(1)} %copy-done.1, bf16[512,512]{1,0:T(8,128)(2,1)S(1)} %copy-done.2, ...), custom_call_target="tpu_custom_call" | custom-call | flops 1024 | bytes 1024 | tf_op jit(solution)/shard_map/attend/pallas_call | solution.py:254
  24.4 1.7 %collective-permute-start.13 = (bf16[528,128]{1,0:T(8,128)(2,1)S(1)}, bf16[528,128]{1,0:T(8,128)(2,1)S(1)}, u32[]{:S(2)}, u32[]{:S(2)}) collective-permute-start(bf16[528,128]{1,0:T(8,128)(2,1)S(1)} %get-tuple-element.44), channel_id=1, source_target_pairs={{0,1},{1,0},{2,3},{3,2},{4,5},{5,4},{6,7},{7,6},{8,9},{9,8},{10,11... | collective-permute-start | bytes 405512 | tf_op jit(solution)/shard_map/ppermute | solution.py:389
  26.1 1.2 %collective-permute-start.14 = (bf16[528,128]{1,0:T(8,128)(2,1)S(1)}, bf16[528,128]{1,0:T(8,128)(2,1)S(1)}, u32[]{:S(2)}, u32[]{:S(2)}) collective-permute-start(bf16[528,128]{1,0:T(8,128)(2,1)S(1)} %get-tuple-element.45), channel_id=1, source_target_pairs={{0,2},{1,3},{2,0},{3,1},{4,6},{5,7},{6,4},{7,5},{8,10},{9,11},{10,... | collective-permute-start | bytes 405512 | tf_op jit(solution)/shard_map/ppermute | solution.py:384
  27.3 0.0 collective-permute-done.5.b.refs_4_
  27.4 1.5 %collective-permute-start.15 = (bf16[528,128]{1,0:T(8,128)(2,1)S(1)}, bf16[528,128]{1,0:T(8,128)(2,1)S(1)}, u32[]{:S(2)}, u32[]{:S(2)}) collective-permute-start(bf16[528,128]{1,0:T(8,128)(2,1)S(1)} %get-tuple-element.46), channel_id=1, source_target_pairs={{0,3},{1,2},{2,1},{3,0},{4,7},{5,6},{6,5},{7,4},{8,11},{9,10},{10,... | collective-permute-start | bytes 405512 | tf_op jit(solution)/shard_map/ppermute | solution.py:384
  28.9 0.4 collective-permute-done.4.a.refs_3_
  29.2 2.7 %collective-permute-done.8.refs_2_ = bf16[528,128]{1,0:T(8,128)(2,1)S(1)} collective-permute-done((bf16[528,128]{1,0:T(8,128)(2,1)S(1)}, bf16[528,128]{1,0:T(8,128)(2,1)S(1)}, u32[]{:S(2)}, u32[]{:S(2)}) %collective-permute-start.8) | collective-permute-done | bytes 135200 | tf_op jit(solution)/shard_map/ppermute | solution.py:389
  31.9 0.9 %merge.2 = (bf16[2,128,128]{2,1,0:T(8,128)(2,1)S(1)}, bf16[2,128,128]{2,1,0:T(8,128)(2,1)S(1)}, bf16[2,128,128]{2,1,0:T(8,128)(2,1)S(1)}, bf16[2,128,128]{2,1,0:T(8,128)(2,1)S(1)}) custom-call(f32[8,128]{1,0:T(8,128)S(1)} %mark.1.refs_0_, bf16[528,128]{1,0:T(8,128)(2,1)S(1)} %get-tuple-element.36.refs_1_.refs_0_, ...), custom_call_target="tpu_custom_call" | custom-call | flops 1024 | bytes 1024 | tf_op jit(solution)/shard_map/merge/pallas_call | solution.py:326
  32.8 0.1 collective-permute-start.9
  32.9 0.1 collective-permute-start.10
  33.0 1.6 %collective-permute-done.13.refs_2_ = bf16[528,128]{1,0:T(8,128)(2,1)S(1)} collective-permute-done((bf16[528,128]{1,0:T(8,128)(2,1)S(1)}, bf16[528,128]{1,0:T(8,128)(2,1)S(1)}, u32[]{:S(2)}, u32[]{:S(2)}) %collective-permute-start.13) | collective-permute-done | bytes 135200 | tf_op jit(solution)/shard_map/ppermute | solution.py:389
  34.6 0.2 collective-permute-start.11
  34.8 4.5 %collective-permute-done.14.refs_3_ = bf16[528,128]{1,0:T(8,128)(2,1)S(1)} collective-permute-done((bf16[528,128]{1,0:T(8,128)(2,1)S(1)}, bf16[528,128]{1,0:T(8,128)(2,1)S(1)}, u32[]{:S(2)}, u32[]{:S(2)}) %collective-permute-start.14) | collective-permute-done | bytes 135200 | tf_op jit(solution)/shard_map/ppermute | solution.py:384
  39.3 0.0 collective-permute-done.15.refs_4_
  39.3 0.7 %merge.3 = (bf16[2,128,128]{2,1,0:T(8,128)(2,1)S(1)}, bf16[2,128,128]{2,1,0:T(8,128)(2,1)S(1)}, bf16[2,128,128]{2,1,0:T(8,128)(2,1)S(1)}, bf16[2,128,128]{2,1,0:T(8,128)(2,1)S(1)}) custom-call(bf16[2,128,128]{2,1,0:T(8,128)(2,1)S(1)} %get-tuple-element.41.refs_3_.refs_0_, bf16[528,128]{1,0:T(8,128)(2,1)S(1)} %get-tuple-element.43.refs_1_, ...), custom_call_target="tpu_custom_call" | custom-call | flops 1024 | bytes 1024 | tf_op jit(solution)/shard_map/merge/pallas_call | solution.py:326
  40.0 0.1 collective-permute-start.16
  40.1 0.2 collective-permute-start.17
  40.4 0.0 collective-permute-done.9.refs_0_
  40.4 1.6 %collective-permute-start.18 = (bf16[2,128,128]{2,1,0:T(8,128)(2,1)S(1)}, bf16[2,128,128]{2,1,0:T(8,128)(2,1)S(1)}, u32[]{:S(2)}, u32[]{:S(2)}) collective-permute-start(bf16[2,128,128]{2,1,0:T(8,128)(2,1)S(1)} %get-tuple-element.49), channel_id=1, source_target_pairs={{0,4},{4,0},{8,12},{12,8},{1,5},{5,1},{9,13},{13,9},{2,6},{6,2},{1... | collective-permute-start | bytes 196616 | tf_op jit(solution)/shard_map/ppermute | solution.py:390
  41.9 0.0 collective-permute-done.10.refs_1_
  41.9 0.0 collective-permute-done.11.refs_2_
  41.9 0.8 %assemble.2.refs_0_ = bf16[128,2048]{1,0:T(8,128)(2,1)} custom-call(bf16[2,128,128]{2,1,0:T(8,128)(2,1)S(1)} %collective-permute-done.9.refs_0_, bf16[2,128,128]{2,1,0:T(8,128)(2,1)S(1)} %collective-permute-done.10.refs_1_, bf16[2,128,128]{2,1,0:T(8,128)(2,1)S(1)} %collective-permute-done.11.refs_2_, bf16[2,128,128]{2,1,0:T(8,128)(2,1)S(1)} %get-tuple-element.41.refs_3_.refs_0_), custom_call_target="tpu_custom_call" | custom-call | flops 1073741824 | bytes 33554432 | tf_op jit(solution)/shard_map/assemble/pallas_call | solution.py:351
  42.7 1.1 %collective-permute-done.16.refs_1_ = bf16[2,128,128]{2,1,0:T(8,128)(2,1)S(1)} collective-permute-done((bf16[2,128,128]{2,1,0:T(8,128)(2,1)S(1)}, bf16[2,128,128]{2,1,0:T(8,128)(2,1)S(1)}, u32[]{:S(2)}, u32[]{:S(2)}) %collective-permute-start.16) | collective-permute-done | bytes 65568 | tf_op jit(solution)/shard_map/ppermute | solution.py:390
  43.8 1.2 %collective-permute-done.17.refs_2_ = bf16[2,128,128]{2,1,0:T(8,128)(2,1)S(1)} collective-permute-done((bf16[2,128,128]{2,1,0:T(8,128)(2,1)S(1)}, bf16[2,128,128]{2,1,0:T(8,128)(2,1)S(1)}, u32[]{:S(2)}, u32[]{:S(2)}) %collective-permute-start.17) | collective-permute-done | bytes 65568 | tf_op jit(solution)/shard_map/ppermute | solution.py:390
  45.1 0.0 collective-permute-done.18.refs_3_
  45.1 0.8 %assemble.3 = bf16[128,2048]{1,0:T(8,128)(2,1)} custom-call(bf16[128,2048]{1,0:T(8,128)(2,1)} %assemble.2.refs_0_, bf16[2,128,128]{2,1,0:T(8,128)(2,1)S(1)} %collective-permute-done.16.refs_1_, bf16[2,128,128]{2,1,0:T(8,128)(2,1)S(1)} %collective-permute-done.17.refs_2_, ...), custom_call_target="tpu_custom_call", output_to_operand_aliasing={{}: (0, {})} | custom-call | flops 1073741824 | bytes 33554432 | tf_op jit(solution)/shard_map/assemble/pallas_call | solution.py:351
  (7 shorter events, 0.0 us)
Async XLA Ops:
  0.0 12.0 %copy-start.2 = (bf16[512,512]{1,0:T(8,128)(2,1)S(1)}, bf16[512,512]{1,0:T(8,128)(2,1)}, u32[]{:S(2)}) copy-start(bf16[512,512]{1,0:T(8,128)(2,1)} %values.7) | copy-start | bytes 1572868
  0.0 12.0 %copy-start.1 = (bf16[512,512]{1,0:T(8,128)(2,1)S(1)}, bf16[512,512]{1,0:T(8,128)(2,1)}, u32[]{:S(2)}) copy-start(bf16[512,512]{1,0:T(8,128)(2,1)} %keys.7) | copy-start | bytes 1572868
  0.0 12.0 %copy-start = (bf16[512,2048]{1,0:T(8,128)(2,1)S(1)}, bf16[512,2048]{1,0:T(8,128)(2,1)}, u32[]{:S(2)}) copy-start(bf16[512,2048]{1,0:T(8,128)(2,1)} %queries.7) | copy-start | bytes 6291460
  0.0 12.0 %copy-start.3 = (s32[2048]{0:T(1024)S(1)}, s32[2048]{0:T(1024)}, u32[]{:S(2)}) copy-start(s32[2048]{0:T(1024)} %param.7) | copy-start | bytes 24580
  1.7 10.0 %collective-permute-start = (bf16[1024,128]{1,0:T(8,128)(2,1)S(1)}, bf16[1024,128]{1,0:T(8,128)(2,1)S(1)}, u32[]{:S(2)}, u32[]{:S(2)}) collective-permute-start(bf16[1024,128]{1,0:T(8,128)(2,1)S(1)} %get-tuple-element.28), channel_id=1, source_target_pairs={{0,4},{4,0},{8,12},{12,8},{1,5},{5,1},{9,13},{13,9},{2,6},{6,2},{1... | collective-permute-start | bytes 786440 | tf_op jit(solution)/shard_map/ppermute | solution.py:375
  2.2 9.8 %collective-permute-start.3 = (bf16[2,512,128]{2,1,0:T(8,128)(2,1)S(1)}, bf16[2,512,128]{2,1,0:T(8,128)(2,1)S(1)}, u32[]{:S(2)}, u32[]{:S(2)}) collective-permute-start(bf16[2,512,128]{2,1,0:T(8,128)(2,1)S(1)} %get-tuple-element.31), channel_id=1, source_target_pairs={{0,1},{1,0},{2,3},{3,2},{4,5},{5,4},{6,7},{7,6},{8,9},{9,8},{10,11... | collective-permute-start | bytes 786440 | tf_op jit(solution)/shard_map/ppermute | solution.py:369
  4.8 4.3 %collective-permute-start.1 = (bf16[256,128]{1,0:T(8,128)(2,1)S(1)}, bf16[256,128]{1,0:T(8,128)(2,1)S(1)}, u32[]{:S(2)}, u32[]{:S(2)}) collective-permute-start(bf16[256,128]{1,0:T(8,128)(2,1)S(1)} %get-tuple-element.29), channel_id=1, source_target_pairs={{0,8},{4,12},{8,0},{12,4},{1,9},{5,13},{9,1},{13,5},{2,10},{6,14},... | collective-permute-start | bytes 196616 | tf_op jit(solution)/shard_map/ppermute | solution.py:375
  6.3 4.9 %collective-permute-start.2 = (bf16[256,128]{1,0:T(8,128)(2,1)S(1)}, bf16[256,128]{1,0:T(8,128)(2,1)S(1)}, u32[]{:S(2)}, u32[]{:S(2)}) collective-permute-start(bf16[256,128]{1,0:T(8,128)(2,1)S(1)} %get-tuple-element.30), channel_id=1, source_target_pairs={{0,12},{4,8},{8,4},{12,0},{1,13},{5,9},{9,5},{13,1},{2,14},{6,10},... | collective-permute-start | bytes 196616 | tf_op jit(solution)/shard_map/ppermute | solution.py:375
  6.4 14.7 %collective-permute-start.12 = (bf16[2,512,128]{2,1,0:T(8,128)(2,1)S(1)}, bf16[2,512,128]{2,1,0:T(8,128)(2,1)S(1)}, u32[]{:S(2)}, u32[]{:S(2)}) collective-permute-start(bf16[2,512,128]{2,1,0:T(8,128)(2,1)S(1)} %get-tuple-element.42), channel_id=1, source_target_pairs={{0,1},{1,0},{2,3},{3,2},{4,5},{5,4},{6,7},{7,6},{8,9},{9,8},{10,11... | collective-permute-start | bytes 786440 | tf_op jit(solution)/shard_map/ppermute | solution.py:369
  9.1 8.4 %collective-permute-start.6 = (bf16[768,128]{1,0:T(8,128)(2,1)S(1)}, bf16[768,128]{1,0:T(8,128)(2,1)S(1)}, u32[]{:S(2)}, u32[]{:S(2)}) collective-permute-start(bf16[768,128]{1,0:T(8,128)(2,1)S(1)} %get-tuple-element.34), channel_id=1, source_target_pairs={{0,8},{4,12},{8,0},{12,4},{1,9},{5,13},{9,1},{13,5},{2,10},{6,14},... | collective-permute-start | bytes 589832 | tf_op jit(solution)/shard_map/ppermute | solution.py:375
  11.3 7.3 %collective-permute-start.7 = (bf16[768,128]{1,0:T(8,128)(2,1)S(1)}, bf16[768,128]{1,0:T(8,128)(2,1)S(1)}, u32[]{:S(2)}, u32[]{:S(2)}) collective-permute-start(bf16[768,128]{1,0:T(8,128)(2,1)S(1)} %get-tuple-element.35), channel_id=1, source_target_pairs={{0,12},{4,8},{8,4},{12,0},{1,13},{5,9},{9,5},{13,1},{2,14},{6,10},... | collective-permute-start | bytes 589832 | tf_op jit(solution)/shard_map/ppermute | solution.py:375
  14.0 13.3 %collective-permute-start.5 = (bf16[528,128]{1,0:T(8,128)(2,1)S(1)}, bf16[528,128]{1,0:T(8,128)(2,1)S(1)}, u32[]{:S(2)}, u32[]{:S(2)}) collective-permute-start(bf16[528,128]{1,0:T(8,128)(2,1)S(1)} %get-tuple-element.33), channel_id=1, source_target_pairs={{0,3},{1,2},{2,1},{3,0},{4,7},{5,6},{6,5},{7,4},{8,11},{9,10},{10,... | collective-permute-start | bytes 405512 | tf_op jit(solution)/shard_map/ppermute | solution.py:384
  17.5 11.8 %collective-permute-start.4 = (bf16[528,128]{1,0:T(8,128)(2,1)S(1)}, bf16[528,128]{1,0:T(8,128)(2,1)S(1)}, u32[]{:S(2)}, u32[]{:S(2)}) collective-permute-start(bf16[528,128]{1,0:T(8,128)(2,1)S(1)} %get-tuple-element.32.refs_0_), channel_id=1, source_target_pairs={{0,2},{1,3},{2,0},{3,1},{4,6},{5,7},{6,4},{7,5},{8,10},{9,11},{10,... | collective-permute-start | bytes 405512 | tf_op jit(solution)/shard_map/ppermute | solution.py:384
  20.7 11.2 %collective-permute-start.8 = (bf16[528,128]{1,0:T(8,128)(2,1)S(1)}, bf16[528,128]{1,0:T(8,128)(2,1)S(1)}, u32[]{:S(2)}, u32[]{:S(2)}) collective-permute-start(bf16[528,128]{1,0:T(8,128)(2,1)S(1)} %get-tuple-element.37), channel_id=1, source_target_pairs={{0,1},{1,0},{2,3},{3,2},{4,5},{5,4},{6,7},{7,6},{8,9},{9,8},{10,11... | collective-permute-start | bytes 405512 | tf_op jit(solution)/shard_map/ppermute | solution.py:389
  24.4 10.1 %collective-permute-start.13 = (bf16[528,128]{1,0:T(8,128)(2,1)S(1)}, bf16[528,128]{1,0:T(8,128)(2,1)S(1)}, u32[]{:S(2)}, u32[]{:S(2)}) collective-permute-start(bf16[528,128]{1,0:T(8,128)(2,1)S(1)} %get-tuple-element.44), channel_id=1, source_target_pairs={{0,1},{1,0},{2,3},{3,2},{4,5},{5,4},{6,7},{7,6},{8,9},{9,8},{10,11... | collective-permute-start | bytes 405512 | tf_op jit(solution)/shard_map/ppermute | solution.py:389
  26.1 13.2 %collective-permute-start.14 = (bf16[528,128]{1,0:T(8,128)(2,1)S(1)}, bf16[528,128]{1,0:T(8,128)(2,1)S(1)}, u32[]{:S(2)}, u32[]{:S(2)}) collective-permute-start(bf16[528,128]{1,0:T(8,128)(2,1)S(1)} %get-tuple-element.45), channel_id=1, source_target_pairs={{0,2},{1,3},{2,0},{3,1},{4,6},{5,7},{6,4},{7,5},{8,10},{9,11},{10,... | collective-permute-start | bytes 405512 | tf_op jit(solution)/shard_map/ppermute | solution.py:384
  27.4 12.0 %collective-permute-start.15 = (bf16[528,128]{1,0:T(8,128)(2,1)S(1)}, bf16[528,128]{1,0:T(8,128)(2,1)S(1)}, u32[]{:S(2)}, u32[]{:S(2)}) collective-permute-start(bf16[528,128]{1,0:T(8,128)(2,1)S(1)} %get-tuple-element.46), channel_id=1, source_target_pairs={{0,3},{1,2},{2,1},{3,0},{4,7},{5,6},{6,5},{7,4},{8,11},{9,10},{10,... | collective-permute-start | bytes 405512 | tf_op jit(solution)/shard_map/ppermute | solution.py:384
  32.8 7.5 %collective-permute-start.9 = (bf16[2,128,128]{2,1,0:T(8,128)(2,1)S(1)}, bf16[2,128,128]{2,1,0:T(8,128)(2,1)S(1)}, u32[]{:S(2)}, u32[]{:S(2)}) collective-permute-start(bf16[2,128,128]{2,1,0:T(8,128)(2,1)S(1)} %get-tuple-element.38), channel_id=1, source_target_pairs={{0,12},{4,8},{8,4},{12,0},{1,13},{5,9},{9,5},{13,1},{2,14},{6,10},... | collective-permute-start | bytes 196616 | tf_op jit(solution)/shard_map/ppermute | solution.py:390
  32.9 9.0 %collective-permute-start.10 = (bf16[2,128,128]{2,1,0:T(8,128)(2,1)S(1)}, bf16[2,128,128]{2,1,0:T(8,128)(2,1)S(1)}, u32[]{:S(2)}, u32[]{:S(2)}) collective-permute-start(bf16[2,128,128]{2,1,0:T(8,128)(2,1)S(1)} %get-tuple-element.39), channel_id=1, source_target_pairs={{0,8},{4,12},{8,0},{12,4},{1,9},{5,13},{9,1},{13,5},{2,10},{6,14},... | collective-permute-start | bytes 196616 | tf_op jit(solution)/shard_map/ppermute | solution.py:390
  34.6 7.3 %collective-permute-start.11 = (bf16[2,128,128]{2,1,0:T(8,128)(2,1)S(1)}, bf16[2,128,128]{2,1,0:T(8,128)(2,1)S(1)}, u32[]{:S(2)}, u32[]{:S(2)}) collective-permute-start(bf16[2,128,128]{2,1,0:T(8,128)(2,1)S(1)} %get-tuple-element.40), channel_id=1, source_target_pairs={{0,4},{4,0},{8,12},{12,8},{1,5},{5,1},{9,13},{13,9},{2,6},{6,2},{1... | collective-permute-start | bytes 196616 | tf_op jit(solution)/shard_map/ppermute | solution.py:390
  40.0 3.8 %collective-permute-start.16 = (bf16[2,128,128]{2,1,0:T(8,128)(2,1)S(1)}, bf16[2,128,128]{2,1,0:T(8,128)(2,1)S(1)}, u32[]{:S(2)}, u32[]{:S(2)}) collective-permute-start(bf16[2,128,128]{2,1,0:T(8,128)(2,1)S(1)} %get-tuple-element.47), channel_id=1, source_target_pairs={{0,12},{4,8},{8,4},{12,0},{1,13},{5,9},{9,5},{13,1},{2,14},{6,10},... | collective-permute-start | bytes 196616 | tf_op jit(solution)/shard_map/ppermute | solution.py:390
  40.1 4.9 %collective-permute-start.17 = (bf16[2,128,128]{2,1,0:T(8,128)(2,1)S(1)}, bf16[2,128,128]{2,1,0:T(8,128)(2,1)S(1)}, u32[]{:S(2)}, u32[]{:S(2)}) collective-permute-start(bf16[2,128,128]{2,1,0:T(8,128)(2,1)S(1)} %get-tuple-element.48), channel_id=1, source_target_pairs={{0,8},{4,12},{8,0},{12,4},{1,9},{5,13},{9,1},{13,5},{2,10},{6,14},... | collective-permute-start | bytes 196616 | tf_op jit(solution)/shard_map/ppermute | solution.py:390
  40.4 4.7 %collective-permute-start.18 = (bf16[2,128,128]{2,1,0:T(8,128)(2,1)S(1)}, bf16[2,128,128]{2,1,0:T(8,128)(2,1)S(1)}, u32[]{:S(2)}, u32[]{:S(2)}) collective-permute-start(bf16[2,128,128]{2,1,0:T(8,128)(2,1)S(1)} %get-tuple-element.49), channel_id=1, source_target_pairs={{0,4},{4,0},{8,12},{12,8},{1,5},{5,1},{9,13},{13,9},{2,6},{6,2},{1... | collective-permute-start | bytes 196616 | tf_op jit(solution)/shard_map/ppermute | solution.py:390
